TPU v7x, 32 devices: a whole 2x2x4 slice. The times are simulated.
32 devices in a mesh: seq: 16 (over z, y, x), dp: 2 (over core).
Axes of the slice: x: 2, y: 2, z: 4, core: 2. Of those that a mesh axis runs over, the one named last changes fastest.
Arguments:
- queries: bfloat16 [2, 2048, 2048], P('dp', 'seq'), may hold values from -40 to 40
- keys: bfloat16 [2, 2048, 2048], P('dp', 'seq'), may hold values from -6 to 6
- values: bfloat16 [2, 2048, 2048], P('dp', 'seq'), may hold values from -6 to 6
- grad_out: bfloat16 [2, 2048, 2048], P('dp', 'seq'), may hold values from -48 to 48
- lengths: int32 [2], P('dp'), may hold values from 256 to 2048, as said below
- fields: int32 [2, 2048], P('dp', 'seq'), may hold values from 0 to 63
- field_bias: bfloat16 [16, 64], replicated, may hold values from -6 to 6
Outputs:
- grad_queries: bfloat16 [2, 2048, 2048], P('dp', 'seq')
- grad_keys: bfloat16 [2, 2048, 2048], P('dp', 'seq')
- grad_values: bfloat16 [2, 2048, 2048], P('dp', 'seq')
- grad_bias: float32 [16, 64], replicated
Inputs may be any that keep to these rules, and one draw needn't show every extreme that they name: `lengths`: the valid positions of a sequence form a prefix; in every draw some sequence is full.
All inputs are finite; a program needn't handle non-finite values.
Results may differ from a plain program's by a relative error of at most 0.0077.
Values may be sent and summed in bfloat16 or wider, within the bound.
No kernel may reach another device: no remote copies, remote signals or barrier semaphores. Data moves between devices by JAX's collectives and lax.ppermute only.
A program may use at most 128 MiB of HBM per device.

v0:
```python
import jax
import jax.numpy as jnp
from jax import lax
from jax.sharding import PartitionSpec as P

HEADS = 16
HEAD_DIM = 128
WINDOW = 512
FIELDS = 64


def passed_along(value, axis, steps):
    count = lax.axis_size(axis)
    first, last = (max(0, -steps), min(count, count - steps))
    return lax.ppermute(value, axis, [(source, source + steps) for source in range(first, last)])


def split_heads(rows):
    return rows.reshape(rows.shape[0], HEADS, HEAD_DIM)


def band_mask(query_places, key_places, length):
    not_after = key_places[None, :] <= query_places[:, None]
    inside = key_places[None, :] > query_places[:, None] - WINDOW
    started = key_places[None, :] >= 0
    live_rows = query_places[:, None] < length
    return not_after & inside & started & live_rows


def logits_of(query_heads, key_heads, key_bias):
    factor = HEAD_DIM ** (-0.5)
    products = jnp.einsum(
        "qhd,khd->hqk", query_heads, key_heads, preferred_element_type=jnp.float32
    )
    return products * factor + key_bias[:, None, :]


def grad_logits_of(attn_weights, row_delta, grad_heads, value_heads):
    grad_probs = jnp.einsum(
        "qhd,khd->hqk", grad_heads, value_heads, preferred_element_type=jnp.float32
    )
    return attn_weights * (grad_probs - row_delta[:, :, None])


def shards(queries, keys, values, grad_out, lengths, fields, field_bias):
    tok_rows = queries.shape[1]
    row_width = queries.shape[2]
    length = lengths[0]
    query_own = queries[0]
    key_own = keys[0]
    value_own = values[0]
    grad_own = grad_out[0]
    reach_blocks = WINDOW // tok_rows
    factor = HEAD_DIM ** (-0.5)
    block_index = lax.axis_index("seq")
    onehot = (fields[0][:, None] == jnp.arange(FIELDS, dtype=jnp.int32)[None, :]).astype(
        jnp.bfloat16
    )
    own_bias = jnp.dot(field_bias, onehot.T, preferred_element_type=jnp.float32).astype(
        jnp.bfloat16
    )
    package = (key_own, value_own, own_bias)
    arrived = []
    for distance in range(1, reach_blocks + 1):
        arrived.append(passed_along((package[0], package[1], package[2]), "seq", distance))
    ordered = arrived[::-1] + [package]
    key_all = jnp.concatenate([arrival[0] for arrival in ordered], axis=0)
    value_all = jnp.concatenate([arrival[1] for arrival in ordered], axis=0)
    bias_all = jnp.concatenate([arrival[2] for arrival in ordered], axis=1).astype(jnp.float32)
    query_places = block_index * tok_rows + jnp.arange(tok_rows, dtype=jnp.int32)
    key_places = (block_index - reach_blocks) * tok_rows + jnp.arange(
        (reach_blocks + 1) * tok_rows, dtype=jnp.int32
    )
    query_heads = split_heads(query_own)
    grad_heads = split_heads(grad_own)
    key_heads = split_heads(key_all)
    value_heads = split_heads(value_all)
    logits = logits_of(query_heads, key_heads, bias_all)
    visible = band_mask(query_places, key_places, length)[None]
    live_rows = (query_places < length)[None, :, None]
    row_peak = jnp.max(jnp.where(visible, logits, -1e30), axis=2, keepdims=True)
    powers = jnp.where(visible, jnp.exp(logits - row_peak), 0.0)
    totals = jnp.where(live_rows, jnp.sum(powers, axis=2, keepdims=True), 1.0)
    attn_weights = powers / totals
    weights_low = attn_weights.astype(jnp.bfloat16)
    outputs = jnp.einsum(
        "hqk,khd->qhd", weights_low, value_heads, preferred_element_type=jnp.float32
    )
    row_delta = jnp.einsum("qhd,qhd->hq", grad_heads.astype(jnp.float32), outputs)
    grad_logits = grad_logits_of(attn_weights, row_delta, grad_heads, value_heads)
    grad_low = grad_logits.astype(jnp.bfloat16)
    grad_query = (
        jnp.einsum("hqk,khd->qhd", grad_low, key_heads, preferred_element_type=jnp.float32) * factor
    )
    own_cols = reach_blocks * tok_rows
    grad_key = (
        jnp.einsum(
            "hqk,qhd->khd", grad_low, query_heads, preferred_element_type=jnp.float32
        ).reshape(-1, row_width)
        * factor
    )
    grad_value = jnp.einsum(
        "hqk,qhd->khd", weights_low, grad_heads, preferred_element_type=jnp.float32
    ).reshape(-1, row_width)
    column = jnp.sum(grad_logits, axis=1)
    key_total = grad_key[own_cols:]
    value_total = grad_value[own_cols:]
    column_total = column[:, own_cols:]
    for distance in range(1, reach_blocks + 1):
        first_row = (reach_blocks - distance) * tok_rows
        returned = passed_along(
            (
                grad_key[first_row : first_row + tok_rows],
                grad_value[first_row : first_row + tok_rows],
                column[:, first_row : first_row + tok_rows],
            ),
            "seq",
            -distance,
        )
        key_total = key_total + returned[0]
        value_total = value_total + returned[1]
        column_total = column_total + returned[2]
    bias_local = jnp.dot(column_total, onehot.astype(jnp.float32), precision=lax.Precision.HIGHEST)
    query_low = grad_query.reshape(tok_rows, row_width).astype(jnp.bfloat16)
    key_low = key_total.astype(jnp.bfloat16)
    value_low = value_total.astype(jnp.bfloat16)
    bias_total = lax.psum(bias_local, ("seq", "dp"))
    return (
        query_low.reshape(1, tok_rows, row_width),
        key_low.reshape(1, tok_rows, row_width),
        value_low.reshape(1, tok_rows, row_width),
        bias_total,
    )


def solution(mesh):
    return jax.shard_map(
        shards,
        mesh=mesh,
        in_specs=(
            P("dp", "seq", None),
            P("dp", "seq", None),
            P("dp", "seq", None),
            P("dp", "seq", None),
            P("dp"),
            P("dp", "seq"),
            P(),
        ),
        out_specs=(P("dp", "seq", None), P("dp", "seq", None), P("dp", "seq", None), P()),
        check_vma=False,
    )
```

profile of v0, /device:TPU:0, one launch (start us, length us, event | category | flops | bytes accessed | tf_op | source)
XLA Modules:
  0.0 417.0 jit_solution(2699877956279051602)
XLA Ops:
  2.2 5.0 %collective-permute-start.7 = (bf16[16,128]{1,0:T(8,128)(2,1)S(1)}, bf16[16,128]{1,0:T(8,128)(2,1)S(1)}, u32[]{:S(2)}, u32[]{:S(2)}) collective-permute-start(bf16[16,128]{1,0:T(8,128)(2,1)S(1)} %fusion.14), channel_id=1, source_target_pairs={{0,2},{2,4},{4,6},{6,8},{8,10},{10,12},{12,14},{14,16},{16,18},{18... | collective-permute-start | bytes 12296 | tf_op jit(solution)/shard_map/ppermute | solution.py:15
  7.2 3.4 collective-permute-start.6
  10.6 1.3 copy.35
  11.9 3.4 collective-permute-start.11
  15.4 3.4 collective-permute-start.10
  18.8 5.1 %collective-permute-start.9 = (bf16[128,2048]{0,1:T(8,128)(2,1)S(1)}, bf16[128,2048]{0,1:T(8,128)(2,1)}, u32[]{:S(2)}, u32[]{:S(2)}) collective-permute-start(bf16[128,2048]{0,1:T(8,128)(2,1)S(1)} %bitcast.98), channel_id=1, source_target_pairs={{0,6},{2,8},{4,10},{6,12},{8,14},{10,16},{12,18},{14,20},{16,22},{... | collective-permute-start | bytes 1572872 | tf_op jit(solution)/shard_map/ppermute | solution.py:15
  24.7 2.6 collective-permute-start.5
  27.3 2.0 collective-permute-start.4
  29.6 1.3 copy.27
  34.2 1.3 copy.55
  35.4 1.9 collective-permute-done.5
  37.3 3.5 collective-permute-start.8
  40.8 21.7 %collective-permute-start.3 = (bf16[128,2048]{0,1:T(8,128)(2,1)S(1)}, bf16[128,2048]{0,1:T(8,128)(2,1)}, u32[]{:S(2)}, u32[]{:S(2)}) collective-permute-start(bf16[128,2048]{0,1:T(8,128)(2,1)S(1)} %bitcast.102), channel_id=1, source_target_pairs={{0,2},{2,4},{4,6},{6,8},{8,10},{10,12},{12,14},{14,16},{16,18},{18... | collective-permute-start | bytes 1572872 | tf_op jit(solution)/shard_map/ppermute | solution.py:15
  62.5 3.9 collective-permute-start.2
  66.4 5.8 %collective-permute-start.1 = (bf16[128,2048]{0,1:T(8,128)(2,1)S(1)}, bf16[128,2048]{0,1:T(8,128)(2,1)}, u32[]{:S(2)}, u32[]{:S(2)}) collective-permute-start(bf16[128,2048]{0,1:T(8,128)(2,1)S(1)} %bitcast.104), channel_id=1, source_target_pairs={{0,6},{2,8},{4,10},{6,12},{8,14},{10,16},{12,18},{14,20},{16,22},{... | collective-permute-start | bytes 1572872 | tf_op jit(solution)/shard_map/ppermute | solution.py:15
  72.3 5.6 %collective-permute-start = (bf16[128,2048]{0,1:T(8,128)(2,1)S(1)}, bf16[128,2048]{0,1:T(8,128)(2,1)}, u32[]{:S(2)}, u32[]{:S(2)}) collective-permute-start(bf16[128,2048]{0,1:T(8,128)(2,1)S(1)} %bitcast.105), channel_id=1, source_target_pairs={{0,8},{2,10},{4,12},{6,14},{8,16},{10,18},{12,20},{14,22},{16,24},... | collective-permute-start | bytes 1572872 | tf_op jit(solution)/shard_map/ppermute | solution.py:15
  80.0 2.0 copy.38
  83.1 2.0 copy.32
  85.2 2.0 copy.31
  87.3 2.0 copy.30
  89.3 1.3 copy.29
  91.5 1.1 constant_dynamic-update-slice_fusion.14
  92.6 2.0 constant_dynamic-update-slice_fusion.3
  94.6 2.0 constant_dynamic-update-slice_fusion.2
  98.4 7.6 %fusion.34 = (f32[16,128]{1,0:T(8,128)S(1)}, f32[16,128,640]{1,2,0:T(8,128)}) fusion(f32[16,640]{1,0:T(8,128)S(1)} %convert_element_type.46, pred[128,640]{0,1:T(8,128)(4,1)S(1)} %and_and_fusion, bf16[640,16,128]{2,0,1:T(8,128)(2,1)} %constant_dynamic-update-slice_fusion, bf16[128,16,128]{0,2,1:T(8,128)(2,1)} %bitcast.94), kind=kOutput, calls=%fused_computation.67 | convolution fusion | flops 681575040 | bytes 8519680 | tf_op jit(solution)/shard_map/sub | solution.py:82
  106.0 1.2 constant_dynamic-update-slice_fusion.13
  107.2 1.1 constant_dynamic-update-slice_fusion.12
  108.4 1.1 constant_dynamic-update-slice_fusion.11
  109.6 1.5 copy-done.5
  111.1 3.3 fusion.8
  114.4 2.0 convolution_bitcast_fusion.1
  116.3 2.6 copy.69
  119.0 1.6 multiply_reduce_fusion
  120.6 5.2 %fusion.35 = (f32[16,640]{1,0:T(8,128)S(1)}, bf16[16,128,640]{1,2,0:T(8,128)(2,1)S(1)}) fusion(f32[16,128]{1,0:T(8,128)S(1)} %copy.70, bf16[640,16,128]{2,0,1:T(8,128)(2,1)} %copy-done.5, bf16[128,16,128]{0,2,1:T(8,128)(2,1)} %copy.55, f32[16,128,640]{1,2,0:T(8,128)} %get-tuple-element.27, f32[16,128]{1,0:T(8,128)S(1)} %broadcast_select_fusion), kind=kOutput, calls=%fused_computation.68 | convolution fusion | flops 342087680 | bytes 11067392 | tf_op jit(solution)/shard_map/qhd,khd->hqk/dot_general | solution.py:39
  127.3 2.4 fusion.32
  129.7 2.5 copy.52
  132.2 2.5 copy.51
  134.7 2.6 copy.50
  137.3 1.3 collective-permute-start.12
  138.6 1.3 collective-permute-start.13
  139.9 1.3 collective-permute-start.14
  141.2 1.3 collective-permute-start.20
  142.5 1.3 collective-permute-start.23
  143.8 2.6 copy.53
  146.4 18.3 %collective-permute-done.20 = f32[16,128]{1,0:T(8,128)S(1)} collective-permute-done((f32[16,128]{1,0:T(8,128)S(1)}, f32[16,128]{1,0:T(8,128)S(1)}, u32[]{:S(2)}, u32[]{:S(2)}) %collective-permute-start.20) | collective-permute-done | bytes 8224 | tf_op jit(solution)/shard_map/ppermute | solution.py:15
  164.7 1.3 collective-permute-start.22
  166.0 99.1 %collective-permute-done.23 = f32[16,128]{1,0:T(8,128)S(1)} collective-permute-done((f32[16,128]{1,0:T(8,128)S(1)}, f32[16,128]{1,0:T(8,128)S(1)}, u32[]{:S(2)}, u32[]{:S(2)}) %collective-permute-start.23) | collective-permute-done | bytes 8224 | tf_op jit(solution)/shard_map/ppermute | solution.py:15
  265.0 1.3 collective-permute-start.15
  267.4 3.5 collective-permute-done.22
  270.9 1.5 collective-permute-start.21
  272.4 2.0 fusion.31
  274.3 1.4 copy.56
  275.7 1.4 copy.60
  277.0 2.7 copy.59
  279.7 2.6 copy.58
  282.3 1.3 collective-permute-start.17
  283.6 1.3 collective-permute-start.18
  284.9 1.3 collective-permute-start.19
  286.2 1.3 collective-permute-start.16
  287.5 2.8 fusion.11
  291.3 1.6 copy.57
  293.5 116.7 %psum.7 = f32[16,64]{1,0:T(8,128)} all-reduce(f32[16,64]{1,0:T(8,128)S(1)} %fusion.22), channel_id=1, replica_groups=mesh['seq'=16,'dp'=2] {'seq','dp'}, use_global_device_ids=true, to_apply=%region_3.4 | all-reduce | flops 1024 | bytes 8192 | tf_op jit(solution)/shard_map/psum | solution.py:127
  410.1 2.4 fusion.18
  413.6 3.4 fusion.19
  (81 shorter events, 16.4 us)
Async XLA Ops:
  0.6 0.7 copy-start
  0.6 32.3 %copy-start.12 = (bf16[1,128,2048]{2,1,0:T(8,128)(2,1)S(1)}, bf16[1,128,2048]{2,1,0:T(8,128)(2,1)}, u32[]{:S(2)}) copy-start(bf16[1,128,2048]{2,1,0:T(8,128)(2,1)} %param.7) | copy-start | bytes 1572868
  2.2 31.9 %copy-start.13 = (bf16[1,128,2048]{2,1,0:T(8,128)(2,1)S(1)}, bf16[1,128,2048]{2,1,0:T(8,128)(2,1)}, u32[]{:S(2)}) copy-start(bf16[1,128,2048]{2,1,0:T(8,128)(2,1)} %param.10) | copy-start | bytes 1572868
  2.2 22.5 %collective-permute-start.7 = (bf16[16,128]{1,0:T(8,128)(2,1)S(1)}, bf16[16,128]{1,0:T(8,128)(2,1)S(1)}, u32[]{:S(2)}, u32[]{:S(2)}) collective-permute-start(bf16[16,128]{1,0:T(8,128)(2,1)S(1)} %fusion.14), channel_id=1, source_target_pairs={{0,2},{2,4},{4,6},{6,8},{8,10},{10,12},{12,14},{14,16},{16,18},{18... | collective-permute-start | bytes 12296 | tf_op jit(solution)/shard_map/ppermute | solution.py:15
  7.2 20.1 %collective-permute-start.6 = (bf16[16,128]{1,0:T(8,128)(2,1)S(1)}, bf16[16,128]{1,0:T(8,128)(2,1)S(1)}, u32[]{:S(2)}, u32[]{:S(2)}) collective-permute-start(bf16[16,128]{1,0:T(8,128)(2,1)S(1)} %fusion.14), channel_id=1, source_target_pairs={{0,4},{2,6},{4,8},{6,10},{8,12},{10,14},{12,16},{14,18},{16,20},{1... | collective-permute-start | bytes 12296 | tf_op jit(solution)/shard_map/ppermute | solution.py:15
  11.9 50.6 %collective-permute-start.11 = (bf16[128,2048]{0,1:T(8,128)(2,1)S(1)}, bf16[128,2048]{0,1:T(8,128)(2,1)S(1)}, u32[]{:S(2)}, u32[]{:S(2)}) collective-permute-start(bf16[128,2048]{0,1:T(8,128)(2,1)S(1)} %bitcast.96), channel_id=1, source_target_pairs={{0,2},{2,4},{4,6},{6,8},{8,10},{10,12},{12,14},{14,16},{16,18},{18... | collective-permute-start | bytes 1572872 | tf_op jit(solution)/shard_map/ppermute | solution.py:15
  15.4 51.1 %collective-permute-start.10 = (bf16[128,2048]{0,1:T(8,128)(2,1)S(1)}, bf16[128,2048]{0,1:T(8,128)(2,1)S(1)}, u32[]{:S(2)}, u32[]{:S(2)}) collective-permute-start(bf16[128,2048]{0,1:T(8,128)(2,1)S(1)} %bitcast.97), channel_id=1, source_target_pairs={{0,4},{2,6},{4,8},{6,10},{8,12},{10,14},{12,16},{14,18},{16,20},{1... | collective-permute-start | bytes 1572872 | tf_op jit(solution)/shard_map/ppermute | solution.py:15
  18.8 53.5 %collective-permute-start.9 = (bf16[128,2048]{0,1:T(8,128)(2,1)S(1)}, bf16[128,2048]{0,1:T(8,128)(2,1)}, u32[]{:S(2)}, u32[]{:S(2)}) collective-permute-start(bf16[128,2048]{0,1:T(8,128)(2,1)S(1)} %bitcast.98), channel_id=1, source_target_pairs={{0,6},{2,8},{4,10},{6,12},{8,14},{10,16},{12,18},{14,20},{16,22},{... | collective-permute-start | bytes 1572872 | tf_op jit(solution)/shard_map/ppermute | solution.py:15
  24.7 12.6 %collective-permute-start.5 = (bf16[16,128]{1,0:T(8,128)(2,1)S(1)}, bf16[16,128]{1,0:T(8,128)(2,1)S(1)}, u32[]{:S(2)}, u32[]{:S(2)}) collective-permute-start(bf16[16,128]{1,0:T(8,128)(2,1)S(1)} %fusion.14), channel_id=1, source_target_pairs={{0,6},{2,8},{4,10},{6,12},{8,14},{10,16},{12,18},{14,20},{16,22},{... | collective-permute-start | bytes 12296 | tf_op jit(solution)/shard_map/ppermute | solution.py:15
  27.3 13.5 %collective-permute-start.4 = (bf16[16,128]{1,0:T(8,128)(2,1)S(1)}, bf16[16,128]{1,0:T(8,128)(2,1)S(1)}, u32[]{:S(2)}, u32[]{:S(2)}) collective-permute-start(bf16[16,128]{1,0:T(8,128)(2,1)S(1)} %fusion.14), channel_id=1, source_target_pairs={{0,8},{2,10},{4,12},{6,14},{8,16},{10,18},{12,20},{14,22},{16,24},... | collective-permute-start | bytes 12296 | tf_op jit(solution)/shard_map/ppermute | solution.py:15
  37.3 44.7 %collective-permute-start.8 = (bf16[128,2048]{0,1:T(8,128)(2,1)S(1)}, bf16[128,2048]{0,1:T(8,128)(2,1)S(1)}, u32[]{:S(2)}, u32[]{:S(2)}) collective-permute-start(bf16[128,2048]{0,1:T(8,128)(2,1)S(1)} %bitcast.100), channel_id=1, source_target_pairs={{0,8},{2,10},{4,12},{6,14},{8,16},{10,18},{12,20},{14,22},{16,24},... | collective-permute-start | bytes 1572872 | tf_op jit(solution)/shard_map/ppermute | solution.py:15
  40.8 42.3 %collective-permute-start.3 = (bf16[128,2048]{0,1:T(8,128)(2,1)S(1)}, bf16[128,2048]{0,1:T(8,128)(2,1)}, u32[]{:S(2)}, u32[]{:S(2)}) collective-permute-start(bf16[128,2048]{0,1:T(8,128)(2,1)S(1)} %bitcast.102), channel_id=1, source_target_pairs={{0,2},{2,4},{4,6},{6,8},{8,10},{10,12},{12,14},{14,16},{16,18},{18... | collective-permute-start | bytes 1572872 | tf_op jit(solution)/shard_map/ppermute | solution.py:15
  62.5 22.7 %collective-permute-start.2 = (bf16[128,2048]{0,1:T(8,128)(2,1)S(1)}, bf16[128,2048]{0,1:T(8,128)(2,1)}, u32[]{:S(2)}, u32[]{:S(2)}) collective-permute-start(bf16[128,2048]{0,1:T(8,128)(2,1)S(1)} %bitcast.103), channel_id=1, source_target_pairs={{0,4},{2,6},{4,8},{6,10},{8,12},{10,14},{12,16},{14,18},{16,20},{1... | collective-permute-start | bytes 1572872 | tf_op jit(solution)/shard_map/ppermute | solution.py:15
  66.4 20.8 %collective-permute-start.1 = (bf16[128,2048]{0,1:T(8,128)(2,1)S(1)}, bf16[128,2048]{0,1:T(8,128)(2,1)}, u32[]{:S(2)}, u32[]{:S(2)}) collective-permute-start(bf16[128,2048]{0,1:T(8,128)(2,1)S(1)} %bitcast.104), channel_id=1, source_target_pairs={{0,6},{2,8},{4,10},{6,12},{8,14},{10,16},{12,18},{14,20},{16,22},{... | collective-permute-start | bytes 1572872 | tf_op jit(solution)/shard_map/ppermute | solution.py:15
  72.3 17.0 %collective-permute-start = (bf16[128,2048]{0,1:T(8,128)(2,1)S(1)}, bf16[128,2048]{0,1:T(8,128)(2,1)}, u32[]{:S(2)}, u32[]{:S(2)}) collective-permute-start(bf16[128,2048]{0,1:T(8,128)(2,1)S(1)} %bitcast.105), channel_id=1, source_target_pairs={{0,8},{2,10},{4,12},{6,14},{8,16},{10,18},{12,20},{14,22},{16,24},... | collective-permute-start | bytes 1572872 | tf_op jit(solution)/shard_map/ppermute | solution.py:15
  90.6 6.0 %copy-start.11 = (bf16[128,16,128]{2,0,1:T(8,128)(2,1)S(1)}, bf16[128,16,128]{2,0,1:T(8,128)(2,1)}, u32[]{:S(2)}) copy-start(bf16[128,16,128]{2,0,1:T(8,128)(2,1)} %copy.32) | copy-start | bytes 1572868
  90.6 6.9 %copy-start.10 = (bf16[128,16,128]{2,0,1:T(8,128)(2,1)S(1)}, bf16[128,16,128]{2,0,1:T(8,128)(2,1)}, u32[]{:S(2)}) copy-start(bf16[128,16,128]{2,0,1:T(8,128)(2,1)} %copy.33) | copy-start | bytes 1572868
  106.0 3.5 copy-start.9
  109.6 1.5 copy-start.5
  111.1 3.3 copy-start.6
  120.6 5.2 %copy-start.8 = (bf16[1,128,2048]{1,2,0:T(8,128)(2,1)S(1)}, bf16[1,128,2048]{1,2,0:T(8,128)(2,1)}, u32[]{:S(2)}) copy-start(bf16[1,128,2048]{1,2,0:T(8,128)(2,1)} %copy.76) | copy-start | bytes 1572868
  125.8 1.5 copy-start.2
  134.7 131.6 %copy-start.7 = (bf16[128,16,128]{0,2,1:T(8,128)(2,1)S(1)}, bf16[128,16,128]{0,2,1:T(8,128)(2,1)}, u32[]{:S(2)}) copy-start(bf16[128,16,128]{0,2,1:T(8,128)(2,1)} %copy.55) | copy-start | bytes 1572868
  137.3 146.3 %collective-permute-start.12 = (f32[128,2048]{0,1:T(8,128)}, f32[128,2048]{0,1:T(8,128)}, u32[]{:S(2)}, u32[]{:S(2)}) collective-permute-start(f32[128,2048]{0,1:T(8,128)} %bitcast.111), channel_id=1, source_target_pairs={{2,0},{4,2},{6,4},{8,6},{10,8},{12,10},{14,12},{16,14},{18,16},{20... | collective-permute-start | bytes 3145736 | tf_op jit(solution)/shard_map/ppermute | solution.py:15
  138.6 146.3 %collective-permute-start.13 = (f32[128,2048]{0,1:T(8,128)}, f32[128,2048]{0,1:T(8,128)}, u32[]{:S(2)}, u32[]{:S(2)}) collective-permute-start(f32[128,2048]{0,1:T(8,128)} %bitcast.110), channel_id=1, source_target_pairs={{4,0},{6,2},{8,4},{10,6},{12,8},{14,10},{16,12},{18,14},{20,16},{2... | collective-permute-start | bytes 3145736 | tf_op jit(solution)/shard_map/ppermute | solution.py:15
  139.9 146.3 %collective-permute-start.14 = (f32[128,2048]{0,1:T(8,128)}, f32[128,2048]{0,1:T(8,128)}, u32[]{:S(2)}, u32[]{:S(2)}) collective-permute-start(f32[128,2048]{0,1:T(8,128)} %bitcast.108), channel_id=1, source_target_pairs={{6,0},{8,2},{10,4},{12,6},{14,8},{16,10},{18,12},{20,14},{22,16},{... | collective-permute-start | bytes 3145736 | tf_op jit(solution)/shard_map/ppermute | solution.py:15
  141.2 23.5 %collective-permute-start.20 = (f32[16,128]{1,0:T(8,128)S(1)}, f32[16,128]{1,0:T(8,128)S(1)}, u32[]{:S(2)}, u32[]{:S(2)}) collective-permute-start(f32[16,128]{1,0:T(8,128)S(1)} %get-tuple-element.22), channel_id=1, source_target_pairs={{2,0},{4,2},{6,4},{8,6},{10,8},{12,10},{14,12},{16,14},{18,16},{20... | collective-permute-start | bytes 24584 | tf_op jit(solution)/shard_map/ppermute | solution.py:15
  142.5 122.5 %collective-permute-start.23 = (f32[16,128]{1,0:T(8,128)S(1)}, f32[16,128]{1,0:T(8,128)S(1)}, u32[]{:S(2)}, u32[]{:S(2)}) collective-permute-start(f32[16,128]{1,0:T(8,128)S(1)} %get-tuple-element.23), channel_id=1, source_target_pairs={{8,0},{10,2},{12,4},{14,6},{16,8},{18,10},{20,12},{22,14},{24,16},... | collective-permute-start | bytes 24584 | tf_op jit(solution)/shard_map/ppermute | solution.py:15
  164.7 106.2 %collective-permute-start.22 = (f32[16,128]{1,0:T(8,128)S(1)}, f32[16,128]{1,0:T(8,128)S(1)}, u32[]{:S(2)}, u32[]{:S(2)}) collective-permute-start(f32[16,128]{1,0:T(8,128)S(1)} %get-tuple-element.24), channel_id=1, source_target_pairs={{6,0},{8,2},{10,4},{12,6},{14,8},{16,10},{18,12},{20,14},{22,16},{... | collective-permute-start | bytes 24584 | tf_op jit(solution)/shard_map/ppermute | solution.py:15
  265.0 145.1 %collective-permute-start.15 = (f32[128,2048]{0,1:T(8,128)}, f32[128,2048]{0,1:T(8,128)}, u32[]{:S(2)}, u32[]{:S(2)}) collective-permute-start(f32[128,2048]{0,1:T(8,128)} %bitcast.109), channel_id=1, source_target_pairs={{8,0},{10,2},{12,4},{14,6},{16,8},{18,10},{20,12},{22,14},{24,16},... | collective-permute-start | bytes 3145736 | tf_op jit(solution)/shard_map/ppermute | solution.py:15
  270.9 11.4 %collective-permute-start.21 = (f32[16,128]{1,0:T(8,128)S(1)}, f32[16,128]{1,0:T(8,128)S(1)}, u32[]{:S(2)}, u32[]{:S(2)}) collective-permute-start(f32[16,128]{1,0:T(8,128)S(1)} %get-tuple-element.25), channel_id=1, source_target_pairs={{4,0},{6,2},{8,4},{10,6},{12,8},{14,10},{16,12},{18,14},{20,16},{2... | collective-permute-start | bytes 24584 | tf_op jit(solution)/shard_map/ppermute | solution.py:15
  277.0 10.5 %copy-start.3 = (bf16[16,128,640]{1,2,0:T(8,128)(2,1)S(1)}, bf16[16,128,640]{1,2,0:T(8,128)(2,1)}, u32[]{:S(2)}) copy-start(bf16[16,128,640]{1,2,0:T(8,128)(2,1)} %copy-done.2) | copy-start | bytes 7864324
  282.3 131.3 %collective-permute-start.17 = (f32[128,2048]{1,0:T(8,128)}, f32[128,2048]{1,0:T(8,128)}, u32[]{:S(2)}, u32[]{:S(2)}) collective-permute-start(f32[128,2048]{1,0:T(8,128)} %copy.58), channel_id=1, source_target_pairs={{4,0},{6,2},{8,4},{10,6},{12,8},{14,10},{16,12},{18,14},{20,16},{2... | collective-permute-start | bytes 3145736 | tf_op jit(solution)/shard_map/ppermute | solution.py:15
  283.6 130.0 %collective-permute-start.18 = (f32[128,2048]{1,0:T(8,128)}, f32[128,2048]{1,0:T(8,128)}, u32[]{:S(2)}, u32[]{:S(2)}) collective-permute-start(f32[128,2048]{1,0:T(8,128)} %copy.59), channel_id=1, source_target_pairs={{6,0},{8,2},{10,4},{12,6},{14,8},{16,10},{18,12},{20,14},{22,16},{... | collective-permute-start | bytes 3145736 | tf_op jit(solution)/shard_map/ppermute | solution.py:15
  284.9 128.7 %collective-permute-start.19 = (f32[128,2048]{1,0:T(8,128)}, f32[128,2048]{1,0:T(8,128)}, u32[]{:S(2)}, u32[]{:S(2)}) collective-permute-start(f32[128,2048]{1,0:T(8,128)} %copy.60), channel_id=1, source_target_pairs={{8,0},{10,2},{12,4},{14,6},{16,8},{18,10},{20,12},{22,14},{24,16},... | collective-permute-start | bytes 3145736 | tf_op jit(solution)/shard_map/ppermute | solution.py:15
  286.2 127.4 %collective-permute-start.16 = (f32[128,2048]{1,0:T(8,128)}, f32[128,2048]{1,0:T(8,128)}, u32[]{:S(2)}, u32[]{:S(2)}) collective-permute-start(f32[128,2048]{1,0:T(8,128)} %copy.56), channel_id=1, source_target_pairs={{2,0},{4,2},{6,4},{8,6},{10,8},{12,10},{14,12},{16,14},{18,16},{20... | collective-permute-start | bytes 3145736 | tf_op jit(solution)/shard_map/ppermute | solution.py:15
  290.3 2.6 copy-start.4
  290.3 3.0 copy-start.14
  412.5 4.5 %copy-start.1 = (bf16[16,64]{1,0:T(8,128)(2,1)S(1)}, bf16[16,64]{1,0:T(8,128)(2,1)}, u32[]{:S(2)}) copy-start(bf16[16,64]{1,0:T(8,128)(2,1)} %param.13) | copy-start | bytes 6148
where the time goes:
time: 419 us; the launch traced here: 417 us
  waiting for transfers between devices  123 us (29%)
  blocking collectives  117 us (28%)
  starting transfers between devices  81.2 us (19%)
  local copies, waits for them, and re-layouts  63.1 us (15%)
  matrix products  20.4 us (5%)
  other arithmetic  10.9 us (3%)
    ppermute x24, waiting for transfers between devices, passed_along(): lax.ppermute(value, axis, [(source, source + steps) for source in range(f...  123 us
    psum x1, blocking collectives, shards(): bias_total = lax.psum(bias_local, ('seq', 'dp'))  117 us
    ppermute x24, starting transfers between devices, passed_along(): lax.ppermute(value, axis, [(source, source + steps) for source in range(f...  81.2 us
    unnamed x48, local copies, waits for them, and re-layouts  20.6 us
    slice x4, local copies, waits for them, and re-layouts, shards(): grad_key[first_row:first_row + tok_rows]  10.2 us
    slice x5, local copies, waits for them, and re-layouts, shards(): grad_value[first_row:first_row + tok_rows]  9.92 us
    concatenate x6, local copies, waits for them, and re-layouts, shards(): key_all = jnp.concatenate([arrival[0] for arrival in ordered], axis=0)  9.36 us
  transfers between devices with their start and end apart: 24, of which 5 were waited for; matrix products, arithmetic and copies ran while one was open for 10% of the time, Pallas kernels for 0%

commit v1 on v0

v1 whole, which is shorter than its diff:
```python
import functools

import jax
import jax.numpy as jnp
from jax import lax
from jax.experimental import pallas as pl
from jax.experimental.pallas import tpu as pltpu
from jax.sharding import PartitionSpec as P

HEADS = 16
HEAD_DIM = 128
WINDOW = 512
FIELDS = 64
FACTOR = HEAD_DIM ** (-0.5)
LOG2E = 1.4426950408889634
HIDDEN = -1e30
PAD = 16
CHUNKS = 2
MIB = 1 << 20
BF16, F32 = jnp.bfloat16, jnp.float32
ANY = pl.BlockSpec(memory_space=pl.ANY)
SMEM = pl.BlockSpec(memory_space=pltpu.SMEM)
NT = (((1,), (1,)), ((), ()))


def dot(a, b):
    return jnp.dot(a, b, preferred_element_type=F32)


def dot_nt(a, b):
    return lax.dot_general(a, b, NT, preferred_element_type=F32)


def run_copies(copies):
    for copy in copies:
        copy.start()
    for copy in copies:
        copy.wait()


def fields_row(fields_ref, width):
    row = fields_ref[...].astype(F32)
    row = jnp.concatenate([row] * (width // row.shape[1]), axis=1)
    return jnp.broadcast_to(row, (PAD, width)).astype(BF16)


def pack_kernel(reach, tok, width, chunk, meta, q, g, k, v, fields, *rest):
    outs, field_scr, sems = rest[: reach - 1], rest[-2], rest[-1]
    p = meta[0]
    field_scr[...] = fields_row(fields, width)
    copies = []
    for m in range(1, reach):
        first = pl.multiple_of((p ^ m) * (HEADS // reach * HEAD_DIM) + chunk * width, 128)
        pairs = [
            (src.at[0, :, pl.ds(first, width)], outs[m - 1].at[pl.ds(at * tok, tok)])
            for at, src in enumerate((q, g, k, v))
        ]
        pairs.append((field_scr, outs[m - 1].at[pl.ds(4 * tok, PAD)]))
        for src, dst in pairs:
            copies.append(pltpu.make_async_copy(src, dst, sems.at[len(copies)]))
    run_copies(copies)


def gather_kernel(reach, tok, width, chunk, meta, q, g, k, v, fields, *rest):
    arrived = rest[: reach - 1]
    qd, kv, field_scr, sems = rest[reach - 1 :]
    p = meta[0]
    field_scr[...] = fields_row(fields, width)
    first = pl.multiple_of(p * (HEADS // reach * HEAD_DIM) + chunk * width, 128)
    own = pl.ds(first, width)
    pairs = [
        (q.at[0, :, own], qd.at[0, pl.ds(0, tok)]),
        (g.at[0, :, own], qd.at[0, pl.ds(tok, tok)]),
        (k.at[0, :, own], kv.at[0, pl.ds(0, tok)]),
        (v.at[0, :, own], kv.at[0, pl.ds(tok, tok)]),
        (field_scr, kv.at[0, pl.ds(2 * tok, PAD)]),
    ]
    for m in range(1, reach):
        pairs.append((arrived[m - 1].at[pl.ds(0, 2 * tok)], qd.at[m]))
        pairs.append((arrived[m - 1].at[pl.ds(2 * tok, 2 * tok + PAD)], kv.at[m]))
    run_copies([pltpu.make_async_copy(s, d, sems.at[i]) for i, (s, d) in enumerate(pairs)])


def unpack_kernel(reach, tok, width, meta, *rest):
    parts, outs, sems = rest[: CHUNKS * reach * 2], rest[CHUNKS * reach * 2 : -1], rest[-1]
    p = meta[0]
    copies = []
    for chunk in range(CHUNKS):
        for m in range(reach):
            dq, dkv = parts[(chunk * reach + m) * 2 : (chunk * reach + m) * 2 + 2]
            first = pl.multiple_of((p ^ m) * (HEADS // reach * HEAD_DIM) + chunk * width, 128)
            there = pl.ds(first, width)
            for src, out in (
                (dq, outs[0]),
                (dkv.at[pl.ds(0, tok)], outs[1]),
                (dkv.at[pl.ds(tok, tok)], outs[2]),
            ):
                copies.append(pltpu.make_async_copy(src, out.at[0, :, there], sems.at[len(copies)]))
    run_copies(copies)


def key_columns(kv, slot, tok):
    row = kv[slot, 2 * tok : 2 * tok + PAD, :].astype(F32)[0:1]
    spread = jnp.broadcast_to(row, (tok, tok))
    lane = lax.broadcasted_iota(jnp.int32, (tok, tok), 1).astype(F32)
    sub = lax.broadcasted_iota(jnp.int32, (tok, tok), 0).astype(F32)
    onehot = jnp.where(spread.T == lane, 1.0, 0.0).astype(BF16)
    onehot_t = jnp.where(spread == sub, 1.0, 0.0).astype(BF16)
    return onehot, onehot_t


def three_parts(x):
    high = x.astype(BF16)
    rest = x - high.astype(F32)
    mid = rest.astype(BF16)
    return high, mid, (rest - mid.astype(F32)).astype(BF16)


def rows_kernel(reach, tok, meta, qd, kvo, kvp, bias_ref, *rest):
    dq_outs = rest[:reach]
    dk_out, dv_out, stats_out, gb_out = rest[reach : reach + 4]
    k_scr, v_scr, kt_scr, oh_scr, oht_scr, bias_scr, acc_scr, dq_scr = rest[reach + 4 :]
    p, plane, length = meta[0], meta[1], meta[2]
    span = reach * tok

    @pl.when(pl.program_id(0) == 0)
    def _():
        for blk in range(2 * reach):
            rows = slice(blk * tok, (blk + 1) * tok)
            onehot, onehot_t = key_columns(kvp if blk < reach else kvo, p ^ (blk % reach), tok)
            oh_scr[rows] = onehot
            oht_scr[:, rows] = onehot_t

    shut = jnp.where(plane == 0, HIDDEN, 0.0).astype(F32)
    for blk in range(2 * reach):
        rows = slice(blk * tok, (blk + 1) * tok)
        src, slot = (kvp if blk < reach else kvo), p ^ (blk % reach)
        key = src[slot, 0:tok, :]
        k_scr[rows] = key
        kt_scr[:, rows] = key.T
        v_scr[rows] = src[slot, tok : 2 * tok, :]
        col = dot(oh_scr[rows], bias_ref[0]) * LOG2E
        bias_scr[rows] = col + shut if blk < reach else col
    acc_scr[...] = jnp.zeros_like(acc_scr)
    key_at = lax.broadcasted_iota(jnp.int32, (tok, tok), 0)
    query_at = lax.broadcasted_iota(jnp.int32, (tok, tok), 1)
    lane = lax.broadcasted_iota(jnp.int32, (1, tok), 1)
    for a in range(reach):
        slot = p ^ a
        query, grad = qd[slot, 0:tok, :], qd[slot, tok : 2 * tok, :]
        rows = slice(a * tok, (a + reach + 1) * tok)
        s = dot_nt(k_scr[rows], query) * (FACTOR * LOG2E) + bias_scr[rows]
        s = jnp.concatenate(
            [
                jnp.where(key_at > query_at, s[:tok], HIDDEN),
                s[tok:-tok],
                jnp.where(key_at <= query_at, s[-tok:], HIDDEN),
            ],
            axis=0,
        )
        peak = jnp.max(s, axis=0, keepdims=True)
        power = jnp.exp2(s - peak)
        total = jnp.sum(power, axis=0, keepdims=True)
        live = plane * span + a * tok + lane < length
        weight = power * jnp.where(live, 1.0 / total, 0.0)
        low = weight.astype(BF16)
        probs = dot_nt(v_scr[rows], grad)
        delta = jnp.sum(low.astype(F32) * probs, axis=0, keepdims=True)
        ds = weight * (probs - delta)
        ds_low = ds.astype(BF16)
        acc_scr[rows] += ds
        dq_scr[slot] = (dot(kt_scr[:, rows], ds_low).T * FACTOR).astype(BF16)
        own = slice((reach - a) * tok, (reach + 1) * tok)
        dv = dot(low[own], grad)
        dk = dot(ds_low[own], query)
        if a:
            dv_out[0 : a * tok] += dv[: a * tok]
            dk_out[0 : a * tok] += dk[: a * tok]
        dv_out[a * tok : (a + 1) * tok] = dv[a * tok :]
        dk_out[a * tok : (a + 1) * tok] = dk[a * tok :]
        there = slice(a * tok, (a + 1) * tok)
        stats_out[0, 0:1, there] = peak + jnp.log2(total)
        stats_out[0, 1:2, there] = delta
    for m in range(reach):
        dq_outs[m][...] = dq_scr[m]
    by_field = sum(dot(oht_scr[...], part) for part in three_parts(acc_scr[...]))
    gb_out[0] = jnp.sum(by_field.T.reshape(tok // 8, 8, tok), axis=0)


def columns_kernel(reach, tok, meta, qd, kvo, stats, bias_ref, dk_in, dv_in, *rest):
    outs = rest[:reach]
    k_scr, v_scr, bias_scr, dk_scr, dv_scr, out_scr = rest[reach:]
    p, plane, length = meta[0], meta[1], meta[2]
    span = reach * tok
    for blk in range(reach):
        rows = slice(blk * tok, (blk + 1) * tok)
        slot = p ^ blk
        k_scr[rows] = kvo[slot, 0:tok, :]
        v_scr[rows] = kvo[slot, tok : 2 * tok, :]
        onehot, _ = key_columns(kvo, slot, tok)
        bias_scr[rows] = dot(onehot, bias_ref[0]) * LOG2E
    dk_scr[...] = dk_in[...]
    dv_scr[...] = dv_in[...]
    key_at = lax.broadcasted_iota(jnp.int32, (tok, tok), 0)
    query_at = lax.broadcasted_iota(jnp.int32, (tok, tok), 1)
    lane = lax.broadcasted_iota(jnp.int32, (1, tok), 1)
    for a in range(reach):
        slot = p ^ a
        query, grad = qd[slot, 0:tok, :], qd[slot, tok : 2 * tok, :]
        rows = slice(a * tok, span)
        there = slice(a * tok, (a + 1) * tok)
        live = (plane + 1) * span + a * tok + lane < length
        norm = jnp.where(live, stats[0, 0:1, there], -HIDDEN)
        delta = stats[0, 1:2, there]
        s = dot_nt(k_scr[rows], query) * (FACTOR * LOG2E) + bias_scr[rows]
        weight = jnp.exp2(s - norm)
        first = jnp.where(key_at > query_at, weight[:tok], 0.0)
        weight = jnp.concatenate([first, weight[tok:]], axis=0) if a < reach - 1 else first
        ds = weight * (dot_nt(v_scr[rows], grad) - delta)
        dv_scr[rows] += dot(weight.astype(BF16), grad)
        dk_scr[rows] += dot(ds.astype(BF16), query)
    for blk in range(reach):
        rows = slice(blk * tok, (blk + 1) * tok)
        out_scr[p ^ blk, 0:tok] = (dk_scr[rows] * FACTOR).astype(BF16)
        out_scr[p ^ blk, tok : 2 * tok] = dv_scr[rows].astype(BF16)
    for m in range(reach):
        outs[m][...] = out_scr[m]


def params(*semantics):
    return pltpu.CompilerParams(
        vmem_limit_bytes=40 * MIB, dimension_semantics=semantics if semantics else None
    )


def cost(flops, nbytes, trans=0):
    return pl.CostEstimate(flops=flops, bytes_accessed=nbytes, transcendentals=trans)


def swapped(value, axis, mask):
    count = lax.axis_size(axis)
    return lax.ppermute(value, axis, [(source, source ^ mask) for source in range(count)])


def passed_along(value, axis, steps):
    count = lax.axis_size(axis)
    first, last = max(0, -steps), min(count, count - steps)
    return lax.ppermute(value, axis, [(source, source + steps) for source in range(first, last)])


def shards(queries, keys, values, grad_out, lengths, fields, field_bias):
    tok = queries.shape[1]
    row_width = queries.shape[2]
    reach = WINDOW // tok
    group = HEADS // reach
    per = group // CHUNKS
    width = per * HEAD_DIM
    span = reach * tok
    index = lax.axis_index("seq")
    p = lax.rem(index, reach)
    meta = jnp.stack([p, lax.div(index, reach), lengths[0]]).astype(jnp.int32)
    raw = (queries, grad_out, keys, values)

    def sds(shape, dtype=BF16):
        return jax.ShapeDtypeStruct(shape, dtype)

    vmem = pl.BlockSpec(memory_space=pltpu.VMEM)

    def pack(chunk):
        return pl.pallas_call(
            functools.partial(pack_kernel, reach, tok, width, chunk),
            in_specs=[SMEM] + [ANY] * 4 + [vmem],
            out_specs=[ANY] * (reach - 1),
            out_shape=[sds((4 * tok + PAD, width))] * (reach - 1),
            scratch_shapes=[
                pltpu.VMEM((PAD, width), BF16),
                pltpu.SemaphoreType.DMA((5 * (reach - 1),)),
            ],
            compiler_params=params(),
            name="pack",
        )(meta, *raw, fields)

    def gather(chunk, arrived):
        return pl.pallas_call(
            functools.partial(gather_kernel, reach, tok, width, chunk),
            in_specs=[SMEM] + [ANY] * 4 + [vmem] + [ANY] * (reach - 1),
            out_specs=[ANY] * 2,
            out_shape=[sds((reach, 2 * tok, width)), sds((reach, 2 * tok + PAD, width))],
            scratch_shapes=[
                pltpu.VMEM((PAD, width), BF16),
                pltpu.SemaphoreType.DMA((5 + 2 * (reach - 1),)),
            ],
            compiler_params=params(),
            name="gather",
        )(meta, *raw, fields, *arrived)

    qd_spec = pl.BlockSpec((reach, 2 * tok, HEAD_DIM), lambda h: (0, 0, h))
    kv_spec = pl.BlockSpec((reach, 2 * tok + PAD, HEAD_DIM), lambda h: (0, 0, h))
    bias_spec = pl.BlockSpec((1, tok, HEAD_DIM), lambda h: (h, 0, 0))
    stats_spec = pl.BlockSpec((1, 8, span), lambda h: (h, 0, 0))
    part_spec = pl.BlockSpec((span, HEAD_DIM), lambda h: (0, h))

    def rows_of(qd, kvo, kvp, bias):
        return pl.pallas_call(
            functools.partial(rows_kernel, reach, tok),
            grid=(per,),
            in_specs=[SMEM, qd_spec, kv_spec, kv_spec, bias_spec],
            out_specs=[pl.BlockSpec((tok, HEAD_DIM), lambda h: (0, h))] * reach
            + [part_spec, part_spec, stats_spec, pl.BlockSpec((1, 8, tok), lambda h: (h, 0, 0))],
            out_shape=[sds((tok, width))] * reach
            + [
                sds((span, width), F32),
                sds((span, width), F32),
                sds((per, 8, span), F32),
                sds((per, 8, tok), F32),
            ],
            scratch_shapes=[
                pltpu.VMEM((2 * span, HEAD_DIM), BF16),
                pltpu.VMEM((2 * span, HEAD_DIM), BF16),
                pltpu.VMEM((HEAD_DIM, 2 * span), BF16),
                pltpu.VMEM((2 * span, tok), BF16),
                pltpu.VMEM((tok, 2 * span), BF16),
                pltpu.VMEM((2 * span, tok), F32),
                pltpu.VMEM((2 * span, tok), F32),
                pltpu.VMEM((reach, tok, HEAD_DIM), BF16),
            ],
            compiler_params=params("arbitrary"),
            cost_estimate=cost(per * 12 * span * (span + tok) * HEAD_DIM, 4 * MIB, per * span * span),
            name="rows",
        )(meta, qd, kvo, kvp, bias)

    def columns_of(qd, kvo, stats, bias, dk, dv):
        return pl.pallas_call(
            functools.partial(columns_kernel, reach, tok),
            grid=(per,),
            in_specs=[SMEM, qd_spec, kv_spec, stats_spec, bias_spec, part_spec, part_spec],
            out_specs=[pl.BlockSpec((2 * tok, HEAD_DIM), lambda h: (0, h))] * reach,
            out_shape=[sds((2 * tok, width))] * reach,
            scratch_shapes=[
                pltpu.VMEM((span, HEAD_DIM), BF16),
                pltpu.VMEM((span, HEAD_DIM), BF16),
                pltpu.VMEM((span, tok), F32),
                pltpu.VMEM((span, HEAD_DIM), F32),
                pltpu.VMEM((span, HEAD_DIM), F32),
                pltpu.VMEM((reach, 2 * tok, HEAD_DIM), BF16),
            ],
            compiler_params=params("arbitrary"),
            cost_estimate=cost(per * 4 * span * (span + tok) * HEAD_DIM, 4 * MIB, per * span * span // 2),
            name="columns",
        )(meta, qd, kvo, stats, bias, dk, dv)

    padded = jnp.pad(field_bias, ((0, 0), (0, tok - FIELDS)))
    my_bias = lax.dynamic_slice_in_dim(padded, p * group, group, 0)
    my_bias = jnp.broadcast_to(my_bias[:, :, None], (group, tok, HEAD_DIM))

    packed = [pack(c) for c in range(CHUNKS)]
    arrived = [[swapped(packed[c][m - 1], "seq", m) for m in range(1, reach)] for c in range(CHUNKS)]
    planes = [gather(c, arrived[c]) for c in range(CHUNKS)]
    before = [passed_along(kv, "seq", reach) for _, kv in planes]
    after = [passed_along(qd, "seq", -reach) for qd, _ in planes]
    parts, bias_parts, pending = [], [], []
    for c in range(CHUNKS):
        qd, kv = planes[c]
        bias = my_bias[c * per : (c + 1) * per]
        *dq, dk, dv, stats, gb = rows_of(qd, kv, before[c], bias)
        bias_parts.append(jnp.sum(gb, axis=1)[:, :FIELDS])
        dq = [dq[0]] + [swapped(dq[m], "seq", m) for m in range(1, reach)]
        pending.append((dq, dk, dv, passed_along(stats, "seq", -reach), bias))
    for c in range(CHUNKS):
        dq, dk, dv, stats, bias = pending[c]
        dkv = columns_of(after[c], planes[c][1], stats, bias, dk, dv)
        dkv = [dkv[0]] + [swapped(dkv[m], "seq", m) for m in range(1, reach)]
        for m in range(reach):
            parts += [dq[m], dkv[m]]

    total = jnp.concatenate(bias_parts, axis=0)
    mask = reach
    while mask < lax.axis_size("seq"):
        total = total + swapped(total, "seq", mask)
        mask *= 2
    mask = 1
    while mask < lax.axis_size("dp"):
        total = total + swapped(total, "dp", mask)
        mask *= 2
    mask = 1
    while mask < reach:
        other = swapped(total, "seq", mask)
        total = jnp.where(
            p & mask > 0,
            jnp.concatenate([other, total], axis=0),
            jnp.concatenate([total, other], axis=0),
        )
        mask *= 2

    grads = pl.pallas_call(
        functools.partial(unpack_kernel, reach, tok, width),
        in_specs=[SMEM] + [ANY] * len(parts),
        out_specs=[ANY] * 3,
        out_shape=[sds((1, tok, row_width))] * 3,
        scratch_shapes=[pltpu.SemaphoreType.DMA((CHUNKS * reach * 3,))],
        compiler_params=params(),
        name="unpack",
    )(meta, *parts)
    return (*grads, total)


def solution(mesh):
    return jax.shard_map(
        shards,
        mesh=mesh,
        in_specs=(
            P("dp", "seq", None),
            P("dp", "seq", None),
            P("dp", "seq", None),
            P("dp", "seq", None),
            P("dp"),
            P("dp", "seq"),
            P(),
        ),
        out_specs=(P("dp", "seq", None), P("dp", "seq", None), P("dp", "seq", None), P()),
        check_vma=False,
    )
```

time: 419 us -> 115 us (0.27)
  blocking collectives: 117 us -> 0 us
  waiting for transfers between devices: 123 us -> 21.3 us
  local copies, waits for them, and re-layouts: 63.1 us -> 15 us
  starting transfers between devices: 81.2 us -> 47.1 us
  Pallas kernels: 0 us -> 28.4 us
  matrix products: 20.4 us -> 0 us
  other arithmetic: 10.9 us -> 0.75 us
    ppermute x24 -> x6, waiting for transfers between devices: 123 us -> 0.02 us  [passed_along(): lax.ppermute(value, axis, [(source, source + steps) for source in range(f...]
    psum x1 -> x0, blocking collectives: 117 us -> none  [shards(): bias_total = lax.psum(bias_local, ('seq', 'dp'))]
    ppermute x24 -> x6, starting transfers between devices: 81.2 us -> 13 us  [passed_along(): lax.ppermute(value, axis, [(source, source + steps) for source in range(f...]
    ppermute x0 -> x23, starting transfers between devices: none -> 34.1 us  [swapped(): lax.ppermute(value, axis, [(source, source ^ mask) for source in range(co...]
    pallas_call x0 -> x9, Pallas kernels: none -> 28.4 us  [the longest x2 15 us: rows_of(): pl.pallas_call(functools.partial(rows_kernel, reach, tok), grid=(per,), i...]
    slice x13 -> x1, local copies, waits for them, and re-layouts: 24.4 us -> 0.01 us  [shards(): bias = my_bias[c * per:(c + 1) * per]]
    ppermute x0 -> x23, waiting for transfers between devices: none -> 21.3 us  [swapped(): lax.ppermute(value, axis, [(source, source ^ mask) for source in range(co...]
    concatenate x13 -> x0, local copies, waits for them, and re-layouts: 15.7 us -> none  [the longest x6 9.36 us: shards(): key_all = jnp.concatenate([arrival[0] for arrival in ordered], axis=0)]
  transfers between devices with their start and end apart: 24 -> 29, of which waited for: 5 -> 8; matrix products, arithmetic and copies ran while one was open for 10% -> 1% of each run, Pallas kernels for 0% -> 22%
where the time goes in v1:
time: 115 us; the launch traced here: 114 us
  starting transfers between devices  47.1 us (41%)
  Pallas kernels  28.4 us (25%)
  waiting for transfers between devices  21.3 us (19%)
  local copies, waits for them, and re-layouts  15 us (13%)
  between operations  1.54 us (1%)
    ppermute x23, starting transfers between devices, swapped(): lax.ppermute(value, axis, [(source, source ^ mask) for source in range(co...  34.1 us
    ppermute x23, waiting for transfers between devices, swapped(): lax.ppermute(value, axis, [(source, source ^ mask) for source in range(co...  21.3 us
    pallas_call x2, Pallas kernels, rows_of(): pl.pallas_call(functools.partial(rows_kernel, reach, tok), grid=(per,), i...  15 us
    unnamed x60, local copies, waits for them, and re-layouts  14.8 us
    ppermute x6, starting transfers between devices, passed_along(): lax.ppermute(value, axis, [(source, source + steps) for source in range(f...  13 us
    pallas_call x2, Pallas kernels, columns_of(): pl.pallas_call(functools.partial(columns_kernel, reach, tok), grid=(per,)...  6.38 us
    pallas_call x2, Pallas kernels, gather(): pl.pallas_call(functools.partial(gather_kernel, reach, tok, width, chunk)...  3.37 us
  transfers between devices with their start and end apart: 29, of which 8 were waited for; matrix products, arithmetic and copies ran while one was open for 1% of the time, Pallas kernels for 22%

profile of v1, /device:TPU:0, one launch (start us, length us, event | category | flops | bytes accessed | tf_op | source)
XLA Modules:
  0.0 114.1 jit_solution(15568838286032824883)
XLA Ops:
  1.4 0.6 copy-done.16
  1.9 1.0 copy-done
  3.0 1.0 copy-done.1
  4.0 1.0 copy-done.2
  5.1 1.0 copy-done.3
  6.1 0.9 pack.2
  7.0 3.0 %collective-permute-start = (bf16[528,256]{1,0:T(8,128)(2,1)S(1)}, bf16[528,256]{1,0:T(8,128)(2,1)S(1)}, u32[]{:S(2)}, u32[]{:S(2)}) collective-permute-start(bf16[528,256]{1,0:T(8,128)(2,1)S(1)} %get-tuple-element.41), channel_id=1, source_target_pairs={{0,2},{2,0},{4,6},{6,4},{8,10},{10,8},{12,14},{14,12},{16,18},{18,... | collective-permute-start | bytes 811016 | tf_op jit(solution)/shard_map/ppermute | solution.py:242
  10.0 1.5 %collective-permute-start.1 = (bf16[528,256]{1,0:T(8,128)(2,1)S(1)}, bf16[528,256]{1,0:T(8,128)(2,1)S(1)}, u32[]{:S(2)}, u32[]{:S(2)}) collective-permute-start(bf16[528,256]{1,0:T(8,128)(2,1)S(1)} %get-tuple-element.42), channel_id=1, source_target_pairs={{0,4},{2,6},{4,0},{6,2},{8,12},{10,14},{12,8},{14,10},{16,20},{18,... | collective-permute-start | bytes 811016 | tf_op jit(solution)/shard_map/ppermute | solution.py:242
  11.5 0.9 pack.3
  12.4 2.0 %collective-permute-start.12 = (bf16[528,256]{1,0:T(8,128)(2,1)S(1)}, bf16[528,256]{1,0:T(8,128)(2,1)S(1)}, u32[]{:S(2)}, u32[]{:S(2)}) collective-permute-start(bf16[528,256]{1,0:T(8,128)(2,1)S(1)} %get-tuple-element.57), channel_id=1, source_target_pairs={{0,2},{2,0},{4,6},{6,4},{8,10},{10,8},{12,14},{14,12},{16,18},{18,... | collective-permute-start | bytes 811016 | tf_op jit(solution)/shard_map/ppermute | solution.py:242
  14.4 1.5 %collective-permute-start.13 = (bf16[528,256]{1,0:T(8,128)(2,1)S(1)}, bf16[528,256]{1,0:T(8,128)(2,1)S(1)}, u32[]{:S(2)}, u32[]{:S(2)}) collective-permute-start(bf16[528,256]{1,0:T(8,128)(2,1)S(1)} %get-tuple-element.58), channel_id=1, source_target_pairs={{0,4},{2,6},{4,0},{6,2},{8,12},{10,14},{12,8},{14,10},{16,20},{18,... | collective-permute-start | bytes 811016 | tf_op jit(solution)/shard_map/ppermute | solution.py:242
  15.9 1.4 %collective-permute-done.rest_0_ = bf16[528,256]{1,0:T(8,128)(2,1)S(1)} collective-permute-done((bf16[528,256]{1,0:T(8,128)(2,1)S(1)}, bf16[528,256]{1,0:T(8,128)(2,1)S(1)}, u32[]{:S(2)}, u32[]{:S(2)}) %collective-permute-start) | collective-permute-done | bytes 270368 | tf_op jit(solution)/shard_map/ppermute | solution.py:242
  17.3 3.0 %collective-permute-start.14 = (bf16[528,256]{1,0:T(8,128)(2,1)S(1)}, bf16[528,256]{1,0:T(8,128)(2,1)S(1)}, u32[]{:S(2)}, u32[]{:S(2)}) collective-permute-start(bf16[528,256]{1,0:T(8,128)(2,1)S(1)} %get-tuple-element.59), channel_id=1, source_target_pairs={{0,6},{2,4},{4,2},{6,0},{8,14},{10,12},{12,10},{14,8},{16,22},{18,... | collective-permute-start | bytes 811016 | tf_op jit(solution)/shard_map/ppermute | solution.py:242
  20.3 4.9 %collective-permute-done.1.rest_1_ = bf16[528,256]{1,0:T(8,128)(2,1)S(1)} collective-permute-done((bf16[528,256]{1,0:T(8,128)(2,1)S(1)}, bf16[528,256]{1,0:T(8,128)(2,1)S(1)}, u32[]{:S(2)}, u32[]{:S(2)}) %collective-permute-start.1) | collective-permute-done | bytes 270368 | tf_op jit(solution)/shard_map/ppermute | solution.py:242
  25.2 1.7 %gather.2 = (bf16[4,256,256]{2,1,0:T(8,128)(2,1)}, bf16[4,272,256]{2,1,0:T(8,128)(2,1)S(1)}) custom-call(s32[3]{0:T(128)S(1)} %pad_add_fusion.meta, bf16[1,128,2048]{2,1,0:T(8,128)(2,1)S(1)} %copy-done, bf16[1,128,2048]{2,1,0:T(8,128)(2,1)S(1)} %copy-done.1, bf16[1,128,2048]{2,1,0:T(8,128)(2,1)S(1)} %copy-done.2, bf16[1,128,2048]{2,1,0:T(8,128)(2,1)S(1)} %copy-done.3, ...), custom_call_target="tpu_custom_call" | custom-call | tf_op jit(solution)/shard_map/gather/pallas_call | solution.py:284
  26.9 3.5 %collective-permute-start.3 = (bf16[4,272,256]{2,1,0:T(8,128)(2,1)S(1)}, bf16[4,272,256]{2,1,0:T(8,128)(2,1)S(1)}, u32[]{:S(2)}, u32[]{:S(2)}) collective-permute-start(bf16[4,272,256]{2,1,0:T(8,128)(2,1)S(1)} %get-tuple-element.45.kvo), channel_id=1, source_target_pairs={{0,8},{2,10},{4,12},{6,14},{8,16},{10,18},{12,20},{14,22},{16,24},... | collective-permute-start | bytes 1671176 | tf_op jit(solution)/shard_map/ppermute | solution.py:248
  30.4 4.9 %collective-permute-done.13.rest_1_ = bf16[528,256]{1,0:T(8,128)(2,1)S(1)} collective-permute-done((bf16[528,256]{1,0:T(8,128)(2,1)S(1)}, bf16[528,256]{1,0:T(8,128)(2,1)S(1)}, u32[]{:S(2)}, u32[]{:S(2)}) %collective-permute-start.13) | collective-permute-done | bytes 270368 | tf_op jit(solution)/shard_map/ppermute | solution.py:242
  35.3 1.7 %gather.3 = (bf16[4,256,256]{2,1,0:T(8,128)(2,1)}, bf16[4,272,256]{2,1,0:T(8,128)(2,1)S(1)}) custom-call(s32[3]{0:T(128)S(1)} %pad_add_fusion.meta, bf16[1,128,2048]{2,1,0:T(8,128)(2,1)S(1)} %copy-done, bf16[1,128,2048]{2,1,0:T(8,128)(2,1)S(1)} %copy-done.1, bf16[1,128,2048]{2,1,0:T(8,128)(2,1)S(1)} %copy-done.2, bf16[1,128,2048]{2,1,0:T(8,128)(2,1)S(1)} %copy-done.3, ...), custom_call_target="tpu_custom_call" | custom-call | tf_op jit(solution)/shard_map/gather/pallas_call | solution.py:284
  37.0 4.3 %collective-permute-start.15 = (bf16[4,272,256]{2,1,0:T(8,128)(2,1)S(1)}, bf16[4,272,256]{2,1,0:T(8,128)(2,1)}, u32[]{:S(2)}, u32[]{:S(2)}) collective-permute-start(bf16[4,272,256]{2,1,0:T(8,128)(2,1)S(1)} %get-tuple-element.61.kvo), channel_id=1, source_target_pairs={{0,8},{2,10},{4,12},{6,14},{8,16},{10,18},{12,20},{14,22},{16,24},... | collective-permute-start | bytes 1671176 | tf_op jit(solution)/shard_map/ppermute | solution.py:248
  41.3 1.3 %collective-permute-start.4 = (bf16[4,256,256]{2,1,0:T(8,128)(2,1)}, bf16[4,256,256]{2,1,0:T(8,128)(2,1)S(1)}, u32[]{:S(2)}, u32[]{:S(2)}) collective-permute-start(bf16[4,256,256]{2,1,0:T(8,128)(2,1)} %get-tuple-element.44.qd), channel_id=1, source_target_pairs={{8,0},{10,2},{12,4},{14,6},{16,8},{18,10},{20,12},{22,14},{24,16},... | collective-permute-start | bytes 1572872 | tf_op jit(solution)/shard_map/ppermute | solution.py:248
  42.6 1.3 %collective-permute-start.16 = (bf16[4,256,256]{2,1,0:T(8,128)(2,1)}, bf16[4,256,256]{2,1,0:T(8,128)(2,1)S(1)}, u32[]{:S(2)}, u32[]{:S(2)}) collective-permute-start(bf16[4,256,256]{2,1,0:T(8,128)(2,1)} %get-tuple-element.60.qd), channel_id=1, source_target_pairs={{8,0},{10,2},{12,4},{14,6},{16,8},{18,10},{20,12},{22,14},{24,16},... | collective-permute-start | bytes 1572872 | tf_op jit(solution)/shard_map/ppermute | solution.py:248
  44.1 7.1 %rows.2 = (bf16[128,256]{1,0:T(8,128)(2,1)S(1)}, bf16[128,256]{1,0:T(8,128)(2,1)S(1)}, bf16[128,256]{1,0:T(8,128)(2,1)S(1)}, bf16[128,256]{1,0:T(8,128)(2,1)S(1)...) custom-call(s32[3]{0:T(128)S(1)} %pad_add_fusion.meta, ...), custom_call_target="tpu_custom_call" | custom-call | flops 1006632960 | bytes 4194304 | tf_op jit(solution)/shard_map/rows/pallas_call | solution.py:304
  51.1 0.6 copy-done.21
  51.7 0.6 copy-done.25
  52.4 0.6 copy-done.26
  53.0 0.6 copy-done.27
  53.7 8.0 %rows.3 = (bf16[128,256]{1,0:T(8,128)(2,1)S(1)}, bf16[128,256]{1,0:T(8,128)(2,1)S(1)}, bf16[128,256]{1,0:T(8,128)(2,1)S(1)}, bf16[128,256]{1,0:T(8,128)(2,1)S(1)...) custom-call(s32[3]{0:T(128)S(1)} %pad_add_fusion.meta, ...), custom_call_target="tpu_custom_call" | custom-call | flops 1006632960 | bytes 4194304 | tf_op jit(solution)/shard_map/rows/pallas_call | solution.py:304
  61.7 0.6 copy-done.8
  62.3 0.6 copy-done.17
  62.9 0.6 copy-done.19
  63.5 0.6 copy-done.23
  64.2 3.3 %collective-permute-start.24 = (f32[4,64]{1,0:T(4,128)S(1)}, f32[4,64]{1,0:T(4,128)S(1)}, u32[]{:S(2)}, u32[]{:S(2)}) collective-permute-start(f32[4,64]{1,0:T(4,128)S(1)} %pad_maximum_fusion), channel_id=1, source_target_pairs={{0,8},{2,10},{4,12},{6,14},{8,0},{10,2},{12,4},{14,6},{16,24},{18,... | collective-permute-start | bytes 3080 | tf_op jit(solution)/shard_map/ppermute | solution.py:242
  67.5 1.3 %collective-permute-start.5 = (f32[2,8,512]{2,1,0:T(8,128)S(1)}, f32[2,8,512]{2,1,0:T(8,128)S(1)}, u32[]{:S(2)}, u32[]{:S(2)}) collective-permute-start(f32[2,8,512]{2,1,0:T(8,128)S(1)} %copy-done.28), channel_id=1, source_target_pairs={{8,0},{10,2},{12,4},{14,6},{16,8},{18,10},{20,12},{22,14},{24,16},... | collective-permute-start | bytes 98312 | tf_op jit(solution)/shard_map/ppermute | solution.py:248
  68.8 0.3 collective-permute-done.24
  69.1 3.6 %collective-permute-start.25 = (f32[4,64]{1,0:T(4,128)S(1)}, f32[4,64]{1,0:T(4,128)S(1)}, u32[]{:S(2)}, u32[]{:S(2)}) collective-permute-start(f32[4,64]{1,0:T(4,128)S(1)} %fusion), channel_id=1, source_target_pairs={{0,16},{2,18},{4,20},{6,22},{8,24},{10,26},{12,28},{14,30},{16,0},... | collective-permute-start | bytes 3080 | tf_op jit(solution)/shard_map/ppermute | solution.py:242
  72.6 1.6 %collective-permute-done.25 = f32[4,64]{1,0:T(4,128)S(1)} collective-permute-done((f32[4,64]{1,0:T(4,128)S(1)}, f32[4,64]{1,0:T(4,128)S(1)}, u32[]{:S(2)}, u32[]{:S(2)}) %collective-permute-start.25) | collective-permute-done | bytes 1056 | tf_op jit(solution)/shard_map/ppermute | solution.py:242
  74.2 1.3 %collective-permute-start.6 = (bf16[128,256]{1,0:T(8,128)(2,1)}, bf16[128,256]{1,0:T(8,128)(2,1)S(1)}, u32[]{:S(2)}, u32[]{:S(2)}) collective-permute-start(bf16[128,256]{1,0:T(8,128)(2,1)} %copy-done.26), channel_id=1, source_target_pairs={{0,2},{2,0},{4,6},{6,4},{8,10},{10,8},{12,14},{14,12},{16,18},{18,... | collective-permute-start | bytes 196616 | tf_op jit(solution)/shard_map/ppermute | solution.py:242
  75.5 1.4 %collective-permute-start.8 = (bf16[128,256]{1,0:T(8,128)(2,1)}, bf16[128,256]{1,0:T(8,128)(2,1)S(1)}, u32[]{:S(2)}, u32[]{:S(2)}) collective-permute-start(bf16[128,256]{1,0:T(8,128)(2,1)} %copy-done.25), channel_id=1, source_target_pairs={{0,4},{2,6},{4,0},{6,2},{8,12},{10,14},{12,8},{14,10},{16,20},{18,... | collective-permute-start | bytes 196616 | tf_op jit(solution)/shard_map/ppermute | solution.py:242
  76.8 1.3 %collective-permute-start.17 = (f32[2,8,512]{2,1,0:T(8,128)}, f32[2,8,512]{2,1,0:T(8,128)S(1)}, u32[]{:S(2)}, u32[]{:S(2)}) collective-permute-start(f32[2,8,512]{2,1,0:T(8,128)} %get-tuple-element.63), channel_id=1, source_target_pairs={{8,0},{10,2},{12,4},{14,6},{16,8},{18,10},{20,12},{22,14},{24,16},... | collective-permute-start | bytes 98312 | tf_op jit(solution)/shard_map/ppermute | solution.py:248
  78.2 0.6 copy-done.14
  78.8 0.9 collective-permute-start.27
  79.6 1.0 copy-done.5
  80.7 1.0 copy-done.7
  81.7 0.8 copy-done.15
  82.5 3.5 %columns.2 = (bf16[256,256]{1,0:T(8,128)(2,1)S(1)}, bf16[256,256]{1,0:T(8,128)(2,1)S(1)}, bf16[256,256]{1,0:T(8,128)(2,1)}, bf16[256,256]{1,0:T(8,128)(2,1)}) custom-call(s32[3]{0:T(128)S(1)} %pad_add_fusion.meta, bf16[4,256,256]{2,1,0:T(8,128)(2,1)S(1)} %collective-permute-done.4.qd, bf16[4,272,256]{2,1,0:T(8,128)(2,1)S(1)} %get-tuple-element.45.kvo, ...), custom_call_target="tpu_custom_call" | custom-call | flops 335544320 | bytes 4194304 | tf_op jit(solution)/shard_map/columns/pallas_call | solution.py:333
  86.0 1.1 %collective-permute-start.7 = (bf16[256,256]{1,0:T(8,128)(2,1)S(1)}, bf16[256,256]{1,0:T(8,128)(2,1)S(1)}, u32[]{:S(2)}, u32[]{:S(2)}) collective-permute-start(bf16[256,256]{1,0:T(8,128)(2,1)S(1)} %get-tuple-element.52), channel_id=1, source_target_pairs={{0,2},{2,0},{4,6},{6,4},{8,10},{10,8},{12,14},{14,12},{16,18},{18,... | collective-permute-start | bytes 393224 | tf_op jit(solution)/shard_map/ppermute | solution.py:242
  87.2 0.7 collective-permute-start.28
  87.9 2.9 %collective-permute-done.28 = f32[8,64]{1,0:T(8,128)S(1)} collective-permute-done((f32[8,64]{1,0:T(8,128)S(1)}, f32[8,64]{1,0:T(8,128)S(1)}, u32[]{:S(2)}, u32[]{:S(2)}) %collective-permute-start.28) | collective-permute-done | bytes 2080 | tf_op jit(solution)/shard_map/ppermute | solution.py:242
  90.8 1.2 %collective-permute-start.10 = (bf16[128,256]{1,0:T(8,128)(2,1)S(1)}, bf16[128,256]{1,0:T(8,128)(2,1)S(1)}, u32[]{:S(2)}, u32[]{:S(2)}) collective-permute-start(bf16[128,256]{1,0:T(8,128)(2,1)S(1)} %copy-done.22), channel_id=1, source_target_pairs={{0,6},{2,4},{4,2},{6,0},{8,14},{10,12},{12,10},{14,8},{16,22},{18,... | collective-permute-start | bytes 196616 | tf_op jit(solution)/shard_map/ppermute | solution.py:242
  92.1 0.9 collective-permute-start.18
  93.0 1.4 %collective-permute-start.20 = (bf16[128,256]{1,0:T(8,128)(2,1)S(1)}, bf16[128,256]{1,0:T(8,128)(2,1)S(1)}, u32[]{:S(2)}, u32[]{:S(2)}) collective-permute-start(bf16[128,256]{1,0:T(8,128)(2,1)S(1)} %copy-done.20), channel_id=1, source_target_pairs={{0,4},{2,6},{4,0},{6,2},{8,12},{10,14},{12,8},{14,10},{16,20},{18,... | collective-permute-start | bytes 196616 | tf_op jit(solution)/shard_map/ppermute | solution.py:242
  94.4 1.3 %collective-permute-start.22 = (bf16[128,256]{1,0:T(8,128)(2,1)S(1)}, bf16[128,256]{1,0:T(8,128)(2,1)S(1)}, u32[]{:S(2)}, u32[]{:S(2)}) collective-permute-start(bf16[128,256]{1,0:T(8,128)(2,1)S(1)} %copy-done.18), channel_id=1, source_target_pairs={{0,6},{2,4},{4,2},{6,0},{8,14},{10,12},{12,10},{14,8},{16,22},{18,... | collective-permute-start | bytes 196616 | tf_op jit(solution)/shard_map/ppermute | solution.py:242
  95.7 2.9 %columns.3 = (bf16[256,256]{1,0:T(8,128)(2,1)S(1)}, bf16[256,256]{1,0:T(8,128)(2,1)S(1)}, bf16[256,256]{1,0:T(8,128)(2,1)S(1)}, bf16[256,256]{1,0:T(8,128)(2,1)S(1)}) custom-call(s32[3]{0:T(128)S(1)} %pad_add_fusion.meta, bf16[4,256,256]{2,1,0:T(8,128)(2,1)S(1)} %collective-permute-done.16.qd, bf16[4,272,256]{2,1,0:T(8,128)(2,1)S(1)} %get-tuple-element.61.kvo, ...), custom_call_target="tpu_custom_call" | custom-call | flops 335544320 | bytes 4194304 | tf_op jit(solution)/shard_map/columns/pallas_call | solution.py:333
  98.6 1.2 %collective-permute-start.9 = (bf16[256,256]{1,0:T(8,128)(2,1)}, bf16[256,256]{1,0:T(8,128)(2,1)S(1)}, u32[]{:S(2)}, u32[]{:S(2)}) collective-permute-start(bf16[256,256]{1,0:T(8,128)(2,1)} %get-tuple-element.54), channel_id=1, source_target_pairs={{0,4},{2,6},{4,0},{6,2},{8,12},{10,14},{12,8},{14,10},{16,20},{18,... | collective-permute-start | bytes 393224 | tf_op jit(solution)/shard_map/ppermute | solution.py:242
  99.8 1.3 %collective-permute-start.11 = (bf16[256,256]{1,0:T(8,128)(2,1)}, bf16[256,256]{1,0:T(8,128)(2,1)S(1)}, u32[]{:S(2)}, u32[]{:S(2)}) collective-permute-start(bf16[256,256]{1,0:T(8,128)(2,1)} %get-tuple-element.56), channel_id=1, source_target_pairs={{0,6},{2,4},{4,2},{6,0},{8,14},{10,12},{12,10},{14,8},{16,22},{18,... | collective-permute-start | bytes 393224 | tf_op jit(solution)/shard_map/ppermute | solution.py:242
  101.1 1.1 %collective-permute-start.19 = (bf16[256,256]{1,0:T(8,128)(2,1)S(1)}, bf16[256,256]{1,0:T(8,128)(2,1)S(1)}, u32[]{:S(2)}, u32[]{:S(2)}) collective-permute-start(bf16[256,256]{1,0:T(8,128)(2,1)S(1)} %get-tuple-element.68), channel_id=1, source_target_pairs={{0,2},{2,0},{4,6},{6,4},{8,10},{10,8},{12,14},{14,12},{16,18},{18,... | collective-permute-start | bytes 393224 | tf_op jit(solution)/shard_map/ppermute | solution.py:242
  102.2 1.1 collective-permute-start.21
  103.3 1.3 %collective-permute-start.23 = (bf16[256,256]{1,0:T(8,128)(2,1)S(1)}, bf16[256,256]{1,0:T(8,128)(2,1)S(1)}, u32[]{:S(2)}, u32[]{:S(2)}) collective-permute-start(bf16[256,256]{1,0:T(8,128)(2,1)S(1)} %get-tuple-element.72), channel_id=1, source_target_pairs={{0,6},{2,4},{4,2},{6,0},{8,14},{10,12},{12,10},{14,8},{16,22},{18,... | collective-permute-start | bytes 393224 | tf_op jit(solution)/shard_map/ppermute | solution.py:242
  104.6 0.6 maximum_select_fusion
  105.2 2.5 %collective-permute-done.9.rest_5_ = bf16[256,256]{1,0:T(8,128)(2,1)S(1)} collective-permute-done((bf16[256,256]{1,0:T(8,128)(2,1)}, bf16[256,256]{1,0:T(8,128)(2,1)S(1)}, u32[]{:S(2)}, u32[]{:S(2)}) %collective-permute-start.9) | collective-permute-done | bytes 131104 | tf_op jit(solution)/shard_map/ppermute | solution.py:242
  107.7 2.8 %collective-permute-done.21.rest_13_ = bf16[256,256]{1,0:T(8,128)(2,1)S(1)} collective-permute-done((bf16[256,256]{1,0:T(8,128)(2,1)S(1)}, bf16[256,256]{1,0:T(8,128)(2,1)S(1)}, u32[]{:S(2)}, u32[]{:S(2)}) %collective-permute-start.21) | collective-permute-done | bytes 131104 | tf_op jit(solution)/shard_map/ppermute | solution.py:242
  110.5 0.8 copy-done.11
  111.3 0.8 copy-done.13
  112.2 1.9 %unpack.1 = (bf16[1,128,2048]{2,1,0:T(8,128)(2,1)}, bf16[1,128,2048]{2,1,0:T(8,128)(2,1)}, bf16[1,128,2048]{2,1,0:T(8,128)(2,1)}) custom-call(s32[3]{0:T(128)S(1)} %pad_add_fusion.meta, bf16[128,256]{1,0:T(8,128)(2,1)S(1)} %get-tuple-element.46.rest_0_, bf16[256,256]{1,0:T(8,128)(2,1)S(1)} %get-tuple-element.50.rest_1_, bf16[128,256]{1,0:T(8,128)(2,1)S(1)} %copy-done.11, ...), custom_call_target="tpu_custom_call" | custom-call | tf_op jit(solution)/shard_map/unpack/pallas_call | solution.py:395
  (76 shorter events, 0.5 us)
Async XLA Ops:
  1.3 0.7 copy-start.16
  1.9 1.0 copy-start
  3.0 1.0 copy-start.1
  4.0 1.0 copy-start.2
  5.1 1.0 copy-start.3
  7.0 10.3 %collective-permute-start = (bf16[528,256]{1,0:T(8,128)(2,1)S(1)}, bf16[528,256]{1,0:T(8,128)(2,1)S(1)}, u32[]{:S(2)}, u32[]{:S(2)}) collective-permute-start(bf16[528,256]{1,0:T(8,128)(2,1)S(1)} %get-tuple-element.41), channel_id=1, source_target_pairs={{0,2},{2,0},{4,6},{6,4},{8,10},{10,8},{12,14},{14,12},{16,18},{18,... | collective-permute-start | bytes 811016 | tf_op jit(solution)/shard_map/ppermute | solution.py:242
  10.0 15.2 %collective-permute-start.1 = (bf16[528,256]{1,0:T(8,128)(2,1)S(1)}, bf16[528,256]{1,0:T(8,128)(2,1)S(1)}, u32[]{:S(2)}, u32[]{:S(2)}) collective-permute-start(bf16[528,256]{1,0:T(8,128)(2,1)S(1)} %get-tuple-element.42), channel_id=1, source_target_pairs={{0,4},{2,6},{4,0},{6,2},{8,12},{10,14},{12,8},{14,10},{16,20},{18,... | collective-permute-start | bytes 811016 | tf_op jit(solution)/shard_map/ppermute | solution.py:242
  11.5 13.7 %collective-permute-start.2 = (bf16[528,256]{1,0:T(8,128)(2,1)S(1)}, bf16[528,256]{1,0:T(8,128)(2,1)S(1)}, u32[]{:S(2)}, u32[]{:S(2)}) collective-permute-start(bf16[528,256]{1,0:T(8,128)(2,1)S(1)} %get-tuple-element.43), channel_id=1, source_target_pairs={{0,6},{2,4},{4,2},{6,0},{8,14},{10,12},{12,10},{14,8},{16,22},{18,... | collective-permute-start | bytes 811016 | tf_op jit(solution)/shard_map/ppermute | solution.py:242
  12.4 18.0 %collective-permute-start.12 = (bf16[528,256]{1,0:T(8,128)(2,1)S(1)}, bf16[528,256]{1,0:T(8,128)(2,1)S(1)}, u32[]{:S(2)}, u32[]{:S(2)}) collective-permute-start(bf16[528,256]{1,0:T(8,128)(2,1)S(1)} %get-tuple-element.57), channel_id=1, source_target_pairs={{0,2},{2,0},{4,6},{6,4},{8,10},{10,8},{12,14},{14,12},{16,18},{18,... | collective-permute-start | bytes 811016 | tf_op jit(solution)/shard_map/ppermute | solution.py:242
  14.4 20.9 %collective-permute-start.13 = (bf16[528,256]{1,0:T(8,128)(2,1)S(1)}, bf16[528,256]{1,0:T(8,128)(2,1)S(1)}, u32[]{:S(2)}, u32[]{:S(2)}) collective-permute-start(bf16[528,256]{1,0:T(8,128)(2,1)S(1)} %get-tuple-element.58), channel_id=1, source_target_pairs={{0,4},{2,6},{4,0},{6,2},{8,12},{10,14},{12,8},{14,10},{16,20},{18,... | collective-permute-start | bytes 811016 | tf_op jit(solution)/shard_map/ppermute | solution.py:242
  17.3 18.0 %collective-permute-start.14 = (bf16[528,256]{1,0:T(8,128)(2,1)S(1)}, bf16[528,256]{1,0:T(8,128)(2,1)S(1)}, u32[]{:S(2)}, u32[]{:S(2)}) collective-permute-start(bf16[528,256]{1,0:T(8,128)(2,1)S(1)} %get-tuple-element.59), channel_id=1, source_target_pairs={{0,6},{2,4},{4,2},{6,0},{8,14},{10,12},{12,10},{14,8},{16,22},{18,... | collective-permute-start | bytes 811016 | tf_op jit(solution)/shard_map/ppermute | solution.py:242
  26.9 17.1 %collective-permute-start.3 = (bf16[4,272,256]{2,1,0:T(8,128)(2,1)S(1)}, bf16[4,272,256]{2,1,0:T(8,128)(2,1)S(1)}, u32[]{:S(2)}, u32[]{:S(2)}) collective-permute-start(bf16[4,272,256]{2,1,0:T(8,128)(2,1)S(1)} %get-tuple-element.45.kvo), channel_id=1, source_target_pairs={{0,8},{2,10},{4,12},{6,14},{8,16},{10,18},{12,20},{14,22},{16,24},... | collective-permute-start | bytes 1671176 | tf_op jit(solution)/shard_map/ppermute | solution.py:248
  37.0 4.3 %copy-start.29 = (bf16[16,64]{1,0:T(8,128)(2,1)S(1)}, bf16[16,64]{1,0:T(8,128)(2,1)}, u32[]{:S(2)}) copy-start(bf16[16,64]{1,0:T(8,128)(2,1)} %param.13) | copy-start | bytes 6148
  37.0 16.6 %collective-permute-start.15 = (bf16[4,272,256]{2,1,0:T(8,128)(2,1)S(1)}, bf16[4,272,256]{2,1,0:T(8,128)(2,1)}, u32[]{:S(2)}, u32[]{:S(2)}) collective-permute-start(bf16[4,272,256]{2,1,0:T(8,128)(2,1)S(1)} %get-tuple-element.61.kvo), channel_id=1, source_target_pairs={{0,8},{2,10},{4,12},{6,14},{8,16},{10,18},{12,20},{14,22},{16,24},... | collective-permute-start | bytes 1671176 | tf_op jit(solution)/shard_map/ppermute | solution.py:248
  41.3 35.5 %collective-permute-start.4 = (bf16[4,256,256]{2,1,0:T(8,128)(2,1)}, bf16[4,256,256]{2,1,0:T(8,128)(2,1)S(1)}, u32[]{:S(2)}, u32[]{:S(2)}) collective-permute-start(bf16[4,256,256]{2,1,0:T(8,128)(2,1)} %get-tuple-element.44.qd), channel_id=1, source_target_pairs={{8,0},{10,2},{12,4},{14,6},{16,8},{18,10},{20,12},{22,14},{24,16},... | collective-permute-start | bytes 1572872 | tf_op jit(solution)/shard_map/ppermute | solution.py:248
  42.6 44.5 %collective-permute-start.16 = (bf16[4,256,256]{2,1,0:T(8,128)(2,1)}, bf16[4,256,256]{2,1,0:T(8,128)(2,1)S(1)}, u32[]{:S(2)}, u32[]{:S(2)}) collective-permute-start(bf16[4,256,256]{2,1,0:T(8,128)(2,1)} %get-tuple-element.60.qd), channel_id=1, source_target_pairs={{8,0},{10,2},{12,4},{14,6},{16,8},{18,10},{20,12},{22,14},{24,16},... | collective-permute-start | bytes 1572872 | tf_op jit(solution)/shard_map/ppermute | solution.py:248
  51.1 0.6 copy-start.21
  51.7 0.6 copy-start.25
  52.4 0.6 copy-start.26
  53.0 0.6 copy-start.27
  53.6 8.1 %copy-start.4 = (f32[512,256]{1,0:T(8,128)}, f32[512,256]{1,0:T(8,128)S(1)}, u32[]{:S(2)}) copy-start(f32[512,256]{1,0:T(8,128)S(1)} %get-tuple-element.48.dk_in) | copy-start | bytes 1572868
  53.6 8.1 %copy-start.6 = (f32[512,256]{1,0:T(8,128)}, f32[512,256]{1,0:T(8,128)S(1)}, u32[]{:S(2)}) copy-start(f32[512,256]{1,0:T(8,128)S(1)} %get-tuple-element.49.dv_in) | copy-start | bytes 1572868
  61.7 0.6 copy-start.8
  62.3 0.6 copy-start.17
  62.9 0.6 copy-start.19
  63.5 0.6 copy-start.23
  64.1 3.4 %copy-start.28 = (f32[2,8,512]{2,1,0:T(8,128)S(1)}, f32[2,8,512]{2,1,0:T(8,128)}, u32[]{:S(2)}) copy-start(f32[2,8,512]{2,1,0:T(8,128)} %copy-done.27) | copy-start | bytes 98308
  64.2 4.9 %collective-permute-start.24 = (f32[4,64]{1,0:T(4,128)S(1)}, f32[4,64]{1,0:T(4,128)S(1)}, u32[]{:S(2)}, u32[]{:S(2)}) collective-permute-start(f32[4,64]{1,0:T(4,128)S(1)} %pad_maximum_fusion), channel_id=1, source_target_pairs={{0,8},{2,10},{4,12},{6,14},{8,0},{10,2},{12,4},{14,6},{16,24},{18,... | collective-permute-start | bytes 3080 | tf_op jit(solution)/shard_map/ppermute | solution.py:242
  67.5 10.6 %collective-permute-start.5 = (f32[2,8,512]{2,1,0:T(8,128)S(1)}, f32[2,8,512]{2,1,0:T(8,128)S(1)}, u32[]{:S(2)}, u32[]{:S(2)}) collective-permute-start(f32[2,8,512]{2,1,0:T(8,128)S(1)} %copy-done.28), channel_id=1, source_target_pairs={{8,0},{10,2},{12,4},{14,6},{16,8},{18,10},{20,12},{22,14},{24,16},... | collective-permute-start | bytes 98312 | tf_op jit(solution)/shard_map/ppermute | solution.py:248
  69.1 5.1 %collective-permute-start.25 = (f32[4,64]{1,0:T(4,128)S(1)}, f32[4,64]{1,0:T(4,128)S(1)}, u32[]{:S(2)}, u32[]{:S(2)}) collective-permute-start(f32[4,64]{1,0:T(4,128)S(1)} %fusion), channel_id=1, source_target_pairs={{0,16},{2,18},{4,20},{6,22},{8,24},{10,26},{12,28},{14,30},{16,0},... | collective-permute-start | bytes 3080 | tf_op jit(solution)/shard_map/ppermute | solution.py:242
  74.2 1.3 %collective-permute-start.26 = (f32[4,64]{1,0:T(4,128)S(1)}, f32[4,64]{1,0:T(4,128)S(1)}, u32[]{:S(2)}, u32[]{:S(2)}) collective-permute-start(f32[4,64]{1,0:T(4,128)S(1)} %add.16), channel_id=1, source_target_pairs={{0,1},{1,0},{2,3},{3,2},{4,5},{5,4},{6,7},{7,6},{8,9},{9,8},{10,11... | collective-permute-start | bytes 3080 | tf_op jit(solution)/shard_map/ppermute | solution.py:242
  74.2 18.8 %collective-permute-start.6 = (bf16[128,256]{1,0:T(8,128)(2,1)}, bf16[128,256]{1,0:T(8,128)(2,1)S(1)}, u32[]{:S(2)}, u32[]{:S(2)}) collective-permute-start(bf16[128,256]{1,0:T(8,128)(2,1)} %copy-done.26), channel_id=1, source_target_pairs={{0,2},{2,0},{4,6},{6,4},{8,10},{10,8},{12,14},{14,12},{16,18},{18,... | collective-permute-start | bytes 196616 | tf_op jit(solution)/shard_map/ppermute | solution.py:242
  75.5 18.9 %collective-permute-start.8 = (bf16[128,256]{1,0:T(8,128)(2,1)}, bf16[128,256]{1,0:T(8,128)(2,1)S(1)}, u32[]{:S(2)}, u32[]{:S(2)}) collective-permute-start(bf16[128,256]{1,0:T(8,128)(2,1)} %copy-done.25), channel_id=1, source_target_pairs={{0,4},{2,6},{4,0},{6,2},{8,12},{10,14},{12,8},{14,10},{16,20},{18,... | collective-permute-start | bytes 196616 | tf_op jit(solution)/shard_map/ppermute | solution.py:242
  76.8 15.2 %collective-permute-start.17 = (f32[2,8,512]{2,1,0:T(8,128)}, f32[2,8,512]{2,1,0:T(8,128)S(1)}, u32[]{:S(2)}, u32[]{:S(2)}) collective-permute-start(f32[2,8,512]{2,1,0:T(8,128)} %get-tuple-element.63), channel_id=1, source_target_pairs={{8,0},{10,2},{12,4},{14,6},{16,8},{18,10},{20,12},{22,14},{24,16},... | collective-permute-start | bytes 98312 | tf_op jit(solution)/shard_map/ppermute | solution.py:248
  78.1 0.6 copy-start.14
  78.8 7.2 %collective-permute-start.27 = (f32[4,64]{1,0:T(4,128)S(1)}, f32[4,64]{1,0:T(4,128)S(1)}, u32[]{:S(2)}, u32[]{:S(2)}) collective-permute-start(f32[4,64]{1,0:T(4,128)S(1)} %add.17), channel_id=1, source_target_pairs={{0,2},{2,0},{4,6},{6,4},{8,10},{10,8},{12,14},{14,12},{16,18},{18,... | collective-permute-start | bytes 3080 | tf_op jit(solution)/shard_map/ppermute | solution.py:242
  79.6 1.0 copy-start.5
  80.7 1.0 copy-start.7
  81.7 0.8 copy-start.15
  82.5 8.4 %copy-start.22 = (bf16[128,256]{1,0:T(8,128)(2,1)S(1)}, bf16[128,256]{1,0:T(8,128)(2,1)}, u32[]{:S(2)}) copy-start(bf16[128,256]{1,0:T(8,128)(2,1)} %copy-done.21) | copy-start | bytes 196612
  82.5 9.6 %copy-start.24 = (bf16[128,256]{1,0:T(8,128)(2,1)S(1)}, bf16[128,256]{1,0:T(8,128)(2,1)}, u32[]{:S(2)}) copy-start(bf16[128,256]{1,0:T(8,128)(2,1)} %copy-done.23) | copy-start | bytes 196612
  82.5 10.5 %copy-start.20 = (bf16[128,256]{1,0:T(8,128)(2,1)S(1)}, bf16[128,256]{1,0:T(8,128)(2,1)}, u32[]{:S(2)}) copy-start(bf16[128,256]{1,0:T(8,128)(2,1)} %copy-done.19) | copy-start | bytes 196612
  82.5 11.9 %copy-start.18 = (bf16[128,256]{1,0:T(8,128)(2,1)S(1)}, bf16[128,256]{1,0:T(8,128)(2,1)}, u32[]{:S(2)}) copy-start(bf16[128,256]{1,0:T(8,128)(2,1)} %copy-done.17) | copy-start | bytes 196612
  86.0 17.3 %collective-permute-start.7 = (bf16[256,256]{1,0:T(8,128)(2,1)S(1)}, bf16[256,256]{1,0:T(8,128)(2,1)S(1)}, u32[]{:S(2)}, u32[]{:S(2)}) collective-permute-start(bf16[256,256]{1,0:T(8,128)(2,1)S(1)} %get-tuple-element.52), channel_id=1, source_target_pairs={{0,2},{2,0},{4,6},{6,4},{8,10},{10,8},{12,14},{14,12},{16,18},{18,... | collective-permute-start | bytes 393224 | tf_op jit(solution)/shard_map/ppermute | solution.py:242
  87.2 3.7 %collective-permute-start.28 = (f32[8,64]{1,0:T(8,128)S(1)}, f32[8,64]{1,0:T(8,128)S(1)}, u32[]{:S(2)}, u32[]{:S(2)}) collective-permute-start(f32[8,64]{1,0:T(8,128)S(1)} %maximum_select_fusion.1), channel_id=1, source_target_pairs={{0,4},{2,6},{4,0},{6,2},{8,12},{10,14},{12,8},{14,10},{16,20},{18,... | collective-permute-start | bytes 6152 | tf_op jit(solution)/shard_map/ppermute | solution.py:242
  90.8 7.8 %collective-permute-start.10 = (bf16[128,256]{1,0:T(8,128)(2,1)S(1)}, bf16[128,256]{1,0:T(8,128)(2,1)S(1)}, u32[]{:S(2)}, u32[]{:S(2)}) collective-permute-start(bf16[128,256]{1,0:T(8,128)(2,1)S(1)} %copy-done.22), channel_id=1, source_target_pairs={{0,6},{2,4},{4,2},{6,0},{8,14},{10,12},{12,10},{14,8},{16,22},{18,... | collective-permute-start | bytes 196616 | tf_op jit(solution)/shard_map/ppermute | solution.py:242
  92.1 7.7 %collective-permute-start.18 = (bf16[128,256]{1,0:T(8,128)(2,1)S(1)}, bf16[128,256]{1,0:T(8,128)(2,1)S(1)}, u32[]{:S(2)}, u32[]{:S(2)}) collective-permute-start(bf16[128,256]{1,0:T(8,128)(2,1)S(1)} %copy-done.24), channel_id=1, source_target_pairs={{0,2},{2,0},{4,6},{6,4},{8,10},{10,8},{12,14},{14,12},{16,18},{18,... | collective-permute-start | bytes 196616 | tf_op jit(solution)/shard_map/ppermute | solution.py:242
  93.0 5.6 %copy-start.10 = (bf16[128,256]{1,0:T(8,128)(2,1)}, bf16[128,256]{1,0:T(8,128)(2,1)S(1)}, u32[]{:S(2)}) copy-start(bf16[128,256]{1,0:T(8,128)(2,1)S(1)} %collective-permute-done.6.rest_2_) | copy-start | bytes 196612
  93.0 8.1 %collective-permute-start.20 = (bf16[128,256]{1,0:T(8,128)(2,1)S(1)}, bf16[128,256]{1,0:T(8,128)(2,1)S(1)}, u32[]{:S(2)}, u32[]{:S(2)}) collective-permute-start(bf16[128,256]{1,0:T(8,128)(2,1)S(1)} %copy-done.20), channel_id=1, source_target_pairs={{0,4},{2,6},{4,0},{6,2},{8,12},{10,14},{12,8},{14,10},{16,20},{18,... | collective-permute-start | bytes 196616 | tf_op jit(solution)/shard_map/ppermute | solution.py:242
  94.4 4.2 %copy-start.12 = (bf16[128,256]{1,0:T(8,128)(2,1)}, bf16[128,256]{1,0:T(8,128)(2,1)S(1)}, u32[]{:S(2)}) copy-start(bf16[128,256]{1,0:T(8,128)(2,1)S(1)} %collective-permute-done.8.rest_4_) | copy-start | bytes 196612
  94.4 7.8 %collective-permute-start.22 = (bf16[128,256]{1,0:T(8,128)(2,1)S(1)}, bf16[128,256]{1,0:T(8,128)(2,1)S(1)}, u32[]{:S(2)}, u32[]{:S(2)}) collective-permute-start(bf16[128,256]{1,0:T(8,128)(2,1)S(1)} %copy-done.18), channel_id=1, source_target_pairs={{0,6},{2,4},{4,2},{6,0},{8,14},{10,12},{12,10},{14,8},{16,22},{18,... | collective-permute-start | bytes 196616 | tf_op jit(solution)/shard_map/ppermute | solution.py:242
  95.7 14.8 %copy-start.9 = (bf16[128,256]{1,0:T(8,128)(2,1)S(1)}, bf16[128,256]{1,0:T(8,128)(2,1)}, u32[]{:S(2)}) copy-start(bf16[128,256]{1,0:T(8,128)(2,1)} %copy-done.8) | copy-start | bytes 196612
  98.6 9.1 %collective-permute-start.9 = (bf16[256,256]{1,0:T(8,128)(2,1)}, bf16[256,256]{1,0:T(8,128)(2,1)S(1)}, u32[]{:S(2)}, u32[]{:S(2)}) collective-permute-start(bf16[256,256]{1,0:T(8,128)(2,1)} %get-tuple-element.54), channel_id=1, source_target_pairs={{0,4},{2,6},{4,0},{6,2},{8,12},{10,14},{12,8},{14,10},{16,20},{18,... | collective-permute-start | bytes 393224 | tf_op jit(solution)/shard_map/ppermute | solution.py:242
  99.8 7.9 %collective-permute-start.11 = (bf16[256,256]{1,0:T(8,128)(2,1)}, bf16[256,256]{1,0:T(8,128)(2,1)S(1)}, u32[]{:S(2)}, u32[]{:S(2)}) collective-permute-start(bf16[256,256]{1,0:T(8,128)(2,1)} %get-tuple-element.56), channel_id=1, source_target_pairs={{0,6},{2,4},{4,2},{6,0},{8,14},{10,12},{12,10},{14,8},{16,22},{18,... | collective-permute-start | bytes 393224 | tf_op jit(solution)/shard_map/ppermute | solution.py:242
  101.1 6.6 %collective-permute-start.19 = (bf16[256,256]{1,0:T(8,128)(2,1)S(1)}, bf16[256,256]{1,0:T(8,128)(2,1)S(1)}, u32[]{:S(2)}, u32[]{:S(2)}) collective-permute-start(bf16[256,256]{1,0:T(8,128)(2,1)S(1)} %get-tuple-element.68), channel_id=1, source_target_pairs={{0,2},{2,0},{4,6},{6,4},{8,10},{10,8},{12,14},{14,12},{16,18},{18,... | collective-permute-start | bytes 393224 | tf_op jit(solution)/shard_map/ppermute | solution.py:242
  102.2 8.3 %collective-permute-start.21 = (bf16[256,256]{1,0:T(8,128)(2,1)S(1)}, bf16[256,256]{1,0:T(8,128)(2,1)S(1)}, u32[]{:S(2)}, u32[]{:S(2)}) collective-permute-start(bf16[256,256]{1,0:T(8,128)(2,1)S(1)} %get-tuple-element.70), channel_id=1, source_target_pairs={{0,4},{2,6},{4,0},{6,2},{8,12},{10,14},{12,8},{14,10},{16,20},{18,... | collective-permute-start | bytes 393224 | tf_op jit(solution)/shard_map/ppermute | solution.py:242
  103.3 7.2 %collective-permute-start.23 = (bf16[256,256]{1,0:T(8,128)(2,1)S(1)}, bf16[256,256]{1,0:T(8,128)(2,1)S(1)}, u32[]{:S(2)}, u32[]{:S(2)}) collective-permute-start(bf16[256,256]{1,0:T(8,128)(2,1)S(1)} %get-tuple-element.72), channel_id=1, source_target_pairs={{0,6},{2,4},{4,2},{6,0},{8,14},{10,12},{12,10},{14,8},{16,22},{18,... | collective-permute-start | bytes 393224 | tf_op jit(solution)/shard_map/ppermute | solution.py:242
  110.5 0.8 copy-start.11
  111.3 0.8 copy-start.13

commit v2 on v1

v2 whole, which is shorter than its diff:
```python
import functools

import jax
import jax.numpy as jnp
from jax import lax
from jax.experimental import pallas as pl
from jax.experimental.pallas import tpu as pltpu
from jax.sharding import PartitionSpec as P

HEADS = 16
HEAD_DIM = 128
WINDOW = 512
FIELDS = 64
FACTOR = HEAD_DIM ** (-0.5)
LOG2E = 1.4426950408889634
HIDDEN = -1e30
PAD = 16
CHUNKS = 2
MIB = 1 << 20
BF16, F32 = jnp.bfloat16, jnp.float32
ANY = pl.BlockSpec(memory_space=pl.ANY)
SMEM = pl.BlockSpec(memory_space=pltpu.SMEM)
NT = (((1,), (1,)), ((), ()))


def dot(a, b):
    return jnp.dot(a, b, preferred_element_type=F32)


def dot_nt(a, b):
    return lax.dot_general(a, b, NT, preferred_element_type=F32)


def run_copies(copies):
    for copy in copies:
        copy.start()
    for copy in copies:
        copy.wait()


def fields_row(fields_ref, width):
    row = fields_ref[...].astype(F32)
    row = jnp.concatenate([row] * (width // row.shape[1]), axis=1)
    return jnp.broadcast_to(row, (PAD, width)).astype(BF16)


def pack_kernel(reach, tok, width, chunk, meta, q, g, k, v, fields, *rest):
    outs, field_scr, sems = rest[:reach], rest[-2], rest[-1]
    p = meta[0]
    half = outs[0].shape[0] // 2
    field_scr[...] = fields_row(fields, width)
    copies = []
    for m in range(reach):
        first = pl.multiple_of((p ^ m) * (HEADS // reach * HEAD_DIM) + chunk * width, 128)
        pairs = [
            (src.at[0, :, pl.ds(first, width)], outs[m].at[pl.ds(at, tok)])
            for src, at in ((q, 0), (g, tok), (k, half), (v, half + tok))
        ]
        if half > 2 * tok:
            pairs += [(field_scr, outs[m].at[pl.ds(at + 2 * tok, PAD)]) for at in (0, half)]
        for src, dst in pairs:
            copies.append(pltpu.make_async_copy(src, dst, sems.at[len(copies)]))
    run_copies(copies)


def gather_kernel(reach, *refs):
    arrived, outs, sems = refs[:reach], refs[reach:-1], refs[-1]
    half = arrived[0].shape[0] // 2
    copies = []
    for m in range(reach):
        for at, out in enumerate(outs):
            src = arrived[m].at[pl.ds(at * half, half)]
            copies.append(pltpu.make_async_copy(src, out.at[m], sems.at[len(copies)]))
    run_copies(copies)


def unpack_kernel(reach, tok, meta, *rest):
    parts, outs, stage, sems = rest[:reach], rest[reach:-2], rest[-2], rest[-1]
    p = meta[0]
    width = stage.shape[1]
    staging = pltpu.make_async_copy(parts[0], stage, sems.at[3 * reach])
    staging.start()
    copies = []
    for m in list(range(1, reach)) + [0]:
        part = parts[m] if m else stage
        first = pl.multiple_of((p ^ m) * width, 128)
        if m == 0:
            staging.wait()
        for at, out in enumerate(outs):
            src, dst = part.at[pl.ds(at * tok, tok)], out.at[0, :, pl.ds(first, width)]
            copies.append(pltpu.make_async_copy(src, dst, sems.at[len(copies)]))
            copies[-1].start()
    for copy in copies:
        copy.wait()


def key_columns(fields, slot, tok):
    row = fields[slot].astype(F32)[0:1]
    spread = jnp.broadcast_to(row, (tok, tok))
    lane = lax.broadcasted_iota(jnp.int32, (tok, tok), 1).astype(F32)
    sub = lax.broadcasted_iota(jnp.int32, (tok, tok), 0).astype(F32)
    onehot = jnp.where(spread.T == lane, 1.0, 0.0).astype(BF16)
    onehot_t = jnp.where(spread == sub, 1.0, 0.0).astype(BF16)
    return onehot, onehot_t


def three_parts(x):
    high = x.astype(BF16)
    rest = x - high.astype(F32)
    mid = rest.astype(BF16)
    return high, mid, (rest - mid.astype(F32)).astype(BF16)


def masks(tok):
    key_at = lax.broadcasted_iota(jnp.int32, (tok, tok), 0)
    query_at = lax.broadcasted_iota(jnp.int32, (tok, tok), 1)
    return key_at > query_at, lax.broadcasted_iota(jnp.int32, (1, tok), 1)


def query_pair(qd, p, a, tok):
    slots = (p ^ a, p ^ (a + 1))
    query = jnp.concatenate([qd[slot, 0:tok, :] for slot in slots], axis=0)
    grad = jnp.concatenate([qd[slot, tok : 2 * tok, :] for slot in slots], axis=0)
    return query, grad


def side_by_side(first, second, tok, ends):
    gap = jnp.zeros((tok, tok), first.dtype)
    first = jnp.concatenate([first, gap], axis=0) if ends else first
    return jnp.concatenate([first, jnp.concatenate([gap, second], axis=0)], axis=1)


def rows_kernel(reach, tok, meta, qd, kvo, kvp, fo, fp, bias_ref, dq_out, dk_out, dv_out, stats_out, gb_out, *scratch):
    k_scr, v_scr, kt_scr, oh_scr, oht_scr, bias_scr, acc_scr = scratch
    p, plane, length = meta[0], meta[1], meta[2]
    span = reach * tok

    @pl.when(pl.program_id(0) == 0)
    def _():
        for blk in range(2 * reach):
            rows = slice(blk * tok, (blk + 1) * tok)
            onehot, onehot_t = key_columns(fp if blk < reach else fo, p ^ (blk % reach), tok)
            oh_scr[rows] = onehot
            oht_scr[:, rows] = onehot_t

    shut = jnp.where(plane == 0, HIDDEN, 0.0).astype(F32)
    for blk in range(2 * reach):
        rows = slice(blk * tok, (blk + 1) * tok)
        src, slot = (kvp if blk < reach else kvo), p ^ (blk % reach)
        key = src[slot, 0:tok, :]
        k_scr[rows] = key
        kt_scr[:, rows] = key.T
        v_scr[rows] = src[slot, tok : 2 * tok, :]
        col = dot(oh_scr[rows], bias_ref[0]) * LOG2E
        bias_scr[rows] = col + shut if blk < reach else col
    acc_scr[...] = jnp.zeros_like(acc_scr)
    later, lane = masks(tok)
    for pair in range(0, reach, 2):
        query, grad = query_pair(qd, p, pair, tok)
        wide = slice(pair * tok, (pair + reach + 2) * tok)
        logits = dot_nt(k_scr[wide], query)
        probs_both = dot_nt(v_scr[wide], grad)
        lows, ds_lows = [], []
        for half in range(2):
            a = pair + half
            rows = slice(a * tok, (a + reach + 1) * tok)
            mine = slice(half * tok, (half + reach + 1) * tok)
            there = slice(a * tok, (a + 1) * tok)
            cols = slice(half * tok, (half + 1) * tok)
            s = logits[mine, cols] * (FACTOR * LOG2E) + bias_scr[rows]
            s = jnp.concatenate(
                [jnp.where(later, s[:tok], HIDDEN), s[tok:-tok], jnp.where(later, HIDDEN, s[-tok:])],
                axis=0,
            )
            peak = jnp.max(s, axis=0, keepdims=True)
            power = jnp.exp2(s - peak)
            total = jnp.sum(power, axis=0, keepdims=True)
            live = plane * span + a * tok + lane < length
            weight = power * jnp.where(live, 1.0 / total, 0.0)
            low = weight.astype(BF16)
            probs = probs_both[mine, cols]
            delta = jnp.sum(low.astype(F32) * probs, axis=0, keepdims=True)
            ds = weight * (probs - delta)
            acc_scr[rows] += ds
            lows.append(low)
            ds_lows.append(ds.astype(BF16))
            stats_out[0, 0:1, there] = peak + jnp.log2(total)
            stats_out[0, 1:2, there] = delta
        low = side_by_side(*lows, tok, True)
        ds_low = side_by_side(*ds_lows, tok, True)
        dq = dot(kt_scr[:, wide], ds_low)
        for half in range(2):
            dq_half = dq[:, half * tok : (half + 1) * tok]
            dq_out[p ^ (pair + half)] = (dq_half.T * FACTOR).astype(BF16)
        own = slice((reach - pair) * tok, (reach + 2) * tok)
        dv = dot(low[own], grad)
        dk = dot(ds_low[own], query)
        done = pair * tok
        if pair:
            dv_out[0:done] += dv[:done]
            dk_out[0:done] += dk[:done]
        dv_out[done : done + 2 * tok] = dv[done:]
        dk_out[done : done + 2 * tok] = dk[done:]
    by_field = sum(dot(oht_scr[...], part) for part in three_parts(acc_scr[...]))
    gb_out[0] = jnp.sum(by_field.T.reshape(tok // 8, 8, tok), axis=0)


def columns_kernel(reach, tok, meta, qd, kvo, fo, stats, bias_ref, dq_in, dk_in, dv_in, *rest):
    outs = rest[-6 - reach : -6]
    k_scr, v_scr, bias_scr, dk_scr, dv_scr, out_scr = rest[-6:]
    p, plane, length = meta[0], meta[1], meta[2]
    span = reach * tok
    for blk in range(reach):
        rows = slice(blk * tok, (blk + 1) * tok)
        slot = p ^ blk
        k_scr[rows] = kvo[slot, 0:tok, :]
        v_scr[rows] = kvo[slot, tok : 2 * tok, :]
        onehot, _ = key_columns(fo, slot, tok)
        bias_scr[rows] = dot(onehot, bias_ref[0]) * LOG2E
    later, lane = masks(tok)
    for pair in range(0, reach, 2):
        query, grad = query_pair(qd, p, pair, tok)
        wide = slice(pair * tok, span)
        logits = dot_nt(k_scr[wide], query)
        probs_both = dot_nt(v_scr[wide], grad)
        lows, ds_lows = [], []
        for half in range(2):
            a = pair + half
            there = slice(a * tok, (a + 1) * tok)
            cols = slice(half * tok, (half + 1) * tok)
            live = (plane + 1) * span + a * tok + lane < length
            norm = jnp.where(live, stats[0, 0:1, there], -HIDDEN)
            delta = stats[0, 1:2, there]
            s = logits[half * tok :, cols] * (FACTOR * LOG2E) + bias_scr[a * tok :]
            weight = jnp.exp2(s - norm)
            first = jnp.where(later, weight[:tok], 0.0)
            weight = jnp.concatenate([first, weight[tok:]], axis=0) if a < reach - 1 else first
            lows.append(weight.astype(BF16))
            ds_lows.append((weight * (probs_both[half * tok :, cols] - delta)).astype(BF16))
        dv = dot(side_by_side(*lows, tok, False), grad)
        dk = dot(side_by_side(*ds_lows, tok, False), query)
        dv_scr[wide] = dv + (dv_scr if pair else dv_in)[wide]
        dk_scr[wide] = dk + (dk_scr if pair else dk_in)[wide]
    for blk in range(reach):
        rows = slice(blk * tok, (blk + 1) * tok)
        out_scr[p ^ blk, 0:tok] = (dk_scr[rows] * FACTOR).astype(BF16)
        out_scr[p ^ blk, tok : 2 * tok] = dv_scr[rows].astype(BF16)
    for m in range(reach):
        outs[m][0:tok] = dq_in[m]
        outs[m][tok : 3 * tok] = out_scr[m]


def params(mib, *semantics):
    return pltpu.CompilerParams(
        vmem_limit_bytes=mib * MIB, dimension_semantics=semantics if semantics else None
    )


def cost(flops, nbytes, trans=0):
    return pl.CostEstimate(flops=flops, bytes_accessed=nbytes, transcendentals=trans)


def in_hbm(*arrays):
    return [pltpu.with_memory_space_constraint(array, pltpu.HBM) for array in arrays]


def in_vmem(*arrays):
    return [pltpu.with_memory_space_constraint(array, pltpu.VMEM) for array in arrays]


def following(value, mark):
    return lax.optimization_barrier((value, mark))[0]


def swapped(value, axis, mask):
    count = lax.axis_size(axis)
    return lax.ppermute(value, axis, [(source, source ^ mask) for source in range(count)])


def passed_along(value, axis, steps):
    count = lax.axis_size(axis)
    first, last = max(0, -steps), min(count, count - steps)
    return lax.ppermute(value, axis, [(source, source + steps) for source in range(first, last)])


def shards(queries, keys, values, grad_out, lengths, fields, field_bias):
    tok = queries.shape[1]
    row_width = queries.shape[2]
    reach = WINDOW // tok
    group = HEADS // reach
    per = group // CHUNKS
    width = per * HEAD_DIM
    span = reach * tok
    index = lax.axis_index("seq")
    p = lax.rem(index, reach)
    meta = jnp.stack([p, lax.div(index, reach), lengths[0]]).astype(jnp.int32)
    raw = in_hbm(queries, grad_out, keys, values)

    def hbm(shape, dtype=BF16):
        return pltpu.HBM(shape, dtype)

    vmem = pl.BlockSpec(memory_space=pltpu.VMEM)

    def rows_in(chunk):
        return 2 * tok + (PAD if chunk == 0 else 0)

    def pack(chunk):
        return pl.pallas_call(
            functools.partial(pack_kernel, reach, tok, width, chunk),
            in_specs=[SMEM] + [ANY] * 4 + [vmem],
            out_specs=[ANY] * reach,
            out_shape=[pltpu.VMEM((2 * rows_in(chunk), width), BF16)] * reach,
            scratch_shapes=[
                pltpu.VMEM((PAD, width), BF16),
                pltpu.SemaphoreType.DMA((6 * reach,)),
            ],
            compiler_params=params(2),
            cost_estimate=cost(0, 2 * MIB),
            name="pack",
        )(meta, *raw, fields)

    def gather(chunk, arrived):
        return pl.pallas_call(
            functools.partial(gather_kernel, reach),
            in_specs=[ANY] * reach,
            out_specs=[ANY] * 2,
            out_shape=[hbm((reach, rows_in(chunk), width))] * 2,
            scratch_shapes=[pltpu.SemaphoreType.DMA((2 * reach,))],
            compiler_params=params(2),
            cost_estimate=cost(2 * 10**9 if chunk else 0, 2 * MIB),
            name="gather",
        )(*in_vmem(*arrived))

    qd_spec = pl.BlockSpec((reach, 2 * tok, HEAD_DIM), lambda h: (0, 0, h))
    fields_spec = pl.BlockSpec((reach, PAD, HEAD_DIM), lambda h: (0, 2 * tok // PAD, 0))
    bias_spec = pl.BlockSpec((1, tok, HEAD_DIM), lambda h: (h, 0, 0))
    stats_spec = pl.BlockSpec((1, 8, span), lambda h: (h, 0, 0))
    part_spec = pl.BlockSpec((span, HEAD_DIM), lambda h: (0, h))

    dq_spec = pl.BlockSpec((reach, tok, HEAD_DIM), lambda h: (0, 0, h))

    def rows_of(qd, kvo, kvp, fo, fp, bias):
        return pl.pallas_call(
            functools.partial(rows_kernel, reach, tok),
            grid=(per,),
            in_specs=[SMEM, qd_spec, qd_spec, qd_spec, fields_spec, fields_spec, bias_spec],
            out_specs=[dq_spec, part_spec, part_spec, stats_spec, pl.BlockSpec((1, 8, tok), lambda h: (h, 0, 0))],
            out_shape=[
                hbm((reach, tok, width)),
                hbm((span, width), F32),
                hbm((span, width), F32),
                hbm((per, 8, span), F32),
                jax.ShapeDtypeStruct((per, 8, tok), F32),
            ],
            scratch_shapes=[
                pltpu.VMEM((2 * span, HEAD_DIM), BF16),
                pltpu.VMEM((2 * span, HEAD_DIM), BF16),
                pltpu.VMEM((HEAD_DIM, 2 * span), BF16),
                pltpu.VMEM((2 * span, tok), BF16),
                pltpu.VMEM((tok, 2 * span), BF16),
                pltpu.VMEM((2 * span, tok), F32),
                pltpu.VMEM((2 * span, tok), F32),
            ],
            compiler_params=params(20, "arbitrary"),
            cost_estimate=cost(per * 56 * span * (span + tok) * HEAD_DIM * 1, 4 * MIB),
            name="rows",
        )(meta, *in_hbm(qd, kvo), kvp, *in_hbm(fo), fp, bias)

    def columns_of(chunk, qd, kvo, fo, stats, bias, dq, dk, dv, *messages):
        return pl.pallas_call(
            functools.partial(columns_kernel, reach, tok),
            grid=(per,),
            in_specs=[SMEM, qd_spec, qd_spec, fields_spec, stats_spec, bias_spec, dq_spec, part_spec, part_spec]
            + [ANY] * len(messages),
            out_specs=[pl.BlockSpec((3 * tok, HEAD_DIM), lambda h: (0, chunk * per + h))] * reach,
            out_shape=[hbm((3 * tok, group * HEAD_DIM))] * reach,
            input_output_aliases={9 + m: m for m in range(len(messages))},
            scratch_shapes=[
                pltpu.VMEM((span, HEAD_DIM), BF16),
                pltpu.VMEM((span, HEAD_DIM), BF16),
                pltpu.VMEM((span, tok), F32),
                pltpu.VMEM((span, HEAD_DIM), F32),
                pltpu.VMEM((span, HEAD_DIM), F32),
                pltpu.VMEM((reach, 2 * tok, HEAD_DIM), BF16),
            ],
            compiler_params=params(20, "arbitrary"),
            cost_estimate=cost(per * 28 * span * (span + tok) * HEAD_DIM * 1, 4 * MIB),
            name="columns",
        )(meta, qd, *in_hbm(kvo, fo), stats, bias, *in_hbm(dq, dk, dv, *messages))

    padded = jnp.pad(field_bias, ((0, 0), (0, tok - FIELDS)))
    my_bias = lax.dynamic_slice_in_dim(padded, p * group, group, 0)
    my_bias = jnp.broadcast_to(my_bias[:, :, None], (group, tok, HEAD_DIM))

    packed = [list(pack(c)) for c in range(CHUNKS)]
    packed[0][0] = following(packed[0][0], packed[1][0])
    planes, before, after = [], [], []
    for c in range(CHUNKS):
        arrived = packed[c][:1] + [swapped(packed[c][m], "seq", m) for m in range(1, reach)]
        qd, kv = gather(c, arrived)
        planes.append((qd, kv))
        moved = passed_along(kv, "seq", reach), passed_along(qd, "seq", -reach)
        before.append(following(moved[0], moved[1]) if c == 0 else moved[0])
        after.append(moved[1])
    bias_parts, pending = [], []
    for c in range(CHUNKS):
        bias = my_bias[c * per : (c + 1) * per]
        dq, dk, dv, stats, gb = rows_of(*planes[c], before[c], planes[0][1], before[0], bias)
        bias_parts.append(jnp.sum(gb, axis=1)[:, :FIELDS])
        pending.append((passed_along(stats, "seq", -reach), bias, dq, dk, dv))
    messages = []
    for c in range(CHUNKS):
        messages = columns_of(c, after[c], planes[c][1], planes[0][1], *pending[c], *messages)
    parts = [messages[0]] + [swapped(messages[m], "seq", m) for m in range(1, reach)]

    total = jnp.concatenate(bias_parts, axis=0)
    total = following(total, messages[0])
    mask = reach
    while mask < lax.axis_size("seq"):
        total = total + swapped(total, "seq", mask)
        mask *= 2
    mask = 1
    while mask < lax.axis_size("dp"):
        total = total + swapped(total, "dp", mask)
        mask *= 2
    mask = 1
    while mask < reach:
        other = swapped(total, "seq", mask)
        total = jnp.where(
            p & mask > 0,
            jnp.concatenate([other, total], axis=0),
            jnp.concatenate([total, other], axis=0),
        )
        mask *= 2

    grads = pl.pallas_call(
        functools.partial(unpack_kernel, reach, tok),
        in_specs=[SMEM] + [ANY] * reach,
        out_specs=[ANY] * 3,
        out_shape=[jax.ShapeDtypeStruct((1, tok, row_width), BF16)] * 3,
        scratch_shapes=[
            pltpu.VMEM((3 * tok, group * HEAD_DIM), BF16),
            pltpu.SemaphoreType.DMA((3 * reach + 1,)),
        ],
        compiler_params=params(4),
        name="unpack",
    )(meta, *in_hbm(parts[0]), *in_vmem(*parts[1:]))
    return (*grads, total)


def solution(mesh):
    return jax.shard_map(
        shards,
        mesh=mesh,
        in_specs=(
            P("dp", "seq", None),
            P("dp", "seq", None),
            P("dp", "seq", None),
            P("dp", "seq", None),
            P("dp"),
            P("dp", "seq"),
            P(),
        ),
        out_specs=(P("dp", "seq", None), P("dp", "seq", None), P("dp", "seq", None), P()),
        check_vma=False,
    )
```

time: 115 us -> 90.6 us (0.79)
  local copies, waits for them, and re-layouts: 15 us -> 0.79 us
  starting transfers between devices: 47.1 us -> 34.1 us
  waiting for transfers between devices: 21.3 us -> 23.6 us
    unnamed x60 -> x4, local copies, waits for them, and re-layouts: 14.8 us -> 0.58 us
    ppermute x23 -> x14, starting transfers between devices: 34.1 us -> 21.9 us  [swapped(): lax.ppermute(value, axis, [(source, source ^ mask) for source in range(co...]
    ppermute x6, waiting for transfers between devices: 0.02 us -> 4.94 us  [passed_along(): lax.ppermute(value, axis, [(source, source + steps) for source in range(f...]
    ppermute x23 -> x14, waiting for transfers between devices: 21.3 us -> 18.7 us  [swapped(): lax.ppermute(value, axis, [(source, source ^ mask) for source in range(co...]
    pallas_call x2, Pallas kernels: 1.73 us -> 4.03 us  [pack(): pl.pallas_call(functools.partial(pack_kernel, reach, tok, width, chunk),...]
    pallas_call x2, Pallas kernels: 15 us -> 13.1 us  [rows_of(): pl.pallas_call(functools.partial(rows_kernel, reach, tok), grid=(per,), i...]
  transfers between devices with their start and end apart: 29 -> 20, of which waited for: 8 -> 10; matrix products, arithmetic and copies ran while one was open for 1% -> 1% of each run, Pallas kernels for 22% -> 23%
where the time goes in v2:
time: 90.6 us; the launch traced here: 90 us
  starting transfers between devices  34.1 us (38%)
  Pallas kernels  29.3 us (32%)
  waiting for transfers between devices  23.6 us (26%)
  between operations  1.49 us (2%)
    ppermute x14, starting transfers between devices, swapped(): lax.ppermute(value, axis, [(source, source ^ mask) for source in range(co...  21.9 us
    ppermute x14, waiting for transfers between devices, swapped(): lax.ppermute(value, axis, [(source, source ^ mask) for source in range(co...  18.7 us
    pallas_call x2, Pallas kernels, rows_of(): pl.pallas_call(functools.partial(rows_kernel, reach, tok), grid=(per,), i...  13.1 us
    ppermute x6, starting transfers between devices, passed_along(): lax.ppermute(value, axis, [(source, source + steps) for source in range(f...  12.2 us
    pallas_call x2, Pallas kernels, columns_of(): pl.pallas_call(functools.partial(columns_kernel, reach, tok), grid=(per,)...  7.35 us
    ppermute x6, waiting for transfers between devices, passed_along(): lax.ppermute(value, axis, [(source, source + steps) for source in range(f...  4.94 us
    pallas_call x2, Pallas kernels, pack(): pl.pallas_call(functools.partial(pack_kernel, reach, tok, width, chunk),...  4.03 us
    pallas_call x1, Pallas kernels, shards(): pl.pallas_call(functools.partial(unpack_kernel, reach, tok), in_specs=[SM...  2.63 us
  transfers between devices with their start and end apart: 20, of which 10 were waited for; matrix products, arithmetic and copies ran while one was open for 1% of the time, Pallas kernels for 23%

profile of v2, /device:TPU:0, one launch (start us, length us, event | category | flops | bytes accessed | tf_op | source)
XLA Modules:
  0.0 90.0 jit_solution(9927444948517194095)
XLA Ops:
  1.3 0.0 copy-start
  1.3 0.1 pad_add_fusion.meta
  1.4 0.6 copy-done
  1.9 2.0 %pack.3 = (bf16[544,256]{1,0:T(8,128)(2,1)S(1)}, bf16[544,256]{1,0:T(8,128)(2,1)S(1)}, bf16[544,256]{1,0:T(8,128)(2,1)S(1)}, bf16[544,256]{1,0:T(8,128)(2,1)S(1)}) custom-call(s32[3]{0:T(128)S(1)} %pad_add_fusion.meta, bf16[1,128,2048]{2,1,0:T(8,128)(2,1)} %q.3, bf16[1,128,2048]{2,1,0:T(8,128)(2,1)} %g.3, bf16[1,128,2048]{2,1,0:T(8,128)(2,1)} %k.3, ...), custom_call_target="tpu_custom_call" | custom-call | bytes 2097152 | tf_op jit(solution)/shard_map/pack/pallas_call | solution.py:308
  4.0 3.0 %collective-permute-start.4 = (bf16[544,256]{1,0:T(8,128)(2,1)S(1)}, bf16[544,256]{1,0:T(8,128)(2,1)S(1)}, u32[]{:S(2)}, u32[]{:S(2)}) collective-permute-start(bf16[544,256]{1,0:T(8,128)(2,1)S(1)} %get-tuple-element.48), channel_id=1, source_target_pairs={{0,2},{2,0},{4,6},{6,4},{8,10},{10,8},{12,14},{14,12},{16,18},{18,... | collective-permute-start | bytes 835592 | tf_op jit(solution)/shard_map/ppermute | solution.py:277
  7.0 1.5 %collective-permute-start.5 = (bf16[544,256]{1,0:T(8,128)(2,1)S(1)}, bf16[544,256]{1,0:T(8,128)(2,1)S(1)}, u32[]{:S(2)}, u32[]{:S(2)}) collective-permute-start(bf16[544,256]{1,0:T(8,128)(2,1)S(1)} %get-tuple-element.49), channel_id=1, source_target_pairs={{0,4},{2,6},{4,0},{6,2},{8,12},{10,14},{12,8},{14,10},{16,20},{18,... | collective-permute-start | bytes 835592 | tf_op jit(solution)/shard_map/ppermute | solution.py:277
  8.5 0.0 collective-permute-start.6
  8.5 2.0 %pack.2 = (bf16[512,256]{1,0:T(8,128)(2,1)S(1)}, bf16[512,256]{1,0:T(8,128)(2,1)S(1)}, bf16[512,256]{1,0:T(8,128)(2,1)S(1)}, bf16[512,256]{1,0:T(8,128)(2,1)S(1)}) custom-call(s32[3]{0:T(128)S(1)} %pad_add_fusion.meta, bf16[1,128,2048]{2,1,0:T(8,128)(2,1)} %q.3, bf16[1,128,2048]{2,1,0:T(8,128)(2,1)} %g.3, bf16[1,128,2048]{2,1,0:T(8,128)(2,1)} %k.3, ...), custom_call_target="tpu_custom_call" | custom-call | bytes 2097152 | tf_op jit(solution)/shard_map/pack/pallas_call | solution.py:308
  10.5 2.0 %collective-permute-start = (bf16[512,256]{1,0:T(8,128)(2,1)S(1)}, bf16[512,256]{1,0:T(8,128)(2,1)S(1)}, u32[]{:S(2)}, u32[]{:S(2)}) collective-permute-start(bf16[512,256]{1,0:T(8,128)(2,1)S(1)} %get-tuple-element.41), channel_id=1, source_target_pairs={{0,2},{2,0},{4,6},{6,4},{8,10},{10,8},{12,14},{14,12},{16,18},{18,... | collective-permute-start | bytes 786440 | tf_op jit(solution)/shard_map/ppermute | solution.py:277
  12.5 1.5 %collective-permute-start.1 = (bf16[512,256]{1,0:T(8,128)(2,1)S(1)}, bf16[512,256]{1,0:T(8,128)(2,1)S(1)}, u32[]{:S(2)}, u32[]{:S(2)}) collective-permute-start(bf16[512,256]{1,0:T(8,128)(2,1)S(1)} %get-tuple-element.42), channel_id=1, source_target_pairs={{0,4},{2,6},{4,0},{6,2},{8,12},{10,14},{12,8},{14,10},{16,20},{18,... | collective-permute-start | bytes 786440 | tf_op jit(solution)/shard_map/ppermute | solution.py:277
  14.1 0.4 collective-permute-done.4.refs_1_
  14.5 3.0 %collective-permute-start.2 = (bf16[512,256]{1,0:T(8,128)(2,1)S(1)}, bf16[512,256]{1,0:T(8,128)(2,1)S(1)}, u32[]{:S(2)}, u32[]{:S(2)}) collective-permute-start(bf16[512,256]{1,0:T(8,128)(2,1)S(1)} %get-tuple-element.43), channel_id=1, source_target_pairs={{0,6},{2,4},{4,2},{6,0},{8,14},{10,12},{12,10},{14,8},{16,22},{18,... | collective-permute-start | bytes 786440 | tf_op jit(solution)/shard_map/ppermute | solution.py:277
  17.5 4.8 %collective-permute-done.5.refs_2_ = bf16[544,256]{1,0:T(8,128)(2,1)S(1)} collective-permute-done((bf16[544,256]{1,0:T(8,128)(2,1)S(1)}, bf16[544,256]{1,0:T(8,128)(2,1)S(1)}, u32[]{:S(2)}, u32[]{:S(2)}) %collective-permute-start.5) | collective-permute-done | bytes 278560 | tf_op jit(solution)/shard_map/ppermute | solution.py:277
  22.3 0.0 collective-permute-done.6.refs_3_
  22.3 1.1 %gather.3 = (bf16[4,272,256]{2,1,0:T(8,128)(2,1)}, bf16[4,272,256]{2,1,0:T(8,128)(2,1)}) custom-call(bf16[544,256]{1,0:T(8,128)(2,1)S(1)} %get-tuple-element.47.refs_0_, bf16[544,256]{1,0:T(8,128)(2,1)S(1)} %collective-permute-done.4.refs_1_, bf16[544,256]{1,0:T(8,128)(2,1)S(1)} %collective-permute-done.5.refs_2_, ...), custom_call_target="tpu_custom_call" | custom-call | bytes 2097152 | tf_op jit(solution)/shard_map/gather/pallas_call | solution.py:323
  23.4 3.5 %collective-permute-start.8 = (bf16[4,272,256]{2,1,0:T(8,128)(2,1)}, bf16[4,272,256]{2,1,0:T(8,128)(2,1)S(1)}, u32[]{:S(2)}, u32[]{:S(2)}) collective-permute-start(bf16[4,272,256]{2,1,0:T(8,128)(2,1)} %get-tuple-element.51.fo.kvo), channel_id=1, source_target_pairs={{0,8},{2,10},{4,12},{6,14},{8,16},{10,18},{12,20},{14,22},{16,24},... | collective-permute-start | bytes 1671176 | tf_op jit(solution)/shard_map/ppermute | solution.py:283
  26.9 0.0 copy-start.1
  27.0 1.3 %collective-permute-start.9 = (bf16[4,272,256]{2,1,0:T(8,128)(2,1)}, bf16[4,272,256]{2,1,0:T(8,128)(2,1)S(1)}, u32[]{:S(2)}, u32[]{:S(2)}) collective-permute-start(bf16[4,272,256]{2,1,0:T(8,128)(2,1)} %get-tuple-element.52.qd), channel_id=1, source_target_pairs={{8,0},{10,2},{12,4},{14,6},{16,8},{18,10},{20,12},{22,14},{24,16},... | collective-permute-start | bytes 1671176 | tf_op jit(solution)/shard_map/ppermute | solution.py:283
  28.3 0.0 copy-done.1
  28.3 0.0 collective-permute-done.refs_1_
  28.3 4.0 %collective-permute-done.1.refs_2_ = bf16[512,256]{1,0:T(8,128)(2,1)S(1)} collective-permute-done((bf16[512,256]{1,0:T(8,128)(2,1)S(1)}, bf16[512,256]{1,0:T(8,128)(2,1)S(1)}, u32[]{:S(2)}, u32[]{:S(2)}) %collective-permute-start.1) | collective-permute-done | bytes 262176 | tf_op jit(solution)/shard_map/ppermute | solution.py:277
  32.3 0.0 collective-permute-done.2.refs_3_
  32.3 1.0 %gather.2 = (bf16[4,256,256]{2,1,0:T(8,128)(2,1)}, bf16[4,256,256]{2,1,0:T(8,128)(2,1)}) custom-call(bf16[512,256]{1,0:T(8,128)(2,1)S(1)} %get-tuple-element.40.refs_0_, bf16[512,256]{1,0:T(8,128)(2,1)S(1)} %collective-permute-done.refs_1_, bf16[512,256]{1,0:T(8,128)(2,1)S(1)} %collective-permute-done.1.refs_2_, ...), custom_call_target="tpu_custom_call" | custom-call | flops 2000000000 | bytes 2097152 | tf_op jit(solution)/shard_map/gather/pallas_call | solution.py:323
  33.3 3.5 %collective-permute-start.7 = (bf16[4,256,256]{2,1,0:T(8,128)(2,1)}, bf16[4,256,256]{2,1,0:T(8,128)(2,1)S(1)}, u32[]{:S(2)}, u32[]{:S(2)}) collective-permute-start(bf16[4,256,256]{2,1,0:T(8,128)(2,1)} %get-tuple-element.45.kvo), channel_id=1, source_target_pairs={{0,8},{2,10},{4,12},{6,14},{8,16},{10,18},{12,20},{14,22},{16,24},... | collective-permute-start | bytes 1572872 | tf_op jit(solution)/shard_map/ppermute | solution.py:283
  36.9 1.3 %collective-permute-start.3 = (bf16[4,256,256]{2,1,0:T(8,128)(2,1)}, bf16[4,256,256]{2,1,0:T(8,128)(2,1)S(1)}, u32[]{:S(2)}, u32[]{:S(2)}) collective-permute-start(bf16[4,256,256]{2,1,0:T(8,128)(2,1)} %get-tuple-element.44.qd), channel_id=1, source_target_pairs={{8,0},{10,2},{12,4},{14,6},{16,8},{18,10},{20,12},{22,14},{24,16},... | collective-permute-start | bytes 1572872 | tf_op jit(solution)/shard_map/ppermute | solution.py:283
  38.2 0.0 collective-permute-done.8.fp.kvp
  38.2 3.3 %collective-permute-done.9.qd = bf16[4,272,256]{2,1,0:T(8,128)(2,1)S(1)} collective-permute-done((bf16[4,272,256]{2,1,0:T(8,128)(2,1)}, bf16[4,272,256]{2,1,0:T(8,128)(2,1)S(1)}, u32[]{:S(2)}, u32[]{:S(2)}) %collective-permute-start.9) | collective-permute-done | bytes 557088 | tf_op jit(solution)/shard_map/ppermute | solution.py:283
  41.5 0.1 broadcast_in_dim.9.bias_ref
  41.6 6.6 %rows.3 = (bf16[4,128,256]{2,1,0:T(8,128)(2,1)}, f32[512,256]{1,0:T(8,128)}, f32[512,256]{1,0:T(8,128)}, f32[2,8,512]{2,1,0:T(8,128)}, f32[2,8,128]{2,1,0:T(8,128)S(1)}) custom-call(s32[3]{0:T(128)S(1)} %pad_add_fusion.meta, bf16[4,272,256]{2,1,0:T(8,128)(2,1)} %get-tuple-element.52.qd, bf16[4,272,256]{2,1,0:T(8,128)(2,1)} %get-tuple-element.51.fo.kvo, ...), custom_call_target="tpu_custom_call" | custom-call | flops 4697620480 | bytes 4194304 | tf_op jit(solution)/shard_map/rows/pallas_call | solution.py:343
  48.2 1.3 %collective-permute-start.11 = (f32[2,8,512]{2,1,0:T(8,128)}, f32[2,8,512]{2,1,0:T(8,128)S(1)}, u32[]{:S(2)}, u32[]{:S(2)}) collective-permute-start(f32[2,8,512]{2,1,0:T(8,128)} %get-tuple-element.58), channel_id=1, source_target_pairs={{8,0},{10,2},{12,4},{14,6},{16,8},{18,10},{20,12},{22,14},{24,16},... | collective-permute-start | bytes 98312 | tf_op jit(solution)/shard_map/ppermute | solution.py:283
  49.5 0.0 collective-permute-done.7.kvp
  49.5 0.1 broadcast_in_dim.8.bias_ref
  49.6 6.5 %rows.2 = (bf16[4,128,256]{2,1,0:T(8,128)(2,1)}, f32[512,256]{1,0:T(8,128)}, f32[512,256]{1,0:T(8,128)}, f32[2,8,512]{2,1,0:T(8,128)}, f32[2,8,128]{2,1,0:T(8,128)S(1)}) custom-call(s32[3]{0:T(128)S(1)} %pad_add_fusion.meta, bf16[4,256,256]{2,1,0:T(8,128)(2,1)} %get-tuple-element.44.qd, bf16[4,256,256]{2,1,0:T(8,128)(2,1)} %get-tuple-element.45.kvo, ...), custom_call_target="tpu_custom_call" | custom-call | flops 4697620480 | bytes 4194304 | tf_op jit(solution)/shard_map/rows/pallas_call | solution.py:343
  56.1 1.3 %collective-permute-start.10 = (f32[2,8,512]{2,1,0:T(8,128)}, f32[2,8,512]{2,1,0:T(8,128)S(1)}, u32[]{:S(2)}, u32[]{:S(2)}) collective-permute-start(f32[2,8,512]{2,1,0:T(8,128)} %get-tuple-element.54), channel_id=1, source_target_pairs={{8,0},{10,2},{12,4},{14,6},{16,8},{18,10},{20,12},{22,14},{24,16},... | collective-permute-start | bytes 98312 | tf_op jit(solution)/shard_map/ppermute | solution.py:283
  57.4 0.0 collective-permute-done.11.stats
  57.4 3.7 %columns.2 = (bf16[384,512]{1,0:T(8,128)(2,1)}, bf16[384,512]{1,0:T(8,128)(2,1)}, bf16[384,512]{1,0:T(8,128)(2,1)}, bf16[384,512]{1,0:T(8,128)(2,1)}) custom-call(s32[3]{0:T(128)S(1)} %pad_add_fusion.meta, bf16[4,272,256]{2,1,0:T(8,128)(2,1)S(1)} %collective-permute-done.9.qd, bf16[4,272,256]{2,1,0:T(8,128)(2,1)} %get-tuple-element.51.fo.kvo, ...), custom_call_target="tpu_custom_call" | custom-call | flops 2348810240 | bytes 4194304 | tf_op jit(solution)/shard_map/columns/pallas_call | solution.py:370
  61.1 0.0 collective-permute-done.3.qd
  61.1 1.6 %collective-permute-done.10.stats = f32[2,8,512]{2,1,0:T(8,128)S(1)} collective-permute-done((f32[2,8,512]{2,1,0:T(8,128)}, f32[2,8,512]{2,1,0:T(8,128)S(1)}, u32[]{:S(2)}, u32[]{:S(2)}) %collective-permute-start.10) | collective-permute-done | bytes 32800 | tf_op jit(solution)/shard_map/ppermute | solution.py:283
  62.8 3.7 %columns.3 = (bf16[384,512]{1,0:T(8,128)(2,1)}, bf16[384,512]{1,0:T(8,128)(2,1)}, bf16[384,512]{1,0:T(8,128)(2,1)}, bf16[384,512]{1,0:T(8,128)(2,1)}) custom-call(s32[3]{0:T(128)S(1)} %pad_add_fusion.meta, bf16[4,256,256]{2,1,0:T(8,128)(2,1)S(1)} %collective-permute-done.3.qd, ...), custom_call_target="tpu_custom_call", output_to_operand_aliasing={{0}: (9, {}), {1}: (10, {}), {2}: (11, {}), {3}: (12, {})} | custom-call | flops 2348810240 | bytes 4194304 | tf_op jit(solution)/shard_map/columns/pallas_call | solution.py:370
  66.5 1.6 %collective-permute-start.12 = (bf16[384,512]{1,0:T(8,128)(2,1)}, bf16[384,512]{1,0:T(8,128)(2,1)S(1)}, u32[]{:S(2)}, u32[]{:S(2)}) collective-permute-start(bf16[384,512]{1,0:T(8,128)(2,1)} %get-tuple-element.67), channel_id=1, source_target_pairs={{0,2},{2,0},{4,6},{6,4},{8,10},{10,8},{12,14},{14,12},{16,18},{18,... | collective-permute-start | bytes 1179656 | tf_op jit(solution)/shard_map/ppermute | solution.py:277
  68.0 0.5 collective-permute-start.13
  68.5 1.5 %collective-permute-start.14 = (bf16[384,512]{1,0:T(8,128)(2,1)}, bf16[384,512]{1,0:T(8,128)(2,1)S(1)}, u32[]{:S(2)}, u32[]{:S(2)}) collective-permute-start(bf16[384,512]{1,0:T(8,128)(2,1)} %get-tuple-element.69), channel_id=1, source_target_pairs={{0,6},{2,4},{4,2},{6,0},{8,14},{10,12},{12,10},{14,8},{16,22},{18,... | collective-permute-start | bytes 1179656 | tf_op jit(solution)/shard_map/ppermute | solution.py:277
  70.0 2.1 %collective-permute-start.15 = (f32[4,64]{1,0:T(4,128)S(1)}, f32[4,64]{1,0:T(4,128)S(1)}, u32[]{:S(2)}, u32[]{:S(2)}) collective-permute-start(f32[4,64]{1,0:T(4,128)S(1)} %pad_maximum_fusion), channel_id=1, source_target_pairs={{0,8},{2,10},{4,12},{6,14},{8,0},{10,2},{12,4},{14,6},{16,24},{18,... | collective-permute-start | bytes 3080 | tf_op jit(solution)/shard_map/ppermute | solution.py:277
  72.1 1.6 %collective-permute-done.15 = f32[4,64]{1,0:T(4,128)S(1)} collective-permute-done((f32[4,64]{1,0:T(4,128)S(1)}, f32[4,64]{1,0:T(4,128)S(1)}, u32[]{:S(2)}, u32[]{:S(2)}) %collective-permute-start.15) | collective-permute-done | bytes 1056 | tf_op jit(solution)/shard_map/ppermute | solution.py:277
  73.7 3.1 %collective-permute-start.16 = (f32[4,64]{1,0:T(4,128)S(1)}, f32[4,64]{1,0:T(4,128)S(1)}, u32[]{:S(2)}, u32[]{:S(2)}) collective-permute-start(f32[4,64]{1,0:T(4,128)S(1)} %add.15), channel_id=1, source_target_pairs={{0,16},{2,18},{4,20},{6,22},{8,24},{10,26},{12,28},{14,30},{16,0},... | collective-permute-start | bytes 3080 | tf_op jit(solution)/shard_map/ppermute | solution.py:277
  76.8 1.6 %collective-permute-done.16 = f32[4,64]{1,0:T(4,128)S(1)} collective-permute-done((f32[4,64]{1,0:T(4,128)S(1)}, f32[4,64]{1,0:T(4,128)S(1)}, u32[]{:S(2)}, u32[]{:S(2)}) %collective-permute-start.16) | collective-permute-done | bytes 1056 | tf_op jit(solution)/shard_map/ppermute | solution.py:277
  78.4 0.0 collective-permute-start.17
  78.4 1.2 %collective-permute-done.17 = f32[4,64]{1,0:T(4,128)S(1)} collective-permute-done((f32[4,64]{1,0:T(4,128)S(1)}, f32[4,64]{1,0:T(4,128)S(1)}, u32[]{:S(2)}, u32[]{:S(2)}) %collective-permute-start.17) | collective-permute-done | bytes 1056 | tf_op jit(solution)/shard_map/ppermute | solution.py:277
  79.5 1.5 %collective-permute-start.18 = (f32[4,64]{1,0:T(4,128)S(1)}, f32[4,64]{1,0:T(4,128)S(1)}, u32[]{:S(2)}, u32[]{:S(2)}) collective-permute-start(f32[4,64]{1,0:T(4,128)S(1)} %add.17), channel_id=1, source_target_pairs={{0,2},{2,0},{4,6},{6,4},{8,10},{10,8},{12,14},{14,12},{16,18},{18,... | collective-permute-start | bytes 3080 | tf_op jit(solution)/shard_map/ppermute | solution.py:277
  81.1 2.0 %collective-permute-done.18 = f32[4,64]{1,0:T(4,128)S(1)} collective-permute-done((f32[4,64]{1,0:T(4,128)S(1)}, f32[4,64]{1,0:T(4,128)S(1)}, u32[]{:S(2)}, u32[]{:S(2)}) %collective-permute-start.18) | collective-permute-done | bytes 1056 | tf_op jit(solution)/shard_map/ppermute | solution.py:277
  83.1 0.6 collective-permute-start.19
  83.7 3.1 %collective-permute-done.19 = f32[8,64]{1,0:T(8,128)S(1)} collective-permute-done((f32[8,64]{1,0:T(8,128)S(1)}, f32[8,64]{1,0:T(8,128)S(1)}, u32[]{:S(2)}, u32[]{:S(2)}) %collective-permute-start.19) | collective-permute-done | bytes 2080 | tf_op jit(solution)/shard_map/ppermute | solution.py:277
  86.8 0.6 maximum_select_fusion
  87.4 0.0 collective-permute-done.12.rest_1_
  87.4 0.0 collective-permute-done.13.rest_2_
  87.4 0.0 collective-permute-done.14.rest_3_
  87.4 2.6 %unpack.1 = (bf16[1,128,2048]{2,1,0:T(8,128)(2,1)}, bf16[1,128,2048]{2,1,0:T(8,128)(2,1)}, bf16[1,128,2048]{2,1,0:T(8,128)(2,1)}) custom-call(s32[3]{0:T(128)S(1)} %pad_add_fusion.meta, bf16[384,512]{1,0:T(8,128)(2,1)} %get-tuple-element.66.rest_0_, bf16[384,512]{1,0:T(8,128)(2,1)S(1)} %collective-permute-done.12.rest_1_, ...), custom_call_target="tpu_custom_call" | custom-call | tf_op jit(solution)/shard_map/unpack/pallas_call | solution.py:436
  (9 shorter events, 0.1 us)
Async XLA Ops:
  1.3 0.7 copy-start
  4.0 10.5 %collective-permute-start.4 = (bf16[544,256]{1,0:T(8,128)(2,1)S(1)}, bf16[544,256]{1,0:T(8,128)(2,1)S(1)}, u32[]{:S(2)}, u32[]{:S(2)}) collective-permute-start(bf16[544,256]{1,0:T(8,128)(2,1)S(1)} %get-tuple-element.48), channel_id=1, source_target_pairs={{0,2},{2,0},{4,6},{6,4},{8,10},{10,8},{12,14},{14,12},{16,18},{18,... | collective-permute-start | bytes 835592 | tf_op jit(solution)/shard_map/ppermute | solution.py:277
  7.0 15.3 %collective-permute-start.5 = (bf16[544,256]{1,0:T(8,128)(2,1)S(1)}, bf16[544,256]{1,0:T(8,128)(2,1)S(1)}, u32[]{:S(2)}, u32[]{:S(2)}) collective-permute-start(bf16[544,256]{1,0:T(8,128)(2,1)S(1)} %get-tuple-element.49), channel_id=1, source_target_pairs={{0,4},{2,6},{4,0},{6,2},{8,12},{10,14},{12,8},{14,10},{16,20},{18,... | collective-permute-start | bytes 835592 | tf_op jit(solution)/shard_map/ppermute | solution.py:277
  8.5 13.8 %collective-permute-start.6 = (bf16[544,256]{1,0:T(8,128)(2,1)S(1)}, bf16[544,256]{1,0:T(8,128)(2,1)S(1)}, u32[]{:S(2)}, u32[]{:S(2)}) collective-permute-start(bf16[544,256]{1,0:T(8,128)(2,1)S(1)} %get-tuple-element.50), channel_id=1, source_target_pairs={{0,6},{2,4},{4,2},{6,0},{8,14},{10,12},{12,10},{14,8},{16,22},{18,... | collective-permute-start | bytes 835592 | tf_op jit(solution)/shard_map/ppermute | solution.py:277
  10.5 17.8 %collective-permute-start = (bf16[512,256]{1,0:T(8,128)(2,1)S(1)}, bf16[512,256]{1,0:T(8,128)(2,1)S(1)}, u32[]{:S(2)}, u32[]{:S(2)}) collective-permute-start(bf16[512,256]{1,0:T(8,128)(2,1)S(1)} %get-tuple-element.41), channel_id=1, source_target_pairs={{0,2},{2,0},{4,6},{6,4},{8,10},{10,8},{12,14},{14,12},{16,18},{18,... | collective-permute-start | bytes 786440 | tf_op jit(solution)/shard_map/ppermute | solution.py:277
  12.5 19.8 %collective-permute-start.1 = (bf16[512,256]{1,0:T(8,128)(2,1)S(1)}, bf16[512,256]{1,0:T(8,128)(2,1)S(1)}, u32[]{:S(2)}, u32[]{:S(2)}) collective-permute-start(bf16[512,256]{1,0:T(8,128)(2,1)S(1)} %get-tuple-element.42), channel_id=1, source_target_pairs={{0,4},{2,6},{4,0},{6,2},{8,12},{10,14},{12,8},{14,10},{16,20},{18,... | collective-permute-start | bytes 786440 | tf_op jit(solution)/shard_map/ppermute | solution.py:277
  14.5 17.8 %collective-permute-start.2 = (bf16[512,256]{1,0:T(8,128)(2,1)S(1)}, bf16[512,256]{1,0:T(8,128)(2,1)S(1)}, u32[]{:S(2)}, u32[]{:S(2)}) collective-permute-start(bf16[512,256]{1,0:T(8,128)(2,1)S(1)} %get-tuple-element.43), channel_id=1, source_target_pairs={{0,6},{2,4},{4,2},{6,0},{8,14},{10,12},{12,10},{14,8},{16,22},{18,... | collective-permute-start | bytes 786440 | tf_op jit(solution)/shard_map/ppermute | solution.py:277
  23.4 14.7 %collective-permute-start.8 = (bf16[4,272,256]{2,1,0:T(8,128)(2,1)}, bf16[4,272,256]{2,1,0:T(8,128)(2,1)S(1)}, u32[]{:S(2)}, u32[]{:S(2)}) collective-permute-start(bf16[4,272,256]{2,1,0:T(8,128)(2,1)} %get-tuple-element.51.fo.kvo), channel_id=1, source_target_pairs={{0,8},{2,10},{4,12},{6,14},{8,16},{10,18},{12,20},{14,22},{16,24},... | collective-permute-start | bytes 1671176 | tf_op jit(solution)/shard_map/ppermute | solution.py:283
  26.9 1.3 %copy-start.1 = (bf16[16,64]{1,0:T(8,128)(2,1)S(1)}, bf16[16,64]{1,0:T(8,128)(2,1)}, u32[]{:S(2)}) copy-start(bf16[16,64]{1,0:T(8,128)(2,1)} %param.13) | copy-start | bytes 6148
  27.0 14.5 %collective-permute-start.9 = (bf16[4,272,256]{2,1,0:T(8,128)(2,1)}, bf16[4,272,256]{2,1,0:T(8,128)(2,1)S(1)}, u32[]{:S(2)}, u32[]{:S(2)}) collective-permute-start(bf16[4,272,256]{2,1,0:T(8,128)(2,1)} %get-tuple-element.52.qd), channel_id=1, source_target_pairs={{8,0},{10,2},{12,4},{14,6},{16,8},{18,10},{20,12},{22,14},{24,16},... | collective-permute-start | bytes 1671176 | tf_op jit(solution)/shard_map/ppermute | solution.py:283
  33.3 16.1 %collective-permute-start.7 = (bf16[4,256,256]{2,1,0:T(8,128)(2,1)}, bf16[4,256,256]{2,1,0:T(8,128)(2,1)S(1)}, u32[]{:S(2)}, u32[]{:S(2)}) collective-permute-start(bf16[4,256,256]{2,1,0:T(8,128)(2,1)} %get-tuple-element.45.kvo), channel_id=1, source_target_pairs={{0,8},{2,10},{4,12},{6,14},{8,16},{10,18},{12,20},{14,22},{16,24},... | collective-permute-start | bytes 1572872 | tf_op jit(solution)/shard_map/ppermute | solution.py:283
  36.9 24.3 %collective-permute-start.3 = (bf16[4,256,256]{2,1,0:T(8,128)(2,1)}, bf16[4,256,256]{2,1,0:T(8,128)(2,1)S(1)}, u32[]{:S(2)}, u32[]{:S(2)}) collective-permute-start(bf16[4,256,256]{2,1,0:T(8,128)(2,1)} %get-tuple-element.44.qd), channel_id=1, source_target_pairs={{8,0},{10,2},{12,4},{14,6},{16,8},{18,10},{20,12},{22,14},{24,16},... | collective-permute-start | bytes 1572872 | tf_op jit(solution)/shard_map/ppermute | solution.py:283
  48.2 9.3 %collective-permute-start.11 = (f32[2,8,512]{2,1,0:T(8,128)}, f32[2,8,512]{2,1,0:T(8,128)S(1)}, u32[]{:S(2)}, u32[]{:S(2)}) collective-permute-start(f32[2,8,512]{2,1,0:T(8,128)} %get-tuple-element.58), channel_id=1, source_target_pairs={{8,0},{10,2},{12,4},{14,6},{16,8},{18,10},{20,12},{22,14},{24,16},... | collective-permute-start | bytes 98312 | tf_op jit(solution)/shard_map/ppermute | solution.py:283
  56.1 6.6 %collective-permute-start.10 = (f32[2,8,512]{2,1,0:T(8,128)}, f32[2,8,512]{2,1,0:T(8,128)S(1)}, u32[]{:S(2)}, u32[]{:S(2)}) collective-permute-start(f32[2,8,512]{2,1,0:T(8,128)} %get-tuple-element.54), channel_id=1, source_target_pairs={{8,0},{10,2},{12,4},{14,6},{16,8},{18,10},{20,12},{22,14},{24,16},... | collective-permute-start | bytes 98312 | tf_op jit(solution)/shard_map/ppermute | solution.py:283
  66.5 20.9 %collective-permute-start.12 = (bf16[384,512]{1,0:T(8,128)(2,1)}, bf16[384,512]{1,0:T(8,128)(2,1)S(1)}, u32[]{:S(2)}, u32[]{:S(2)}) collective-permute-start(bf16[384,512]{1,0:T(8,128)(2,1)} %get-tuple-element.67), channel_id=1, source_target_pairs={{0,2},{2,0},{4,6},{6,4},{8,10},{10,8},{12,14},{14,12},{16,18},{18,... | collective-permute-start | bytes 1179656 | tf_op jit(solution)/shard_map/ppermute | solution.py:277
  68.0 19.4 %collective-permute-start.13 = (bf16[384,512]{1,0:T(8,128)(2,1)}, bf16[384,512]{1,0:T(8,128)(2,1)S(1)}, u32[]{:S(2)}, u32[]{:S(2)}) collective-permute-start(bf16[384,512]{1,0:T(8,128)(2,1)} %get-tuple-element.68), channel_id=1, source_target_pairs={{0,4},{2,6},{4,0},{6,2},{8,12},{10,14},{12,8},{14,10},{16,20},{18,... | collective-permute-start | bytes 1179656 | tf_op jit(solution)/shard_map/ppermute | solution.py:277
  68.5 18.9 %collective-permute-start.14 = (bf16[384,512]{1,0:T(8,128)(2,1)}, bf16[384,512]{1,0:T(8,128)(2,1)S(1)}, u32[]{:S(2)}, u32[]{:S(2)}) collective-permute-start(bf16[384,512]{1,0:T(8,128)(2,1)} %get-tuple-element.69), channel_id=1, source_target_pairs={{0,6},{2,4},{4,2},{6,0},{8,14},{10,12},{12,10},{14,8},{16,22},{18,... | collective-permute-start | bytes 1179656 | tf_op jit(solution)/shard_map/ppermute | solution.py:277
  70.0 3.6 %collective-permute-start.15 = (f32[4,64]{1,0:T(4,128)S(1)}, f32[4,64]{1,0:T(4,128)S(1)}, u32[]{:S(2)}, u32[]{:S(2)}) collective-permute-start(f32[4,64]{1,0:T(4,128)S(1)} %pad_maximum_fusion), channel_id=1, source_target_pairs={{0,8},{2,10},{4,12},{6,14},{8,0},{10,2},{12,4},{14,6},{16,24},{18,... | collective-permute-start | bytes 3080 | tf_op jit(solution)/shard_map/ppermute | solution.py:277
  73.7 4.7 %collective-permute-start.16 = (f32[4,64]{1,0:T(4,128)S(1)}, f32[4,64]{1,0:T(4,128)S(1)}, u32[]{:S(2)}, u32[]{:S(2)}) collective-permute-start(f32[4,64]{1,0:T(4,128)S(1)} %add.15), channel_id=1, source_target_pairs={{0,16},{2,18},{4,20},{6,22},{8,24},{10,26},{12,28},{14,30},{16,0},... | collective-permute-start | bytes 3080 | tf_op jit(solution)/shard_map/ppermute | solution.py:277
  78.4 1.2 %collective-permute-start.17 = (f32[4,64]{1,0:T(4,128)S(1)}, f32[4,64]{1,0:T(4,128)S(1)}, u32[]{:S(2)}, u32[]{:S(2)}) collective-permute-start(f32[4,64]{1,0:T(4,128)S(1)} %add.16), channel_id=1, source_target_pairs={{0,1},{1,0},{2,3},{3,2},{4,5},{5,4},{6,7},{7,6},{8,9},{9,8},{10,11... | collective-permute-start | bytes 3080 | tf_op jit(solution)/shard_map/ppermute | solution.py:277
  79.5 3.6 %collective-permute-start.18 = (f32[4,64]{1,0:T(4,128)S(1)}, f32[4,64]{1,0:T(4,128)S(1)}, u32[]{:S(2)}, u32[]{:S(2)}) collective-permute-start(f32[4,64]{1,0:T(4,128)S(1)} %add.17), channel_id=1, source_target_pairs={{0,2},{2,0},{4,6},{6,4},{8,10},{10,8},{12,14},{14,12},{16,18},{18,... | collective-permute-start | bytes 3080 | tf_op jit(solution)/shard_map/ppermute | solution.py:277
  83.1 3.7 %collective-permute-start.19 = (f32[8,64]{1,0:T(8,128)S(1)}, f32[8,64]{1,0:T(8,128)S(1)}, u32[]{:S(2)}, u32[]{:S(2)}) collective-permute-start(f32[8,64]{1,0:T(8,128)S(1)} %maximum_select_fusion.1), channel_id=1, source_target_pairs={{0,4},{2,6},{4,0},{6,2},{8,12},{10,14},{12,8},{14,10},{16,20},{18,... | collective-permute-start | bytes 6152 | tf_op jit(solution)/shard_map/ppermute | solution.py:277

commit v3 on v0

v3 whole, which is shorter than its diff:
```python
import functools

import jax
import jax.numpy as jnp
from jax import lax
from jax.experimental import pallas as pl
from jax.experimental.pallas import tpu as pltpu
from jax.sharding import PartitionSpec as P

HEADS = 16
HEAD_DIM = 128
WINDOW = 512
FIELDS = 64
FACTOR = HEAD_DIM ** (-0.5)
LOG2E = 1.4426950408889634
HIDDEN = -1e30
PAD = 16
CHUNKS = 2
MIB = 1 << 20
BF16, F32 = jnp.bfloat16, jnp.float32
ANY = pl.BlockSpec(memory_space=pl.ANY)
SMEM = pl.BlockSpec(memory_space=pltpu.SMEM)
VMEM = pl.BlockSpec(memory_space=pltpu.VMEM)
GATHER_FLOPS, ROWS_FLOPS, COLUMNS_FLOPS, UNPACK_FLOPS = 2 * 10**9, 2 * 10**9, (4 * 10**9, 0), 0
NT = (((1,), (1,)), ((), ()))


def dot(a, b):
    return jnp.dot(a, b, preferred_element_type=F32)


def dot_nt(a, b):
    return lax.dot_general(a, b, NT, preferred_element_type=F32)


def pack_kernel(reach, tok, width, chunk, meta, q, g, k, v, fields, *rest):
    outs, field_scr, sems = rest[:reach], rest[-2], rest[-1]
    p = meta[0]
    field_copy = pltpu.make_async_copy(fields, field_scr, sems.at[4 * reach])
    field_copy.start()
    copies = []
    for m in list(range(1, reach)) + [0]:
        first = pl.multiple_of((p ^ m) * (HEADS // reach * HEAD_DIM) + chunk * width, 128)
        for at, src in enumerate((q, g, k, v)):
            dst = outs[m].at[pl.ds(at * tok, tok)]
            copies.append(pltpu.make_async_copy(src.at[0, :, pl.ds(first, width)], dst, sems.at[len(copies)]))
            copies[-1].start()
    field_copy.wait()
    row = jnp.concatenate([field_scr[...].astype(F32)] * (width // tok), axis=1)
    for out in outs:
        if out.shape[0] > 4 * tok:
            out[4 * tok :] = jnp.broadcast_to(row, (PAD, width)).astype(BF16)
    for copy in copies:
        copy.wait()


def gather_kernel(reach, tok, *refs):
    arrived, qd, kv = refs[:reach], *refs[reach:]
    for m in range(reach):
        qd[m] = arrived[m][: 2 * tok]
        kv[m] = arrived[m][2 * tok :]


def unpack_kernel(reach, tok, group_width, blocks, meta, *rest):
    parts, outs, sems = rest[:reach], rest[-4:-1], rest[-1]
    p = meta[0]
    width = parts[0].shape[1]
    copies = []
    for m in range(reach):
        for at, (which, chunk) in enumerate(blocks):
            first = pl.multiple_of((p ^ m) * group_width + chunk * width, 128)
            dst = outs[which].at[0, :, pl.ds(first, width)]
            copies.append(pltpu.make_async_copy(parts[m].at[pl.ds(at * tok, tok)], dst, sems.at[len(copies)]))
            copies[-1].start()
    for copy in copies:
        copy.wait()


def finish_kernel(reach, tok, group_width, blocks, meta, *rest):
    total, sems = rest[-2:]
    join(reach, tok, len(blocks) * tok, meta[0], rest[:reach], total)
    unpack_kernel(reach, tok, group_width, blocks, meta, *rest[:-2], sems)


def key_columns(fields, slot, tok):
    row = fields[slot, 2 * tok : 2 * tok + PAD, 0:tok].astype(F32)[0:1]
    spread = jnp.broadcast_to(row, (tok, tok))
    lane = lax.broadcasted_iota(jnp.int32, (tok, tok), 1).astype(F32)
    sub = lax.broadcasted_iota(jnp.int32, (tok, tok), 0).astype(F32)
    onehot = jnp.where(spread.T == lane, 1.0, 0.0).astype(BF16)
    onehot_t = jnp.where(spread == sub, 1.0, 0.0).astype(BF16)
    return onehot, onehot_t


def head_bias(bias_ref, head, tok):
    table = bias_ref[...].astype(F32)
    at = lax.broadcasted_iota(jnp.int32, table.shape, 0)
    row = jnp.sum(jnp.where(at == head, table, 0.0), axis=0, keepdims=True)
    row = jnp.concatenate([row, jnp.zeros((1, tok - FIELDS), F32)], axis=1)
    return jnp.broadcast_to(row, (tok, tok)).T.astype(BF16)


def three_parts(x):
    high = x.astype(BF16)
    rest = x - high.astype(F32)
    mid = rest.astype(BF16)
    return high, mid, (rest - mid.astype(F32)).astype(BF16)


def masks(tok):
    key_at = lax.broadcasted_iota(jnp.int32, (tok, tok), 0)
    query_at = lax.broadcasted_iota(jnp.int32, (tok, tok), 1)
    return key_at > query_at, lax.broadcasted_iota(jnp.int32, (1, tok), 1)


def query_pair(qd, p, a, tok, head):
    slots = (p ^ a, p ^ (a + 1))
    query = jnp.concatenate([qd[slot, 0:tok, head] for slot in slots], axis=0)
    grad = jnp.concatenate([qd[slot, tok : 2 * tok, head] for slot in slots], axis=0)
    return query, grad


def side_by_side(first, second, tok, ends):
    gap = jnp.zeros((tok, tok), first.dtype)
    first = jnp.concatenate([first, gap], axis=0) if ends else first
    return jnp.concatenate([first, jnp.concatenate([gap, second], axis=0)], axis=1)


def rows_kernel(reach, tok, chunk, meta, qd, kvo, kvp, fo, fp, bias_ref, sums_in, *rest):
    dq_out, dk_out, dv_out, stats_out, sums_out, *scratch = rest
    k_scr, v_scr, kt_scr, oh_scr, oht_scr, bias_scr, acc_scr = scratch
    p, plane, length = meta[0], meta[1], meta[2]
    span = reach * tok

    for blk in range(2 * reach):
        rows = slice(blk * tok, (blk + 1) * tok)
        onehot, onehot_t = key_columns(fp if blk < reach else fo, p ^ (blk % reach), tok)
        oh_scr[rows] = onehot
        oht_scr[:, rows] = onehot_t
    per = kvo.shape[2] // HEAD_DIM
    sums_out[...] = sums_in[...]
    shut = jnp.where(plane == 0, HIDDEN, 0.0).astype(F32)
    later, lane = masks(tok)

    @pl.loop(0, kvo.shape[2] // HEAD_DIM)
    def _(h):
        head = pl.ds(pl.multiple_of(h * HEAD_DIM, HEAD_DIM), HEAD_DIM)
        at = chunk * per + h
        bias = head_bias(bias_ref, p * (HEADS // reach) + at, tok)
        for blk in range(2 * reach):
            rows = slice(blk * tok, (blk + 1) * tok)
            src, slot = (kvp if blk < reach else kvo), p ^ (blk % reach)
            key = src[slot, 0:tok, head]
            k_scr[rows] = key
            kt_scr[:, rows] = key.T
            v_scr[rows] = src[slot, tok : 2 * tok, head]
            col = dot(oh_scr[rows], bias) * LOG2E
            bias_scr[rows] = col + shut if blk < reach else col
        acc_scr[...] = jnp.zeros_like(acc_scr)
        for pair in range(0, reach, 2):
            query, grad = query_pair(qd, p, pair, tok, head)
            wide = slice(pair * tok, (pair + reach + 2) * tok)
            logits = dot_nt(k_scr[wide], query)
            probs_both = dot_nt(v_scr[wide], grad)
            lows, ds_lows = [], []
            for half in range(2):
                a = pair + half
                rows = slice(a * tok, (a + reach + 1) * tok)
                mine = slice(half * tok, (half + reach + 1) * tok)
                there = slice(a * tok, (a + 1) * tok)
                cols = slice(half * tok, (half + 1) * tok)
                s = logits[mine, cols] * (FACTOR * LOG2E) + bias_scr[rows]
                s = jnp.concatenate(
                    [jnp.where(later, s[:tok], HIDDEN), s[tok:-tok], jnp.where(later, HIDDEN, s[-tok:])],
                    axis=0,
                )
                peak = jnp.max(s, axis=0, keepdims=True)
                power = jnp.exp2(s - peak)
                total = jnp.sum(power, axis=0, keepdims=True)
                live = plane * span + a * tok + lane < length
                weight = power * jnp.where(live, 1.0 / total, 0.0)
                low = weight.astype(BF16)
                probs = probs_both[mine, cols]
                delta = jnp.sum(low.astype(F32) * probs, axis=0, keepdims=True)
                ds = weight * (probs - delta)
                acc_scr[rows] += ds
                lows.append(low)
                ds_lows.append(ds.astype(BF16))
                stats_out[h, 0:1, there] = peak + jnp.log2(total)
                stats_out[h, 1:2, there] = delta
            low = side_by_side(*lows, tok, True)
            ds_low = side_by_side(*ds_lows, tok, True)
            dq = dot(kt_scr[:, wide], ds_low)
            for half in range(2):
                dq_half = dq[:, half * tok : (half + 1) * tok]
                dq_out[p ^ (pair + half), :, head] = (dq_half.T * FACTOR).astype(BF16)
            own = slice((reach - pair) * tok, (reach + 2) * tok)
            dv = dot(low[own], grad)
            dk = dot(ds_low[own], query)
            done = pair * tok
            if pair:
                dv_out[0:done, head] += dv[:done]
                dk_out[0:done, head] += dk[:done]
            dv_out[done : done + 2 * tok, head] = dv[done:]
            dk_out[done : done + 2 * tok, head] = dk[done:]
        by_field = sum(dot(oht_scr[...], part) for part in three_parts(acc_scr[...]))
        row = jnp.sum(by_field.T, axis=0, keepdims=True)
        sums_out[...] += jnp.where(lax.broadcasted_iota(jnp.int32, (8, tok), 0) == at, row, 0.0)


def columns_kernel(reach, tok, chunk, meta, qd, kvo, fo, stats, bias_ref, dk_in, dv_in, *rest):
    k_scr, v_scr, oh_scr, bias_scr, dk_scr, dv_scr = rest[-6:]
    outs, extras = rest[-6 - reach : -6], rest[: -6 - reach]
    last = len(extras) == 1
    if last:
        parts = [part.astype(F32) for part in three_parts(extras[0][...])]
        parts = [jnp.concatenate(parts[:2], axis=1), jnp.concatenate([parts[2], jnp.zeros_like(parts[2])], axis=1)]
        for m in range(reach):
            outs[m][2 * tok :] = jnp.concatenate(parts, axis=0).astype(BF16)
    p, plane, length = meta[0], meta[1], meta[2]
    span = reach * tok
    for blk in range(reach):
        oh_scr[blk * tok : (blk + 1) * tok], _ = key_columns(fo, p ^ blk, tok)
    later, lane = masks(tok)

    @pl.loop(0, kvo.shape[2] // HEAD_DIM)
    def _(h):
        head = pl.ds(pl.multiple_of(h * HEAD_DIM, HEAD_DIM), HEAD_DIM)
        at = chunk * (kvo.shape[2] // HEAD_DIM) + h
        bias = head_bias(bias_ref, p * (HEADS // reach) + at, tok)
        for blk in range(reach):
            rows = slice(blk * tok, (blk + 1) * tok)
            k_scr[rows] = kvo[p ^ blk, 0:tok, head]
            v_scr[rows] = kvo[p ^ blk, tok : 2 * tok, head]
            bias_scr[rows] = dot(oh_scr[rows], bias) * LOG2E
        for pair in range(0, reach, 2):
            query, grad = query_pair(qd, p, pair, tok, head)
            wide = slice(pair * tok, span)
            logits = dot_nt(k_scr[wide], query)
            probs_both = dot_nt(v_scr[wide], grad)
            lows, ds_lows = [], []
            for half in range(2):
                a = pair + half
                there = slice(a * tok, (a + 1) * tok)
                cols = slice(half * tok, (half + 1) * tok)
                live = (plane + 1) * span + a * tok + lane < length
                norm = jnp.where(live, stats[h, 0:1, there], -HIDDEN)
                delta = stats[h, 1:2, there]
                s = logits[half * tok :, cols] * (FACTOR * LOG2E) + bias_scr[a * tok :]
                weight = jnp.exp2(s - norm)
                first = jnp.where(later, weight[:tok], 0.0)
                weight = jnp.concatenate([first, weight[tok:]], axis=0) if a < reach - 1 else first
                lows.append(weight.astype(BF16))
                ds_lows.append((weight * (probs_both[half * tok :, cols] - delta)).astype(BF16))
            dv = dot(side_by_side(*lows, tok, False), grad)
            dk = dot(side_by_side(*ds_lows, tok, False), query)
            if pair:
                dv_scr[wide] += dv
                dk_scr[wide] += dk
            else:
                dv_scr[...] = dv + dv_in[:, head]
                dk_scr[...] = dk + dk_in[:, head]
        for m in range(reach):
            mine = pl.ds(pl.multiple_of((p ^ m) * tok, tok), tok)
            outs[m][0:tok, head] = (dk_scr[mine] * FACTOR).astype(BF16)
            outs[m][tok : 2 * tok, head] = dv_scr[mine].astype(BF16)
            for at, dq in enumerate(() if last else extras):
                outs[m][(2 + at) * tok : (3 + at) * tok, head] = dq[m, :, head]


def add_kernel(reach, tok, a, b, out):
    out[...] = a[...] + b[...]


def join(reach, tok, first, p, slots, out):
    heads = HEADS // reach
    found = []
    for slot in slots:
        rows = slot[first : first + PAD].astype(F32)
        found.append(rows[:8, :FIELDS] + rows[:8, tok : tok + FIELDS] + rows[8:, :FIELDS])
    for q in range(reach):
        part = found[0]
        for m in range(1, reach):
            part = jnp.where(p == q ^ m, found[m], part)
        out[q * heads : (q + 1) * heads] = part[:heads]


def params(mib, *semantics):
    return pltpu.CompilerParams(
        vmem_limit_bytes=mib * MIB, dimension_semantics=semantics if semantics else None
    )


def cost(flops, nbytes, trans=0):
    return pl.CostEstimate(flops=flops, bytes_accessed=nbytes, transcendentals=trans)


def in_hbm(*arrays):
    return [pltpu.with_memory_space_constraint(array, pltpu.HBM) for array in arrays]


def in_vmem(*arrays):
    return [pltpu.with_memory_space_constraint(array, pltpu.VMEM) for array in arrays]


def following(value, mark):
    return lax.optimization_barrier((value, mark))[0]


def swapped(value, axis, mask):
    count = lax.axis_size(axis)
    return lax.ppermute(value, axis, [(source, source ^ mask) for source in range(count)])


def passed_along(value, axis, steps):
    count = lax.axis_size(axis)
    first, last = max(0, -steps), min(count, count - steps)
    return lax.ppermute(value, axis, [(source, source + steps) for source in range(first, last)])


def shards(queries, keys, values, grad_out, lengths, fields, field_bias):
    tok = queries.shape[1]
    row_width = queries.shape[2]
    reach = WINDOW // tok
    group = HEADS // reach
    per = group // CHUNKS
    width = per * HEAD_DIM
    span = reach * tok
    index = lax.axis_index("seq")
    p = lax.rem(index, reach)
    meta = jnp.stack([p, lax.div(index, reach), lengths[0]]).astype(jnp.int32)
    raw = in_hbm(queries, grad_out, keys, values)

    def vmem(shape, dtype=BF16):
        return pltpu.VMEM(shape, dtype)


    def pad(chunk):
        return 0 if chunk else PAD

    def pack(chunk):
        return pl.pallas_call(
            functools.partial(pack_kernel, reach, tok, width, chunk),
            in_specs=[SMEM] + [ANY] * 5,
            out_specs=[VMEM] * reach,
            out_shape=[pltpu.VMEM((4 * tok + pad(chunk), width), BF16)] * reach,
            scratch_shapes=[
                pltpu.VMEM((1, tok), jnp.int32),
                pltpu.SemaphoreType.DMA((4 * reach + 1,)),
            ],
            compiler_params=params(2),
            cost_estimate=cost(0, 2 * MIB),
            name="pack",
        )(meta, *raw, *in_hbm(fields))

    def local(kernel, name, flops, out_shape, *args, scratch=()):
        return pl.pallas_call(
            kernel,
            in_specs=[SMEM if arg is meta else VMEM for arg in args],
            out_specs=[VMEM] * len(out_shape),
            out_shape=out_shape,
            scratch_shapes=scratch,
            compiler_params=params(12),
            cost_estimate=cost(flops, 2 * MIB),
            name=name,
        )(*[arg if arg is meta else in_vmem(arg)[0] for arg in args])

    def gather(chunk, arrived):
        out = [vmem((reach, 2 * tok, width)), vmem((reach, 2 * tok + pad(chunk), width))]
        return local(functools.partial(gather_kernel, reach, tok), "gather", GATHER_FLOPS if chunk else 0, out, *arrived)

    def rows_of(chunk, qd, kvo, kvp, fo, fp, sums):
        out = [
            vmem((reach, tok, width)),
            vmem((span, width), F32),
            vmem((span, width), F32),
            vmem((per, 2, span), F32),
            vmem((8, tok), F32),
        ]
        scratch = [
            pltpu.VMEM((2 * span, HEAD_DIM), BF16),
            pltpu.VMEM((2 * span, HEAD_DIM), BF16),
            pltpu.VMEM((HEAD_DIM, 2 * span), BF16),
            pltpu.VMEM((2 * span, tok), BF16),
            pltpu.VMEM((tok, 2 * span), BF16),
            pltpu.VMEM((2 * span, tok), F32),
            pltpu.VMEM((2 * span, tok), F32),
        ]
        kernel = functools.partial(rows_kernel, reach, tok, chunk)
        return local(kernel, "rows", ROWS_FLOPS, out, meta, qd, kvo, kvp, fo, fp, field_bias, sums, scratch=scratch)

    def columns_of(chunk, qd, kvo, fo, stats, dk, dv, *extras):
        out = [vmem((2 * tok + (PAD if len(extras) == 1 else len(extras) * tok), width))] * reach
        scratch = [
            pltpu.VMEM((span, HEAD_DIM), BF16),
            pltpu.VMEM((span, HEAD_DIM), BF16),
            pltpu.VMEM((span, tok), BF16),
            pltpu.VMEM((span, tok), F32),
            pltpu.VMEM((span, HEAD_DIM), F32),
            pltpu.VMEM((span, HEAD_DIM), F32),
        ]
        kernel = functools.partial(columns_kernel, reach, tok, chunk)
        args = (meta, qd, kvo, fo, stats, field_bias, dk, dv, *extras)
        return local(kernel, "columns", COLUMNS_FLOPS[chunk], out, *args, scratch=scratch)

    def add(a, b):
        return local(functools.partial(add_kernel, reach, tok), "add", 0, [vmem(a.shape, F32)], a, b)[0]

    packed = [list(pack(c)) for c in range(CHUNKS)]
    packed[0][0] = following(packed[0][0], packed[1][0])
    planes, before, after = [], [], []
    for c in range(CHUNKS):
        arrived = packed[c][:1] + [swapped(packed[c][m], "seq", m) for m in range(1, reach)]
        qd, kv = gather(c, arrived)
        planes.append((qd, kv))
        moved = passed_along(kv, "seq", reach), passed_along(qd, "seq", -reach)
        before.append(following(moved[0], moved[1]) if c == 0 else moved[0])
        after.append(moved[1])
    sums = jnp.zeros((8, tok), F32)
    pending, dqs = [], []
    for c in range(CHUNKS):
        dq, dk, dv, stats, sums = rows_of(c, *planes[c], before[c], planes[0][1], before[0], sums)
        dqs.append(dq)
        pending.append((after[c], planes[c][1], planes[0][1], passed_along(following(stats, after[c]), "seq", -reach), dk, dv))
    messages = [columns_of(0, *pending[0], *dqs)]
    count = lax.axis_size("seq")
    mask = reach
    while mask < count:
        sums = add(sums, swapped(sums, "seq", mask))
        if mask == reach:
            messages[0] = [following(following(own, sums), pending[1][3]) for own in messages[0]]
        mask *= 2
    mask = 1
    while mask < lax.axis_size("dp"):
        sums = add(sums, swapped(sums, "dp", mask))
        mask *= 2
    messages.append(columns_of(1, *pending[1], sums))
    parts = [[own[0]] + [swapped(own[m], "seq", m) for m in range(1, reach)] for own in messages]

    blocks = [((1, 0), (2, 0), (0, 0), (0, 1)), ((1, 1), (2, 1))]
    grads = []
    for c in range(CHUNKS):
        last = c == CHUNKS - 1
        kernel = finish_kernel if last else unpack_kernel
        out = [jax.ShapeDtypeStruct((1, tok, row_width), BF16)] * 3
        grads = pl.pallas_call(
            functools.partial(kernel, reach, tok, group * HEAD_DIM, blocks[c]),
            in_specs=[SMEM] + [VMEM] * reach + [ANY] * len(grads),
            out_specs=[ANY] * 3 + [VMEM] * last,
            out_shape=out + [jax.ShapeDtypeStruct((HEADS, FIELDS), F32)] * last,
            scratch_shapes=[pltpu.SemaphoreType.DMA((len(blocks[c]) * reach,))],
            input_output_aliases={1 + reach + at: at for at in range(len(grads))},
            compiler_params=params(2),
            cost_estimate=cost(0 if last else UNPACK_FLOPS, 2 * MIB),
            name="unpack",
        )(meta, *in_vmem(*parts[c]), *grads)
    return grads


def solution(mesh):
    return jax.shard_map(
        shards,
        mesh=mesh,
        in_specs=(
            P("dp", "seq", None),
            P("dp", "seq", None),
            P("dp", "seq", None),
            P("dp", "seq", None),
            P("dp"),
            P("dp", "seq"),
            P(),
        ),
        out_specs=(P("dp", "seq", None), P("dp", "seq", None), P("dp", "seq", None), P()),
        check_vma=False,
    )
```

time: 419 us -> 83.2 us (0.20)
  blocking collectives: 117 us -> 0 us
  waiting for transfers between devices: 123 us -> 22.3 us
  local copies, waits for them, and re-layouts: 63.1 us -> 0.01 us
  starting transfers between devices: 81.2 us -> 35.5 us
  Pallas kernels: 0 us -> 23.6 us
  matrix products: 20.4 us -> 0 us
  other arithmetic: 10.9 us -> 0.08 us
    ppermute x24 -> x6, waiting for transfers between devices: 123 us -> 4.12 us  [passed_along(): lax.ppermute(value, axis, [(source, source + steps) for source in range(f...]
    psum x1 -> x0, blocking collectives: 117 us -> none  [shards(): bias_total = lax.psum(bias_local, ('seq', 'dp'))]
    ppermute x24 -> x6, starting transfers between devices: 81.2 us -> 12.2 us  [passed_along(): lax.ppermute(value, axis, [(source, source + steps) for source in range(f...]
    slice x13 -> x0, local copies, waits for them, and re-layouts: 24.4 us -> none  [the longest x4 10.2 us: shards(): grad_key[first_row:first_row + tok_rows]]
    pallas_call x0 -> x13, Pallas kernels: none -> 23.6 us  [the longest x9 16 us: local(): pl.pallas_call(kernel, in_specs=[SMEM if arg is meta else VMEM for arg in...]
    ppermute x0 -> x15, starting transfers between devices: none -> 23.3 us  [swapped(): lax.ppermute(value, axis, [(source, source ^ mask) for source in range(co...]
    unnamed x48 -> x2, local copies, waits for them, and re-layouts: 20.6 us -> 0.01 us
    ppermute x0 -> x15, waiting for transfers between devices: none -> 18.2 us  [swapped(): lax.ppermute(value, axis, [(source, source ^ mask) for source in range(co...]
  transfers between devices with their start and end apart: 24 -> 21, of which waited for: 5 -> 11; matrix products, arithmetic and copies ran while one was open for 10% -> 0% of each run, Pallas kernels for 0% -> 24%
where the time goes in v3:
time: 83.2 us; the launch traced here: 82.8 us
  starting transfers between devices  35.5 us (43%)
  Pallas kernels  23.6 us (28%)
  waiting for transfers between devices  22.3 us (27%)
  between operations  1.42 us (2%)
    ppermute x15, starting transfers between devices, swapped(): lax.ppermute(value, axis, [(source, source ^ mask) for source in range(co...  23.3 us
    ppermute x15, waiting for transfers between devices, swapped(): lax.ppermute(value, axis, [(source, source ^ mask) for source in range(co...  18.2 us
    pallas_call x9, Pallas kernels, local(): pl.pallas_call(kernel, in_specs=[SMEM if arg is meta else VMEM for arg in...  16 us
    ppermute x6, starting transfers between devices, passed_along(): lax.ppermute(value, axis, [(source, source + steps) for source in range(f...  12.2 us
    ppermute x6, waiting for transfers between devices, passed_along(): lax.ppermute(value, axis, [(source, source + steps) for source in range(f...  4.12 us
    pallas_call x2, Pallas kernels, pack(): pl.pallas_call(functools.partial(pack_kernel, reach, tok, width, chunk),...  3.91 us
    pallas_call x2, Pallas kernels, shards(): pl.pallas_call(functools.partial(kernel, reach, tok, group * HEAD_DIM, bl...  3.62 us
  transfers between devices with their start and end apart: 21, of which 11 were waited for; matrix products, arithmetic and copies ran while one was open for 0% of the time, Pallas kernels for 24%

profile of v3, /device:TPU:0, one launch (start us, length us, event | category | flops | bytes accessed | tf_op | source)
XLA Modules:
  0.0 82.8 jit_solution(16495707253581972327)
XLA Ops:
  1.3 0.1 pad_add_fusion.meta
  1.4 2.0 %pack.3 = (bf16[528,256]{1,0:T(8,128)(2,1)S(1)}, bf16[528,256]{1,0:T(8,128)(2,1)S(1)}, bf16[528,256]{1,0:T(8,128)(2,1)S(1)}, bf16[528,256]{1,0:T(8,128)(2,1)S(1)}) custom-call(s32[3]{0:T(128)S(1)} %pad_add_fusion.meta, bf16[1,128,2048]{2,1,0:T(8,128)(2,1)} %q.3, bf16[1,128,2048]{2,1,0:T(8,128)(2,1)} %g.3, bf16[1,128,2048]{2,1,0:T(8,128)(2,1)} %k.3, ...), custom_call_target="tpu_custom_call" | custom-call | bytes 2097152 | tf_op jit(solution)/shard_map/pack/pallas_call | solution.py:342
  3.3 3.0 %collective-permute-start.4 = (bf16[528,256]{1,0:T(8,128)(2,1)S(1)}, bf16[528,256]{1,0:T(8,128)(2,1)S(1)}, u32[]{:S(2)}, u32[]{:S(2)}) collective-permute-start(bf16[528,256]{1,0:T(8,128)(2,1)S(1)} %get-tuple-element.57), channel_id=1, source_target_pairs={{0,2},{2,0},{4,6},{6,4},{8,10},{10,8},{12,14},{14,12},{16,18},{18,... | collective-permute-start | bytes 811016 | tf_op jit(solution)/shard_map/ppermute | solution.py:312
  6.3 1.5 %collective-permute-start.5 = (bf16[528,256]{1,0:T(8,128)(2,1)S(1)}, bf16[528,256]{1,0:T(8,128)(2,1)S(1)}, u32[]{:S(2)}, u32[]{:S(2)}) collective-permute-start(bf16[528,256]{1,0:T(8,128)(2,1)S(1)} %get-tuple-element.58), channel_id=1, source_target_pairs={{0,4},{2,6},{4,0},{6,2},{8,12},{10,14},{12,8},{14,10},{16,20},{18,... | collective-permute-start | bytes 811016 | tf_op jit(solution)/shard_map/ppermute | solution.py:312
  7.8 0.0 collective-permute-start.6
  7.9 2.0 %pack.2 = (bf16[512,256]{1,0:T(8,128)(2,1)S(1)}, bf16[512,256]{1,0:T(8,128)(2,1)S(1)}, bf16[512,256]{1,0:T(8,128)(2,1)S(1)}, bf16[512,256]{1,0:T(8,128)(2,1)S(1)}) custom-call(s32[3]{0:T(128)S(1)} %pad_add_fusion.meta, bf16[1,128,2048]{2,1,0:T(8,128)(2,1)} %q.3, bf16[1,128,2048]{2,1,0:T(8,128)(2,1)} %g.3, bf16[1,128,2048]{2,1,0:T(8,128)(2,1)} %k.3, ...), custom_call_target="tpu_custom_call" | custom-call | bytes 2097152 | tf_op jit(solution)/shard_map/pack/pallas_call | solution.py:342
  9.8 2.0 %collective-permute-start = (bf16[512,256]{1,0:T(8,128)(2,1)S(1)}, bf16[512,256]{1,0:T(8,128)(2,1)S(1)}, u32[]{:S(2)}, u32[]{:S(2)}) collective-permute-start(bf16[512,256]{1,0:T(8,128)(2,1)S(1)} %get-tuple-element.50), channel_id=1, source_target_pairs={{0,2},{2,0},{4,6},{6,4},{8,10},{10,8},{12,14},{14,12},{16,18},{18,... | collective-permute-start | bytes 786440 | tf_op jit(solution)/shard_map/ppermute | solution.py:312
  11.8 1.5 %collective-permute-start.1 = (bf16[512,256]{1,0:T(8,128)(2,1)S(1)}, bf16[512,256]{1,0:T(8,128)(2,1)S(1)}, u32[]{:S(2)}, u32[]{:S(2)}) collective-permute-start(bf16[512,256]{1,0:T(8,128)(2,1)S(1)} %get-tuple-element.51), channel_id=1, source_target_pairs={{0,4},{2,6},{4,0},{6,2},{8,12},{10,14},{12,8},{14,10},{16,20},{18,... | collective-permute-start | bytes 786440 | tf_op jit(solution)/shard_map/ppermute | solution.py:312
  13.4 0.3 collective-permute-done.4.refs_1_
  13.6 3.0 %collective-permute-start.2 = (bf16[512,256]{1,0:T(8,128)(2,1)S(1)}, bf16[512,256]{1,0:T(8,128)(2,1)S(1)}, u32[]{:S(2)}, u32[]{:S(2)}) collective-permute-start(bf16[512,256]{1,0:T(8,128)(2,1)S(1)} %get-tuple-element.52), channel_id=1, source_target_pairs={{0,6},{2,4},{4,2},{6,0},{8,14},{10,12},{12,10},{14,8},{16,22},{18,... | collective-permute-start | bytes 786440 | tf_op jit(solution)/shard_map/ppermute | solution.py:312
  16.6 4.6 %collective-permute-done.5.refs_2_ = bf16[528,256]{1,0:T(8,128)(2,1)S(1)} collective-permute-done((bf16[528,256]{1,0:T(8,128)(2,1)S(1)}, bf16[528,256]{1,0:T(8,128)(2,1)S(1)}, u32[]{:S(2)}, u32[]{:S(2)}) %collective-permute-start.5) | collective-permute-done | bytes 270368 | tf_op jit(solution)/shard_map/ppermute | solution.py:312
  21.2 0.0 collective-permute-done.6.refs_3_
  21.3 0.1 gather.3
  21.3 3.5 %collective-permute-start.8 = (bf16[4,272,256]{2,1,0:T(8,128)(2,1)S(1)}, bf16[4,272,256]{2,1,0:T(8,128)(2,1)S(1)}, u32[]{:S(2)}, u32[]{:S(2)}) collective-permute-start(bf16[4,272,256]{2,1,0:T(8,128)(2,1)S(1)} %get-tuple-element.60.kvo.fo), channel_id=1, source_target_pairs={{0,8},{2,10},{4,12},{6,14},{8,16},{10,18},{12,20},{14,22},{16,24},... | collective-permute-start | bytes 1671176 | tf_op jit(solution)/shard_map/ppermute | solution.py:318
  24.8 1.3 %collective-permute-start.9 = (bf16[4,256,256]{2,1,0:T(8,128)(2,1)S(1)}, bf16[4,256,256]{2,1,0:T(8,128)(2,1)S(1)}, u32[]{:S(2)}, u32[]{:S(2)}) collective-permute-start(bf16[4,256,256]{2,1,0:T(8,128)(2,1)S(1)} %get-tuple-element.61.qd), channel_id=1, source_target_pairs={{8,0},{10,2},{12,4},{14,6},{16,8},{18,10},{20,12},{22,14},{24,16},... | collective-permute-start | bytes 1572872 | tf_op jit(solution)/shard_map/ppermute | solution.py:318
  26.1 0.0 collective-permute-done.refs_1_
  26.2 5.1 %collective-permute-done.1.refs_2_ = bf16[512,256]{1,0:T(8,128)(2,1)S(1)} collective-permute-done((bf16[512,256]{1,0:T(8,128)(2,1)S(1)}, bf16[512,256]{1,0:T(8,128)(2,1)S(1)}, u32[]{:S(2)}, u32[]{:S(2)}) %collective-permute-start.1) | collective-permute-done | bytes 262176 | tf_op jit(solution)/shard_map/ppermute | solution.py:312
  31.3 0.0 collective-permute-done.2.refs_3_
  31.3 0.1 gather.2
  31.4 0.0 copy-start
  31.4 3.5 %collective-permute-start.7 = (bf16[4,256,256]{2,1,0:T(8,128)(2,1)S(1)}, bf16[4,256,256]{2,1,0:T(8,128)(2,1)S(1)}, u32[]{:S(2)}, u32[]{:S(2)}) collective-permute-start(bf16[4,256,256]{2,1,0:T(8,128)(2,1)S(1)} %get-tuple-element.54.kvo), channel_id=1, source_target_pairs={{0,8},{2,10},{4,12},{6,14},{8,16},{10,18},{12,20},{14,22},{16,24},... | collective-permute-start | bytes 1572872 | tf_op jit(solution)/shard_map/ppermute | solution.py:318
  34.9 1.3 %collective-permute-start.3 = (bf16[4,256,256]{2,1,0:T(8,128)(2,1)S(1)}, bf16[4,256,256]{2,1,0:T(8,128)(2,1)S(1)}, u32[]{:S(2)}, u32[]{:S(2)}) collective-permute-start(bf16[4,256,256]{2,1,0:T(8,128)(2,1)S(1)} %get-tuple-element.53.qd), channel_id=1, source_target_pairs={{8,0},{10,2},{12,4},{14,6},{16,8},{18,10},{20,12},{22,14},{24,16},... | collective-permute-start | bytes 1572872 | tf_op jit(solution)/shard_map/ppermute | solution.py:318
  36.2 1.6 %collective-permute-done.9.qd = bf16[4,256,256]{2,1,0:T(8,128)(2,1)S(1)} collective-permute-done((bf16[4,256,256]{2,1,0:T(8,128)(2,1)S(1)}, bf16[4,256,256]{2,1,0:T(8,128)(2,1)S(1)}, u32[]{:S(2)}, u32[]{:S(2)}) %collective-permute-start.9) | collective-permute-done | bytes 524320 | tf_op jit(solution)/shard_map/ppermute | solution.py:318
  37.9 0.0 collective-permute-done.8.kvp.fp
  37.9 0.0 copy-done
  37.9 5.5 %rows.2 = (bf16[4,128,256]{2,1,0:T(8,128)(2,1)S(1)}, f32[512,256]{1,0:T(8,128)S(1)}, f32[512,256]{1,0:T(8,128)S(1)}, f32[2,2,512]{2,1,0:T(2,128)S(1)}, f32[8,128]{1,0:T(8,128)S(1)}) custom-call(s32[3]{0:T(128)S(1)} %pad_add_fusion.meta, bf16[4,256,256]{2,1,0:T(8,128)(2,1)S(1)} %get-tuple-element.61.qd, bf16[4,272,256]{2,1,0:T(8,128)(2,1)S(1)} %get-tuple-element.60.kvo.fo, ...), custom_call_target="tpu_custom_call" | custom-call | flops 2000000000 | bytes 2097152 | tf_op jit(solution)/shard_map/rows/pallas_call | solution.py:357
  43.4 1.3 %collective-permute-start.17 = (f32[2,2,512]{2,1,0:T(2,128)S(1)}, f32[2,2,512]{2,1,0:T(2,128)S(1)}, u32[]{:S(2)}, u32[]{:S(2)}) collective-permute-start(f32[2,2,512]{2,1,0:T(2,128)S(1)} %get-tuple-element.74), channel_id=1, source_target_pairs={{8,0},{10,2},{12,4},{14,6},{16,8},{18,10},{20,12},{22,14},{24,16},... | collective-permute-start | bytes 24584 | tf_op jit(solution)/shard_map/ppermute | solution.py:318
  44.7 1.0 %collective-permute-done.7.kvp = bf16[4,256,256]{2,1,0:T(8,128)(2,1)S(1)} collective-permute-done((bf16[4,256,256]{2,1,0:T(8,128)(2,1)S(1)}, bf16[4,256,256]{2,1,0:T(8,128)(2,1)S(1)}, u32[]{:S(2)}, u32[]{:S(2)}) %collective-permute-start.7) | collective-permute-done | bytes 524320 | tf_op jit(solution)/shard_map/ppermute | solution.py:318
  45.6 5.5 %rows.3 = (bf16[4,128,256]{2,1,0:T(8,128)(2,1)S(1)}, f32[512,256]{1,0:T(8,128)S(1)}, f32[512,256]{1,0:T(8,128)S(1)}, f32[2,2,512]{2,1,0:T(2,128)S(1)}, f32[8,128]{1,0:T(8,128)S(1)}) custom-call(s32[3]{0:T(128)S(1)} %pad_add_fusion.meta, bf16[4,256,256]{2,1,0:T(8,128)(2,1)S(1)} %get-tuple-element.53.qd, bf16[4,256,256]{2,1,0:T(8,128)(2,1)S(1)} %get-tuple-element.54.kvo, ...), custom_call_target="tpu_custom_call" | custom-call | flops 2000000000 | bytes 2097152 | tf_op jit(solution)/shard_map/rows/pallas_call | solution.py:357
  51.1 2.5 %collective-permute-start.11 = (f32[8,128]{1,0:T(8,128)S(1)}, f32[8,128]{1,0:T(8,128)S(1)}, u32[]{:S(2)}, u32[]{:S(2)}) collective-permute-start(f32[8,128]{1,0:T(8,128)S(1)} %get-tuple-element.68.a), channel_id=1, source_target_pairs={{0,8},{2,10},{4,12},{6,14},{8,0},{10,2},{12,4},{14,6},{16,24},{18,... | collective-permute-start | bytes 12296 | tf_op jit(solution)/shard_map/ppermute | solution.py:312
  53.7 0.0 collective-permute-done.3.qd
  53.7 1.3 %collective-permute-start.10 = (f32[2,2,512]{2,1,0:T(2,128)S(1)}, f32[2,2,512]{2,1,0:T(2,128)S(1)}, u32[]{:S(2)}, u32[]{:S(2)}) collective-permute-start(f32[2,2,512]{2,1,0:T(2,128)S(1)} %get-tuple-element.65), channel_id=1, source_target_pairs={{8,0},{10,2},{12,4},{14,6},{16,8},{18,10},{20,12},{22,14},{24,16},... | collective-permute-start | bytes 24584 | tf_op jit(solution)/shard_map/ppermute | solution.py:318
  55.0 0.3 collective-permute-done.11.b
  55.3 0.0 collective-permute-done.17.stats
  55.3 2.4 %columns.3 = (bf16[512,256]{1,0:T(8,128)(2,1)S(1)}, bf16[512,256]{1,0:T(8,128)(2,1)S(1)}, bf16[512,256]{1,0:T(8,128)(2,1)S(1)}, bf16[512,256]{1,0:T(8,128)(2,1)S(1)}) custom-call(s32[3]{0:T(128)S(1)} %pad_add_fusion.meta, bf16[4,256,256]{2,1,0:T(8,128)(2,1)S(1)} %collective-permute-done.9.qd, bf16[4,272,256]{2,1,0:T(8,128)(2,1)S(1)} %get-tuple-element.60.kvo.fo, ...), custom_call_target="tpu_custom_call" | custom-call | flops 4000000000 | bytes 2097152 | tf_op jit(solution)/shard_map/columns/pallas_call | solution.py:357
  57.7 1.5 %collective-permute-done.10.stats = f32[2,2,512]{2,1,0:T(2,128)S(1)} collective-permute-done((f32[2,2,512]{2,1,0:T(2,128)S(1)}, f32[2,2,512]{2,1,0:T(2,128)S(1)}, u32[]{:S(2)}, u32[]{:S(2)}) %collective-permute-start.10) | collective-permute-done | bytes 8224 | tf_op jit(solution)/shard_map/ppermute | solution.py:318
  59.2 1.4 %collective-permute-start.20 = (bf16[512,256]{1,0:T(8,128)(2,1)S(1)}, bf16[512,256]{1,0:T(8,128)(2,1)S(1)}, u32[]{:S(2)}, u32[]{:S(2)}) collective-permute-start(bf16[512,256]{1,0:T(8,128)(2,1)S(1)} %get-tuple-element.90), channel_id=1, source_target_pairs={{0,6},{2,4},{4,2},{6,0},{8,14},{10,12},{12,10},{14,8},{16,22},{18,... | collective-permute-start | bytes 786440 | tf_op jit(solution)/shard_map/ppermute | solution.py:312
  60.7 1.5 %collective-permute-start.19 = (bf16[512,256]{1,0:T(8,128)(2,1)S(1)}, bf16[512,256]{1,0:T(8,128)(2,1)S(1)}, u32[]{:S(2)}, u32[]{:S(2)}) collective-permute-start(bf16[512,256]{1,0:T(8,128)(2,1)S(1)} %get-tuple-element.87), channel_id=1, source_target_pairs={{0,4},{2,6},{4,0},{6,2},{8,12},{10,14},{12,8},{14,10},{16,20},{18,... | collective-permute-start | bytes 786440 | tf_op jit(solution)/shard_map/ppermute | solution.py:312
  62.2 0.5 collective-permute-start.18
  62.7 2.6 %collective-permute-start.12 = (f32[8,128]{1,0:T(8,128)S(1)}, f32[8,128]{1,0:T(8,128)S(1)}, u32[]{:S(2)}, u32[]{:S(2)}) collective-permute-start(f32[8,128]{1,0:T(8,128)S(1)} %add.7.a), channel_id=1, source_target_pairs={{0,16},{2,18},{4,20},{6,22},{8,24},{10,26},{12,28},{14,30},{16,0},... | collective-permute-start | bytes 12296 | tf_op jit(solution)/shard_map/ppermute | solution.py:312
  65.3 1.9 %collective-permute-done.12.b = f32[8,128]{1,0:T(8,128)S(1)} collective-permute-done((f32[8,128]{1,0:T(8,128)S(1)}, f32[8,128]{1,0:T(8,128)S(1)}, u32[]{:S(2)}, u32[]{:S(2)}) %collective-permute-start.12) | collective-permute-done | bytes 4128 | tf_op jit(solution)/shard_map/ppermute | solution.py:312
  67.2 0.0 collective-permute-start.13
  67.2 1.2 %collective-permute-done.13.b = f32[8,128]{1,0:T(8,128)S(1)} collective-permute-done((f32[8,128]{1,0:T(8,128)S(1)}, f32[8,128]{1,0:T(8,128)S(1)}, u32[]{:S(2)}, u32[]{:S(2)}) %collective-permute-start.13) | collective-permute-done | bytes 4128 | tf_op jit(solution)/shard_map/ppermute | solution.py:312
  68.4 2.4 %columns.2 = (bf16[272,256]{1,0:T(8,128)(2,1)S(1)}, bf16[272,256]{1,0:T(8,128)(2,1)S(1)}, bf16[272,256]{1,0:T(8,128)(2,1)S(1)}, bf16[272,256]{1,0:T(8,128)(2,1)S(1)}) custom-call(s32[3]{0:T(128)S(1)} %pad_add_fusion.meta, bf16[4,256,256]{2,1,0:T(8,128)(2,1)S(1)} %collective-permute-done.3.qd, bf16[4,256,256]{2,1,0:T(8,128)(2,1)S(1)} %get-tuple-element.54.kvo, ...), custom_call_target="tpu_custom_call" | custom-call | bytes 2097152 | tf_op jit(solution)/shard_map/columns/pallas_call | solution.py:357
  70.8 1.6 %collective-permute-start.14 = (bf16[272,256]{1,0:T(8,128)(2,1)S(1)}, bf16[272,256]{1,0:T(8,128)(2,1)S(1)}, u32[]{:S(2)}, u32[]{:S(2)}) collective-permute-start(bf16[272,256]{1,0:T(8,128)(2,1)S(1)} %get-tuple-element.70), channel_id=1, source_target_pairs={{0,2},{2,0},{4,6},{6,4},{8,10},{10,8},{12,14},{14,12},{16,18},{18,... | collective-permute-start | bytes 417800 | tf_op jit(solution)/shard_map/ppermute | solution.py:312
  72.4 0.5 collective-permute-start.15
  72.9 0.0 collective-permute-done.20.rest_3_
  72.9 1.5 %collective-permute-start.16 = (bf16[272,256]{1,0:T(8,128)(2,1)S(1)}, bf16[272,256]{1,0:T(8,128)(2,1)S(1)}, u32[]{:S(2)}, u32[]{:S(2)}) collective-permute-start(bf16[272,256]{1,0:T(8,128)(2,1)S(1)} %get-tuple-element.72), channel_id=1, source_target_pairs={{0,6},{2,4},{4,2},{6,0},{8,14},{10,12},{12,10},{14,8},{16,22},{18,... | collective-permute-start | bytes 417800 | tf_op jit(solution)/shard_map/ppermute | solution.py:312
  74.4 0.0 collective-permute-done.19.rest_2_
  74.4 0.0 collective-permute-done.18.rest_1_
  74.4 1.6 %unpack.2 = (bf16[1,128,2048]{2,1,0:T(8,128)(2,1)}, bf16[1,128,2048]{2,1,0:T(8,128)(2,1)}, bf16[1,128,2048]{2,1,0:T(8,128)(2,1)}) custom-call(s32[3]{0:T(128)S(1)} %pad_add_fusion.meta, bf16[512,256]{1,0:T(8,128)(2,1)S(1)} %get-tuple-element.81.rest_0_, bf16[512,256]{1,0:T(8,128)(2,1)S(1)} %collective-permute-done.18.rest_1_, ...), custom_call_target="tpu_custom_call" | custom-call | bytes 2097152 | tf_op jit(solution)/shard_map/unpack/pallas_call | solution.py:446
  76.0 1.1 %collective-permute-done.14.rest_1_ = bf16[272,256]{1,0:T(8,128)(2,1)S(1)} collective-permute-done((bf16[272,256]{1,0:T(8,128)(2,1)S(1)}, bf16[272,256]{1,0:T(8,128)(2,1)S(1)}, u32[]{:S(2)}, u32[]{:S(2)}) %collective-permute-start.14) | collective-permute-done | bytes 139296 | tf_op jit(solution)/shard_map/ppermute | solution.py:312
  77.2 3.7 %collective-permute-done.15.rest_2_ = bf16[272,256]{1,0:T(8,128)(2,1)S(1)} collective-permute-done((bf16[272,256]{1,0:T(8,128)(2,1)S(1)}, bf16[272,256]{1,0:T(8,128)(2,1)S(1)}, u32[]{:S(2)}, u32[]{:S(2)}) %collective-permute-start.15) | collective-permute-done | bytes 139296 | tf_op jit(solution)/shard_map/ppermute | solution.py:312
  80.8 0.0 collective-permute-done.16.rest_3_
  80.8 2.0 %unpack.3 = (bf16[1,128,2048]{2,1,0:T(8,128)(2,1)}, bf16[1,128,2048]{2,1,0:T(8,128)(2,1)}, bf16[1,128,2048]{2,1,0:T(8,128)(2,1)}, f32[16,64]{1,0:T(8,128)}) custom-call(s32[3]{0:T(128)S(1)} %pad_add_fusion.meta, bf16[272,256]{1,0:T(8,128)(2,1)S(1)} %get-tuple-element.69.rest_0_, ...), custom_call_target="tpu_custom_call", output_to_operand_aliasing={{0}: (5, {}), {1}: (6, {}), {2}: (7, {})} | custom-call | bytes 2097152 | tf_op jit(solution)/shard_map/unpack/pallas_call | solution.py:446
  (4 shorter events, 0.0 us)
Async XLA Ops:
  3.3 10.3 %collective-permute-start.4 = (bf16[528,256]{1,0:T(8,128)(2,1)S(1)}, bf16[528,256]{1,0:T(8,128)(2,1)S(1)}, u32[]{:S(2)}, u32[]{:S(2)}) collective-permute-start(bf16[528,256]{1,0:T(8,128)(2,1)S(1)} %get-tuple-element.57), channel_id=1, source_target_pairs={{0,2},{2,0},{4,6},{6,4},{8,10},{10,8},{12,14},{14,12},{16,18},{18,... | collective-permute-start | bytes 811016 | tf_op jit(solution)/shard_map/ppermute | solution.py:312
  6.3 14.9 %collective-permute-start.5 = (bf16[528,256]{1,0:T(8,128)(2,1)S(1)}, bf16[528,256]{1,0:T(8,128)(2,1)S(1)}, u32[]{:S(2)}, u32[]{:S(2)}) collective-permute-start(bf16[528,256]{1,0:T(8,128)(2,1)S(1)} %get-tuple-element.58), channel_id=1, source_target_pairs={{0,4},{2,6},{4,0},{6,2},{8,12},{10,14},{12,8},{14,10},{16,20},{18,... | collective-permute-start | bytes 811016 | tf_op jit(solution)/shard_map/ppermute | solution.py:312
  7.8 13.4 %collective-permute-start.6 = (bf16[528,256]{1,0:T(8,128)(2,1)S(1)}, bf16[528,256]{1,0:T(8,128)(2,1)S(1)}, u32[]{:S(2)}, u32[]{:S(2)}) collective-permute-start(bf16[528,256]{1,0:T(8,128)(2,1)S(1)} %get-tuple-element.59), channel_id=1, source_target_pairs={{0,6},{2,4},{4,2},{6,0},{8,14},{10,12},{12,10},{14,8},{16,22},{18,... | collective-permute-start | bytes 811016 | tf_op jit(solution)/shard_map/ppermute | solution.py:312
  9.8 16.3 %collective-permute-start = (bf16[512,256]{1,0:T(8,128)(2,1)S(1)}, bf16[512,256]{1,0:T(8,128)(2,1)S(1)}, u32[]{:S(2)}, u32[]{:S(2)}) collective-permute-start(bf16[512,256]{1,0:T(8,128)(2,1)S(1)} %get-tuple-element.50), channel_id=1, source_target_pairs={{0,2},{2,0},{4,6},{6,4},{8,10},{10,8},{12,14},{14,12},{16,18},{18,... | collective-permute-start | bytes 786440 | tf_op jit(solution)/shard_map/ppermute | solution.py:312
  11.8 19.5 %collective-permute-start.1 = (bf16[512,256]{1,0:T(8,128)(2,1)S(1)}, bf16[512,256]{1,0:T(8,128)(2,1)S(1)}, u32[]{:S(2)}, u32[]{:S(2)}) collective-permute-start(bf16[512,256]{1,0:T(8,128)(2,1)S(1)} %get-tuple-element.51), channel_id=1, source_target_pairs={{0,4},{2,6},{4,0},{6,2},{8,12},{10,14},{12,8},{14,10},{16,20},{18,... | collective-permute-start | bytes 786440 | tf_op jit(solution)/shard_map/ppermute | solution.py:312
  13.6 17.7 %collective-permute-start.2 = (bf16[512,256]{1,0:T(8,128)(2,1)S(1)}, bf16[512,256]{1,0:T(8,128)(2,1)S(1)}, u32[]{:S(2)}, u32[]{:S(2)}) collective-permute-start(bf16[512,256]{1,0:T(8,128)(2,1)S(1)} %get-tuple-element.52), channel_id=1, source_target_pairs={{0,6},{2,4},{4,2},{6,0},{8,14},{10,12},{12,10},{14,8},{16,22},{18,... | collective-permute-start | bytes 786440 | tf_op jit(solution)/shard_map/ppermute | solution.py:312
  21.3 16.5 %collective-permute-start.8 = (bf16[4,272,256]{2,1,0:T(8,128)(2,1)S(1)}, bf16[4,272,256]{2,1,0:T(8,128)(2,1)S(1)}, u32[]{:S(2)}, u32[]{:S(2)}) collective-permute-start(bf16[4,272,256]{2,1,0:T(8,128)(2,1)S(1)} %get-tuple-element.60.kvo.fo), channel_id=1, source_target_pairs={{0,8},{2,10},{4,12},{6,14},{8,16},{10,18},{12,20},{14,22},{16,24},... | collective-permute-start | bytes 1671176 | tf_op jit(solution)/shard_map/ppermute | solution.py:318
  24.8 13.0 %collective-permute-start.9 = (bf16[4,256,256]{2,1,0:T(8,128)(2,1)S(1)}, bf16[4,256,256]{2,1,0:T(8,128)(2,1)S(1)}, u32[]{:S(2)}, u32[]{:S(2)}) collective-permute-start(bf16[4,256,256]{2,1,0:T(8,128)(2,1)S(1)} %get-tuple-element.61.qd), channel_id=1, source_target_pairs={{8,0},{10,2},{12,4},{14,6},{16,8},{18,10},{20,12},{22,14},{24,16},... | collective-permute-start | bytes 1572872 | tf_op jit(solution)/shard_map/ppermute | solution.py:318
  31.4 6.5 %copy-start = (bf16[16,64]{1,0:T(8,128)(2,1)S(1)}, bf16[16,64]{1,0:T(8,128)(2,1)}, u32[]{:S(2)}) copy-start(bf16[16,64]{1,0:T(8,128)(2,1)} %bias_ref.7) | copy-start | bytes 6148
  31.4 14.3 %collective-permute-start.7 = (bf16[4,256,256]{2,1,0:T(8,128)(2,1)S(1)}, bf16[4,256,256]{2,1,0:T(8,128)(2,1)S(1)}, u32[]{:S(2)}, u32[]{:S(2)}) collective-permute-start(bf16[4,256,256]{2,1,0:T(8,128)(2,1)S(1)} %get-tuple-element.54.kvo), channel_id=1, source_target_pairs={{0,8},{2,10},{4,12},{6,14},{8,16},{10,18},{12,20},{14,22},{16,24},... | collective-permute-start | bytes 1572872 | tf_op jit(solution)/shard_map/ppermute | solution.py:318
  34.9 18.8 %collective-permute-start.3 = (bf16[4,256,256]{2,1,0:T(8,128)(2,1)S(1)}, bf16[4,256,256]{2,1,0:T(8,128)(2,1)S(1)}, u32[]{:S(2)}, u32[]{:S(2)}) collective-permute-start(bf16[4,256,256]{2,1,0:T(8,128)(2,1)S(1)} %get-tuple-element.53.qd), channel_id=1, source_target_pairs={{8,0},{10,2},{12,4},{14,6},{16,8},{18,10},{20,12},{22,14},{24,16},... | collective-permute-start | bytes 1572872 | tf_op jit(solution)/shard_map/ppermute | solution.py:318
  43.4 11.9 %collective-permute-start.17 = (f32[2,2,512]{2,1,0:T(2,128)S(1)}, f32[2,2,512]{2,1,0:T(2,128)S(1)}, u32[]{:S(2)}, u32[]{:S(2)}) collective-permute-start(f32[2,2,512]{2,1,0:T(2,128)S(1)} %get-tuple-element.74), channel_id=1, source_target_pairs={{8,0},{10,2},{12,4},{14,6},{16,8},{18,10},{20,12},{22,14},{24,16},... | collective-permute-start | bytes 24584 | tf_op jit(solution)/shard_map/ppermute | solution.py:318
  51.1 4.1 %collective-permute-start.11 = (f32[8,128]{1,0:T(8,128)S(1)}, f32[8,128]{1,0:T(8,128)S(1)}, u32[]{:S(2)}, u32[]{:S(2)}) collective-permute-start(f32[8,128]{1,0:T(8,128)S(1)} %get-tuple-element.68.a), channel_id=1, source_target_pairs={{0,8},{2,10},{4,12},{6,14},{8,0},{10,2},{12,4},{14,6},{16,24},{18,... | collective-permute-start | bytes 12296 | tf_op jit(solution)/shard_map/ppermute | solution.py:312
  53.7 5.5 %collective-permute-start.10 = (f32[2,2,512]{2,1,0:T(2,128)S(1)}, f32[2,2,512]{2,1,0:T(2,128)S(1)}, u32[]{:S(2)}, u32[]{:S(2)}) collective-permute-start(f32[2,2,512]{2,1,0:T(2,128)S(1)} %get-tuple-element.65), channel_id=1, source_target_pairs={{8,0},{10,2},{12,4},{14,6},{16,8},{18,10},{20,12},{22,14},{24,16},... | collective-permute-start | bytes 24584 | tf_op jit(solution)/shard_map/ppermute | solution.py:318
  59.2 13.7 %collective-permute-start.20 = (bf16[512,256]{1,0:T(8,128)(2,1)S(1)}, bf16[512,256]{1,0:T(8,128)(2,1)S(1)}, u32[]{:S(2)}, u32[]{:S(2)}) collective-permute-start(bf16[512,256]{1,0:T(8,128)(2,1)S(1)} %get-tuple-element.90), channel_id=1, source_target_pairs={{0,6},{2,4},{4,2},{6,0},{8,14},{10,12},{12,10},{14,8},{16,22},{18,... | collective-permute-start | bytes 786440 | tf_op jit(solution)/shard_map/ppermute | solution.py:312
  60.7 13.7 %collective-permute-start.19 = (bf16[512,256]{1,0:T(8,128)(2,1)S(1)}, bf16[512,256]{1,0:T(8,128)(2,1)S(1)}, u32[]{:S(2)}, u32[]{:S(2)}) collective-permute-start(bf16[512,256]{1,0:T(8,128)(2,1)S(1)} %get-tuple-element.87), channel_id=1, source_target_pairs={{0,4},{2,6},{4,0},{6,2},{8,12},{10,14},{12,8},{14,10},{16,20},{18,... | collective-permute-start | bytes 786440 | tf_op jit(solution)/shard_map/ppermute | solution.py:312
  62.2 12.2 %collective-permute-start.18 = (bf16[512,256]{1,0:T(8,128)(2,1)S(1)}, bf16[512,256]{1,0:T(8,128)(2,1)S(1)}, u32[]{:S(2)}, u32[]{:S(2)}) collective-permute-start(bf16[512,256]{1,0:T(8,128)(2,1)S(1)} %get-tuple-element.84), channel_id=1, source_target_pairs={{0,2},{2,0},{4,6},{6,4},{8,10},{10,8},{12,14},{14,12},{16,18},{18,... | collective-permute-start | bytes 786440 | tf_op jit(solution)/shard_map/ppermute | solution.py:312
  62.7 4.5 %collective-permute-start.12 = (f32[8,128]{1,0:T(8,128)S(1)}, f32[8,128]{1,0:T(8,128)S(1)}, u32[]{:S(2)}, u32[]{:S(2)}) collective-permute-start(f32[8,128]{1,0:T(8,128)S(1)} %add.7.a), channel_id=1, source_target_pairs={{0,16},{2,18},{4,20},{6,22},{8,24},{10,26},{12,28},{14,30},{16,0},... | collective-permute-start | bytes 12296 | tf_op jit(solution)/shard_map/ppermute | solution.py:312
  67.2 1.2 %collective-permute-start.13 = (f32[8,128]{1,0:T(8,128)S(1)}, f32[8,128]{1,0:T(8,128)S(1)}, u32[]{:S(2)}, u32[]{:S(2)}) collective-permute-start(f32[8,128]{1,0:T(8,128)S(1)} %add.8.a), channel_id=1, source_target_pairs={{0,1},{1,0},{2,3},{3,2},{4,5},{5,4},{6,7},{7,6},{8,9},{9,8},{10,11... | collective-permute-start | bytes 12296 | tf_op jit(solution)/shard_map/ppermute | solution.py:312
  70.8 6.3 %collective-permute-start.14 = (bf16[272,256]{1,0:T(8,128)(2,1)S(1)}, bf16[272,256]{1,0:T(8,128)(2,1)S(1)}, u32[]{:S(2)}, u32[]{:S(2)}) collective-permute-start(bf16[272,256]{1,0:T(8,128)(2,1)S(1)} %get-tuple-element.70), channel_id=1, source_target_pairs={{0,2},{2,0},{4,6},{6,4},{8,10},{10,8},{12,14},{14,12},{16,18},{18,... | collective-permute-start | bytes 417800 | tf_op jit(solution)/shard_map/ppermute | solution.py:312
  72.4 8.4 %collective-permute-start.15 = (bf16[272,256]{1,0:T(8,128)(2,1)S(1)}, bf16[272,256]{1,0:T(8,128)(2,1)S(1)}, u32[]{:S(2)}, u32[]{:S(2)}) collective-permute-start(bf16[272,256]{1,0:T(8,128)(2,1)S(1)} %get-tuple-element.71), channel_id=1, source_target_pairs={{0,4},{2,6},{4,0},{6,2},{8,12},{10,14},{12,8},{14,10},{16,20},{18,... | collective-permute-start | bytes 417800 | tf_op jit(solution)/shard_map/ppermute | solution.py:312
  72.9 7.9 %collective-permute-start.16 = (bf16[272,256]{1,0:T(8,128)(2,1)S(1)}, bf16[272,256]{1,0:T(8,128)(2,1)S(1)}, u32[]{:S(2)}, u32[]{:S(2)}) collective-permute-start(bf16[272,256]{1,0:T(8,128)(2,1)S(1)} %get-tuple-element.72), channel_id=1, source_target_pairs={{0,6},{2,4},{4,2},{6,0},{8,14},{10,12},{12,10},{14,8},{16,22},{18,... | collective-permute-start | bytes 417800 | tf_op jit(solution)/shard_map/ppermute | solution.py:312

commit v4 on v3

--- a/solution.py
+++ b/solution.py
@@ -19,9 +19,8 @@
 MIB = 1 << 20
 BF16, F32 = jnp.bfloat16, jnp.float32
 ANY = pl.BlockSpec(memory_space=pl.ANY)
-SMEM = pl.BlockSpec(memory_space=pltpu.SMEM)
 VMEM = pl.BlockSpec(memory_space=pltpu.VMEM)
-GATHER_FLOPS, ROWS_FLOPS, COLUMNS_FLOPS, UNPACK_FLOPS = 2 * 10**9, 2 * 10**9, (4 * 10**9, 0), 0
+GATHER_FLOPS, ROWS_FLOPS, COLUMNS_FLOPS, PAIR_FLOPS = 2 * 10**9, 2 * 10**9, (4 * 10**9, 0), 8 * 10**9
 NT = (((1,), (1,)), ((), ()))
 
 
@@ -33,9 +32,14 @@
     return lax.dot_general(a, b, NT, preferred_element_type=F32)
 
 
-def pack_kernel(reach, tok, width, chunk, meta, q, g, k, v, fields, *rest):
+def place(reach):
+    index = lax.axis_index("seq")
+    return lax.rem(index, reach), lax.div(index, reach)
+
+
+def pack_kernel(reach, tok, width, chunk, q, g, k, v, fields, *rest):
     outs, field_scr, sems = rest[:reach], rest[-2], rest[-1]
-    p = meta[0]
+    p, _ = place(reach)
     field_copy = pltpu.make_async_copy(fields, field_scr, sems.at[4 * reach])
     field_copy.start()
     copies = []
@@ -61,9 +65,9 @@
         kv[m] = arrived[m][2 * tok :]
 
 
-def unpack_kernel(reach, tok, group_width, blocks, meta, *rest):
+def unpack_kernel(reach, tok, group_width, blocks, *rest):
     parts, outs, sems = rest[:reach], rest[-4:-1], rest[-1]
-    p = meta[0]
+    p, _ = place(reach)
     width = parts[0].shape[1]
     copies = []
     for m in range(reach):
@@ -76,28 +80,25 @@
         copy.wait()
 
 
-def finish_kernel(reach, tok, group_width, blocks, meta, *rest):
+def finish_kernel(reach, tok, group_width, blocks, *rest):
     total, sems = rest[-2:]
-    join(reach, tok, len(blocks) * tok, meta[0], rest[:reach], total)
-    unpack_kernel(reach, tok, group_width, blocks, meta, *rest[:-2], sems)
-
-
-def key_columns(fields, slot, tok):
+    join(reach, tok, len(blocks) * tok, place(reach)[0], rest[:reach], total)
+    unpack_kernel(reach, tok, group_width, blocks, *rest[:-2], sems)
+
+
+def onehot_of(fields, slot, tok):
     row = fields[slot, 2 * tok : 2 * tok + PAD, 0:tok].astype(F32)[0:1]
-    spread = jnp.broadcast_to(row, (tok, tok))
-    lane = lax.broadcasted_iota(jnp.int32, (tok, tok), 1).astype(F32)
-    sub = lax.broadcasted_iota(jnp.int32, (tok, tok), 0).astype(F32)
-    onehot = jnp.where(spread.T == lane, 1.0, 0.0).astype(BF16)
-    onehot_t = jnp.where(spread == sub, 1.0, 0.0).astype(BF16)
-    return onehot, onehot_t
-
-
-def head_bias(bias_ref, head, tok):
+    lane = lax.broadcasted_iota(jnp.int32, (tok, tok), 1)
+    lane = jnp.where(lane < FIELDS, lane, lane - FIELDS).astype(F32)
+    return jnp.where(jnp.broadcast_to(row, (tok, tok)).T == lane, 1.0, 0.0).astype(BF16)
+
+
+def bias_rows(bias_ref, head, tok):
     table = bias_ref[...].astype(F32)
     at = lax.broadcasted_iota(jnp.int32, table.shape, 0)
-    row = jnp.sum(jnp.where(at == head, table, 0.0), axis=0, keepdims=True)
-    row = jnp.concatenate([row, jnp.zeros((1, tok - FIELDS), F32)], axis=1)
-    return jnp.broadcast_to(row, (tok, tok)).T.astype(BF16)
+    row = jnp.sum(jnp.where(at == head, table, 0.0), axis=0, keepdims=True) * (1.0 / FACTOR)
+    high = row.astype(BF16).astype(F32)
+    return jnp.broadcast_to(jnp.concatenate([high, row - high], axis=1), (2 * tok, tok)).astype(BF16)
 
 
 def three_parts(x):
@@ -126,41 +127,40 @@
     return jnp.concatenate([first, jnp.concatenate([gap, second], axis=0)], axis=1)
 
 
-def rows_kernel(reach, tok, chunk, meta, qd, kvo, kvp, fo, fp, bias_ref, sums_in, *rest):
-    dq_out, dk_out, dv_out, stats_out, sums_out, *scratch = rest
-    k_scr, v_scr, kt_scr, oh_scr, oht_scr, bias_scr, acc_scr = scratch
-    p, plane, length = meta[0], meta[1], meta[2]
+def rows_kernel(reach, tok, chunk, lengths, qd, kvo, kvp, bias_ref, sums_in, *rest):
+    *onehots, dq_out, dk_out, dv_out, stats_out, sums_out, k_scr, v_scr, kt_scr, acc_scr = rest
+    onehots = onehots[0]
+    p, plane = place(reach)
+    length = lengths[...]
     span = reach * tok
 
     for blk in range(2 * reach):
         rows = slice(blk * tok, (blk + 1) * tok)
-        onehot, onehot_t = key_columns(fp if blk < reach else fo, p ^ (blk % reach), tok)
-        oh_scr[rows] = onehot
-        oht_scr[:, rows] = onehot_t
+        if chunk == 0:
+            onehots[rows] = onehot_of(kvp if blk < reach else kvo, p ^ (blk % reach), tok)
+        k_scr[rows, HEAD_DIM:] = onehots[rows]
     per = kvo.shape[2] // HEAD_DIM
     sums_out[...] = sums_in[...]
     shut = jnp.where(plane == 0, HIDDEN, 0.0).astype(F32)
     later, lane = masks(tok)
 
-    @pl.loop(0, kvo.shape[2] // HEAD_DIM)
+    @pl.loop(0, kvo.shape[2] // HEAD_DIM, unroll=True)
     def _(h):
         head = pl.ds(pl.multiple_of(h * HEAD_DIM, HEAD_DIM), HEAD_DIM)
         at = chunk * per + h
-        bias = head_bias(bias_ref, p * (HEADS // reach) + at, tok)
+        bias = bias_rows(bias_ref, p * (HEADS // reach) + at, tok)
         for blk in range(2 * reach):
             rows = slice(blk * tok, (blk + 1) * tok)
             src, slot = (kvp if blk < reach else kvo), p ^ (blk % reach)
             key = src[slot, 0:tok, head]
-            k_scr[rows] = key
+            k_scr[rows, :HEAD_DIM] = key
             kt_scr[:, rows] = key.T
             v_scr[rows] = src[slot, tok : 2 * tok, head]
-            col = dot(oh_scr[rows], bias) * LOG2E
-            bias_scr[rows] = col + shut if blk < reach else col
         acc_scr[...] = jnp.zeros_like(acc_scr)
         for pair in range(0, reach, 2):
             query, grad = query_pair(qd, p, pair, tok, head)
             wide = slice(pair * tok, (pair + reach + 2) * tok)
-            logits = dot_nt(k_scr[wide], query)
+            logits = dot_nt(k_scr[wide], jnp.concatenate([query, bias], axis=1))
             probs_both = dot_nt(v_scr[wide], grad)
             lows, ds_lows = [], []
             for half in range(2):
@@ -169,11 +169,10 @@
                 mine = slice(half * tok, (half + reach + 1) * tok)
                 there = slice(a * tok, (a + 1) * tok)
                 cols = slice(half * tok, (half + 1) * tok)
-                s = logits[mine, cols] * (FACTOR * LOG2E) + bias_scr[rows]
-                s = jnp.concatenate(
-                    [jnp.where(later, s[:tok], HIDDEN), s[tok:-tok], jnp.where(later, HIDDEN, s[-tok:])],
-                    axis=0,
-                )
+                s = logits[mine, cols] * (FACTOR * LOG2E)
+                seen = [jnp.where(later, s[:tok], HIDDEN) + shut, s[tok : (reach - a) * tok] + shut]
+                seen += [s[(reach - a) * tok : -tok], jnp.where(later, HIDDEN, s[-tok:])]
+                s = jnp.concatenate([part for part in seen if part.shape[0]], axis=0)
                 peak = jnp.max(s, axis=0, keepdims=True)
                 power = jnp.exp2(s - peak)
                 total = jnp.sum(power, axis=0, keepdims=True)
@@ -203,40 +202,64 @@
                 dk_out[0:done, head] += dk[:done]
             dv_out[done : done + 2 * tok, head] = dv[done:]
             dk_out[done : done + 2 * tok, head] = dk[done:]
-        by_field = sum(dot(oht_scr[...], part) for part in three_parts(acc_scr[...]))
-        row = jnp.sum(by_field.T, axis=0, keepdims=True)
+        by_key = jnp.sum(acc_scr[...], axis=1, keepdims=True)
+        row = jnp.sum(by_key * onehots[...].astype(F32), axis=0, keepdims=True)
         sums_out[...] += jnp.where(lax.broadcasted_iota(jnp.int32, (8, tok), 0) == at, row, 0.0)
 
-
-def columns_kernel(reach, tok, chunk, meta, qd, kvo, fo, stats, bias_ref, dk_in, dv_in, *rest):
-    k_scr, v_scr, oh_scr, bias_scr, dk_scr, dv_scr = rest[-6:]
-    outs, extras = rest[-6 - reach : -6], rest[: -6 - reach]
+    if stats_out.shape[0] > per:
+        for h in range(HEADS // reach):
+            stats_out[per, 0:1, h * tok : (h + 1) * tok] = sums_out[h : h + 1]
+            stats_out[per, 1:2, h * tok : (h + 1) * tok] = sums_out[h : h + 1]
+
+
+def pair_kernel(reach, tok, sums, stats, out):
+    out[0] = sums[...]
+    out[1] = jnp.zeros_like(sums)
+    for h in range(HEADS // reach):
+        out[1, h : h + 1] = stats[stats.shape[0] - 1, 0:1, h * tok : (h + 1) * tok]
+
+
+def planes_kernel(reach, tok, *refs):
+    _, plane = place(reach)
+    parts, out, blocks = refs[:-2], refs[-2], refs[-1]
+    count = blocks.shape[0]
+    at = 0
+    for part in parts:
+        blocks[at : at + part.shape[0]] = part[...]
+        at += part.shape[0]
+    out[...] = blocks[lax.rem(count - plane, count)]
+    for q in range(1, count):
+        out[...] += blocks[lax.rem(q + count - plane, count)]
+
+
+def columns_kernel(reach, tok, chunk, lengths, qd, kvo, onehots, stats, bias_ref, dk_in, dv_in, *rest):
+    k_scr, v_scr, dk_scr, dv_scr = rest[-4:]
+    outs, extras = rest[-4 - reach : -4], rest[: -4 - reach]
     last = len(extras) == 1
     if last:
         parts = [part.astype(F32) for part in three_parts(extras[0][...])]
         parts = [jnp.concatenate(parts[:2], axis=1), jnp.concatenate([parts[2], jnp.zeros_like(parts[2])], axis=1)]
         for m in range(reach):
             outs[m][2 * tok :] = jnp.concatenate(parts, axis=0).astype(BF16)
-    p, plane, length = meta[0], meta[1], meta[2]
+    p, plane = place(reach)
+    length = lengths[...]
     span = reach * tok
-    for blk in range(reach):
-        oh_scr[blk * tok : (blk + 1) * tok], _ = key_columns(fo, p ^ blk, tok)
+    k_scr[:, HEAD_DIM:] = onehots[span:]
     later, lane = masks(tok)
 
-    @pl.loop(0, kvo.shape[2] // HEAD_DIM)
+    @pl.loop(0, kvo.shape[2] // HEAD_DIM, unroll=True)
     def _(h):
         head = pl.ds(pl.multiple_of(h * HEAD_DIM, HEAD_DIM), HEAD_DIM)
         at = chunk * (kvo.shape[2] // HEAD_DIM) + h
-        bias = head_bias(bias_ref, p * (HEADS // reach) + at, tok)
+        bias = bias_rows(bias_ref, p * (HEADS // reach) + at, tok)
         for blk in range(reach):
             rows = slice(blk * tok, (blk + 1) * tok)
-            k_scr[rows] = kvo[p ^ blk, 0:tok, head]
+            k_scr[rows, :HEAD_DIM] = kvo[p ^ blk, 0:tok, head]
             v_scr[rows] = kvo[p ^ blk, tok : 2 * tok, head]
-            bias_scr[rows] = dot(oh_scr[rows], bias) * LOG2E
         for pair in range(0, reach, 2):
             query, grad = query_pair(qd, p, pair, tok, head)
             wide = slice(pair * tok, span)
-            logits = dot_nt(k_scr[wide], query)
+            logits = dot_nt(k_scr[wide], jnp.concatenate([query, bias], axis=1))
             probs_both = dot_nt(v_scr[wide], grad)
             lows, ds_lows = [], []
             for half in range(2):
@@ -246,7 +269,7 @@
                 live = (plane + 1) * span + a * tok + lane < length
                 norm = jnp.where(live, stats[h, 0:1, there], -HIDDEN)
                 delta = stats[h, 1:2, there]
-                s = logits[half * tok :, cols] * (FACTOR * LOG2E) + bias_scr[a * tok :]
+                s = logits[half * tok :, cols] * (FACTOR * LOG2E)
                 weight = jnp.exp2(s - norm)
                 first = jnp.where(later, weight[:tok], 0.0)
                 weight = jnp.concatenate([first, weight[tok:]], axis=0) if a < reach - 1 else first
@@ -268,6 +291,14 @@
                 outs[m][(2 + at) * tok : (3 + at) * tok, head] = dq[m, :, head]
 
 
+def stack_kernel(*refs):
+    parts, out = refs[:-1], refs[-1]
+    at = 0
+    for part in parts:
+        out[at : at + part.shape[0]] = part[...]
+        at += part.shape[0]
+
+
 def add_kernel(reach, tok, a, b, out):
     out[...] = a[...] + b[...]
 
@@ -312,6 +343,11 @@
     return lax.ppermute(value, axis, [(source, source ^ mask) for source in range(count)])
 
 
+def passed_round(value, axis, steps):
+    count = lax.axis_size(axis)
+    return lax.ppermute(value, axis, [(source, (source + steps) % count) for source in range(count)])
+
+
 def passed_along(value, axis, steps):
     count = lax.axis_size(axis)
     first, last = max(0, -steps), min(count, count - steps)
@@ -326,9 +362,7 @@
     per = group // CHUNKS
     width = per * HEAD_DIM
     span = reach * tok
-    index = lax.axis_index("seq")
-    p = lax.rem(index, reach)
-    meta = jnp.stack([p, lax.div(index, reach), lengths[0]]).astype(jnp.int32)
+    length = jnp.broadcast_to(lengths[:, None], (1, tok))
     raw = in_hbm(queries, grad_out, keys, values)
 
     def vmem(shape, dtype=BF16):
@@ -341,7 +375,7 @@
     def pack(chunk):
         return pl.pallas_call(
             functools.partial(pack_kernel, reach, tok, width, chunk),
-            in_specs=[SMEM] + [ANY] * 5,
+            in_specs=[ANY] * 5,
             out_specs=[VMEM] * reach,
             out_shape=[pltpu.VMEM((4 * tok + pad(chunk), width), BF16)] * reach,
             scratch_shapes=[
@@ -351,56 +385,54 @@
             compiler_params=params(2),
             cost_estimate=cost(0, 2 * MIB),
             name="pack",
-        )(meta, *raw, *in_hbm(fields))
+        )(*raw, *in_hbm(fields))
 
     def local(kernel, name, flops, out_shape, *args, scratch=()):
         return pl.pallas_call(
             kernel,
-            in_specs=[SMEM if arg is meta else VMEM for arg in args],
+            in_specs=[VMEM] * len(args),
             out_specs=[VMEM] * len(out_shape),
             out_shape=out_shape,
             scratch_shapes=scratch,
             compiler_params=params(12),
             cost_estimate=cost(flops, 2 * MIB),
             name=name,
-        )(*[arg if arg is meta else in_vmem(arg)[0] for arg in args])
+        )(*in_vmem(*args))
 
     def gather(chunk, arrived):
         out = [vmem((reach, 2 * tok, width)), vmem((reach, 2 * tok + pad(chunk), width))]
         return local(functools.partial(gather_kernel, reach, tok), "gather", GATHER_FLOPS if chunk else 0, out, *arrived)
 
-    def rows_of(chunk, qd, kvo, kvp, fo, fp, sums):
+    def rows_of(chunk, qd, kvo, kvp, sums, *onehots):
         out = [
             vmem((reach, tok, width)),
             vmem((span, width), F32),
             vmem((span, width), F32),
-            vmem((per, 2, span), F32),
+            vmem((per + chunk, 2, span), F32),
             vmem((8, tok), F32),
         ]
+        if chunk == 0:
+            out = [vmem((2 * span, tok))] + out
         scratch = [
-            pltpu.VMEM((2 * span, HEAD_DIM), BF16),
+            pltpu.VMEM((2 * span, 2 * HEAD_DIM), BF16),
             pltpu.VMEM((2 * span, HEAD_DIM), BF16),
             pltpu.VMEM((HEAD_DIM, 2 * span), BF16),
-            pltpu.VMEM((2 * span, tok), BF16),
-            pltpu.VMEM((tok, 2 * span), BF16),
-            pltpu.VMEM((2 * span, tok), F32),
             pltpu.VMEM((2 * span, tok), F32),
         ]
         kernel = functools.partial(rows_kernel, reach, tok, chunk)
-        return local(kernel, "rows", ROWS_FLOPS, out, meta, qd, kvo, kvp, fo, fp, field_bias, sums, scratch=scratch)
-
-    def columns_of(chunk, qd, kvo, fo, stats, dk, dv, *extras):
+        args = (length, qd, kvo, kvp, field_bias, sums, *onehots)
+        return local(kernel, "rows", ROWS_FLOPS, out, *args, scratch=scratch)
+
+    def columns_of(chunk, qd, kvo, onehots, stats, dk, dv, *extras):
         out = [vmem((2 * tok + (PAD if len(extras) == 1 else len(extras) * tok), width))] * reach
         scratch = [
+            pltpu.VMEM((span, 2 * HEAD_DIM), BF16),
             pltpu.VMEM((span, HEAD_DIM), BF16),
-            pltpu.VMEM((span, HEAD_DIM), BF16),
-            pltpu.VMEM((span, tok), BF16),
-            pltpu.VMEM((span, tok), F32),
             pltpu.VMEM((span, HEAD_DIM), F32),
             pltpu.VMEM((span, HEAD_DIM), F32),
         ]
         kernel = functools.partial(columns_kernel, reach, tok, chunk)
-        args = (meta, qd, kvo, fo, stats, field_bias, dk, dv, *extras)
+        args = (length, qd, kvo, onehots, stats, field_bias, dk, dv, *extras)
         return local(kernel, "columns", COLUMNS_FLOPS[chunk], out, *args, scratch=scratch)
 
     def add(a, b):
@@ -417,19 +449,28 @@
         before.append(following(moved[0], moved[1]) if c == 0 else moved[0])
         after.append(moved[1])
     sums = jnp.zeros((8, tok), F32)
-    pending, dqs = [], []
+    pending, dqs, onehots = [], [], []
     for c in range(CHUNKS):
-        dq, dk, dv, stats, sums = rows_of(c, *planes[c], before[c], planes[0][1], before[0], sums)
+        *made, dq, dk, dv, stats, sums = rows_of(c, *planes[c], before[c], sums, *onehots)
+        onehots = onehots or made
         dqs.append(dq)
-        pending.append((after[c], planes[c][1], planes[0][1], passed_along(following(stats, after[c]), "seq", -reach), dk, dv))
-    messages = [columns_of(0, *pending[0], *dqs)]
-    count = lax.axis_size("seq")
-    mask = reach
-    while mask < count:
-        sums = add(sums, swapped(sums, "seq", mask))
-        if mask == reach:
-            messages[0] = [following(following(own, sums), pending[1][3]) for own in messages[0]]
-        mask *= 2
+        stats = following(stats, after[c])
+        stats = passed_round(stats, "seq", -reach) if c else passed_along(stats, "seq", -reach)
+        pending.append((after[c], planes[c][1], *onehots, stats, dk, dv))
+    messages = [list(columns_of(0, *pending[0], *dqs))]
+    messages[0][1] = following(messages[0][1], stats)
+    blocks = [local(functools.partial(pair_kernel, reach, tok), "pair", PAIR_FLOPS, [vmem((2, 8, tok), F32)], sums, stats)[0]]
+    count = lax.axis_size("seq") // reach
+    step = 2
+    while step < count:
+        so_far = blocks[0]
+        if len(blocks) > 1:
+            so_far = local(stack_kernel, "stack", 0, [vmem((step, 8, tok), F32)], *blocks)[0]
+        blocks.append(passed_round(so_far, "seq", -step * reach))
+        step *= 2
+    kernel = functools.partial(planes_kernel, reach, tok)
+    scratch = [pltpu.VMEM((count, 8, tok), F32)]
+    sums = local(kernel, "planes", 0, [vmem((8, tok), F32)], *blocks, scratch=scratch)[0]
     mask = 1
     while mask < lax.axis_size("dp"):
         sums = add(sums, swapped(sums, "dp", mask))
@@ -445,15 +486,15 @@
         out = [jax.ShapeDtypeStruct((1, tok, row_width), BF16)] * 3
         grads = pl.pallas_call(
             functools.partial(kernel, reach, tok, group * HEAD_DIM, blocks[c]),
-            in_specs=[SMEM] + [VMEM] * reach + [ANY] * len(grads),
+            in_specs=[VMEM] * reach + [ANY] * len(grads),
             out_specs=[ANY] * 3 + [VMEM] * last,
             out_shape=out + [jax.ShapeDtypeStruct((HEADS, FIELDS), F32)] * last,
             scratch_shapes=[pltpu.SemaphoreType.DMA((len(blocks[c]) * reach,))],
-            input_output_aliases={1 + reach + at: at for at in range(len(grads))},
+            input_output_aliases={reach + at: at for at in range(len(grads))},
             compiler_params=params(2),
-            cost_estimate=cost(0 if last else UNPACK_FLOPS, 2 * MIB),
+            cost_estimate=cost(0, 2 * MIB),
             name="unpack",
-        )(meta, *in_vmem(*parts[c]), *grads)
+        )(*in_vmem(*parts[c]), *grads)
     return grads
 
 

time: 83.2 us -> 76.3 us (0.917)
  Pallas kernels: 23.6 us -> 15.1 us
  waiting for transfers between devices: 22.3 us -> 25.9 us
  starting transfers between devices: 35.5 us -> 33.5 us
    pallas_call x9, Pallas kernels: 16 us -> 9.73 us  [local(): pl.pallas_call(kernel, in_specs=[VMEM] * len(args), out_specs=[VMEM] * le...]
    ppermute x15 -> x13, starting transfers between devices: 23.3 us -> 18.2 us  [swapped(): lax.ppermute(value, axis, [(source, source ^ mask) for source in range(co...]
    ppermute x0 -> x2, waiting for transfers between devices: none -> 4.55 us  [passed_round(): lax.ppermute(value, axis, [(source, (source + steps) % count) for source...]
    ppermute x0 -> x2, starting transfers between devices: none -> 4.38 us  [passed_round(): lax.ppermute(value, axis, [(source, (source + steps) % count) for source...]
    ppermute x6 -> x5, starting transfers between devices: 12.2 us -> 10.9 us  [passed_along(): lax.ppermute(value, axis, [(source, source + steps) for source in range(f...]
    ppermute x15 -> x13, waiting for transfers between devices: 18.2 us -> 17.1 us  [swapped(): lax.ppermute(value, axis, [(source, source ^ mask) for source in range(co...]
    pallas_call x2, Pallas kernels: 3.62 us -> 2.54 us  [shards(): pl.pallas_call(functools.partial(kernel, reach, tok, group * HEAD_DIM, bl...]
    pallas_call x2, Pallas kernels: 3.91 us -> 2.83 us  [pack(): pl.pallas_call(functools.partial(pack_kernel, reach, tok, width, chunk),...]
  transfers between devices with their start and end apart: 21 -> 20, of which waited for: 11 -> 10; matrix products, arithmetic and copies ran while one was open for 0% -> 0% of each run, Pallas kernels for 24% -> 16%
where the time goes in v4:
time: 76.3 us; the launch traced here: 75.9 us
  starting transfers between devices  33.5 us (44%)
  waiting for transfers between devices  25.9 us (34%)
  Pallas kernels  15.1 us (20%)
  between operations  1.42 us (2%)
    ppermute x13, starting transfers between devices, swapped(): lax.ppermute(value, axis, [(source, source ^ mask) for source in range(co...  18.2 us
    ppermute x13, waiting for transfers between devices, swapped(): lax.ppermute(value, axis, [(source, source ^ mask) for source in range(co...  17.1 us
    ppermute x5, starting transfers between devices, passed_along(): lax.ppermute(value, axis, [(source, source + steps) for source in range(f...  10.9 us
    pallas_call x9, Pallas kernels, local(): pl.pallas_call(kernel, in_specs=[VMEM] * len(args), out_specs=[VMEM] * le...  9.73 us
    ppermute x2, waiting for transfers between devices, passed_round(): lax.ppermute(value, axis, [(source, (source + steps) % count) for source...  4.55 us
    ppermute x2, starting transfers between devices, passed_round(): lax.ppermute(value, axis, [(source, (source + steps) % count) for source...  4.38 us
    ppermute x5, waiting for transfers between devices, passed_along(): lax.ppermute(value, axis, [(source, source + steps) for source in range(f...  4.25 us
    pallas_call x2, Pallas kernels, pack(): pl.pallas_call(functools.partial(pack_kernel, reach, tok, width, chunk),...  2.83 us
  transfers between devices with their start and end apart: 20, of which 10 were waited for; matrix products, arithmetic and copies ran while one was open for 0% of the time, Pallas kernels for 16%

profile of v4, /device:TPU:0, one launch (start us, length us, event | category | flops | bytes accessed | tf_op | source)
XLA Modules:
  0.0 75.9 jit_solution(9894267133208573984)
XLA Ops:
  0.6 1.4 %pack.3 = (bf16[528,256]{1,0:T(8,128)(2,1)S(1)}, bf16[528,256]{1,0:T(8,128)(2,1)S(1)}, bf16[528,256]{1,0:T(8,128)(2,1)S(1)}, bf16[528,256]{1,0:T(8,128)(2,1)S(1)}) custom-call(bf16[1,128,2048]{2,1,0:T(8,128)(2,1)} %q.3, bf16[1,128,2048]{2,1,0:T(8,128)(2,1)} %g.3, bf16[1,128,2048]{2,1,0:T(8,128)(2,1)} %k.3, bf16[1,128,2048]{2,1,0:T(8,128)(2,1)} %v.3, ...), custom_call_target="tpu_custom_call" | custom-call | bytes 2097152 | tf_op jit(solution)/shard_map/pack/pallas_call | solution.py:376
  2.1 3.0 %collective-permute-start.4 = (bf16[528,256]{1,0:T(8,128)(2,1)S(1)}, bf16[528,256]{1,0:T(8,128)(2,1)S(1)}, u32[]{:S(2)}, u32[]{:S(2)}) collective-permute-start(bf16[528,256]{1,0:T(8,128)(2,1)S(1)} %get-tuple-element.51), channel_id=1, source_target_pairs={{0,2},{2,0},{4,6},{6,4},{8,10},{10,8},{12,14},{14,12},{16,18},{18,... | collective-permute-start | bytes 811016 | tf_op jit(solution)/shard_map/ppermute | solution.py:343
  5.1 1.5 %collective-permute-start.5 = (bf16[528,256]{1,0:T(8,128)(2,1)S(1)}, bf16[528,256]{1,0:T(8,128)(2,1)S(1)}, u32[]{:S(2)}, u32[]{:S(2)}) collective-permute-start(bf16[528,256]{1,0:T(8,128)(2,1)S(1)} %get-tuple-element.52), channel_id=1, source_target_pairs={{0,4},{2,6},{4,0},{6,2},{8,12},{10,14},{12,8},{14,10},{16,20},{18,... | collective-permute-start | bytes 811016 | tf_op jit(solution)/shard_map/ppermute | solution.py:343
  6.6 0.0 collective-permute-start.6
  6.6 1.4 %pack.2 = (bf16[512,256]{1,0:T(8,128)(2,1)S(1)}, bf16[512,256]{1,0:T(8,128)(2,1)S(1)}, bf16[512,256]{1,0:T(8,128)(2,1)S(1)}, bf16[512,256]{1,0:T(8,128)(2,1)S(1)}) custom-call(bf16[1,128,2048]{2,1,0:T(8,128)(2,1)} %q.3, bf16[1,128,2048]{2,1,0:T(8,128)(2,1)} %g.3, bf16[1,128,2048]{2,1,0:T(8,128)(2,1)} %k.3, bf16[1,128,2048]{2,1,0:T(8,128)(2,1)} %v.3, ...), custom_call_target="tpu_custom_call" | custom-call | bytes 2097152 | tf_op jit(solution)/shard_map/pack/pallas_call | solution.py:376
  8.0 2.0 %collective-permute-start = (bf16[512,256]{1,0:T(8,128)(2,1)S(1)}, bf16[512,256]{1,0:T(8,128)(2,1)S(1)}, u32[]{:S(2)}, u32[]{:S(2)}) collective-permute-start(bf16[512,256]{1,0:T(8,128)(2,1)S(1)} %get-tuple-element.44), channel_id=1, source_target_pairs={{0,2},{2,0},{4,6},{6,4},{8,10},{10,8},{12,14},{14,12},{16,18},{18,... | collective-permute-start | bytes 786440 | tf_op jit(solution)/shard_map/ppermute | solution.py:343
  10.0 1.5 %collective-permute-start.1 = (bf16[512,256]{1,0:T(8,128)(2,1)S(1)}, bf16[512,256]{1,0:T(8,128)(2,1)S(1)}, u32[]{:S(2)}, u32[]{:S(2)}) collective-permute-start(bf16[512,256]{1,0:T(8,128)(2,1)S(1)} %get-tuple-element.45), channel_id=1, source_target_pairs={{0,4},{2,6},{4,0},{6,2},{8,12},{10,14},{12,8},{14,10},{16,20},{18,... | collective-permute-start | bytes 786440 | tf_op jit(solution)/shard_map/ppermute | solution.py:343
  11.6 0.8 %collective-permute-done.4.refs_1_ = bf16[528,256]{1,0:T(8,128)(2,1)S(1)} collective-permute-done((bf16[528,256]{1,0:T(8,128)(2,1)S(1)}, bf16[528,256]{1,0:T(8,128)(2,1)S(1)}, u32[]{:S(2)}, u32[]{:S(2)}) %collective-permute-start.4) | collective-permute-done | bytes 270368 | tf_op jit(solution)/shard_map/ppermute | solution.py:343
  12.4 3.0 %collective-permute-start.2 = (bf16[512,256]{1,0:T(8,128)(2,1)S(1)}, bf16[512,256]{1,0:T(8,128)(2,1)S(1)}, u32[]{:S(2)}, u32[]{:S(2)}) collective-permute-start(bf16[512,256]{1,0:T(8,128)(2,1)S(1)} %get-tuple-element.46), channel_id=1, source_target_pairs={{0,6},{2,4},{4,2},{6,0},{8,14},{10,12},{12,10},{14,8},{16,22},{18,... | collective-permute-start | bytes 786440 | tf_op jit(solution)/shard_map/ppermute | solution.py:343
  15.4 4.9 %collective-permute-done.5.refs_2_ = bf16[528,256]{1,0:T(8,128)(2,1)S(1)} collective-permute-done((bf16[528,256]{1,0:T(8,128)(2,1)S(1)}, bf16[528,256]{1,0:T(8,128)(2,1)S(1)}, u32[]{:S(2)}, u32[]{:S(2)}) %collective-permute-start.5) | collective-permute-done | bytes 270368 | tf_op jit(solution)/shard_map/ppermute | solution.py:343
  20.3 0.0 collective-permute-done.6.refs_3_
  20.3 0.1 gather.3
  20.3 3.5 %collective-permute-start.7 = (bf16[4,272,256]{2,1,0:T(8,128)(2,1)S(1)}, bf16[4,272,256]{2,1,0:T(8,128)(2,1)S(1)}, u32[]{:S(2)}, u32[]{:S(2)}) collective-permute-start(bf16[4,272,256]{2,1,0:T(8,128)(2,1)S(1)} %get-tuple-element.55.kvo), channel_id=1, source_target_pairs={{0,8},{2,10},{4,12},{6,14},{8,16},{10,18},{12,20},{14,22},{16,24},... | collective-permute-start | bytes 1671176 | tf_op jit(solution)/shard_map/ppermute | solution.py:354
  23.9 1.3 %collective-permute-start.8 = (bf16[4,256,256]{2,1,0:T(8,128)(2,1)S(1)}, bf16[4,256,256]{2,1,0:T(8,128)(2,1)S(1)}, u32[]{:S(2)}, u32[]{:S(2)}) collective-permute-start(bf16[4,256,256]{2,1,0:T(8,128)(2,1)S(1)} %get-tuple-element.54.qd), channel_id=1, source_target_pairs={{8,0},{10,2},{12,4},{14,6},{16,8},{18,10},{20,12},{22,14},{24,16},... | collective-permute-start | bytes 1572872 | tf_op jit(solution)/shard_map/ppermute | solution.py:354
  25.2 0.0 collective-permute-done.refs_1_
  25.2 4.9 %collective-permute-done.1.refs_2_ = bf16[512,256]{1,0:T(8,128)(2,1)S(1)} collective-permute-done((bf16[512,256]{1,0:T(8,128)(2,1)S(1)}, bf16[512,256]{1,0:T(8,128)(2,1)S(1)}, u32[]{:S(2)}, u32[]{:S(2)}) %collective-permute-start.1) | collective-permute-done | bytes 262176 | tf_op jit(solution)/shard_map/ppermute | solution.py:343
  30.0 0.0 collective-permute-done.2.refs_3_
  30.0 0.1 gather.2
  30.1 3.5 %collective-permute-start.9 = (bf16[4,256,256]{2,1,0:T(8,128)(2,1)S(1)}, bf16[4,256,256]{2,1,0:T(8,128)(2,1)S(1)}, u32[]{:S(2)}, u32[]{:S(2)}) collective-permute-start(bf16[4,256,256]{2,1,0:T(8,128)(2,1)S(1)} %get-tuple-element.48.kvo), channel_id=1, source_target_pairs={{0,8},{2,10},{4,12},{6,14},{8,16},{10,18},{12,20},{14,22},{16,24},... | collective-permute-start | bytes 1572872 | tf_op jit(solution)/shard_map/ppermute | solution.py:354
  33.6 1.3 %collective-permute-start.3 = (bf16[4,256,256]{2,1,0:T(8,128)(2,1)S(1)}, bf16[4,256,256]{2,1,0:T(8,128)(2,1)S(1)}, u32[]{:S(2)}, u32[]{:S(2)}) collective-permute-start(bf16[4,256,256]{2,1,0:T(8,128)(2,1)S(1)} %get-tuple-element.47.qd), channel_id=1, source_target_pairs={{8,0},{10,2},{12,4},{14,6},{16,8},{18,10},{20,12},{22,14},{24,16},... | collective-permute-start | bytes 1572872 | tf_op jit(solution)/shard_map/ppermute | solution.py:354
  35.6 0.0 copy-start
  35.6 1.0 %collective-permute-done.8.qd = bf16[4,256,256]{2,1,0:T(8,128)(2,1)S(1)} collective-permute-done((bf16[4,256,256]{2,1,0:T(8,128)(2,1)S(1)}, bf16[4,256,256]{2,1,0:T(8,128)(2,1)S(1)}, u32[]{:S(2)}, u32[]{:S(2)}) %collective-permute-start.8) | collective-permute-done | bytes 524320 | tf_op jit(solution)/shard_map/ppermute | solution.py:354
  36.6 0.0 collective-permute-done.7.kvp
  36.6 0.0 copy-done
  36.6 3.4 %rows.2 = (bf16[1024,128]{1,0:T(8,128)(2,1)S(1)}, bf16[4,128,256]{2,1,0:T(8,128)(2,1)S(1)}, f32[512,256]{1,0:T(8,128)S(1)}, f32[512,256]{1,0:T(8,128)S(1)}, f32[...) custom-call(s32[1,128]{1,0:T(1,128)S(1)} %broadcast_in_dim.12.lengths, bf16[4,256,256]{2,1,0:T(8,128)(2,1)S(1)} %get-tuple-element.54.qd, ...), custom_call_target="tpu_custom_call" | custom-call | flops 2000000000 | bytes 2097152 | tf_op jit(solution)/shard_map/rows/pallas_call | solution.py:391
  40.0 1.3 %collective-permute-start.16 = (f32[2,2,512]{2,1,0:T(2,128)S(1)}, f32[2,2,512]{2,1,0:T(2,128)S(1)}, u32[]{:S(2)}, u32[]{:S(2)}) collective-permute-start(f32[2,2,512]{2,1,0:T(2,128)S(1)} %get-tuple-element.69), channel_id=1, source_target_pairs={{8,0},{10,2},{12,4},{14,6},{16,8},{18,10},{20,12},{22,14},{24,16},... | collective-permute-start | bytes 24584 | tf_op jit(solution)/shard_map/ppermute | solution.py:354
  41.3 3.0 %collective-permute-done.9.kvp = bf16[4,256,256]{2,1,0:T(8,128)(2,1)S(1)} collective-permute-done((bf16[4,256,256]{2,1,0:T(8,128)(2,1)S(1)}, bf16[4,256,256]{2,1,0:T(8,128)(2,1)S(1)}, u32[]{:S(2)}, u32[]{:S(2)}) %collective-permute-start.9) | collective-permute-done | bytes 524320 | tf_op jit(solution)/shard_map/ppermute | solution.py:354
  44.4 3.4 %rows.3 = (bf16[4,128,256]{2,1,0:T(8,128)(2,1)S(1)}, f32[512,256]{1,0:T(8,128)S(1)}, f32[512,256]{1,0:T(8,128)S(1)}, f32[3,2,512]{2,1,0:T(2,128)S(1)}, f32[8,128]{1,0:T(8,128)S(1)}) custom-call(s32[1,128]{1,0:T(1,128)S(1)} %broadcast_in_dim.12.lengths, bf16[4,256,256]{2,1,0:T(8,128)(2,1)S(1)} %get-tuple-element.47.qd, ...), custom_call_target="tpu_custom_call" | custom-call | flops 2000000000 | bytes 2097152 | tf_op jit(solution)/shard_map/rows/pallas_call | solution.py:391
  47.8 0.2 collective-permute-done.3.qd
  48.0 4.4 %collective-permute-start.10 = (f32[3,2,512]{2,1,0:T(2,128)S(1)}, f32[3,2,512]{2,1,0:T(2,128)S(1)}, u32[]{:S(2)}, u32[]{:S(2)}) collective-permute-start(f32[3,2,512]{2,1,0:T(2,128)S(1)} %get-tuple-element.60), channel_id=1, source_target_pairs={{0,24},{2,26},{4,28},{6,30},{8,0},{10,2},{12,4},{14,6},{16,8},{18,... | collective-permute-start | bytes 36872 | tf_op jit(solution)/shard_map/ppermute | solution.py:348
  52.3 0.0 collective-permute-done.16.stats
  52.3 1.4 %columns.3 = (bf16[512,256]{1,0:T(8,128)(2,1)S(1)}, bf16[512,256]{1,0:T(8,128)(2,1)S(1)}, bf16[512,256]{1,0:T(8,128)(2,1)S(1)}, bf16[512,256]{1,0:T(8,128)(2,1)S(1)}) custom-call(s32[1,128]{1,0:T(1,128)S(1)} %broadcast_in_dim.12.lengths, bf16[4,256,256]{2,1,0:T(8,128)(2,1)S(1)} %collective-permute-done.8.qd, bf16[4,272,256]{2,1,0:T(8,128)(2,1)S(1)} %get-tuple-element.55.kvo, ...), custom_call_target="tpu_custom_call" | custom-call | flops 4000000000 | bytes 2097152 | tf_op jit(solution)/shard_map/columns/pallas_call | solution.py:391
  53.7 0.6 collective-permute-start.18
  54.3 2.4 %collective-permute-start.19 = (bf16[512,256]{1,0:T(8,128)(2,1)S(1)}, bf16[512,256]{1,0:T(8,128)(2,1)S(1)}, u32[]{:S(2)}, u32[]{:S(2)}) collective-permute-start(bf16[512,256]{1,0:T(8,128)(2,1)S(1)} %get-tuple-element.78), channel_id=1, source_target_pairs={{0,6},{2,4},{4,2},{6,0},{8,14},{10,12},{12,10},{14,8},{16,22},{18,... | collective-permute-start | bytes 786440 | tf_op jit(solution)/shard_map/ppermute | solution.py:343
  56.8 0.0 collective-permute-done.10.stats
  56.8 0.5 collective-permute-start.17
  57.3 0.0 collective-permute-start.11
  57.3 4.5 %collective-permute-done.11.refs_1_ = f32[2,8,128]{2,1,0:T(8,128)S(1)} collective-permute-done((f32[2,8,128]{2,1,0:T(8,128)S(1)}, f32[2,8,128]{2,1,0:T(8,128)S(1)}, u32[]{:S(2)}, u32[]{:S(2)}) %collective-permute-start.11) | collective-permute-done | bytes 8224 | tf_op jit(solution)/shard_map/ppermute | solution.py:348
  61.9 0.0 collective-permute-start.12
  61.9 1.2 %collective-permute-done.12.b = f32[8,128]{1,0:T(8,128)S(1)} collective-permute-done((f32[8,128]{1,0:T(8,128)S(1)}, f32[8,128]{1,0:T(8,128)S(1)}, u32[]{:S(2)}, u32[]{:S(2)}) %collective-permute-start.12) | collective-permute-done | bytes 4128 | tf_op jit(solution)/shard_map/ppermute | solution.py:343
  63.0 1.4 %columns.2 = (bf16[272,256]{1,0:T(8,128)(2,1)S(1)}, bf16[272,256]{1,0:T(8,128)(2,1)S(1)}, bf16[272,256]{1,0:T(8,128)(2,1)S(1)}, bf16[272,256]{1,0:T(8,128)(2,1)S(1)}) custom-call(s32[1,128]{1,0:T(1,128)S(1)} %broadcast_in_dim.12.lengths, bf16[4,256,256]{2,1,0:T(8,128)(2,1)S(1)} %collective-permute-done.3.qd, bf16[4,256,256]{2,1,0:T(8,128)(2,1)S(1)} %get-tuple-element.48.kvo, ...), custom_call_target="tpu_custom_call" | custom-call | bytes 2097152 | tf_op jit(solution)/shard_map/columns/pallas_call | solution.py:391
  64.4 1.5 %collective-permute-start.13 = (bf16[272,256]{1,0:T(8,128)(2,1)S(1)}, bf16[272,256]{1,0:T(8,128)(2,1)S(1)}, u32[]{:S(2)}, u32[]{:S(2)}) collective-permute-start(bf16[272,256]{1,0:T(8,128)(2,1)S(1)} %get-tuple-element.65), channel_id=1, source_target_pairs={{0,2},{2,0},{4,6},{6,4},{8,10},{10,8},{12,14},{14,12},{16,18},{18,... | collective-permute-start | bytes 417800 | tf_op jit(solution)/shard_map/ppermute | solution.py:343
  66.0 0.5 collective-permute-start.14
  66.5 0.0 collective-permute-done.18.rest_2_
  66.5 1.5 %collective-permute-start.15 = (bf16[272,256]{1,0:T(8,128)(2,1)S(1)}, bf16[272,256]{1,0:T(8,128)(2,1)S(1)}, u32[]{:S(2)}, u32[]{:S(2)}) collective-permute-start(bf16[272,256]{1,0:T(8,128)(2,1)S(1)} %get-tuple-element.67), channel_id=1, source_target_pairs={{0,6},{2,4},{4,2},{6,0},{8,14},{10,12},{12,10},{14,8},{16,22},{18,... | collective-permute-start | bytes 417800 | tf_op jit(solution)/shard_map/ppermute | solution.py:343
  68.0 0.0 collective-permute-done.19.rest_3_
  68.0 0.0 collective-permute-done.17.rest_1_
  68.0 1.1 %unpack.2 = (bf16[1,128,2048]{2,1,0:T(8,128)(2,1)}, bf16[1,128,2048]{2,1,0:T(8,128)(2,1)}, bf16[1,128,2048]{2,1,0:T(8,128)(2,1)}) custom-call(bf16[512,256]{1,0:T(8,128)(2,1)S(1)} %get-tuple-element.74.rest_0_, bf16[512,256]{1,0:T(8,128)(2,1)S(1)} %collective-permute-done.17.rest_1_, bf16[512,256]{1,0:T(8,128)(2,1)S(1)} %collective-permute-done.18.rest_2_, ...), custom_call_target="tpu_custom_call" | custom-call | bytes 2097152 | tf_op jit(solution)/shard_map/unpack/pallas_call | solution.py:487
  69.1 1.7 %collective-permute-done.13.rest_1_ = bf16[272,256]{1,0:T(8,128)(2,1)S(1)} collective-permute-done((bf16[272,256]{1,0:T(8,128)(2,1)S(1)}, bf16[272,256]{1,0:T(8,128)(2,1)S(1)}, u32[]{:S(2)}, u32[]{:S(2)}) %collective-permute-start.13) | collective-permute-done | bytes 139296 | tf_op jit(solution)/shard_map/ppermute | solution.py:343
  70.8 3.7 %collective-permute-done.14.rest_2_ = bf16[272,256]{1,0:T(8,128)(2,1)S(1)} collective-permute-done((bf16[272,256]{1,0:T(8,128)(2,1)S(1)}, bf16[272,256]{1,0:T(8,128)(2,1)S(1)}, u32[]{:S(2)}, u32[]{:S(2)}) %collective-permute-start.14) | collective-permute-done | bytes 139296 | tf_op jit(solution)/shard_map/ppermute | solution.py:343
  74.4 0.0 collective-permute-done.15.rest_3_
  74.4 1.5 %unpack.3 = (bf16[1,128,2048]{2,1,0:T(8,128)(2,1)}, bf16[1,128,2048]{2,1,0:T(8,128)(2,1)}, bf16[1,128,2048]{2,1,0:T(8,128)(2,1)}, f32[16,64]{1,0:T(8,128)}) custom-call(bf16[272,256]{1,0:T(8,128)(2,1)S(1)} %get-tuple-element.64.rest_0_, ...), custom_call_target="tpu_custom_call", output_to_operand_aliasing={{0}: (4, {}), {1}: (5, {}), {2}: (6, {})} | custom-call | bytes 2097152 | tf_op jit(solution)/shard_map/unpack/pallas_call | solution.py:487
  (5 shorter events, 0.0 us)
Async XLA Ops:
  2.1 10.3 %collective-permute-start.4 = (bf16[528,256]{1,0:T(8,128)(2,1)S(1)}, bf16[528,256]{1,0:T(8,128)(2,1)S(1)}, u32[]{:S(2)}, u32[]{:S(2)}) collective-permute-start(bf16[528,256]{1,0:T(8,128)(2,1)S(1)} %get-tuple-element.51), channel_id=1, source_target_pairs={{0,2},{2,0},{4,6},{6,4},{8,10},{10,8},{12,14},{14,12},{16,18},{18,... | collective-permute-start | bytes 811016 | tf_op jit(solution)/shard_map/ppermute | solution.py:343
  5.1 15.2 %collective-permute-start.5 = (bf16[528,256]{1,0:T(8,128)(2,1)S(1)}, bf16[528,256]{1,0:T(8,128)(2,1)S(1)}, u32[]{:S(2)}, u32[]{:S(2)}) collective-permute-start(bf16[528,256]{1,0:T(8,128)(2,1)S(1)} %get-tuple-element.52), channel_id=1, source_target_pairs={{0,4},{2,6},{4,0},{6,2},{8,12},{10,14},{12,8},{14,10},{16,20},{18,... | collective-permute-start | bytes 811016 | tf_op jit(solution)/shard_map/ppermute | solution.py:343
  6.6 13.7 %collective-permute-start.6 = (bf16[528,256]{1,0:T(8,128)(2,1)S(1)}, bf16[528,256]{1,0:T(8,128)(2,1)S(1)}, u32[]{:S(2)}, u32[]{:S(2)}) collective-permute-start(bf16[528,256]{1,0:T(8,128)(2,1)S(1)} %get-tuple-element.53), channel_id=1, source_target_pairs={{0,6},{2,4},{4,2},{6,0},{8,14},{10,12},{12,10},{14,8},{16,22},{18,... | collective-permute-start | bytes 811016 | tf_op jit(solution)/shard_map/ppermute | solution.py:343
  8.0 17.1 %collective-permute-start = (bf16[512,256]{1,0:T(8,128)(2,1)S(1)}, bf16[512,256]{1,0:T(8,128)(2,1)S(1)}, u32[]{:S(2)}, u32[]{:S(2)}) collective-permute-start(bf16[512,256]{1,0:T(8,128)(2,1)S(1)} %get-tuple-element.44), channel_id=1, source_target_pairs={{0,2},{2,0},{4,6},{6,4},{8,10},{10,8},{12,14},{14,12},{16,18},{18,... | collective-permute-start | bytes 786440 | tf_op jit(solution)/shard_map/ppermute | solution.py:343
  10.0 20.0 %collective-permute-start.1 = (bf16[512,256]{1,0:T(8,128)(2,1)S(1)}, bf16[512,256]{1,0:T(8,128)(2,1)S(1)}, u32[]{:S(2)}, u32[]{:S(2)}) collective-permute-start(bf16[512,256]{1,0:T(8,128)(2,1)S(1)} %get-tuple-element.45), channel_id=1, source_target_pairs={{0,4},{2,6},{4,0},{6,2},{8,12},{10,14},{12,8},{14,10},{16,20},{18,... | collective-permute-start | bytes 786440 | tf_op jit(solution)/shard_map/ppermute | solution.py:343
  12.4 17.7 %collective-permute-start.2 = (bf16[512,256]{1,0:T(8,128)(2,1)S(1)}, bf16[512,256]{1,0:T(8,128)(2,1)S(1)}, u32[]{:S(2)}, u32[]{:S(2)}) collective-permute-start(bf16[512,256]{1,0:T(8,128)(2,1)S(1)} %get-tuple-element.46), channel_id=1, source_target_pairs={{0,6},{2,4},{4,2},{6,0},{8,14},{10,12},{12,10},{14,8},{16,22},{18,... | collective-permute-start | bytes 786440 | tf_op jit(solution)/shard_map/ppermute | solution.py:343
  20.3 16.3 %collective-permute-start.7 = (bf16[4,272,256]{2,1,0:T(8,128)(2,1)S(1)}, bf16[4,272,256]{2,1,0:T(8,128)(2,1)S(1)}, u32[]{:S(2)}, u32[]{:S(2)}) collective-permute-start(bf16[4,272,256]{2,1,0:T(8,128)(2,1)S(1)} %get-tuple-element.55.kvo), channel_id=1, source_target_pairs={{0,8},{2,10},{4,12},{6,14},{8,16},{10,18},{12,20},{14,22},{16,24},... | collective-permute-start | bytes 1671176 | tf_op jit(solution)/shard_map/ppermute | solution.py:354
  23.9 12.7 %collective-permute-start.8 = (bf16[4,256,256]{2,1,0:T(8,128)(2,1)S(1)}, bf16[4,256,256]{2,1,0:T(8,128)(2,1)S(1)}, u32[]{:S(2)}, u32[]{:S(2)}) collective-permute-start(bf16[4,256,256]{2,1,0:T(8,128)(2,1)S(1)} %get-tuple-element.54.qd), channel_id=1, source_target_pairs={{8,0},{10,2},{12,4},{14,6},{16,8},{18,10},{20,12},{22,14},{24,16},... | collective-permute-start | bytes 1572872 | tf_op jit(solution)/shard_map/ppermute | solution.py:354
  30.1 14.3 %collective-permute-start.9 = (bf16[4,256,256]{2,1,0:T(8,128)(2,1)S(1)}, bf16[4,256,256]{2,1,0:T(8,128)(2,1)S(1)}, u32[]{:S(2)}, u32[]{:S(2)}) collective-permute-start(bf16[4,256,256]{2,1,0:T(8,128)(2,1)S(1)} %get-tuple-element.48.kvo), channel_id=1, source_target_pairs={{0,8},{2,10},{4,12},{6,14},{8,16},{10,18},{12,20},{14,22},{16,24},... | collective-permute-start | bytes 1572872 | tf_op jit(solution)/shard_map/ppermute | solution.py:354
  33.6 14.3 %collective-permute-start.3 = (bf16[4,256,256]{2,1,0:T(8,128)(2,1)S(1)}, bf16[4,256,256]{2,1,0:T(8,128)(2,1)S(1)}, u32[]{:S(2)}, u32[]{:S(2)}) collective-permute-start(bf16[4,256,256]{2,1,0:T(8,128)(2,1)S(1)} %get-tuple-element.47.qd), channel_id=1, source_target_pairs={{8,0},{10,2},{12,4},{14,6},{16,8},{18,10},{20,12},{22,14},{24,16},... | collective-permute-start | bytes 1572872 | tf_op jit(solution)/shard_map/ppermute | solution.py:354
  35.6 1.0 %copy-start = (bf16[16,64]{1,0:T(8,128)(2,1)S(1)}, bf16[16,64]{1,0:T(8,128)(2,1)}, u32[]{:S(2)}) copy-start(bf16[16,64]{1,0:T(8,128)(2,1)} %bias_ref.7) | copy-start | bytes 6148
  40.0 12.3 %collective-permute-start.16 = (f32[2,2,512]{2,1,0:T(2,128)S(1)}, f32[2,2,512]{2,1,0:T(2,128)S(1)}, u32[]{:S(2)}, u32[]{:S(2)}) collective-permute-start(f32[2,2,512]{2,1,0:T(2,128)S(1)} %get-tuple-element.69), channel_id=1, source_target_pairs={{8,0},{10,2},{12,4},{14,6},{16,8},{18,10},{20,12},{22,14},{24,16},... | collective-permute-start | bytes 24584 | tf_op jit(solution)/shard_map/ppermute | solution.py:354
  48.0 8.8 %collective-permute-start.10 = (f32[3,2,512]{2,1,0:T(2,128)S(1)}, f32[3,2,512]{2,1,0:T(2,128)S(1)}, u32[]{:S(2)}, u32[]{:S(2)}) collective-permute-start(f32[3,2,512]{2,1,0:T(2,128)S(1)} %get-tuple-element.60), channel_id=1, source_target_pairs={{0,24},{2,26},{4,28},{6,30},{8,0},{10,2},{12,4},{14,6},{16,8},{18,... | collective-permute-start | bytes 36872 | tf_op jit(solution)/shard_map/ppermute | solution.py:348
  53.7 12.8 %collective-permute-start.18 = (bf16[512,256]{1,0:T(8,128)(2,1)S(1)}, bf16[512,256]{1,0:T(8,128)(2,1)S(1)}, u32[]{:S(2)}, u32[]{:S(2)}) collective-permute-start(bf16[512,256]{1,0:T(8,128)(2,1)S(1)} %get-tuple-element.77), channel_id=1, source_target_pairs={{0,4},{2,6},{4,0},{6,2},{8,12},{10,14},{12,8},{14,10},{16,20},{18,... | collective-permute-start | bytes 786440 | tf_op jit(solution)/shard_map/ppermute | solution.py:343
  54.3 13.7 %collective-permute-start.19 = (bf16[512,256]{1,0:T(8,128)(2,1)S(1)}, bf16[512,256]{1,0:T(8,128)(2,1)S(1)}, u32[]{:S(2)}, u32[]{:S(2)}) collective-permute-start(bf16[512,256]{1,0:T(8,128)(2,1)S(1)} %get-tuple-element.78), channel_id=1, source_target_pairs={{0,6},{2,4},{4,2},{6,0},{8,14},{10,12},{12,10},{14,8},{16,22},{18,... | collective-permute-start | bytes 786440 | tf_op jit(solution)/shard_map/ppermute | solution.py:343
  56.8 11.2 %collective-permute-start.17 = (bf16[512,256]{1,0:T(8,128)(2,1)S(1)}, bf16[512,256]{1,0:T(8,128)(2,1)S(1)}, u32[]{:S(2)}, u32[]{:S(2)}) collective-permute-start(bf16[512,256]{1,0:T(8,128)(2,1)S(1)} %get-tuple-element.76), channel_id=1, source_target_pairs={{0,2},{2,0},{4,6},{6,4},{8,10},{10,8},{12,14},{14,12},{16,18},{18,... | collective-permute-start | bytes 786440 | tf_op jit(solution)/shard_map/ppermute | solution.py:343
  57.3 4.5 %collective-permute-start.11 = (f32[2,8,128]{2,1,0:T(8,128)S(1)}, f32[2,8,128]{2,1,0:T(8,128)S(1)}, u32[]{:S(2)}, u32[]{:S(2)}) collective-permute-start(f32[2,8,128]{2,1,0:T(8,128)S(1)} %pair.1.refs_0_), channel_id=1, source_target_pairs={{0,16},{2,18},{4,20},{6,22},{8,24},{10,26},{12,28},{14,30},{16,0},... | collective-permute-start | bytes 24584 | tf_op jit(solution)/shard_map/ppermute | solution.py:348
  61.9 1.2 %collective-permute-start.12 = (f32[8,128]{1,0:T(8,128)S(1)}, f32[8,128]{1,0:T(8,128)S(1)}, u32[]{:S(2)}, u32[]{:S(2)}) collective-permute-start(f32[8,128]{1,0:T(8,128)S(1)} %planes.1.a), channel_id=1, source_target_pairs={{0,1},{1,0},{2,3},{3,2},{4,5},{5,4},{6,7},{7,6},{8,9},{9,8},{10,11... | collective-permute-start | bytes 12296 | tf_op jit(solution)/shard_map/ppermute | solution.py:343
  64.4 6.3 %collective-permute-start.13 = (bf16[272,256]{1,0:T(8,128)(2,1)S(1)}, bf16[272,256]{1,0:T(8,128)(2,1)S(1)}, u32[]{:S(2)}, u32[]{:S(2)}) collective-permute-start(bf16[272,256]{1,0:T(8,128)(2,1)S(1)} %get-tuple-element.65), channel_id=1, source_target_pairs={{0,2},{2,0},{4,6},{6,4},{8,10},{10,8},{12,14},{14,12},{16,18},{18,... | collective-permute-start | bytes 417800 | tf_op jit(solution)/shard_map/ppermute | solution.py:343
  66.0 8.4 %collective-permute-start.14 = (bf16[272,256]{1,0:T(8,128)(2,1)S(1)}, bf16[272,256]{1,0:T(8,128)(2,1)S(1)}, u32[]{:S(2)}, u32[]{:S(2)}) collective-permute-start(bf16[272,256]{1,0:T(8,128)(2,1)S(1)} %get-tuple-element.66), channel_id=1, source_target_pairs={{0,4},{2,6},{4,0},{6,2},{8,12},{10,14},{12,8},{14,10},{16,20},{18,... | collective-permute-start | bytes 417800 | tf_op jit(solution)/shard_map/ppermute | solution.py:343
  66.5 7.9 %collective-permute-start.15 = (bf16[272,256]{1,0:T(8,128)(2,1)S(1)}, bf16[272,256]{1,0:T(8,128)(2,1)S(1)}, u32[]{:S(2)}, u32[]{:S(2)}) collective-permute-start(bf16[272,256]{1,0:T(8,128)(2,1)S(1)} %get-tuple-element.67), channel_id=1, source_target_pairs={{0,6},{2,4},{4,2},{6,0},{8,14},{10,12},{12,10},{14,8},{16,22},{18,... | collective-permute-start | bytes 417800 | tf_op jit(solution)/shard_map/ppermute | solution.py:343

commit v5 on v4

--- a/solution.py
+++ b/solution.py
@@ -20,7 +20,7 @@
 BF16, F32 = jnp.bfloat16, jnp.float32
 ANY = pl.BlockSpec(memory_space=pl.ANY)
 VMEM = pl.BlockSpec(memory_space=pltpu.VMEM)
-GATHER_FLOPS, ROWS_FLOPS, COLUMNS_FLOPS, PAIR_FLOPS = 2 * 10**9, 2 * 10**9, (4 * 10**9, 0), 8 * 10**9
+GATHER_FLOPS, ROWS_FLOPS, COLUMNS_FLOPS = 2 * 10**9, 2 * 10**9, (4 * 10**9, 0)
 NT = (((1,), (1,)), ((), ()))
 
 
@@ -206,41 +206,10 @@
         row = jnp.sum(by_key * onehots[...].astype(F32), axis=0, keepdims=True)
         sums_out[...] += jnp.where(lax.broadcasted_iota(jnp.int32, (8, tok), 0) == at, row, 0.0)
 
-    if stats_out.shape[0] > per:
-        for h in range(HEADS // reach):
-            stats_out[per, 0:1, h * tok : (h + 1) * tok] = sums_out[h : h + 1]
-            stats_out[per, 1:2, h * tok : (h + 1) * tok] = sums_out[h : h + 1]
-
-
-def pair_kernel(reach, tok, sums, stats, out):
-    out[0] = sums[...]
-    out[1] = jnp.zeros_like(sums)
-    for h in range(HEADS // reach):
-        out[1, h : h + 1] = stats[stats.shape[0] - 1, 0:1, h * tok : (h + 1) * tok]
-
-
-def planes_kernel(reach, tok, *refs):
-    _, plane = place(reach)
-    parts, out, blocks = refs[:-2], refs[-2], refs[-1]
-    count = blocks.shape[0]
-    at = 0
-    for part in parts:
-        blocks[at : at + part.shape[0]] = part[...]
-        at += part.shape[0]
-    out[...] = blocks[lax.rem(count - plane, count)]
-    for q in range(1, count):
-        out[...] += blocks[lax.rem(q + count - plane, count)]
-
 
 def columns_kernel(reach, tok, chunk, lengths, qd, kvo, onehots, stats, bias_ref, dk_in, dv_in, *rest):
     k_scr, v_scr, dk_scr, dv_scr = rest[-4:]
     outs, extras = rest[-4 - reach : -4], rest[: -4 - reach]
-    last = len(extras) == 1
-    if last:
-        parts = [part.astype(F32) for part in three_parts(extras[0][...])]
-        parts = [jnp.concatenate(parts[:2], axis=1), jnp.concatenate([parts[2], jnp.zeros_like(parts[2])], axis=1)]
-        for m in range(reach):
-            outs[m][2 * tok :] = jnp.concatenate(parts, axis=0).astype(BF16)
     p, plane = place(reach)
     length = lengths[...]
     span = reach * tok
@@ -287,16 +256,19 @@
             mine = pl.ds(pl.multiple_of((p ^ m) * tok, tok), tok)
             outs[m][0:tok, head] = (dk_scr[mine] * FACTOR).astype(BF16)
             outs[m][tok : 2 * tok, head] = dv_scr[mine].astype(BF16)
-            for at, dq in enumerate(() if last else extras):
+            for at, dq in enumerate(extras):
                 outs[m][(2 + at) * tok : (3 + at) * tok, head] = dq[m, :, head]
 
 
-def stack_kernel(*refs):
-    parts, out = refs[:-1], refs[-1]
-    at = 0
-    for part in parts:
-        out[at : at + part.shape[0]] = part[...]
-        at += part.shape[0]
+def attach_kernel(sums, *refs):
+    messages, outs = refs[: len(refs) // 2], refs[len(refs) // 2 :]
+    parts = [part.astype(F32) for part in three_parts(sums[...])]
+    parts = [jnp.concatenate(parts[:2], axis=1), jnp.concatenate([parts[2], jnp.zeros_like(parts[2])], axis=1)]
+    below = jnp.concatenate(parts, axis=0).astype(BF16)
+    for message, out in zip(messages, outs):
+        count = message.shape[0]
+        out[:count] = message[...]
+        out[count:] = below
 
 
 def add_kernel(reach, tok, a, b, out):
@@ -341,11 +313,6 @@
 def swapped(value, axis, mask):
     count = lax.axis_size(axis)
     return lax.ppermute(value, axis, [(source, source ^ mask) for source in range(count)])
-
-
-def passed_round(value, axis, steps):
-    count = lax.axis_size(axis)
-    return lax.ppermute(value, axis, [(source, (source + steps) % count) for source in range(count)])
 
 
 def passed_along(value, axis, steps):
@@ -408,7 +375,7 @@
             vmem((reach, tok, width)),
             vmem((span, width), F32),
             vmem((span, width), F32),
-            vmem((per + chunk, 2, span), F32),
+            vmem((per, 2, span), F32),
             vmem((8, tok), F32),
         ]
         if chunk == 0:
@@ -424,7 +391,7 @@
         return local(kernel, "rows", ROWS_FLOPS, out, *args, scratch=scratch)
 
     def columns_of(chunk, qd, kvo, onehots, stats, dk, dv, *extras):
-        out = [vmem((2 * tok + (PAD if len(extras) == 1 else len(extras) * tok), width))] * reach
+        out = [vmem(((2 + len(extras)) * tok, width))] * reach
         scratch = [
             pltpu.VMEM((span, 2 * HEAD_DIM), BF16),
             pltpu.VMEM((span, HEAD_DIM), BF16),
@@ -454,28 +421,21 @@
         *made, dq, dk, dv, stats, sums = rows_of(c, *planes[c], before[c], sums, *onehots)
         onehots = onehots or made
         dqs.append(dq)
-        stats = following(stats, after[c])
-        stats = passed_round(stats, "seq", -reach) if c else passed_along(stats, "seq", -reach)
+        stats = passed_along(following(stats, after[c]), "seq", -reach)
         pending.append((after[c], planes[c][1], *onehots, stats, dk, dv))
     messages = [list(columns_of(0, *pending[0], *dqs))]
-    messages[0][1] = following(messages[0][1], stats)
-    blocks = [local(functools.partial(pair_kernel, reach, tok), "pair", PAIR_FLOPS, [vmem((2, 8, tok), F32)], sums, stats)[0]]
-    count = lax.axis_size("seq") // reach
-    step = 2
-    while step < count:
-        so_far = blocks[0]
-        if len(blocks) > 1:
-            so_far = local(stack_kernel, "stack", 0, [vmem((step, 8, tok), F32)], *blocks)[0]
-        blocks.append(passed_round(so_far, "seq", -step * reach))
-        step *= 2
-    kernel = functools.partial(planes_kernel, reach, tok)
-    scratch = [pltpu.VMEM((count, 8, tok), F32)]
-    sums = local(kernel, "planes", 0, [vmem((8, tok), F32)], *blocks, scratch=scratch)[0]
+    messages.append(columns_of(1, *pending[1]))
+    sums = following(sums, messages[0][0])
+    mask = reach
+    while mask < lax.axis_size("seq"):
+        sums = add(sums, swapped(sums, "seq", mask))
+        mask *= 2
     mask = 1
     while mask < lax.axis_size("dp"):
         sums = add(sums, swapped(sums, "dp", mask))
         mask *= 2
-    messages.append(columns_of(1, *pending[1], sums))
+    out = [vmem((2 * tok + PAD, width))] * reach
+    messages[1] = local(attach_kernel, "attach", 0, out, sums, *messages[1])
     parts = [[own[0]] + [swapped(own[m], "seq", m) for m in range(1, reach)] for own in messages]
 
     blocks = [((1, 0), (2, 0), (0, 0), (0, 1)), ((1, 1), (2, 1))]

time: 76.3 us -> 75.4 us (0.988)
  waiting for transfers between devices: 25.9 us -> 23.9 us
  starting transfers between devices: 33.5 us -> 34.5 us
    ppermute x2 -> x0, waiting for transfers between devices: 4.55 us -> none  [passed_round(): lax.ppermute(value, axis, [(source, (source + steps) % count) for source...]
    ppermute x2 -> x0, starting transfers between devices: 4.38 us -> none  [passed_round(): lax.ppermute(value, axis, [(source, (source + steps) % count) for source...]
    ppermute x13 -> x15, starting transfers between devices: 18.2 us -> 22.3 us  [swapped(): lax.ppermute(value, axis, [(source, source ^ mask) for source in range(co...]
    ppermute x13 -> x15, waiting for transfers between devices: 17.1 us -> 18.9 us  [swapped(): lax.ppermute(value, axis, [(source, source ^ mask) for source in range(co...]
    ppermute x5 -> x6, starting transfers between devices: 10.9 us -> 12.2 us  [passed_along(): lax.ppermute(value, axis, [(source, source + steps) for source in range(f...]
    ppermute x5 -> x6, waiting for transfers between devices: 4.25 us -> 5 us  [passed_along(): lax.ppermute(value, axis, [(source, source + steps) for source in range(f...]
    pallas_call x9 -> x10, Pallas kernels: 9.73 us -> 9.79 us  [local(): pl.pallas_call(kernel, in_specs=[VMEM] * len(args), out_specs=[VMEM] * le...]
  transfers between devices with their start and end apart: 20 -> 21, of which waited for: 10 -> 10; matrix products, arithmetic and copies ran while one was open for 0% -> 0% of each run, Pallas kernels for 16% -> 16%
where the time goes in v5:
time: 75.4 us; the launch traced here: 75 us
  starting transfers between devices  34.5 us (46%)
  waiting for transfers between devices  23.9 us (32%)
  Pallas kernels  15.2 us (20%)
  between operations  1.45 us (2%)
    ppermute x15, starting transfers between devices, swapped(): lax.ppermute(value, axis, [(source, source ^ mask) for source in range(co...  22.3 us
    ppermute x15, waiting for transfers between devices, swapped(): lax.ppermute(value, axis, [(source, source ^ mask) for source in range(co...  18.9 us
    ppermute x6, starting transfers between devices, passed_along(): lax.ppermute(value, axis, [(source, source + steps) for source in range(f...  12.2 us
    pallas_call x10, Pallas kernels, local(): pl.pallas_call(kernel, in_specs=[VMEM] * len(args), out_specs=[VMEM] * le...  9.79 us
    ppermute x6, waiting for transfers between devices, passed_along(): lax.ppermute(value, axis, [(source, source + steps) for source in range(f...  5 us
    pallas_call x2, Pallas kernels, pack(): pl.pallas_call(functools.partial(pack_kernel, reach, tok, width, chunk),...  2.83 us
    pallas_call x2, Pallas kernels, shards(): pl.pallas_call(functools.partial(kernel, reach, tok, group * HEAD_DIM, bl...  2.54 us
  transfers between devices with their start and end apart: 21, of which 10 were waited for; matrix products, arithmetic and copies ran while one was open for 0% of the time, Pallas kernels for 16%

profile of v5, /device:TPU:0, one launch (start us, length us, event | category | flops | bytes accessed | tf_op | source)
XLA Modules:
  0.0 75.0 jit_solution(11159697689074101712)
XLA Ops:
  0.6 1.4 %pack.3 = (bf16[528,256]{1,0:T(8,128)(2,1)S(1)}, bf16[528,256]{1,0:T(8,128)(2,1)S(1)}, bf16[528,256]{1,0:T(8,128)(2,1)S(1)}, bf16[528,256]{1,0:T(8,128)(2,1)S(1)}) custom-call(bf16[1,128,2048]{2,1,0:T(8,128)(2,1)} %q.3, bf16[1,128,2048]{2,1,0:T(8,128)(2,1)} %g.3, bf16[1,128,2048]{2,1,0:T(8,128)(2,1)} %k.3, bf16[1,128,2048]{2,1,0:T(8,128)(2,1)} %v.3, ...), custom_call_target="tpu_custom_call" | custom-call | bytes 2097152 | tf_op jit(solution)/shard_map/pack/pallas_call | solution.py:343
  2.1 3.0 %collective-permute-start.4 = (bf16[528,256]{1,0:T(8,128)(2,1)S(1)}, bf16[528,256]{1,0:T(8,128)(2,1)S(1)}, u32[]{:S(2)}, u32[]{:S(2)}) collective-permute-start(bf16[528,256]{1,0:T(8,128)(2,1)S(1)} %get-tuple-element.55), channel_id=1, source_target_pairs={{0,2},{2,0},{4,6},{6,4},{8,10},{10,8},{12,14},{14,12},{16,18},{18,... | collective-permute-start | bytes 811016 | tf_op jit(solution)/shard_map/ppermute | solution.py:315
  5.1 1.5 %collective-permute-start.5 = (bf16[528,256]{1,0:T(8,128)(2,1)S(1)}, bf16[528,256]{1,0:T(8,128)(2,1)S(1)}, u32[]{:S(2)}, u32[]{:S(2)}) collective-permute-start(bf16[528,256]{1,0:T(8,128)(2,1)S(1)} %get-tuple-element.56), channel_id=1, source_target_pairs={{0,4},{2,6},{4,0},{6,2},{8,12},{10,14},{12,8},{14,10},{16,20},{18,... | collective-permute-start | bytes 811016 | tf_op jit(solution)/shard_map/ppermute | solution.py:315
  6.6 0.0 collective-permute-start.6
  6.6 1.4 %pack.2 = (bf16[512,256]{1,0:T(8,128)(2,1)S(1)}, bf16[512,256]{1,0:T(8,128)(2,1)S(1)}, bf16[512,256]{1,0:T(8,128)(2,1)S(1)}, bf16[512,256]{1,0:T(8,128)(2,1)S(1)}) custom-call(bf16[1,128,2048]{2,1,0:T(8,128)(2,1)} %q.3, bf16[1,128,2048]{2,1,0:T(8,128)(2,1)} %g.3, bf16[1,128,2048]{2,1,0:T(8,128)(2,1)} %k.3, bf16[1,128,2048]{2,1,0:T(8,128)(2,1)} %v.3, ...), custom_call_target="tpu_custom_call" | custom-call | bytes 2097152 | tf_op jit(solution)/shard_map/pack/pallas_call | solution.py:343
  8.0 2.0 %collective-permute-start = (bf16[512,256]{1,0:T(8,128)(2,1)S(1)}, bf16[512,256]{1,0:T(8,128)(2,1)S(1)}, u32[]{:S(2)}, u32[]{:S(2)}) collective-permute-start(bf16[512,256]{1,0:T(8,128)(2,1)S(1)} %get-tuple-element.48), channel_id=1, source_target_pairs={{0,2},{2,0},{4,6},{6,4},{8,10},{10,8},{12,14},{14,12},{16,18},{18,... | collective-permute-start | bytes 786440 | tf_op jit(solution)/shard_map/ppermute | solution.py:315
  10.0 1.5 %collective-permute-start.1 = (bf16[512,256]{1,0:T(8,128)(2,1)S(1)}, bf16[512,256]{1,0:T(8,128)(2,1)S(1)}, u32[]{:S(2)}, u32[]{:S(2)}) collective-permute-start(bf16[512,256]{1,0:T(8,128)(2,1)S(1)} %get-tuple-element.49), channel_id=1, source_target_pairs={{0,4},{2,6},{4,0},{6,2},{8,12},{10,14},{12,8},{14,10},{16,20},{18,... | collective-permute-start | bytes 786440 | tf_op jit(solution)/shard_map/ppermute | solution.py:315
  11.6 0.8 %collective-permute-done.4.refs_1_ = bf16[528,256]{1,0:T(8,128)(2,1)S(1)} collective-permute-done((bf16[528,256]{1,0:T(8,128)(2,1)S(1)}, bf16[528,256]{1,0:T(8,128)(2,1)S(1)}, u32[]{:S(2)}, u32[]{:S(2)}) %collective-permute-start.4) | collective-permute-done | bytes 270368 | tf_op jit(solution)/shard_map/ppermute | solution.py:315
  12.4 3.0 %collective-permute-start.2 = (bf16[512,256]{1,0:T(8,128)(2,1)S(1)}, bf16[512,256]{1,0:T(8,128)(2,1)S(1)}, u32[]{:S(2)}, u32[]{:S(2)}) collective-permute-start(bf16[512,256]{1,0:T(8,128)(2,1)S(1)} %get-tuple-element.50), channel_id=1, source_target_pairs={{0,6},{2,4},{4,2},{6,0},{8,14},{10,12},{12,10},{14,8},{16,22},{18,... | collective-permute-start | bytes 786440 | tf_op jit(solution)/shard_map/ppermute | solution.py:315
  15.4 4.9 %collective-permute-done.5.refs_2_ = bf16[528,256]{1,0:T(8,128)(2,1)S(1)} collective-permute-done((bf16[528,256]{1,0:T(8,128)(2,1)S(1)}, bf16[528,256]{1,0:T(8,128)(2,1)S(1)}, u32[]{:S(2)}, u32[]{:S(2)}) %collective-permute-start.5) | collective-permute-done | bytes 270368 | tf_op jit(solution)/shard_map/ppermute | solution.py:315
  20.3 0.0 collective-permute-done.6.refs_3_
  20.3 0.1 gather.3
  20.3 3.5 %collective-permute-start.7 = (bf16[4,272,256]{2,1,0:T(8,128)(2,1)S(1)}, bf16[4,272,256]{2,1,0:T(8,128)(2,1)S(1)}, u32[]{:S(2)}, u32[]{:S(2)}) collective-permute-start(bf16[4,272,256]{2,1,0:T(8,128)(2,1)S(1)} %get-tuple-element.59.kvo), channel_id=1, source_target_pairs={{0,8},{2,10},{4,12},{6,14},{8,16},{10,18},{12,20},{14,22},{16,24},... | collective-permute-start | bytes 1671176 | tf_op jit(solution)/shard_map/ppermute | solution.py:321
  23.9 1.3 %collective-permute-start.8 = (bf16[4,256,256]{2,1,0:T(8,128)(2,1)S(1)}, bf16[4,256,256]{2,1,0:T(8,128)(2,1)S(1)}, u32[]{:S(2)}, u32[]{:S(2)}) collective-permute-start(bf16[4,256,256]{2,1,0:T(8,128)(2,1)S(1)} %get-tuple-element.58.qd), channel_id=1, source_target_pairs={{8,0},{10,2},{12,4},{14,6},{16,8},{18,10},{20,12},{22,14},{24,16},... | collective-permute-start | bytes 1572872 | tf_op jit(solution)/shard_map/ppermute | solution.py:321
  25.2 0.0 collective-permute-done.refs_1_
  25.2 4.9 %collective-permute-done.1.refs_2_ = bf16[512,256]{1,0:T(8,128)(2,1)S(1)} collective-permute-done((bf16[512,256]{1,0:T(8,128)(2,1)S(1)}, bf16[512,256]{1,0:T(8,128)(2,1)S(1)}, u32[]{:S(2)}, u32[]{:S(2)}) %collective-permute-start.1) | collective-permute-done | bytes 262176 | tf_op jit(solution)/shard_map/ppermute | solution.py:315
  30.0 0.0 collective-permute-done.2.refs_3_
  30.0 0.1 gather.2
  30.1 3.5 %collective-permute-start.3 = (bf16[4,256,256]{2,1,0:T(8,128)(2,1)S(1)}, bf16[4,256,256]{2,1,0:T(8,128)(2,1)S(1)}, u32[]{:S(2)}, u32[]{:S(2)}) collective-permute-start(bf16[4,256,256]{2,1,0:T(8,128)(2,1)S(1)} %get-tuple-element.52.kvo), channel_id=1, source_target_pairs={{0,8},{2,10},{4,12},{6,14},{8,16},{10,18},{12,20},{14,22},{16,24},... | collective-permute-start | bytes 1572872 | tf_op jit(solution)/shard_map/ppermute | solution.py:321
  34.3 0.0 copy-start
  34.3 1.3 %collective-permute-start.13 = (bf16[4,256,256]{2,1,0:T(8,128)(2,1)S(1)}, bf16[4,256,256]{2,1,0:T(8,128)(2,1)S(1)}, u32[]{:S(2)}, u32[]{:S(2)}) collective-permute-start(bf16[4,256,256]{2,1,0:T(8,128)(2,1)S(1)} %get-tuple-element.51.qd), channel_id=1, source_target_pairs={{8,0},{10,2},{12,4},{14,6},{16,8},{18,10},{20,12},{22,14},{24,16},... | collective-permute-start | bytes 1572872 | tf_op jit(solution)/shard_map/ppermute | solution.py:321
  35.6 1.0 %collective-permute-done.8.qd = bf16[4,256,256]{2,1,0:T(8,128)(2,1)S(1)} collective-permute-done((bf16[4,256,256]{2,1,0:T(8,128)(2,1)S(1)}, bf16[4,256,256]{2,1,0:T(8,128)(2,1)S(1)}, u32[]{:S(2)}, u32[]{:S(2)}) %collective-permute-start.8) | collective-permute-done | bytes 524320 | tf_op jit(solution)/shard_map/ppermute | solution.py:321
  36.6 0.0 collective-permute-done.7.kvp
  36.6 0.0 copy-done
  36.6 3.4 %rows.2 = (bf16[1024,128]{1,0:T(8,128)(2,1)S(1)}, bf16[4,128,256]{2,1,0:T(8,128)(2,1)S(1)}, f32[512,256]{1,0:T(8,128)S(1)}, f32[512,256]{1,0:T(8,128)S(1)}, f32[...) custom-call(s32[1,128]{1,0:T(1,128)S(1)} %broadcast_in_dim.12.lengths, bf16[4,256,256]{2,1,0:T(8,128)(2,1)S(1)} %get-tuple-element.58.qd, ...), custom_call_target="tpu_custom_call" | custom-call | flops 2000000000 | bytes 2097152 | tf_op jit(solution)/shard_map/rows/pallas_call | solution.py:358
  40.0 1.3 %collective-permute-start.9 = (f32[2,2,512]{2,1,0:T(2,128)S(1)}, f32[2,2,512]{2,1,0:T(2,128)S(1)}, u32[]{:S(2)}, u32[]{:S(2)}) collective-permute-start(f32[2,2,512]{2,1,0:T(2,128)S(1)} %get-tuple-element.65), channel_id=1, source_target_pairs={{8,0},{10,2},{12,4},{14,6},{16,8},{18,10},{20,12},{22,14},{24,16},... | collective-permute-start | bytes 24584 | tf_op jit(solution)/shard_map/ppermute | solution.py:321
  41.3 3.0 %collective-permute-done.3.kvp = bf16[4,256,256]{2,1,0:T(8,128)(2,1)S(1)} collective-permute-done((bf16[4,256,256]{2,1,0:T(8,128)(2,1)S(1)}, bf16[4,256,256]{2,1,0:T(8,128)(2,1)S(1)}, u32[]{:S(2)}, u32[]{:S(2)}) %collective-permute-start.3) | collective-permute-done | bytes 524320 | tf_op jit(solution)/shard_map/ppermute | solution.py:321
  44.4 3.4 %rows.3 = (bf16[4,128,256]{2,1,0:T(8,128)(2,1)S(1)}, f32[512,256]{1,0:T(8,128)S(1)}, f32[512,256]{1,0:T(8,128)S(1)}, f32[2,2,512]{2,1,0:T(2,128)S(1)}, f32[8,128]{1,0:T(8,128)S(1)}) custom-call(s32[1,128]{1,0:T(1,128)S(1)} %broadcast_in_dim.12.lengths, bf16[4,256,256]{2,1,0:T(8,128)(2,1)S(1)} %get-tuple-element.51.qd, ...), custom_call_target="tpu_custom_call" | custom-call | flops 2000000000 | bytes 2097152 | tf_op jit(solution)/shard_map/rows/pallas_call | solution.py:358
  47.8 0.9 %collective-permute-done.9.stats = f32[2,2,512]{2,1,0:T(2,128)S(1)} collective-permute-done((f32[2,2,512]{2,1,0:T(2,128)S(1)}, f32[2,2,512]{2,1,0:T(2,128)S(1)}, u32[]{:S(2)}, u32[]{:S(2)}) %collective-permute-start.9) | collective-permute-done | bytes 8224 | tf_op jit(solution)/shard_map/ppermute | solution.py:321
  48.7 1.4 %columns.2 = (bf16[512,256]{1,0:T(8,128)(2,1)S(1)}, bf16[512,256]{1,0:T(8,128)(2,1)S(1)}, bf16[512,256]{1,0:T(8,128)(2,1)S(1)}, bf16[512,256]{1,0:T(8,128)(2,1)S(1)}) custom-call(s32[1,128]{1,0:T(1,128)S(1)} %broadcast_in_dim.12.lengths, bf16[4,256,256]{2,1,0:T(8,128)(2,1)S(1)} %collective-permute-done.8.qd, bf16[4,272,256]{2,1,0:T(8,128)(2,1)S(1)} %get-tuple-element.59.kvo, ...), custom_call_target="tpu_custom_call" | custom-call | flops 4000000000 | bytes 2097152 | tf_op jit(solution)/shard_map/columns/pallas_call | solution.py:358
  50.1 1.5 %collective-permute-start.18 = (bf16[512,256]{1,0:T(8,128)(2,1)S(1)}, bf16[512,256]{1,0:T(8,128)(2,1)S(1)}, u32[]{:S(2)}, u32[]{:S(2)}) collective-permute-start(bf16[512,256]{1,0:T(8,128)(2,1)S(1)} %get-tuple-element.84), channel_id=1, source_target_pairs={{0,2},{2,0},{4,6},{6,4},{8,10},{10,8},{12,14},{14,12},{16,18},{18,... | collective-permute-start | bytes 786440 | tf_op jit(solution)/shard_map/ppermute | solution.py:315
  51.6 0.6 collective-permute-start.19
  52.2 1.5 %collective-permute-start.20 = (bf16[512,256]{1,0:T(8,128)(2,1)S(1)}, bf16[512,256]{1,0:T(8,128)(2,1)S(1)}, u32[]{:S(2)}, u32[]{:S(2)}) collective-permute-start(bf16[512,256]{1,0:T(8,128)(2,1)S(1)} %get-tuple-element.86), channel_id=1, source_target_pairs={{0,6},{2,4},{4,2},{6,0},{8,14},{10,12},{12,10},{14,8},{16,22},{18,... | collective-permute-start | bytes 786440 | tf_op jit(solution)/shard_map/ppermute | solution.py:315
  53.7 1.6 %collective-permute-start.10 = (f32[8,128]{1,0:T(8,128)S(1)}, f32[8,128]{1,0:T(8,128)S(1)}, u32[]{:S(2)}, u32[]{:S(2)}) collective-permute-start(f32[8,128]{1,0:T(8,128)S(1)} %get-tuple-element.71.a), channel_id=1, source_target_pairs={{0,8},{2,10},{4,12},{6,14},{8,0},{10,2},{12,4},{14,6},{16,24},{18,... | collective-permute-start | bytes 12296 | tf_op jit(solution)/shard_map/ppermute | solution.py:315
  55.2 0.0 collective-permute-done.13.qd
  55.2 1.3 %collective-permute-start.14 = (f32[2,2,512]{2,1,0:T(2,128)S(1)}, f32[2,2,512]{2,1,0:T(2,128)S(1)}, u32[]{:S(2)}, u32[]{:S(2)}) collective-permute-start(f32[2,2,512]{2,1,0:T(2,128)S(1)} %get-tuple-element.73), channel_id=1, source_target_pairs={{8,0},{10,2},{12,4},{14,6},{16,8},{18,10},{20,12},{22,14},{24,16},... | collective-permute-start | bytes 24584 | tf_op jit(solution)/shard_map/ppermute | solution.py:321
  56.5 0.8 %collective-permute-done.10.b = f32[8,128]{1,0:T(8,128)S(1)} collective-permute-done((f32[8,128]{1,0:T(8,128)S(1)}, f32[8,128]{1,0:T(8,128)S(1)}, u32[]{:S(2)}, u32[]{:S(2)}) %collective-permute-start.10) | collective-permute-done | bytes 4128 | tf_op jit(solution)/shard_map/ppermute | solution.py:315
  57.3 2.6 %collective-permute-start.11 = (f32[8,128]{1,0:T(8,128)S(1)}, f32[8,128]{1,0:T(8,128)S(1)}, u32[]{:S(2)}, u32[]{:S(2)}) collective-permute-start(f32[8,128]{1,0:T(8,128)S(1)} %add.3.a), channel_id=1, source_target_pairs={{0,16},{2,18},{4,20},{6,22},{8,24},{10,26},{12,28},{14,30},{16,0},... | collective-permute-start | bytes 12296 | tf_op jit(solution)/shard_map/ppermute | solution.py:315
  59.9 1.9 %collective-permute-done.11.b = f32[8,128]{1,0:T(8,128)S(1)} collective-permute-done((f32[8,128]{1,0:T(8,128)S(1)}, f32[8,128]{1,0:T(8,128)S(1)}, u32[]{:S(2)}, u32[]{:S(2)}) %collective-permute-start.11) | collective-permute-done | bytes 4128 | tf_op jit(solution)/shard_map/ppermute | solution.py:315
  61.8 0.0 collective-permute-start.12
  61.8 0.0 collective-permute-done.14.stats
  61.8 1.4 %columns.3 = (bf16[256,256]{1,0:T(8,128)(2,1)S(1)}, bf16[256,256]{1,0:T(8,128)(2,1)S(1)}, bf16[256,256]{1,0:T(8,128)(2,1)S(1)}, bf16[256,256]{1,0:T(8,128)(2,1)S(1)}) custom-call(s32[1,128]{1,0:T(1,128)S(1)} %broadcast_in_dim.12.lengths, bf16[4,256,256]{2,1,0:T(8,128)(2,1)S(1)} %collective-permute-done.13.qd, ...), custom_call_target="tpu_custom_call" | custom-call | bytes 2097152 | tf_op jit(solution)/shard_map/columns/pallas_call | solution.py:358
  63.2 0.0 collective-permute-done.12.b
  63.3 1.5 %collective-permute-start.15 = (bf16[272,256]{1,0:T(8,128)(2,1)S(1)}, bf16[272,256]{1,0:T(8,128)(2,1)S(1)}, u32[]{:S(2)}, u32[]{:S(2)}) collective-permute-start(bf16[272,256]{1,0:T(8,128)(2,1)S(1)} %get-tuple-element.81), channel_id=1, source_target_pairs={{0,2},{2,0},{4,6},{6,4},{8,10},{10,8},{12,14},{14,12},{16,18},{18,... | collective-permute-start | bytes 417800 | tf_op jit(solution)/shard_map/ppermute | solution.py:315
  64.8 0.6 collective-permute-start.16
  65.4 0.0 collective-permute-done.18.rest_1_
  65.4 1.5 %collective-permute-start.17 = (bf16[272,256]{1,0:T(8,128)(2,1)S(1)}, bf16[272,256]{1,0:T(8,128)(2,1)S(1)}, u32[]{:S(2)}, u32[]{:S(2)}) collective-permute-start(bf16[272,256]{1,0:T(8,128)(2,1)S(1)} %get-tuple-element.83), channel_id=1, source_target_pairs={{0,6},{2,4},{4,2},{6,0},{8,14},{10,12},{12,10},{14,8},{16,22},{18,... | collective-permute-start | bytes 417800 | tf_op jit(solution)/shard_map/ppermute | solution.py:315
  66.8 0.0 collective-permute-done.19.rest_2_
  66.8 0.0 collective-permute-done.20.rest_3_
  66.8 1.1 %unpack.2 = (bf16[1,128,2048]{2,1,0:T(8,128)(2,1)}, bf16[1,128,2048]{2,1,0:T(8,128)(2,1)}, bf16[1,128,2048]{2,1,0:T(8,128)(2,1)}) custom-call(bf16[512,256]{1,0:T(8,128)(2,1)S(1)} %get-tuple-element.70.rest_0_, bf16[512,256]{1,0:T(8,128)(2,1)S(1)} %collective-permute-done.18.rest_1_, bf16[512,256]{1,0:T(8,128)(2,1)S(1)} %collective-permute-done.19.rest_2_, ...), custom_call_target="tpu_custom_call" | custom-call | bytes 2097152 | tf_op jit(solution)/shard_map/unpack/pallas_call | solution.py:447
  67.9 1.9 %collective-permute-done.15.rest_1_ = bf16[272,256]{1,0:T(8,128)(2,1)S(1)} collective-permute-done((bf16[272,256]{1,0:T(8,128)(2,1)S(1)}, bf16[272,256]{1,0:T(8,128)(2,1)S(1)}, u32[]{:S(2)}, u32[]{:S(2)}) %collective-permute-start.15) | collective-permute-done | bytes 139296 | tf_op jit(solution)/shard_map/ppermute | solution.py:315
  69.8 3.7 %collective-permute-done.16.rest_2_ = bf16[272,256]{1,0:T(8,128)(2,1)S(1)} collective-permute-done((bf16[272,256]{1,0:T(8,128)(2,1)S(1)}, bf16[272,256]{1,0:T(8,128)(2,1)S(1)}, u32[]{:S(2)}, u32[]{:S(2)}) %collective-permute-start.16) | collective-permute-done | bytes 139296 | tf_op jit(solution)/shard_map/ppermute | solution.py:315
  73.6 0.0 collective-permute-done.17.rest_3_
  73.6 1.5 %unpack.3 = (bf16[1,128,2048]{2,1,0:T(8,128)(2,1)}, bf16[1,128,2048]{2,1,0:T(8,128)(2,1)}, bf16[1,128,2048]{2,1,0:T(8,128)(2,1)}, f32[16,64]{1,0:T(8,128)}) custom-call(bf16[272,256]{1,0:T(8,128)(2,1)S(1)} %get-tuple-element.80.rest_0_, ...), custom_call_target="tpu_custom_call", output_to_operand_aliasing={{0}: (4, {}), {1}: (5, {}), {2}: (6, {})} | custom-call | bytes 2097152 | tf_op jit(solution)/shard_map/unpack/pallas_call | solution.py:447
  (6 shorter events, 0.1 us)
Async XLA Ops:
  2.1 10.3 %collective-permute-start.4 = (bf16[528,256]{1,0:T(8,128)(2,1)S(1)}, bf16[528,256]{1,0:T(8,128)(2,1)S(1)}, u32[]{:S(2)}, u32[]{:S(2)}) collective-permute-start(bf16[528,256]{1,0:T(8,128)(2,1)S(1)} %get-tuple-element.55), channel_id=1, source_target_pairs={{0,2},{2,0},{4,6},{6,4},{8,10},{10,8},{12,14},{14,12},{16,18},{18,... | collective-permute-start | bytes 811016 | tf_op jit(solution)/shard_map/ppermute | solution.py:315
  5.1 15.2 %collective-permute-start.5 = (bf16[528,256]{1,0:T(8,128)(2,1)S(1)}, bf16[528,256]{1,0:T(8,128)(2,1)S(1)}, u32[]{:S(2)}, u32[]{:S(2)}) collective-permute-start(bf16[528,256]{1,0:T(8,128)(2,1)S(1)} %get-tuple-element.56), channel_id=1, source_target_pairs={{0,4},{2,6},{4,0},{6,2},{8,12},{10,14},{12,8},{14,10},{16,20},{18,... | collective-permute-start | bytes 811016 | tf_op jit(solution)/shard_map/ppermute | solution.py:315
  6.6 13.7 %collective-permute-start.6 = (bf16[528,256]{1,0:T(8,128)(2,1)S(1)}, bf16[528,256]{1,0:T(8,128)(2,1)S(1)}, u32[]{:S(2)}, u32[]{:S(2)}) collective-permute-start(bf16[528,256]{1,0:T(8,128)(2,1)S(1)} %get-tuple-element.57), channel_id=1, source_target_pairs={{0,6},{2,4},{4,2},{6,0},{8,14},{10,12},{12,10},{14,8},{16,22},{18,... | collective-permute-start | bytes 811016 | tf_op jit(solution)/shard_map/ppermute | solution.py:315
  8.0 17.1 %collective-permute-start = (bf16[512,256]{1,0:T(8,128)(2,1)S(1)}, bf16[512,256]{1,0:T(8,128)(2,1)S(1)}, u32[]{:S(2)}, u32[]{:S(2)}) collective-permute-start(bf16[512,256]{1,0:T(8,128)(2,1)S(1)} %get-tuple-element.48), channel_id=1, source_target_pairs={{0,2},{2,0},{4,6},{6,4},{8,10},{10,8},{12,14},{14,12},{16,18},{18,... | collective-permute-start | bytes 786440 | tf_op jit(solution)/shard_map/ppermute | solution.py:315
  10.0 20.0 %collective-permute-start.1 = (bf16[512,256]{1,0:T(8,128)(2,1)S(1)}, bf16[512,256]{1,0:T(8,128)(2,1)S(1)}, u32[]{:S(2)}, u32[]{:S(2)}) collective-permute-start(bf16[512,256]{1,0:T(8,128)(2,1)S(1)} %get-tuple-element.49), channel_id=1, source_target_pairs={{0,4},{2,6},{4,0},{6,2},{8,12},{10,14},{12,8},{14,10},{16,20},{18,... | collective-permute-start | bytes 786440 | tf_op jit(solution)/shard_map/ppermute | solution.py:315
  12.4 17.7 %collective-permute-start.2 = (bf16[512,256]{1,0:T(8,128)(2,1)S(1)}, bf16[512,256]{1,0:T(8,128)(2,1)S(1)}, u32[]{:S(2)}, u32[]{:S(2)}) collective-permute-start(bf16[512,256]{1,0:T(8,128)(2,1)S(1)} %get-tuple-element.50), channel_id=1, source_target_pairs={{0,6},{2,4},{4,2},{6,0},{8,14},{10,12},{12,10},{14,8},{16,22},{18,... | collective-permute-start | bytes 786440 | tf_op jit(solution)/shard_map/ppermute | solution.py:315
  20.3 16.3 %collective-permute-start.7 = (bf16[4,272,256]{2,1,0:T(8,128)(2,1)S(1)}, bf16[4,272,256]{2,1,0:T(8,128)(2,1)S(1)}, u32[]{:S(2)}, u32[]{:S(2)}) collective-permute-start(bf16[4,272,256]{2,1,0:T(8,128)(2,1)S(1)} %get-tuple-element.59.kvo), channel_id=1, source_target_pairs={{0,8},{2,10},{4,12},{6,14},{8,16},{10,18},{12,20},{14,22},{16,24},... | collective-permute-start | bytes 1671176 | tf_op jit(solution)/shard_map/ppermute | solution.py:321
  23.9 12.7 %collective-permute-start.8 = (bf16[4,256,256]{2,1,0:T(8,128)(2,1)S(1)}, bf16[4,256,256]{2,1,0:T(8,128)(2,1)S(1)}, u32[]{:S(2)}, u32[]{:S(2)}) collective-permute-start(bf16[4,256,256]{2,1,0:T(8,128)(2,1)S(1)} %get-tuple-element.58.qd), channel_id=1, source_target_pairs={{8,0},{10,2},{12,4},{14,6},{16,8},{18,10},{20,12},{22,14},{24,16},... | collective-permute-start | bytes 1572872 | tf_op jit(solution)/shard_map/ppermute | solution.py:321
  30.1 14.3 %collective-permute-start.3 = (bf16[4,256,256]{2,1,0:T(8,128)(2,1)S(1)}, bf16[4,256,256]{2,1,0:T(8,128)(2,1)S(1)}, u32[]{:S(2)}, u32[]{:S(2)}) collective-permute-start(bf16[4,256,256]{2,1,0:T(8,128)(2,1)S(1)} %get-tuple-element.52.kvo), channel_id=1, source_target_pairs={{0,8},{2,10},{4,12},{6,14},{8,16},{10,18},{12,20},{14,22},{16,24},... | collective-permute-start | bytes 1572872 | tf_op jit(solution)/shard_map/ppermute | solution.py:321
  34.3 2.3 %copy-start = (bf16[16,64]{1,0:T(8,128)(2,1)S(1)}, bf16[16,64]{1,0:T(8,128)(2,1)}, u32[]{:S(2)}) copy-start(bf16[16,64]{1,0:T(8,128)(2,1)} %bias_ref.7) | copy-start | bytes 6148
  34.3 20.9 %collective-permute-start.13 = (bf16[4,256,256]{2,1,0:T(8,128)(2,1)S(1)}, bf16[4,256,256]{2,1,0:T(8,128)(2,1)S(1)}, u32[]{:S(2)}, u32[]{:S(2)}) collective-permute-start(bf16[4,256,256]{2,1,0:T(8,128)(2,1)S(1)} %get-tuple-element.51.qd), channel_id=1, source_target_pairs={{8,0},{10,2},{12,4},{14,6},{16,8},{18,10},{20,12},{22,14},{24,16},... | collective-permute-start | bytes 1572872 | tf_op jit(solution)/shard_map/ppermute | solution.py:321
  40.0 8.7 %collective-permute-start.9 = (f32[2,2,512]{2,1,0:T(2,128)S(1)}, f32[2,2,512]{2,1,0:T(2,128)S(1)}, u32[]{:S(2)}, u32[]{:S(2)}) collective-permute-start(f32[2,2,512]{2,1,0:T(2,128)S(1)} %get-tuple-element.65), channel_id=1, source_target_pairs={{8,0},{10,2},{12,4},{14,6},{16,8},{18,10},{20,12},{22,14},{24,16},... | collective-permute-start | bytes 24584 | tf_op jit(solution)/shard_map/ppermute | solution.py:321
  50.1 15.2 %collective-permute-start.18 = (bf16[512,256]{1,0:T(8,128)(2,1)S(1)}, bf16[512,256]{1,0:T(8,128)(2,1)S(1)}, u32[]{:S(2)}, u32[]{:S(2)}) collective-permute-start(bf16[512,256]{1,0:T(8,128)(2,1)S(1)} %get-tuple-element.84), channel_id=1, source_target_pairs={{0,2},{2,0},{4,6},{6,4},{8,10},{10,8},{12,14},{14,12},{16,18},{18,... | collective-permute-start | bytes 786440 | tf_op jit(solution)/shard_map/ppermute | solution.py:315
  51.6 15.2 %collective-permute-start.19 = (bf16[512,256]{1,0:T(8,128)(2,1)S(1)}, bf16[512,256]{1,0:T(8,128)(2,1)S(1)}, u32[]{:S(2)}, u32[]{:S(2)}) collective-permute-start(bf16[512,256]{1,0:T(8,128)(2,1)S(1)} %get-tuple-element.85), channel_id=1, source_target_pairs={{0,4},{2,6},{4,0},{6,2},{8,12},{10,14},{12,8},{14,10},{16,20},{18,... | collective-permute-start | bytes 786440 | tf_op jit(solution)/shard_map/ppermute | solution.py:315
  52.2 14.7 %collective-permute-start.20 = (bf16[512,256]{1,0:T(8,128)(2,1)S(1)}, bf16[512,256]{1,0:T(8,128)(2,1)S(1)}, u32[]{:S(2)}, u32[]{:S(2)}) collective-permute-start(bf16[512,256]{1,0:T(8,128)(2,1)S(1)} %get-tuple-element.86), channel_id=1, source_target_pairs={{0,6},{2,4},{4,2},{6,0},{8,14},{10,12},{12,10},{14,8},{16,22},{18,... | collective-permute-start | bytes 786440 | tf_op jit(solution)/shard_map/ppermute | solution.py:315
  53.7 3.6 %collective-permute-start.10 = (f32[8,128]{1,0:T(8,128)S(1)}, f32[8,128]{1,0:T(8,128)S(1)}, u32[]{:S(2)}, u32[]{:S(2)}) collective-permute-start(f32[8,128]{1,0:T(8,128)S(1)} %get-tuple-element.71.a), channel_id=1, source_target_pairs={{0,8},{2,10},{4,12},{6,14},{8,0},{10,2},{12,4},{14,6},{16,24},{18,... | collective-permute-start | bytes 12296 | tf_op jit(solution)/shard_map/ppermute | solution.py:315
  55.2 6.6 %collective-permute-start.14 = (f32[2,2,512]{2,1,0:T(2,128)S(1)}, f32[2,2,512]{2,1,0:T(2,128)S(1)}, u32[]{:S(2)}, u32[]{:S(2)}) collective-permute-start(f32[2,2,512]{2,1,0:T(2,128)S(1)} %get-tuple-element.73), channel_id=1, source_target_pairs={{8,0},{10,2},{12,4},{14,6},{16,8},{18,10},{20,12},{22,14},{24,16},... | collective-permute-start | bytes 24584 | tf_op jit(solution)/shard_map/ppermute | solution.py:321
  57.3 4.5 %collective-permute-start.11 = (f32[8,128]{1,0:T(8,128)S(1)}, f32[8,128]{1,0:T(8,128)S(1)}, u32[]{:S(2)}, u32[]{:S(2)}) collective-permute-start(f32[8,128]{1,0:T(8,128)S(1)} %add.3.a), channel_id=1, source_target_pairs={{0,16},{2,18},{4,20},{6,22},{8,24},{10,26},{12,28},{14,30},{16,0},... | collective-permute-start | bytes 12296 | tf_op jit(solution)/shard_map/ppermute | solution.py:315
  61.8 1.4 %collective-permute-start.12 = (f32[8,128]{1,0:T(8,128)S(1)}, f32[8,128]{1,0:T(8,128)S(1)}, u32[]{:S(2)}, u32[]{:S(2)}) collective-permute-start(f32[8,128]{1,0:T(8,128)S(1)} %add.4.a), channel_id=1, source_target_pairs={{0,1},{1,0},{2,3},{3,2},{4,5},{5,4},{6,7},{7,6},{8,9},{9,8},{10,11... | collective-permute-start | bytes 12296 | tf_op jit(solution)/shard_map/ppermute | solution.py:315
  63.3 6.5 %collective-permute-start.15 = (bf16[272,256]{1,0:T(8,128)(2,1)S(1)}, bf16[272,256]{1,0:T(8,128)(2,1)S(1)}, u32[]{:S(2)}, u32[]{:S(2)}) collective-permute-start(bf16[272,256]{1,0:T(8,128)(2,1)S(1)} %get-tuple-element.81), channel_id=1, source_target_pairs={{0,2},{2,0},{4,6},{6,4},{8,10},{10,8},{12,14},{14,12},{16,18},{18,... | collective-permute-start | bytes 417800 | tf_op jit(solution)/shard_map/ppermute | solution.py:315
  64.8 8.8 %collective-permute-start.16 = (bf16[272,256]{1,0:T(8,128)(2,1)S(1)}, bf16[272,256]{1,0:T(8,128)(2,1)S(1)}, u32[]{:S(2)}, u32[]{:S(2)}) collective-permute-start(bf16[272,256]{1,0:T(8,128)(2,1)S(1)} %get-tuple-element.82), channel_id=1, source_target_pairs={{0,4},{2,6},{4,0},{6,2},{8,12},{10,14},{12,8},{14,10},{16,20},{18,... | collective-permute-start | bytes 417800 | tf_op jit(solution)/shard_map/ppermute | solution.py:315
  65.4 8.2 %collective-permute-start.17 = (bf16[272,256]{1,0:T(8,128)(2,1)S(1)}, bf16[272,256]{1,0:T(8,128)(2,1)S(1)}, u32[]{:S(2)}, u32[]{:S(2)}) collective-permute-start(bf16[272,256]{1,0:T(8,128)(2,1)S(1)} %get-tuple-element.83), channel_id=1, source_target_pairs={{0,6},{2,4},{4,2},{6,0},{8,14},{10,12},{12,10},{14,8},{16,22},{18,... | collective-permute-start | bytes 417800 | tf_op jit(solution)/shard_map/ppermute | solution.py:315

commit v6 on v5

--- a/solution.py
+++ b/solution.py
@@ -81,9 +81,12 @@
 
 
 def finish_kernel(reach, tok, group_width, blocks, *rest):
-    total, sems = rest[-2:]
-    join(reach, tok, len(blocks) * tok, place(reach)[0], rest[:reach], total)
-    unpack_kernel(reach, tok, group_width, blocks, *rest[:-2], sems)
+    total, sems, total_scr, total_sem = rest[-4:]
+    join(reach, tok, len(blocks) * tok, place(reach)[0], rest[:reach], total_scr)
+    copy = pltpu.make_async_copy(total_scr, total, total_sem)
+    copy.start()
+    unpack_kernel(reach, tok, group_width, blocks, *rest[:-4], sems)
+    copy.wait()
 
 
 def onehot_of(fields, slot, tok):
@@ -447,9 +450,10 @@
         grads = pl.pallas_call(
             functools.partial(kernel, reach, tok, group * HEAD_DIM, blocks[c]),
             in_specs=[VMEM] * reach + [ANY] * len(grads),
-            out_specs=[ANY] * 3 + [VMEM] * last,
+            out_specs=[ANY] * (3 + last),
             out_shape=out + [jax.ShapeDtypeStruct((HEADS, FIELDS), F32)] * last,
-            scratch_shapes=[pltpu.SemaphoreType.DMA((len(blocks[c]) * reach,))],
+            scratch_shapes=[pltpu.SemaphoreType.DMA((len(blocks[c]) * reach,))]
+            + [pltpu.VMEM((HEADS, FIELDS), F32), pltpu.SemaphoreType.DMA] * last,
             input_output_aliases={reach + at: at for at in range(len(grads))},
             compiler_params=params(2),
             cost_estimate=cost(0, 2 * MIB),

time: 75.4 us -> 74.8 us (level)
  transfers between devices with their start and end apart: 21 -> 21, of which waited for: 10 -> 10; matrix products, arithmetic and copies ran while one was open for 0% -> 0% of each run, Pallas kernels for 16% -> 17%
where the time goes in v6:
time: 74.8 us; the launch traced here: 74.4 us
  starting transfers between devices  34.5 us (46%)
  waiting for transfers between devices  23.9 us (32%)
  Pallas kernels  14.6 us (20%)
  between operations  1.45 us (2%)
    ppermute x15, starting transfers between devices, swapped(): lax.ppermute(value, axis, [(source, source ^ mask) for source in range(co...  22.3 us
    ppermute x15, waiting for transfers between devices, swapped(): lax.ppermute(value, axis, [(source, source ^ mask) for source in range(co...  18.9 us
    ppermute x6, starting transfers between devices, passed_along(): lax.ppermute(value, axis, [(source, source + steps) for source in range(f...  12.2 us
    pallas_call x10, Pallas kernels, local(): pl.pallas_call(kernel, in_specs=[VMEM] * len(args), out_specs=[VMEM] * le...  9.79 us
    ppermute x6, waiting for transfers between devices, passed_along(): lax.ppermute(value, axis, [(source, source + steps) for source in range(f...  5 us
    pallas_call x2, Pallas kernels, pack(): pl.pallas_call(functools.partial(pack_kernel, reach, tok, width, chunk),...  2.83 us
    pallas_call x2, Pallas kernels, shards(): pl.pallas_call(functools.partial(kernel, reach, tok, group * HEAD_DIM, bl...  1.96 us
  transfers between devices with their start and end apart: 21, of which 10 were waited for; matrix products, arithmetic and copies ran while one was open for 0% of the time, Pallas kernels for 17%

profile of v6, /device:TPU:0, one launch (start us, length us, event | category | flops | bytes accessed | tf_op | source)
XLA Modules:
  0.0 74.4 jit_solution(4746967365388531913)
XLA Ops:
  0.6 1.4 %pack.3 = (bf16[528,256]{1,0:T(8,128)(2,1)S(1)}, bf16[528,256]{1,0:T(8,128)(2,1)S(1)}, bf16[528,256]{1,0:T(8,128)(2,1)S(1)}, bf16[528,256]{1,0:T(8,128)(2,1)S(1)}) custom-call(bf16[1,128,2048]{2,1,0:T(8,128)(2,1)} %q.3, bf16[1,128,2048]{2,1,0:T(8,128)(2,1)} %g.3, bf16[1,128,2048]{2,1,0:T(8,128)(2,1)} %k.3, bf16[1,128,2048]{2,1,0:T(8,128)(2,1)} %v.3, ...), custom_call_target="tpu_custom_call" | custom-call | bytes 2097152 | tf_op jit(solution)/shard_map/pack/pallas_call | solution.py:346
  2.1 3.0 %collective-permute-start.4 = (bf16[528,256]{1,0:T(8,128)(2,1)S(1)}, bf16[528,256]{1,0:T(8,128)(2,1)S(1)}, u32[]{:S(2)}, u32[]{:S(2)}) collective-permute-start(bf16[528,256]{1,0:T(8,128)(2,1)S(1)} %get-tuple-element.55), channel_id=1, source_target_pairs={{0,2},{2,0},{4,6},{6,4},{8,10},{10,8},{12,14},{14,12},{16,18},{18,... | collective-permute-start | bytes 811016 | tf_op jit(solution)/shard_map/ppermute | solution.py:318
  5.1 1.5 %collective-permute-start.5 = (bf16[528,256]{1,0:T(8,128)(2,1)S(1)}, bf16[528,256]{1,0:T(8,128)(2,1)S(1)}, u32[]{:S(2)}, u32[]{:S(2)}) collective-permute-start(bf16[528,256]{1,0:T(8,128)(2,1)S(1)} %get-tuple-element.56), channel_id=1, source_target_pairs={{0,4},{2,6},{4,0},{6,2},{8,12},{10,14},{12,8},{14,10},{16,20},{18,... | collective-permute-start | bytes 811016 | tf_op jit(solution)/shard_map/ppermute | solution.py:318
  6.6 0.0 collective-permute-start.6
  6.6 1.4 %pack.2 = (bf16[512,256]{1,0:T(8,128)(2,1)S(1)}, bf16[512,256]{1,0:T(8,128)(2,1)S(1)}, bf16[512,256]{1,0:T(8,128)(2,1)S(1)}, bf16[512,256]{1,0:T(8,128)(2,1)S(1)}) custom-call(bf16[1,128,2048]{2,1,0:T(8,128)(2,1)} %q.3, bf16[1,128,2048]{2,1,0:T(8,128)(2,1)} %g.3, bf16[1,128,2048]{2,1,0:T(8,128)(2,1)} %k.3, bf16[1,128,2048]{2,1,0:T(8,128)(2,1)} %v.3, ...), custom_call_target="tpu_custom_call" | custom-call | bytes 2097152 | tf_op jit(solution)/shard_map/pack/pallas_call | solution.py:346
  8.0 2.0 %collective-permute-start = (bf16[512,256]{1,0:T(8,128)(2,1)S(1)}, bf16[512,256]{1,0:T(8,128)(2,1)S(1)}, u32[]{:S(2)}, u32[]{:S(2)}) collective-permute-start(bf16[512,256]{1,0:T(8,128)(2,1)S(1)} %get-tuple-element.48), channel_id=1, source_target_pairs={{0,2},{2,0},{4,6},{6,4},{8,10},{10,8},{12,14},{14,12},{16,18},{18,... | collective-permute-start | bytes 786440 | tf_op jit(solution)/shard_map/ppermute | solution.py:318
  10.0 1.5 %collective-permute-start.1 = (bf16[512,256]{1,0:T(8,128)(2,1)S(1)}, bf16[512,256]{1,0:T(8,128)(2,1)S(1)}, u32[]{:S(2)}, u32[]{:S(2)}) collective-permute-start(bf16[512,256]{1,0:T(8,128)(2,1)S(1)} %get-tuple-element.49), channel_id=1, source_target_pairs={{0,4},{2,6},{4,0},{6,2},{8,12},{10,14},{12,8},{14,10},{16,20},{18,... | collective-permute-start | bytes 786440 | tf_op jit(solution)/shard_map/ppermute | solution.py:318
  11.6 0.8 %collective-permute-done.4.refs_1_ = bf16[528,256]{1,0:T(8,128)(2,1)S(1)} collective-permute-done((bf16[528,256]{1,0:T(8,128)(2,1)S(1)}, bf16[528,256]{1,0:T(8,128)(2,1)S(1)}, u32[]{:S(2)}, u32[]{:S(2)}) %collective-permute-start.4) | collective-permute-done | bytes 270368 | tf_op jit(solution)/shard_map/ppermute | solution.py:318
  12.4 3.0 %collective-permute-start.2 = (bf16[512,256]{1,0:T(8,128)(2,1)S(1)}, bf16[512,256]{1,0:T(8,128)(2,1)S(1)}, u32[]{:S(2)}, u32[]{:S(2)}) collective-permute-start(bf16[512,256]{1,0:T(8,128)(2,1)S(1)} %get-tuple-element.50), channel_id=1, source_target_pairs={{0,6},{2,4},{4,2},{6,0},{8,14},{10,12},{12,10},{14,8},{16,22},{18,... | collective-permute-start | bytes 786440 | tf_op jit(solution)/shard_map/ppermute | solution.py:318
  15.4 4.9 %collective-permute-done.5.refs_2_ = bf16[528,256]{1,0:T(8,128)(2,1)S(1)} collective-permute-done((bf16[528,256]{1,0:T(8,128)(2,1)S(1)}, bf16[528,256]{1,0:T(8,128)(2,1)S(1)}, u32[]{:S(2)}, u32[]{:S(2)}) %collective-permute-start.5) | collective-permute-done | bytes 270368 | tf_op jit(solution)/shard_map/ppermute | solution.py:318
  20.3 0.0 collective-permute-done.6.refs_3_
  20.3 0.1 gather.3
  20.3 3.5 %collective-permute-start.7 = (bf16[4,272,256]{2,1,0:T(8,128)(2,1)S(1)}, bf16[4,272,256]{2,1,0:T(8,128)(2,1)S(1)}, u32[]{:S(2)}, u32[]{:S(2)}) collective-permute-start(bf16[4,272,256]{2,1,0:T(8,128)(2,1)S(1)} %get-tuple-element.59.kvo), channel_id=1, source_target_pairs={{0,8},{2,10},{4,12},{6,14},{8,16},{10,18},{12,20},{14,22},{16,24},... | collective-permute-start | bytes 1671176 | tf_op jit(solution)/shard_map/ppermute | solution.py:324
  23.9 1.3 %collective-permute-start.8 = (bf16[4,256,256]{2,1,0:T(8,128)(2,1)S(1)}, bf16[4,256,256]{2,1,0:T(8,128)(2,1)S(1)}, u32[]{:S(2)}, u32[]{:S(2)}) collective-permute-start(bf16[4,256,256]{2,1,0:T(8,128)(2,1)S(1)} %get-tuple-element.58.qd), channel_id=1, source_target_pairs={{8,0},{10,2},{12,4},{14,6},{16,8},{18,10},{20,12},{22,14},{24,16},... | collective-permute-start | bytes 1572872 | tf_op jit(solution)/shard_map/ppermute | solution.py:324
  25.2 0.0 collective-permute-done.refs_1_
  25.2 4.9 %collective-permute-done.1.refs_2_ = bf16[512,256]{1,0:T(8,128)(2,1)S(1)} collective-permute-done((bf16[512,256]{1,0:T(8,128)(2,1)S(1)}, bf16[512,256]{1,0:T(8,128)(2,1)S(1)}, u32[]{:S(2)}, u32[]{:S(2)}) %collective-permute-start.1) | collective-permute-done | bytes 262176 | tf_op jit(solution)/shard_map/ppermute | solution.py:318
  30.0 0.0 collective-permute-done.2.refs_3_
  30.0 0.1 gather.2
  30.1 3.5 %collective-permute-start.3 = (bf16[4,256,256]{2,1,0:T(8,128)(2,1)S(1)}, bf16[4,256,256]{2,1,0:T(8,128)(2,1)S(1)}, u32[]{:S(2)}, u32[]{:S(2)}) collective-permute-start(bf16[4,256,256]{2,1,0:T(8,128)(2,1)S(1)} %get-tuple-element.52.kvo), channel_id=1, source_target_pairs={{0,8},{2,10},{4,12},{6,14},{8,16},{10,18},{12,20},{14,22},{16,24},... | collective-permute-start | bytes 1572872 | tf_op jit(solution)/shard_map/ppermute | solution.py:324
  34.3 0.0 copy-start
  34.3 1.3 %collective-permute-start.13 = (bf16[4,256,256]{2,1,0:T(8,128)(2,1)S(1)}, bf16[4,256,256]{2,1,0:T(8,128)(2,1)S(1)}, u32[]{:S(2)}, u32[]{:S(2)}) collective-permute-start(bf16[4,256,256]{2,1,0:T(8,128)(2,1)S(1)} %get-tuple-element.51.qd), channel_id=1, source_target_pairs={{8,0},{10,2},{12,4},{14,6},{16,8},{18,10},{20,12},{22,14},{24,16},... | collective-permute-start | bytes 1572872 | tf_op jit(solution)/shard_map/ppermute | solution.py:324
  35.6 1.0 %collective-permute-done.8.qd = bf16[4,256,256]{2,1,0:T(8,128)(2,1)S(1)} collective-permute-done((bf16[4,256,256]{2,1,0:T(8,128)(2,1)S(1)}, bf16[4,256,256]{2,1,0:T(8,128)(2,1)S(1)}, u32[]{:S(2)}, u32[]{:S(2)}) %collective-permute-start.8) | collective-permute-done | bytes 524320 | tf_op jit(solution)/shard_map/ppermute | solution.py:324
  36.6 0.0 collective-permute-done.7.kvp
  36.6 0.0 copy-done
  36.6 3.4 %rows.2 = (bf16[1024,128]{1,0:T(8,128)(2,1)S(1)}, bf16[4,128,256]{2,1,0:T(8,128)(2,1)S(1)}, f32[512,256]{1,0:T(8,128)S(1)}, f32[512,256]{1,0:T(8,128)S(1)}, f32[...) custom-call(s32[1,128]{1,0:T(1,128)S(1)} %broadcast_in_dim.12.lengths, bf16[4,256,256]{2,1,0:T(8,128)(2,1)S(1)} %get-tuple-element.58.qd, ...), custom_call_target="tpu_custom_call" | custom-call | flops 2000000000 | bytes 2097152 | tf_op jit(solution)/shard_map/rows/pallas_call | solution.py:361
  40.0 1.3 %collective-permute-start.9 = (f32[2,2,512]{2,1,0:T(2,128)S(1)}, f32[2,2,512]{2,1,0:T(2,128)S(1)}, u32[]{:S(2)}, u32[]{:S(2)}) collective-permute-start(f32[2,2,512]{2,1,0:T(2,128)S(1)} %get-tuple-element.65), channel_id=1, source_target_pairs={{8,0},{10,2},{12,4},{14,6},{16,8},{18,10},{20,12},{22,14},{24,16},... | collective-permute-start | bytes 24584 | tf_op jit(solution)/shard_map/ppermute | solution.py:324
  41.3 3.0 %collective-permute-done.3.kvp = bf16[4,256,256]{2,1,0:T(8,128)(2,1)S(1)} collective-permute-done((bf16[4,256,256]{2,1,0:T(8,128)(2,1)S(1)}, bf16[4,256,256]{2,1,0:T(8,128)(2,1)S(1)}, u32[]{:S(2)}, u32[]{:S(2)}) %collective-permute-start.3) | collective-permute-done | bytes 524320 | tf_op jit(solution)/shard_map/ppermute | solution.py:324
  44.4 3.4 %rows.3 = (bf16[4,128,256]{2,1,0:T(8,128)(2,1)S(1)}, f32[512,256]{1,0:T(8,128)S(1)}, f32[512,256]{1,0:T(8,128)S(1)}, f32[2,2,512]{2,1,0:T(2,128)S(1)}, f32[8,128]{1,0:T(8,128)S(1)}) custom-call(s32[1,128]{1,0:T(1,128)S(1)} %broadcast_in_dim.12.lengths, bf16[4,256,256]{2,1,0:T(8,128)(2,1)S(1)} %get-tuple-element.51.qd, ...), custom_call_target="tpu_custom_call" | custom-call | flops 2000000000 | bytes 2097152 | tf_op jit(solution)/shard_map/rows/pallas_call | solution.py:361
  47.8 0.9 %collective-permute-done.9.stats = f32[2,2,512]{2,1,0:T(2,128)S(1)} collective-permute-done((f32[2,2,512]{2,1,0:T(2,128)S(1)}, f32[2,2,512]{2,1,0:T(2,128)S(1)}, u32[]{:S(2)}, u32[]{:S(2)}) %collective-permute-start.9) | collective-permute-done | bytes 8224 | tf_op jit(solution)/shard_map/ppermute | solution.py:324
  48.7 1.4 %columns.2 = (bf16[512,256]{1,0:T(8,128)(2,1)S(1)}, bf16[512,256]{1,0:T(8,128)(2,1)S(1)}, bf16[512,256]{1,0:T(8,128)(2,1)S(1)}, bf16[512,256]{1,0:T(8,128)(2,1)S(1)}) custom-call(s32[1,128]{1,0:T(1,128)S(1)} %broadcast_in_dim.12.lengths, bf16[4,256,256]{2,1,0:T(8,128)(2,1)S(1)} %collective-permute-done.8.qd, bf16[4,272,256]{2,1,0:T(8,128)(2,1)S(1)} %get-tuple-element.59.kvo, ...), custom_call_target="tpu_custom_call" | custom-call | flops 4000000000 | bytes 2097152 | tf_op jit(solution)/shard_map/columns/pallas_call | solution.py:361
  50.1 1.5 %collective-permute-start.18 = (bf16[512,256]{1,0:T(8,128)(2,1)S(1)}, bf16[512,256]{1,0:T(8,128)(2,1)S(1)}, u32[]{:S(2)}, u32[]{:S(2)}) collective-permute-start(bf16[512,256]{1,0:T(8,128)(2,1)S(1)} %get-tuple-element.84), channel_id=1, source_target_pairs={{0,2},{2,0},{4,6},{6,4},{8,10},{10,8},{12,14},{14,12},{16,18},{18,... | collective-permute-start | bytes 786440 | tf_op jit(solution)/shard_map/ppermute | solution.py:318
  51.6 0.6 collective-permute-start.19
  52.2 1.5 %collective-permute-start.20 = (bf16[512,256]{1,0:T(8,128)(2,1)S(1)}, bf16[512,256]{1,0:T(8,128)(2,1)S(1)}, u32[]{:S(2)}, u32[]{:S(2)}) collective-permute-start(bf16[512,256]{1,0:T(8,128)(2,1)S(1)} %get-tuple-element.86), channel_id=1, source_target_pairs={{0,6},{2,4},{4,2},{6,0},{8,14},{10,12},{12,10},{14,8},{16,22},{18,... | collective-permute-start | bytes 786440 | tf_op jit(solution)/shard_map/ppermute | solution.py:318
  53.7 1.6 %collective-permute-start.10 = (f32[8,128]{1,0:T(8,128)S(1)}, f32[8,128]{1,0:T(8,128)S(1)}, u32[]{:S(2)}, u32[]{:S(2)}) collective-permute-start(f32[8,128]{1,0:T(8,128)S(1)} %get-tuple-element.71.a), channel_id=1, source_target_pairs={{0,8},{2,10},{4,12},{6,14},{8,0},{10,2},{12,4},{14,6},{16,24},{18,... | collective-permute-start | bytes 12296 | tf_op jit(solution)/shard_map/ppermute | solution.py:318
  55.2 0.0 collective-permute-done.13.qd
  55.2 1.3 %collective-permute-start.14 = (f32[2,2,512]{2,1,0:T(2,128)S(1)}, f32[2,2,512]{2,1,0:T(2,128)S(1)}, u32[]{:S(2)}, u32[]{:S(2)}) collective-permute-start(f32[2,2,512]{2,1,0:T(2,128)S(1)} %get-tuple-element.73), channel_id=1, source_target_pairs={{8,0},{10,2},{12,4},{14,6},{16,8},{18,10},{20,12},{22,14},{24,16},... | collective-permute-start | bytes 24584 | tf_op jit(solution)/shard_map/ppermute | solution.py:324
  56.5 0.8 %collective-permute-done.10.b = f32[8,128]{1,0:T(8,128)S(1)} collective-permute-done((f32[8,128]{1,0:T(8,128)S(1)}, f32[8,128]{1,0:T(8,128)S(1)}, u32[]{:S(2)}, u32[]{:S(2)}) %collective-permute-start.10) | collective-permute-done | bytes 4128 | tf_op jit(solution)/shard_map/ppermute | solution.py:318
  57.3 2.6 %collective-permute-start.11 = (f32[8,128]{1,0:T(8,128)S(1)}, f32[8,128]{1,0:T(8,128)S(1)}, u32[]{:S(2)}, u32[]{:S(2)}) collective-permute-start(f32[8,128]{1,0:T(8,128)S(1)} %add.3.a), channel_id=1, source_target_pairs={{0,16},{2,18},{4,20},{6,22},{8,24},{10,26},{12,28},{14,30},{16,0},... | collective-permute-start | bytes 12296 | tf_op jit(solution)/shard_map/ppermute | solution.py:318
  59.9 1.9 %collective-permute-done.11.b = f32[8,128]{1,0:T(8,128)S(1)} collective-permute-done((f32[8,128]{1,0:T(8,128)S(1)}, f32[8,128]{1,0:T(8,128)S(1)}, u32[]{:S(2)}, u32[]{:S(2)}) %collective-permute-start.11) | collective-permute-done | bytes 4128 | tf_op jit(solution)/shard_map/ppermute | solution.py:318
  61.8 0.0 collective-permute-start.12
  61.8 0.0 collective-permute-done.14.stats
  61.8 1.4 %columns.3 = (bf16[256,256]{1,0:T(8,128)(2,1)S(1)}, bf16[256,256]{1,0:T(8,128)(2,1)S(1)}, bf16[256,256]{1,0:T(8,128)(2,1)S(1)}, bf16[256,256]{1,0:T(8,128)(2,1)S(1)}) custom-call(s32[1,128]{1,0:T(1,128)S(1)} %broadcast_in_dim.12.lengths, bf16[4,256,256]{2,1,0:T(8,128)(2,1)S(1)} %collective-permute-done.13.qd, ...), custom_call_target="tpu_custom_call" | custom-call | bytes 2097152 | tf_op jit(solution)/shard_map/columns/pallas_call | solution.py:361
  63.2 0.0 collective-permute-done.12.b
  63.3 1.5 %collective-permute-start.15 = (bf16[272,256]{1,0:T(8,128)(2,1)S(1)}, bf16[272,256]{1,0:T(8,128)(2,1)S(1)}, u32[]{:S(2)}, u32[]{:S(2)}) collective-permute-start(bf16[272,256]{1,0:T(8,128)(2,1)S(1)} %get-tuple-element.81), channel_id=1, source_target_pairs={{0,2},{2,0},{4,6},{6,4},{8,10},{10,8},{12,14},{14,12},{16,18},{18,... | collective-permute-start | bytes 417800 | tf_op jit(solution)/shard_map/ppermute | solution.py:318
  64.8 0.6 collective-permute-start.16
  65.4 0.0 collective-permute-done.18.rest_1_
  65.4 1.5 %collective-permute-start.17 = (bf16[272,256]{1,0:T(8,128)(2,1)S(1)}, bf16[272,256]{1,0:T(8,128)(2,1)S(1)}, u32[]{:S(2)}, u32[]{:S(2)}) collective-permute-start(bf16[272,256]{1,0:T(8,128)(2,1)S(1)} %get-tuple-element.83), channel_id=1, source_target_pairs={{0,6},{2,4},{4,2},{6,0},{8,14},{10,12},{12,10},{14,8},{16,22},{18,... | collective-permute-start | bytes 417800 | tf_op jit(solution)/shard_map/ppermute | solution.py:318
  66.8 0.0 collective-permute-done.19.rest_2_
  66.8 0.0 collective-permute-done.20.rest_3_
  66.8 1.1 %unpack.2 = (bf16[1,128,2048]{2,1,0:T(8,128)(2,1)}, bf16[1,128,2048]{2,1,0:T(8,128)(2,1)}, bf16[1,128,2048]{2,1,0:T(8,128)(2,1)}) custom-call(bf16[512,256]{1,0:T(8,128)(2,1)S(1)} %get-tuple-element.70.rest_0_, bf16[512,256]{1,0:T(8,128)(2,1)S(1)} %collective-permute-done.18.rest_1_, bf16[512,256]{1,0:T(8,128)(2,1)S(1)} %collective-permute-done.19.rest_2_, ...), custom_call_target="tpu_custom_call" | custom-call | bytes 2097152 | tf_op jit(solution)/shard_map/unpack/pallas_call | solution.py:450
  67.9 1.9 %collective-permute-done.15.rest_1_ = bf16[272,256]{1,0:T(8,128)(2,1)S(1)} collective-permute-done((bf16[272,256]{1,0:T(8,128)(2,1)S(1)}, bf16[272,256]{1,0:T(8,128)(2,1)S(1)}, u32[]{:S(2)}, u32[]{:S(2)}) %collective-permute-start.15) | collective-permute-done | bytes 139296 | tf_op jit(solution)/shard_map/ppermute | solution.py:318
  69.8 3.7 %collective-permute-done.16.rest_2_ = bf16[272,256]{1,0:T(8,128)(2,1)S(1)} collective-permute-done((bf16[272,256]{1,0:T(8,128)(2,1)S(1)}, bf16[272,256]{1,0:T(8,128)(2,1)S(1)}, u32[]{:S(2)}, u32[]{:S(2)}) %collective-permute-start.16) | collective-permute-done | bytes 139296 | tf_op jit(solution)/shard_map/ppermute | solution.py:318
  73.6 0.0 collective-permute-done.17.rest_3_
  73.6 0.9 %unpack.3 = (bf16[1,128,2048]{2,1,0:T(8,128)(2,1)}, bf16[1,128,2048]{2,1,0:T(8,128)(2,1)}, bf16[1,128,2048]{2,1,0:T(8,128)(2,1)}, f32[16,64]{1,0:T(8,128)}) custom-call(bf16[272,256]{1,0:T(8,128)(2,1)S(1)} %get-tuple-element.80.rest_0_, ...), custom_call_target="tpu_custom_call", output_to_operand_aliasing={{0}: (4, {}), {1}: (5, {}), {2}: (6, {})} | custom-call | bytes 2097152 | tf_op jit(solution)/shard_map/unpack/pallas_call | solution.py:450
  (6 shorter events, 0.1 us)
Async XLA Ops:
  2.1 10.3 %collective-permute-start.4 = (bf16[528,256]{1,0:T(8,128)(2,1)S(1)}, bf16[528,256]{1,0:T(8,128)(2,1)S(1)}, u32[]{:S(2)}, u32[]{:S(2)}) collective-permute-start(bf16[528,256]{1,0:T(8,128)(2,1)S(1)} %get-tuple-element.55), channel_id=1, source_target_pairs={{0,2},{2,0},{4,6},{6,4},{8,10},{10,8},{12,14},{14,12},{16,18},{18,... | collective-permute-start | bytes 811016 | tf_op jit(solution)/shard_map/ppermute | solution.py:318
  5.1 15.2 %collective-permute-start.5 = (bf16[528,256]{1,0:T(8,128)(2,1)S(1)}, bf16[528,256]{1,0:T(8,128)(2,1)S(1)}, u32[]{:S(2)}, u32[]{:S(2)}) collective-permute-start(bf16[528,256]{1,0:T(8,128)(2,1)S(1)} %get-tuple-element.56), channel_id=1, source_target_pairs={{0,4},{2,6},{4,0},{6,2},{8,12},{10,14},{12,8},{14,10},{16,20},{18,... | collective-permute-start | bytes 811016 | tf_op jit(solution)/shard_map/ppermute | solution.py:318
  6.6 13.7 %collective-permute-start.6 = (bf16[528,256]{1,0:T(8,128)(2,1)S(1)}, bf16[528,256]{1,0:T(8,128)(2,1)S(1)}, u32[]{:S(2)}, u32[]{:S(2)}) collective-permute-start(bf16[528,256]{1,0:T(8,128)(2,1)S(1)} %get-tuple-element.57), channel_id=1, source_target_pairs={{0,6},{2,4},{4,2},{6,0},{8,14},{10,12},{12,10},{14,8},{16,22},{18,... | collective-permute-start | bytes 811016 | tf_op jit(solution)/shard_map/ppermute | solution.py:318
  8.0 17.1 %collective-permute-start = (bf16[512,256]{1,0:T(8,128)(2,1)S(1)}, bf16[512,256]{1,0:T(8,128)(2,1)S(1)}, u32[]{:S(2)}, u32[]{:S(2)}) collective-permute-start(bf16[512,256]{1,0:T(8,128)(2,1)S(1)} %get-tuple-element.48), channel_id=1, source_target_pairs={{0,2},{2,0},{4,6},{6,4},{8,10},{10,8},{12,14},{14,12},{16,18},{18,... | collective-permute-start | bytes 786440 | tf_op jit(solution)/shard_map/ppermute | solution.py:318
  10.0 20.0 %collective-permute-start.1 = (bf16[512,256]{1,0:T(8,128)(2,1)S(1)}, bf16[512,256]{1,0:T(8,128)(2,1)S(1)}, u32[]{:S(2)}, u32[]{:S(2)}) collective-permute-start(bf16[512,256]{1,0:T(8,128)(2,1)S(1)} %get-tuple-element.49), channel_id=1, source_target_pairs={{0,4},{2,6},{4,0},{6,2},{8,12},{10,14},{12,8},{14,10},{16,20},{18,... | collective-permute-start | bytes 786440 | tf_op jit(solution)/shard_map/ppermute | solution.py:318
  12.4 17.7 %collective-permute-start.2 = (bf16[512,256]{1,0:T(8,128)(2,1)S(1)}, bf16[512,256]{1,0:T(8,128)(2,1)S(1)}, u32[]{:S(2)}, u32[]{:S(2)}) collective-permute-start(bf16[512,256]{1,0:T(8,128)(2,1)S(1)} %get-tuple-element.50), channel_id=1, source_target_pairs={{0,6},{2,4},{4,2},{6,0},{8,14},{10,12},{12,10},{14,8},{16,22},{18,... | collective-permute-start | bytes 786440 | tf_op jit(solution)/shard_map/ppermute | solution.py:318
  20.3 16.3 %collective-permute-start.7 = (bf16[4,272,256]{2,1,0:T(8,128)(2,1)S(1)}, bf16[4,272,256]{2,1,0:T(8,128)(2,1)S(1)}, u32[]{:S(2)}, u32[]{:S(2)}) collective-permute-start(bf16[4,272,256]{2,1,0:T(8,128)(2,1)S(1)} %get-tuple-element.59.kvo), channel_id=1, source_target_pairs={{0,8},{2,10},{4,12},{6,14},{8,16},{10,18},{12,20},{14,22},{16,24},... | collective-permute-start | bytes 1671176 | tf_op jit(solution)/shard_map/ppermute | solution.py:324
  23.9 12.7 %collective-permute-start.8 = (bf16[4,256,256]{2,1,0:T(8,128)(2,1)S(1)}, bf16[4,256,256]{2,1,0:T(8,128)(2,1)S(1)}, u32[]{:S(2)}, u32[]{:S(2)}) collective-permute-start(bf16[4,256,256]{2,1,0:T(8,128)(2,1)S(1)} %get-tuple-element.58.qd), channel_id=1, source_target_pairs={{8,0},{10,2},{12,4},{14,6},{16,8},{18,10},{20,12},{22,14},{24,16},... | collective-permute-start | bytes 1572872 | tf_op jit(solution)/shard_map/ppermute | solution.py:324
  30.1 14.3 %collective-permute-start.3 = (bf16[4,256,256]{2,1,0:T(8,128)(2,1)S(1)}, bf16[4,256,256]{2,1,0:T(8,128)(2,1)S(1)}, u32[]{:S(2)}, u32[]{:S(2)}) collective-permute-start(bf16[4,256,256]{2,1,0:T(8,128)(2,1)S(1)} %get-tuple-element.52.kvo), channel_id=1, source_target_pairs={{0,8},{2,10},{4,12},{6,14},{8,16},{10,18},{12,20},{14,22},{16,24},... | collective-permute-start | bytes 1572872 | tf_op jit(solution)/shard_map/ppermute | solution.py:324
  34.3 2.3 %copy-start = (bf16[16,64]{1,0:T(8,128)(2,1)S(1)}, bf16[16,64]{1,0:T(8,128)(2,1)}, u32[]{:S(2)}) copy-start(bf16[16,64]{1,0:T(8,128)(2,1)} %bias_ref.7) | copy-start | bytes 6148
  34.3 20.9 %collective-permute-start.13 = (bf16[4,256,256]{2,1,0:T(8,128)(2,1)S(1)}, bf16[4,256,256]{2,1,0:T(8,128)(2,1)S(1)}, u32[]{:S(2)}, u32[]{:S(2)}) collective-permute-start(bf16[4,256,256]{2,1,0:T(8,128)(2,1)S(1)} %get-tuple-element.51.qd), channel_id=1, source_target_pairs={{8,0},{10,2},{12,4},{14,6},{16,8},{18,10},{20,12},{22,14},{24,16},... | collective-permute-start | bytes 1572872 | tf_op jit(solution)/shard_map/ppermute | solution.py:324
  40.0 8.7 %collective-permute-start.9 = (f32[2,2,512]{2,1,0:T(2,128)S(1)}, f32[2,2,512]{2,1,0:T(2,128)S(1)}, u32[]{:S(2)}, u32[]{:S(2)}) collective-permute-start(f32[2,2,512]{2,1,0:T(2,128)S(1)} %get-tuple-element.65), channel_id=1, source_target_pairs={{8,0},{10,2},{12,4},{14,6},{16,8},{18,10},{20,12},{22,14},{24,16},... | collective-permute-start | bytes 24584 | tf_op jit(solution)/shard_map/ppermute | solution.py:324
  50.1 15.2 %collective-permute-start.18 = (bf16[512,256]{1,0:T(8,128)(2,1)S(1)}, bf16[512,256]{1,0:T(8,128)(2,1)S(1)}, u32[]{:S(2)}, u32[]{:S(2)}) collective-permute-start(bf16[512,256]{1,0:T(8,128)(2,1)S(1)} %get-tuple-element.84), channel_id=1, source_target_pairs={{0,2},{2,0},{4,6},{6,4},{8,10},{10,8},{12,14},{14,12},{16,18},{18,... | collective-permute-start | bytes 786440 | tf_op jit(solution)/shard_map/ppermute | solution.py:318
  51.6 15.2 %collective-permute-start.19 = (bf16[512,256]{1,0:T(8,128)(2,1)S(1)}, bf16[512,256]{1,0:T(8,128)(2,1)S(1)}, u32[]{:S(2)}, u32[]{:S(2)}) collective-permute-start(bf16[512,256]{1,0:T(8,128)(2,1)S(1)} %get-tuple-element.85), channel_id=1, source_target_pairs={{0,4},{2,6},{4,0},{6,2},{8,12},{10,14},{12,8},{14,10},{16,20},{18,... | collective-permute-start | bytes 786440 | tf_op jit(solution)/shard_map/ppermute | solution.py:318
  52.2 14.7 %collective-permute-start.20 = (bf16[512,256]{1,0:T(8,128)(2,1)S(1)}, bf16[512,256]{1,0:T(8,128)(2,1)S(1)}, u32[]{:S(2)}, u32[]{:S(2)}) collective-permute-start(bf16[512,256]{1,0:T(8,128)(2,1)S(1)} %get-tuple-element.86), channel_id=1, source_target_pairs={{0,6},{2,4},{4,2},{6,0},{8,14},{10,12},{12,10},{14,8},{16,22},{18,... | collective-permute-start | bytes 786440 | tf_op jit(solution)/shard_map/ppermute | solution.py:318
  53.7 3.6 %collective-permute-start.10 = (f32[8,128]{1,0:T(8,128)S(1)}, f32[8,128]{1,0:T(8,128)S(1)}, u32[]{:S(2)}, u32[]{:S(2)}) collective-permute-start(f32[8,128]{1,0:T(8,128)S(1)} %get-tuple-element.71.a), channel_id=1, source_target_pairs={{0,8},{2,10},{4,12},{6,14},{8,0},{10,2},{12,4},{14,6},{16,24},{18,... | collective-permute-start | bytes 12296 | tf_op jit(solution)/shard_map/ppermute | solution.py:318
  55.2 6.6 %collective-permute-start.14 = (f32[2,2,512]{2,1,0:T(2,128)S(1)}, f32[2,2,512]{2,1,0:T(2,128)S(1)}, u32[]{:S(2)}, u32[]{:S(2)}) collective-permute-start(f32[2,2,512]{2,1,0:T(2,128)S(1)} %get-tuple-element.73), channel_id=1, source_target_pairs={{8,0},{10,2},{12,4},{14,6},{16,8},{18,10},{20,12},{22,14},{24,16},... | collective-permute-start | bytes 24584 | tf_op jit(solution)/shard_map/ppermute | solution.py:324
  57.3 4.5 %collective-permute-start.11 = (f32[8,128]{1,0:T(8,128)S(1)}, f32[8,128]{1,0:T(8,128)S(1)}, u32[]{:S(2)}, u32[]{:S(2)}) collective-permute-start(f32[8,128]{1,0:T(8,128)S(1)} %add.3.a), channel_id=1, source_target_pairs={{0,16},{2,18},{4,20},{6,22},{8,24},{10,26},{12,28},{14,30},{16,0},... | collective-permute-start | bytes 12296 | tf_op jit(solution)/shard_map/ppermute | solution.py:318
  61.8 1.4 %collective-permute-start.12 = (f32[8,128]{1,0:T(8,128)S(1)}, f32[8,128]{1,0:T(8,128)S(1)}, u32[]{:S(2)}, u32[]{:S(2)}) collective-permute-start(f32[8,128]{1,0:T(8,128)S(1)} %add.4.a), channel_id=1, source_target_pairs={{0,1},{1,0},{2,3},{3,2},{4,5},{5,4},{6,7},{7,6},{8,9},{9,8},{10,11... | collective-permute-start | bytes 12296 | tf_op jit(solution)/shard_map/ppermute | solution.py:318
  63.3 6.5 %collective-permute-start.15 = (bf16[272,256]{1,0:T(8,128)(2,1)S(1)}, bf16[272,256]{1,0:T(8,128)(2,1)S(1)}, u32[]{:S(2)}, u32[]{:S(2)}) collective-permute-start(bf16[272,256]{1,0:T(8,128)(2,1)S(1)} %get-tuple-element.81), channel_id=1, source_target_pairs={{0,2},{2,0},{4,6},{6,4},{8,10},{10,8},{12,14},{14,12},{16,18},{18,... | collective-permute-start | bytes 417800 | tf_op jit(solution)/shard_map/ppermute | solution.py:318
  64.8 8.8 %collective-permute-start.16 = (bf16[272,256]{1,0:T(8,128)(2,1)S(1)}, bf16[272,256]{1,0:T(8,128)(2,1)S(1)}, u32[]{:S(2)}, u32[]{:S(2)}) collective-permute-start(bf16[272,256]{1,0:T(8,128)(2,1)S(1)} %get-tuple-element.82), channel_id=1, source_target_pairs={{0,4},{2,6},{4,0},{6,2},{8,12},{10,14},{12,8},{14,10},{16,20},{18,... | collective-permute-start | bytes 417800 | tf_op jit(solution)/shard_map/ppermute | solution.py:318
  65.4 8.2 %collective-permute-start.17 = (bf16[272,256]{1,0:T(8,128)(2,1)S(1)}, bf16[272,256]{1,0:T(8,128)(2,1)S(1)}, u32[]{:S(2)}, u32[]{:S(2)}) collective-permute-start(bf16[272,256]{1,0:T(8,128)(2,1)S(1)} %get-tuple-element.83), channel_id=1, source_target_pairs={{0,6},{2,4},{4,2},{6,0},{8,14},{10,12},{12,10},{14,8},{16,22},{18,... | collective-permute-start | bytes 417800 | tf_op jit(solution)/shard_map/ppermute | solution.py:318

commit v7 on v6

--- a/solution.py
+++ b/solution.py
@@ -37,16 +37,16 @@
     return lax.rem(index, reach), lax.div(index, reach)
 
 
-def pack_kernel(reach, tok, width, chunk, q, g, k, v, fields, *rest):
-    outs, field_scr, sems = rest[:reach], rest[-2], rest[-1]
+def pack_kernel(reach, tok, width, wanted, q, g, k, v, fields, *rest):
+    outs, field_scr, sems = rest[: len(wanted)], rest[-2], rest[-1]
     p, _ = place(reach)
-    field_copy = pltpu.make_async_copy(fields, field_scr, sems.at[4 * reach])
+    field_copy = pltpu.make_async_copy(fields, field_scr, sems.at[4 * len(wanted)])
     field_copy.start()
     copies = []
-    for m in list(range(1, reach)) + [0]:
+    for out, (m, chunk) in zip(outs, wanted):
         first = pl.multiple_of((p ^ m) * (HEADS // reach * HEAD_DIM) + chunk * width, 128)
         for at, src in enumerate((q, g, k, v)):
-            dst = outs[m].at[pl.ds(at * tok, tok)]
+            dst = out.at[pl.ds(at * tok, tok)]
             copies.append(pltpu.make_async_copy(src.at[0, :, pl.ds(first, width)], dst, sems.at[len(copies)]))
             copies[-1].start()
     field_copy.wait()
@@ -65,27 +65,26 @@
         kv[m] = arrived[m][2 * tok :]
 
 
-def unpack_kernel(reach, tok, group_width, blocks, *rest):
-    parts, outs, sems = rest[:reach], rest[-4:-1], rest[-1]
+def unpack_kernel(reach, tok, group_width, moves, *rest):
+    outs, sems = rest[-4:-1], rest[-1]
     p, _ = place(reach)
-    width = parts[0].shape[1]
+    width = rest[0].shape[1]
     copies = []
-    for m in range(reach):
-        for at, (which, chunk) in enumerate(blocks):
-            first = pl.multiple_of((p ^ m) * group_width + chunk * width, 128)
-            dst = outs[which].at[0, :, pl.ds(first, width)]
-            copies.append(pltpu.make_async_copy(parts[m].at[pl.ds(at * tok, tok)], dst, sems.at[len(copies)]))
-            copies[-1].start()
+    for i, m, at, which, chunk in moves:
+        first = pl.multiple_of((p ^ m) * group_width + chunk * width, 128)
+        dst = outs[which].at[0, :, pl.ds(first, width)]
+        copies.append(pltpu.make_async_copy(rest[i].at[pl.ds(at * tok, tok)], dst, sems.at[len(copies)]))
+        copies[-1].start()
     for copy in copies:
         copy.wait()
 
 
-def finish_kernel(reach, tok, group_width, blocks, *rest):
+def finish_kernel(reach, tok, group_width, moves, *rest):
     total, sems, total_scr, total_sem = rest[-4:]
-    join(reach, tok, len(blocks) * tok, place(reach)[0], rest[:reach], total_scr)
+    join(reach, tok, 2 * tok, place(reach)[0], rest[:reach], total_scr)
     copy = pltpu.make_async_copy(total_scr, total, total_sem)
     copy.start()
-    unpack_kernel(reach, tok, group_width, blocks, *rest[:-4], sems)
+    unpack_kernel(reach, tok, group_width, moves, *rest[:-4], sems)
     copy.wait()
 
 
@@ -342,15 +341,15 @@
     def pad(chunk):
         return 0 if chunk else PAD
 
-    def pack(chunk):
+    def pack(wanted):
         return pl.pallas_call(
-            functools.partial(pack_kernel, reach, tok, width, chunk),
+            functools.partial(pack_kernel, reach, tok, width, wanted),
             in_specs=[ANY] * 5,
-            out_specs=[VMEM] * reach,
-            out_shape=[pltpu.VMEM((4 * tok + pad(chunk), width), BF16)] * reach,
+            out_specs=[VMEM] * len(wanted),
+            out_shape=[vmem((4 * tok + pad(chunk), width)) for _, chunk in wanted],
             scratch_shapes=[
                 pltpu.VMEM((1, tok), jnp.int32),
-                pltpu.SemaphoreType.DMA((4 * reach + 1,)),
+                pltpu.SemaphoreType.DMA((4 * len(wanted) + 1,)),
             ],
             compiler_params=params(2),
             cost_estimate=cost(0, 2 * MIB),
@@ -408,8 +407,10 @@
     def add(a, b):
         return local(functools.partial(add_kernel, reach, tok), "add", 0, [vmem(a.shape, F32)], a, b)[0]
 
-    packed = [list(pack(c)) for c in range(CHUNKS)]
-    packed[0][0] = following(packed[0][0], packed[1][0])
+    sent = list(range(1, reach))
+    first = pack([(m, 0) for m in sent])
+    *second, own, own_first = pack([(m, 1) for m in sent] + [(0, 1), (0, 0)])
+    packed = [[own_first, *first], [own, *second]]
     planes, before, after = [], [], []
     for c in range(CHUNKS):
         arrived = packed[c][:1] + [swapped(packed[c][m], "seq", m) for m in range(1, reach)]
@@ -442,17 +443,20 @@
     parts = [[own[0]] + [swapped(own[m], "seq", m) for m in range(1, reach)] for own in messages]
 
     blocks = [((1, 0), (2, 0), (0, 0), (0, 1)), ((1, 1), (2, 1))]
+    moves = [[(m, m, at, *to) for m in range(c, reach) for at, to in enumerate(blocks[c])] for c in range(CHUNKS)]
+    moves[0] += [(reach, 0, at, *to) for at, to in enumerate(blocks[1])]
+    parts[0].append(parts[1][0])
     grads = []
     for c in range(CHUNKS):
         last = c == CHUNKS - 1
         kernel = finish_kernel if last else unpack_kernel
         out = [jax.ShapeDtypeStruct((1, tok, row_width), BF16)] * 3
         grads = pl.pallas_call(
-            functools.partial(kernel, reach, tok, group * HEAD_DIM, blocks[c]),
-            in_specs=[VMEM] * reach + [ANY] * len(grads),
+            functools.partial(kernel, reach, tok, group * HEAD_DIM, moves[c]),
+            in_specs=[VMEM] * len(parts[c]) + [ANY] * len(grads),
             out_specs=[ANY] * (3 + last),
             out_shape=out + [jax.ShapeDtypeStruct((HEADS, FIELDS), F32)] * last,
-            scratch_shapes=[pltpu.SemaphoreType.DMA((len(blocks[c]) * reach,))]
+            scratch_shapes=[pltpu.SemaphoreType.DMA((len(moves[c]),))]
             + [pltpu.VMEM((HEADS, FIELDS), F32), pltpu.SemaphoreType.DMA] * last,
             input_output_aliases={reach + at: at for at in range(len(grads))},
             compiler_params=params(2),

time: 74.8 us -> 74.7 us (level)
  no operation moved by 1% of the time
where the time goes in v7:
time: 74.7 us; the launch traced here: 74.2 us
  starting transfers between devices  34.5 us (46%)
  waiting for transfers between devices  23.7 us (32%)
  Pallas kernels  14.6 us (20%)
  between operations  1.45 us (2%)
    ppermute x15, starting transfers between devices, swapped(): lax.ppermute(value, axis, [(source, source ^ mask) for source in range(co...  22.4 us
    ppermute x15, waiting for transfers between devices, swapped(): lax.ppermute(value, axis, [(source, source ^ mask) for source in range(co...  18.7 us
    ppermute x6, starting transfers between devices, passed_along(): lax.ppermute(value, axis, [(source, source + steps) for source in range(f...  12.2 us
    pallas_call x10, Pallas kernels, local(): pl.pallas_call(kernel, in_specs=[VMEM] * len(args), out_specs=[VMEM] * le...  9.8 us
    ppermute x6, waiting for transfers between devices, passed_along(): lax.ppermute(value, axis, [(source, source + steps) for source in range(f...  4.99 us
    pallas_call x2, Pallas kernels, pack(): pl.pallas_call(functools.partial(pack_kernel, reach, tok, width, wanted),...  2.82 us
    pallas_call x2, Pallas kernels, shards(): pl.pallas_call(functools.partial(kernel, reach, tok, group * HEAD_DIM, mo...  1.96 us
  transfers between devices with their start and end apart: 21, of which 10 were waited for; matrix products, arithmetic and copies ran while one was open for 0% of the time, Pallas kernels for 17%

profile of v7, /device:TPU:0, one launch (start us, length us, event | category | flops | bytes accessed | tf_op | source)
XLA Modules:
  0.0 74.2 jit_solution(15227996622842168466)
XLA Ops:
  0.6 1.3 %pack.3 = (bf16[528,256]{1,0:T(8,128)(2,1)S(1)}, bf16[528,256]{1,0:T(8,128)(2,1)S(1)}, bf16[528,256]{1,0:T(8,128)(2,1)S(1)}) custom-call(bf16[1,128,2048]{2,1,0:T(8,128)(2,1)} %q.3, bf16[1,128,2048]{2,1,0:T(8,128)(2,1)} %g.3, bf16[1,128,2048]{2,1,0:T(8,128)(2,1)} %k.3, bf16[1,128,2048]{2,1,0:T(8,128)(2,1)} %v.3, s32[1,128]{1,0:T(1,128)} %fields.3), custom_call_target="tpu_custom_call" | custom-call | bytes 2097152 | tf_op jit(solution)/shard_map/pack/pallas_call | solution.py:345
  1.9 3.0 %collective-permute-start.4 = (bf16[528,256]{1,0:T(8,128)(2,1)S(1)}, bf16[528,256]{1,0:T(8,128)(2,1)S(1)}, u32[]{:S(2)}, u32[]{:S(2)}) collective-permute-start(bf16[528,256]{1,0:T(8,128)(2,1)S(1)} %get-tuple-element.53), channel_id=1, source_target_pairs={{0,2},{2,0},{4,6},{6,4},{8,10},{10,8},{12,14},{14,12},{16,18},{18,... | collective-permute-start | bytes 811016 | tf_op jit(solution)/shard_map/ppermute | solution.py:317
  4.9 1.5 %collective-permute-start.5 = (bf16[528,256]{1,0:T(8,128)(2,1)S(1)}, bf16[528,256]{1,0:T(8,128)(2,1)S(1)}, u32[]{:S(2)}, u32[]{:S(2)}) collective-permute-start(bf16[528,256]{1,0:T(8,128)(2,1)S(1)} %get-tuple-element.54), channel_id=1, source_target_pairs={{0,4},{2,6},{4,0},{6,2},{8,12},{10,14},{12,8},{14,10},{16,20},{18,... | collective-permute-start | bytes 811016 | tf_op jit(solution)/shard_map/ppermute | solution.py:317
  6.5 0.0 collective-permute-start.6
  6.5 1.5 %pack.2 = (bf16[512,256]{1,0:T(8,128)(2,1)S(1)}, bf16[512,256]{1,0:T(8,128)(2,1)S(1)}, bf16[512,256]{1,0:T(8,128)(2,1)S(1)}, bf16[512,256]{1,0:T(8,128)(2,1)S(1)}, bf16[528,256]{1,0:T(8,128)(2,1)S(1)}) custom-call(bf16[1,128,2048]{2,1,0:T(8,128)(2,1)} %q.3, bf16[1,128,2048]{2,1,0:T(8,128)(2,1)} %g.3, bf16[1,128,2048]{2,1,0:T(8,128)(2,1)} %k.3, ...), custom_call_target="tpu_custom_call" | custom-call | bytes 2097152 | tf_op jit(solution)/shard_map/pack/pallas_call | solution.py:345
  8.0 2.0 %collective-permute-start = (bf16[512,256]{1,0:T(8,128)(2,1)S(1)}, bf16[512,256]{1,0:T(8,128)(2,1)S(1)}, u32[]{:S(2)}, u32[]{:S(2)}) collective-permute-start(bf16[512,256]{1,0:T(8,128)(2,1)S(1)} %get-tuple-element.47), channel_id=1, source_target_pairs={{0,2},{2,0},{4,6},{6,4},{8,10},{10,8},{12,14},{14,12},{16,18},{18,... | collective-permute-start | bytes 786440 | tf_op jit(solution)/shard_map/ppermute | solution.py:317
  10.0 1.5 %collective-permute-start.1 = (bf16[512,256]{1,0:T(8,128)(2,1)S(1)}, bf16[512,256]{1,0:T(8,128)(2,1)S(1)}, u32[]{:S(2)}, u32[]{:S(2)}) collective-permute-start(bf16[512,256]{1,0:T(8,128)(2,1)S(1)} %get-tuple-element.48), channel_id=1, source_target_pairs={{0,4},{2,6},{4,0},{6,2},{8,12},{10,14},{12,8},{14,10},{16,20},{18,... | collective-permute-start | bytes 786440 | tf_op jit(solution)/shard_map/ppermute | solution.py:317
  11.5 0.7 collective-permute-done.4.refs_1_
  12.2 3.0 %collective-permute-start.2 = (bf16[512,256]{1,0:T(8,128)(2,1)S(1)}, bf16[512,256]{1,0:T(8,128)(2,1)S(1)}, u32[]{:S(2)}, u32[]{:S(2)}) collective-permute-start(bf16[512,256]{1,0:T(8,128)(2,1)S(1)} %get-tuple-element.49), channel_id=1, source_target_pairs={{0,6},{2,4},{4,2},{6,0},{8,14},{10,12},{12,10},{14,8},{16,22},{18,... | collective-permute-start | bytes 786440 | tf_op jit(solution)/shard_map/ppermute | solution.py:317
  15.3 4.9 %collective-permute-done.5.refs_2_ = bf16[528,256]{1,0:T(8,128)(2,1)S(1)} collective-permute-done((bf16[528,256]{1,0:T(8,128)(2,1)S(1)}, bf16[528,256]{1,0:T(8,128)(2,1)S(1)}, u32[]{:S(2)}, u32[]{:S(2)}) %collective-permute-start.5) | collective-permute-done | bytes 270368 | tf_op jit(solution)/shard_map/ppermute | solution.py:317
  20.1 0.0 collective-permute-done.6.refs_3_
  20.1 0.1 gather.3
  20.2 3.5 %collective-permute-start.7 = (bf16[4,272,256]{2,1,0:T(8,128)(2,1)S(1)}, bf16[4,272,256]{2,1,0:T(8,128)(2,1)S(1)}, u32[]{:S(2)}, u32[]{:S(2)}) collective-permute-start(bf16[4,272,256]{2,1,0:T(8,128)(2,1)S(1)} %get-tuple-element.57.kvo), channel_id=1, source_target_pairs={{0,8},{2,10},{4,12},{6,14},{8,16},{10,18},{12,20},{14,22},{16,24},... | collective-permute-start | bytes 1671176 | tf_op jit(solution)/shard_map/ppermute | solution.py:323
  23.7 1.3 %collective-permute-start.8 = (bf16[4,256,256]{2,1,0:T(8,128)(2,1)S(1)}, bf16[4,256,256]{2,1,0:T(8,128)(2,1)S(1)}, u32[]{:S(2)}, u32[]{:S(2)}) collective-permute-start(bf16[4,256,256]{2,1,0:T(8,128)(2,1)S(1)} %get-tuple-element.56.qd), channel_id=1, source_target_pairs={{8,0},{10,2},{12,4},{14,6},{16,8},{18,10},{20,12},{22,14},{24,16},... | collective-permute-start | bytes 1572872 | tf_op jit(solution)/shard_map/ppermute | solution.py:323
  25.0 0.0 collective-permute-done.refs_1_
  25.1 4.9 %collective-permute-done.1.refs_2_ = bf16[512,256]{1,0:T(8,128)(2,1)S(1)} collective-permute-done((bf16[512,256]{1,0:T(8,128)(2,1)S(1)}, bf16[512,256]{1,0:T(8,128)(2,1)S(1)}, u32[]{:S(2)}, u32[]{:S(2)}) %collective-permute-start.1) | collective-permute-done | bytes 262176 | tf_op jit(solution)/shard_map/ppermute | solution.py:317
  29.9 0.0 collective-permute-done.2.refs_3_
  29.9 0.1 gather.2
  30.0 3.5 %collective-permute-start.3 = (bf16[4,256,256]{2,1,0:T(8,128)(2,1)S(1)}, bf16[4,256,256]{2,1,0:T(8,128)(2,1)S(1)}, u32[]{:S(2)}, u32[]{:S(2)}) collective-permute-start(bf16[4,256,256]{2,1,0:T(8,128)(2,1)S(1)} %get-tuple-element.51.kvo), channel_id=1, source_target_pairs={{0,8},{2,10},{4,12},{6,14},{8,16},{10,18},{12,20},{14,22},{16,24},... | collective-permute-start | bytes 1572872 | tf_op jit(solution)/shard_map/ppermute | solution.py:323
  34.2 0.0 copy-start
  34.2 1.3 %collective-permute-start.13 = (bf16[4,256,256]{2,1,0:T(8,128)(2,1)S(1)}, bf16[4,256,256]{2,1,0:T(8,128)(2,1)S(1)}, u32[]{:S(2)}, u32[]{:S(2)}) collective-permute-start(bf16[4,256,256]{2,1,0:T(8,128)(2,1)S(1)} %get-tuple-element.50.qd), channel_id=1, source_target_pairs={{8,0},{10,2},{12,4},{14,6},{16,8},{18,10},{20,12},{22,14},{24,16},... | collective-permute-start | bytes 1572872 | tf_op jit(solution)/shard_map/ppermute | solution.py:323
  35.5 1.0 %collective-permute-done.8.qd = bf16[4,256,256]{2,1,0:T(8,128)(2,1)S(1)} collective-permute-done((bf16[4,256,256]{2,1,0:T(8,128)(2,1)S(1)}, bf16[4,256,256]{2,1,0:T(8,128)(2,1)S(1)}, u32[]{:S(2)}, u32[]{:S(2)}) %collective-permute-start.8) | collective-permute-done | bytes 524320 | tf_op jit(solution)/shard_map/ppermute | solution.py:323
  36.5 0.0 collective-permute-done.7.kvp
  36.5 0.0 copy-done
  36.5 3.4 %rows.2 = (bf16[1024,128]{1,0:T(8,128)(2,1)S(1)}, bf16[4,128,256]{2,1,0:T(8,128)(2,1)S(1)}, f32[512,256]{1,0:T(8,128)S(1)}, f32[512,256]{1,0:T(8,128)S(1)}, f32[...) custom-call(s32[1,128]{1,0:T(1,128)S(1)} %broadcast_in_dim.12.lengths, bf16[4,256,256]{2,1,0:T(8,128)(2,1)S(1)} %get-tuple-element.56.qd, ...), custom_call_target="tpu_custom_call" | custom-call | flops 2000000000 | bytes 2097152 | tf_op jit(solution)/shard_map/rows/pallas_call | solution.py:360
  39.9 1.3 %collective-permute-start.9 = (f32[2,2,512]{2,1,0:T(2,128)S(1)}, f32[2,2,512]{2,1,0:T(2,128)S(1)}, u32[]{:S(2)}, u32[]{:S(2)}) collective-permute-start(f32[2,2,512]{2,1,0:T(2,128)S(1)} %get-tuple-element.63), channel_id=1, source_target_pairs={{8,0},{10,2},{12,4},{14,6},{16,8},{18,10},{20,12},{22,14},{24,16},... | collective-permute-start | bytes 24584 | tf_op jit(solution)/shard_map/ppermute | solution.py:323
  41.2 3.0 %collective-permute-done.3.kvp = bf16[4,256,256]{2,1,0:T(8,128)(2,1)S(1)} collective-permute-done((bf16[4,256,256]{2,1,0:T(8,128)(2,1)S(1)}, bf16[4,256,256]{2,1,0:T(8,128)(2,1)S(1)}, u32[]{:S(2)}, u32[]{:S(2)}) %collective-permute-start.3) | collective-permute-done | bytes 524320 | tf_op jit(solution)/shard_map/ppermute | solution.py:323
  44.3 3.4 %rows.3 = (bf16[4,128,256]{2,1,0:T(8,128)(2,1)S(1)}, f32[512,256]{1,0:T(8,128)S(1)}, f32[512,256]{1,0:T(8,128)S(1)}, f32[2,2,512]{2,1,0:T(2,128)S(1)}, f32[8,128]{1,0:T(8,128)S(1)}) custom-call(s32[1,128]{1,0:T(1,128)S(1)} %broadcast_in_dim.12.lengths, bf16[4,256,256]{2,1,0:T(8,128)(2,1)S(1)} %get-tuple-element.50.qd, ...), custom_call_target="tpu_custom_call" | custom-call | flops 2000000000 | bytes 2097152 | tf_op jit(solution)/shard_map/rows/pallas_call | solution.py:360
  47.6 0.9 %collective-permute-done.9.stats = f32[2,2,512]{2,1,0:T(2,128)S(1)} collective-permute-done((f32[2,2,512]{2,1,0:T(2,128)S(1)}, f32[2,2,512]{2,1,0:T(2,128)S(1)}, u32[]{:S(2)}, u32[]{:S(2)}) %collective-permute-start.9) | collective-permute-done | bytes 8224 | tf_op jit(solution)/shard_map/ppermute | solution.py:323
  48.6 1.4 %columns.2 = (bf16[512,256]{1,0:T(8,128)(2,1)S(1)}, bf16[512,256]{1,0:T(8,128)(2,1)S(1)}, bf16[512,256]{1,0:T(8,128)(2,1)S(1)}, bf16[512,256]{1,0:T(8,128)(2,1)S(1)}) custom-call(s32[1,128]{1,0:T(1,128)S(1)} %broadcast_in_dim.12.lengths, bf16[4,256,256]{2,1,0:T(8,128)(2,1)S(1)} %collective-permute-done.8.qd, bf16[4,272,256]{2,1,0:T(8,128)(2,1)S(1)} %get-tuple-element.57.kvo, ...), custom_call_target="tpu_custom_call" | custom-call | flops 4000000000 | bytes 2097152 | tf_op jit(solution)/shard_map/columns/pallas_call | solution.py:360
  50.0 1.5 %collective-permute-start.18 = (bf16[512,256]{1,0:T(8,128)(2,1)S(1)}, bf16[512,256]{1,0:T(8,128)(2,1)S(1)}, u32[]{:S(2)}, u32[]{:S(2)}) collective-permute-start(bf16[512,256]{1,0:T(8,128)(2,1)S(1)} %get-tuple-element.82), channel_id=1, source_target_pairs={{0,2},{2,0},{4,6},{6,4},{8,10},{10,8},{12,14},{14,12},{16,18},{18,... | collective-permute-start | bytes 786440 | tf_op jit(solution)/shard_map/ppermute | solution.py:317
  51.5 0.6 collective-permute-start.19
  52.1 1.5 %collective-permute-start.20 = (bf16[512,256]{1,0:T(8,128)(2,1)S(1)}, bf16[512,256]{1,0:T(8,128)(2,1)S(1)}, u32[]{:S(2)}, u32[]{:S(2)}) collective-permute-start(bf16[512,256]{1,0:T(8,128)(2,1)S(1)} %get-tuple-element.84), channel_id=1, source_target_pairs={{0,6},{2,4},{4,2},{6,0},{8,14},{10,12},{12,10},{14,8},{16,22},{18,... | collective-permute-start | bytes 786440 | tf_op jit(solution)/shard_map/ppermute | solution.py:317
  53.6 1.6 %collective-permute-start.10 = (f32[8,128]{1,0:T(8,128)S(1)}, f32[8,128]{1,0:T(8,128)S(1)}, u32[]{:S(2)}, u32[]{:S(2)}) collective-permute-start(f32[8,128]{1,0:T(8,128)S(1)} %get-tuple-element.69.a), channel_id=1, source_target_pairs={{0,8},{2,10},{4,12},{6,14},{8,0},{10,2},{12,4},{14,6},{16,24},{18,... | collective-permute-start | bytes 12296 | tf_op jit(solution)/shard_map/ppermute | solution.py:317
  55.1 0.0 collective-permute-done.13.qd
  55.1 1.3 %collective-permute-start.14 = (f32[2,2,512]{2,1,0:T(2,128)S(1)}, f32[2,2,512]{2,1,0:T(2,128)S(1)}, u32[]{:S(2)}, u32[]{:S(2)}) collective-permute-start(f32[2,2,512]{2,1,0:T(2,128)S(1)} %get-tuple-element.71), channel_id=1, source_target_pairs={{8,0},{10,2},{12,4},{14,6},{16,8},{18,10},{20,12},{22,14},{24,16},... | collective-permute-start | bytes 24584 | tf_op jit(solution)/shard_map/ppermute | solution.py:323
  56.4 0.8 %collective-permute-done.10.b = f32[8,128]{1,0:T(8,128)S(1)} collective-permute-done((f32[8,128]{1,0:T(8,128)S(1)}, f32[8,128]{1,0:T(8,128)S(1)}, u32[]{:S(2)}, u32[]{:S(2)}) %collective-permute-start.10) | collective-permute-done | bytes 4128 | tf_op jit(solution)/shard_map/ppermute | solution.py:317
  57.2 2.6 %collective-permute-start.11 = (f32[8,128]{1,0:T(8,128)S(1)}, f32[8,128]{1,0:T(8,128)S(1)}, u32[]{:S(2)}, u32[]{:S(2)}) collective-permute-start(f32[8,128]{1,0:T(8,128)S(1)} %add.3.a), channel_id=1, source_target_pairs={{0,16},{2,18},{4,20},{6,22},{8,24},{10,26},{12,28},{14,30},{16,0},... | collective-permute-start | bytes 12296 | tf_op jit(solution)/shard_map/ppermute | solution.py:317
  59.8 1.9 %collective-permute-done.11.b = f32[8,128]{1,0:T(8,128)S(1)} collective-permute-done((f32[8,128]{1,0:T(8,128)S(1)}, f32[8,128]{1,0:T(8,128)S(1)}, u32[]{:S(2)}, u32[]{:S(2)}) %collective-permute-start.11) | collective-permute-done | bytes 4128 | tf_op jit(solution)/shard_map/ppermute | solution.py:317
  61.7 0.0 collective-permute-start.12
  61.7 0.0 collective-permute-done.14.stats
  61.7 1.4 %columns.3 = (bf16[256,256]{1,0:T(8,128)(2,1)S(1)}, bf16[256,256]{1,0:T(8,128)(2,1)S(1)}, bf16[256,256]{1,0:T(8,128)(2,1)S(1)}, bf16[256,256]{1,0:T(8,128)(2,1)S(1)}) custom-call(s32[1,128]{1,0:T(1,128)S(1)} %broadcast_in_dim.12.lengths, bf16[4,256,256]{2,1,0:T(8,128)(2,1)S(1)} %collective-permute-done.13.qd, ...), custom_call_target="tpu_custom_call" | custom-call | bytes 2097152 | tf_op jit(solution)/shard_map/columns/pallas_call | solution.py:360
  63.1 0.0 collective-permute-done.12.b
  63.2 1.5 %collective-permute-start.15 = (bf16[272,256]{1,0:T(8,128)(2,1)S(1)}, bf16[272,256]{1,0:T(8,128)(2,1)S(1)}, u32[]{:S(2)}, u32[]{:S(2)}) collective-permute-start(bf16[272,256]{1,0:T(8,128)(2,1)S(1)} %get-tuple-element.79), channel_id=1, source_target_pairs={{0,2},{2,0},{4,6},{6,4},{8,10},{10,8},{12,14},{14,12},{16,18},{18,... | collective-permute-start | bytes 417800 | tf_op jit(solution)/shard_map/ppermute | solution.py:317
  64.7 0.6 collective-permute-start.16
  65.2 0.0 collective-permute-done.18.rest_1_
  65.2 1.5 %collective-permute-start.17 = (bf16[272,256]{1,0:T(8,128)(2,1)S(1)}, bf16[272,256]{1,0:T(8,128)(2,1)S(1)}, u32[]{:S(2)}, u32[]{:S(2)}) collective-permute-start(bf16[272,256]{1,0:T(8,128)(2,1)S(1)} %get-tuple-element.81), channel_id=1, source_target_pairs={{0,6},{2,4},{4,2},{6,0},{8,14},{10,12},{12,10},{14,8},{16,22},{18,... | collective-permute-start | bytes 417800 | tf_op jit(solution)/shard_map/ppermute | solution.py:317
  66.7 0.0 collective-permute-done.19.rest_2_
  66.7 0.0 collective-permute-done.20.rest_3_
  66.7 1.1 %unpack.2 = (bf16[1,128,2048]{2,1,0:T(8,128)(2,1)}, bf16[1,128,2048]{2,1,0:T(8,128)(2,1)}, bf16[1,128,2048]{2,1,0:T(8,128)(2,1)}) custom-call(bf16[512,256]{1,0:T(8,128)(2,1)S(1)} %get-tuple-element.68.rest_0_, bf16[512,256]{1,0:T(8,128)(2,1)S(1)} %collective-permute-done.18.rest_1_, bf16[512,256]{1,0:T(8,128)(2,1)S(1)} %collective-permute-done.19.rest_2_, ...), custom_call_target="tpu_custom_call" | custom-call | bytes 2097152 | tf_op jit(solution)/shard_map/unpack/pallas_call | solution.py:454
  67.9 1.8 %collective-permute-done.15.rest_1_ = bf16[272,256]{1,0:T(8,128)(2,1)S(1)} collective-permute-done((bf16[272,256]{1,0:T(8,128)(2,1)S(1)}, bf16[272,256]{1,0:T(8,128)(2,1)S(1)}, u32[]{:S(2)}, u32[]{:S(2)}) %collective-permute-start.15) | collective-permute-done | bytes 139296 | tf_op jit(solution)/shard_map/ppermute | solution.py:317
  69.7 3.7 %collective-permute-done.16.rest_2_ = bf16[272,256]{1,0:T(8,128)(2,1)S(1)} collective-permute-done((bf16[272,256]{1,0:T(8,128)(2,1)S(1)}, bf16[272,256]{1,0:T(8,128)(2,1)S(1)}, u32[]{:S(2)}, u32[]{:S(2)}) %collective-permute-start.16) | collective-permute-done | bytes 139296 | tf_op jit(solution)/shard_map/ppermute | solution.py:317
  73.4 0.0 collective-permute-done.17.rest_3_
  73.4 0.8 %unpack.3 = (bf16[1,128,2048]{2,1,0:T(8,128)(2,1)}, bf16[1,128,2048]{2,1,0:T(8,128)(2,1)}, bf16[1,128,2048]{2,1,0:T(8,128)(2,1)}, f32[16,64]{1,0:T(8,128)}) custom-call(bf16[272,256]{1,0:T(8,128)(2,1)S(1)} %get-tuple-element.78.rest_4_.rest_0_, ...), custom_call_target="tpu_custom_call", output_to_operand_aliasing={{0}: (4, {}), {1}: (5, {}), {2}: (6, {})} | custom-call | bytes 2097152 | tf_op jit(solution)/shard_map/unpack/pallas_call | solution.py:454
  (6 shorter events, 0.1 us)
Async XLA Ops:
  1.9 10.3 %collective-permute-start.4 = (bf16[528,256]{1,0:T(8,128)(2,1)S(1)}, bf16[528,256]{1,0:T(8,128)(2,1)S(1)}, u32[]{:S(2)}, u32[]{:S(2)}) collective-permute-start(bf16[528,256]{1,0:T(8,128)(2,1)S(1)} %get-tuple-element.53), channel_id=1, source_target_pairs={{0,2},{2,0},{4,6},{6,4},{8,10},{10,8},{12,14},{14,12},{16,18},{18,... | collective-permute-start | bytes 811016 | tf_op jit(solution)/shard_map/ppermute | solution.py:317
  4.9 15.2 %collective-permute-start.5 = (bf16[528,256]{1,0:T(8,128)(2,1)S(1)}, bf16[528,256]{1,0:T(8,128)(2,1)S(1)}, u32[]{:S(2)}, u32[]{:S(2)}) collective-permute-start(bf16[528,256]{1,0:T(8,128)(2,1)S(1)} %get-tuple-element.54), channel_id=1, source_target_pairs={{0,4},{2,6},{4,0},{6,2},{8,12},{10,14},{12,8},{14,10},{16,20},{18,... | collective-permute-start | bytes 811016 | tf_op jit(solution)/shard_map/ppermute | solution.py:317
  6.5 13.7 %collective-permute-start.6 = (bf16[528,256]{1,0:T(8,128)(2,1)S(1)}, bf16[528,256]{1,0:T(8,128)(2,1)S(1)}, u32[]{:S(2)}, u32[]{:S(2)}) collective-permute-start(bf16[528,256]{1,0:T(8,128)(2,1)S(1)} %get-tuple-element.55), channel_id=1, source_target_pairs={{0,6},{2,4},{4,2},{6,0},{8,14},{10,12},{12,10},{14,8},{16,22},{18,... | collective-permute-start | bytes 811016 | tf_op jit(solution)/shard_map/ppermute | solution.py:317
  8.0 17.0 %collective-permute-start = (bf16[512,256]{1,0:T(8,128)(2,1)S(1)}, bf16[512,256]{1,0:T(8,128)(2,1)S(1)}, u32[]{:S(2)}, u32[]{:S(2)}) collective-permute-start(bf16[512,256]{1,0:T(8,128)(2,1)S(1)} %get-tuple-element.47), channel_id=1, source_target_pairs={{0,2},{2,0},{4,6},{6,4},{8,10},{10,8},{12,14},{14,12},{16,18},{18,... | collective-permute-start | bytes 786440 | tf_op jit(solution)/shard_map/ppermute | solution.py:317
  10.0 19.9 %collective-permute-start.1 = (bf16[512,256]{1,0:T(8,128)(2,1)S(1)}, bf16[512,256]{1,0:T(8,128)(2,1)S(1)}, u32[]{:S(2)}, u32[]{:S(2)}) collective-permute-start(bf16[512,256]{1,0:T(8,128)(2,1)S(1)} %get-tuple-element.48), channel_id=1, source_target_pairs={{0,4},{2,6},{4,0},{6,2},{8,12},{10,14},{12,8},{14,10},{16,20},{18,... | collective-permute-start | bytes 786440 | tf_op jit(solution)/shard_map/ppermute | solution.py:317
  12.2 17.7 %collective-permute-start.2 = (bf16[512,256]{1,0:T(8,128)(2,1)S(1)}, bf16[512,256]{1,0:T(8,128)(2,1)S(1)}, u32[]{:S(2)}, u32[]{:S(2)}) collective-permute-start(bf16[512,256]{1,0:T(8,128)(2,1)S(1)} %get-tuple-element.49), channel_id=1, source_target_pairs={{0,6},{2,4},{4,2},{6,0},{8,14},{10,12},{12,10},{14,8},{16,22},{18,... | collective-permute-start | bytes 786440 | tf_op jit(solution)/shard_map/ppermute | solution.py:317
  20.2 16.3 %collective-permute-start.7 = (bf16[4,272,256]{2,1,0:T(8,128)(2,1)S(1)}, bf16[4,272,256]{2,1,0:T(8,128)(2,1)S(1)}, u32[]{:S(2)}, u32[]{:S(2)}) collective-permute-start(bf16[4,272,256]{2,1,0:T(8,128)(2,1)S(1)} %get-tuple-element.57.kvo), channel_id=1, source_target_pairs={{0,8},{2,10},{4,12},{6,14},{8,16},{10,18},{12,20},{14,22},{16,24},... | collective-permute-start | bytes 1671176 | tf_op jit(solution)/shard_map/ppermute | solution.py:323
  23.7 12.7 %collective-permute-start.8 = (bf16[4,256,256]{2,1,0:T(8,128)(2,1)S(1)}, bf16[4,256,256]{2,1,0:T(8,128)(2,1)S(1)}, u32[]{:S(2)}, u32[]{:S(2)}) collective-permute-start(bf16[4,256,256]{2,1,0:T(8,128)(2,1)S(1)} %get-tuple-element.56.qd), channel_id=1, source_target_pairs={{8,0},{10,2},{12,4},{14,6},{16,8},{18,10},{20,12},{22,14},{24,16},... | collective-permute-start | bytes 1572872 | tf_op jit(solution)/shard_map/ppermute | solution.py:323
  30.0 14.3 %collective-permute-start.3 = (bf16[4,256,256]{2,1,0:T(8,128)(2,1)S(1)}, bf16[4,256,256]{2,1,0:T(8,128)(2,1)S(1)}, u32[]{:S(2)}, u32[]{:S(2)}) collective-permute-start(bf16[4,256,256]{2,1,0:T(8,128)(2,1)S(1)} %get-tuple-element.51.kvo), channel_id=1, source_target_pairs={{0,8},{2,10},{4,12},{6,14},{8,16},{10,18},{12,20},{14,22},{16,24},... | collective-permute-start | bytes 1572872 | tf_op jit(solution)/shard_map/ppermute | solution.py:323
  34.2 2.3 %copy-start = (bf16[16,64]{1,0:T(8,128)(2,1)S(1)}, bf16[16,64]{1,0:T(8,128)(2,1)}, u32[]{:S(2)}) copy-start(bf16[16,64]{1,0:T(8,128)(2,1)} %bias_ref.7) | copy-start | bytes 6148
  34.2 21.0 %collective-permute-start.13 = (bf16[4,256,256]{2,1,0:T(8,128)(2,1)S(1)}, bf16[4,256,256]{2,1,0:T(8,128)(2,1)S(1)}, u32[]{:S(2)}, u32[]{:S(2)}) collective-permute-start(bf16[4,256,256]{2,1,0:T(8,128)(2,1)S(1)} %get-tuple-element.50.qd), channel_id=1, source_target_pairs={{8,0},{10,2},{12,4},{14,6},{16,8},{18,10},{20,12},{22,14},{24,16},... | collective-permute-start | bytes 1572872 | tf_op jit(solution)/shard_map/ppermute | solution.py:323
  39.9 8.7 %collective-permute-start.9 = (f32[2,2,512]{2,1,0:T(2,128)S(1)}, f32[2,2,512]{2,1,0:T(2,128)S(1)}, u32[]{:S(2)}, u32[]{:S(2)}) collective-permute-start(f32[2,2,512]{2,1,0:T(2,128)S(1)} %get-tuple-element.63), channel_id=1, source_target_pairs={{8,0},{10,2},{12,4},{14,6},{16,8},{18,10},{20,12},{22,14},{24,16},... | collective-permute-start | bytes 24584 | tf_op jit(solution)/shard_map/ppermute | solution.py:323
  50.0 15.2 %collective-permute-start.18 = (bf16[512,256]{1,0:T(8,128)(2,1)S(1)}, bf16[512,256]{1,0:T(8,128)(2,1)S(1)}, u32[]{:S(2)}, u32[]{:S(2)}) collective-permute-start(bf16[512,256]{1,0:T(8,128)(2,1)S(1)} %get-tuple-element.82), channel_id=1, source_target_pairs={{0,2},{2,0},{4,6},{6,4},{8,10},{10,8},{12,14},{14,12},{16,18},{18,... | collective-permute-start | bytes 786440 | tf_op jit(solution)/shard_map/ppermute | solution.py:317
  51.5 15.2 %collective-permute-start.19 = (bf16[512,256]{1,0:T(8,128)(2,1)S(1)}, bf16[512,256]{1,0:T(8,128)(2,1)S(1)}, u32[]{:S(2)}, u32[]{:S(2)}) collective-permute-start(bf16[512,256]{1,0:T(8,128)(2,1)S(1)} %get-tuple-element.83), channel_id=1, source_target_pairs={{0,4},{2,6},{4,0},{6,2},{8,12},{10,14},{12,8},{14,10},{16,20},{18,... | collective-permute-start | bytes 786440 | tf_op jit(solution)/shard_map/ppermute | solution.py:317
  52.1 14.7 %collective-permute-start.20 = (bf16[512,256]{1,0:T(8,128)(2,1)S(1)}, bf16[512,256]{1,0:T(8,128)(2,1)S(1)}, u32[]{:S(2)}, u32[]{:S(2)}) collective-permute-start(bf16[512,256]{1,0:T(8,128)(2,1)S(1)} %get-tuple-element.84), channel_id=1, source_target_pairs={{0,6},{2,4},{4,2},{6,0},{8,14},{10,12},{12,10},{14,8},{16,22},{18,... | collective-permute-start | bytes 786440 | tf_op jit(solution)/shard_map/ppermute | solution.py:317
  53.6 3.6 %collective-permute-start.10 = (f32[8,128]{1,0:T(8,128)S(1)}, f32[8,128]{1,0:T(8,128)S(1)}, u32[]{:S(2)}, u32[]{:S(2)}) collective-permute-start(f32[8,128]{1,0:T(8,128)S(1)} %get-tuple-element.69.a), channel_id=1, source_target_pairs={{0,8},{2,10},{4,12},{6,14},{8,0},{10,2},{12,4},{14,6},{16,24},{18,... | collective-permute-start | bytes 12296 | tf_op jit(solution)/shard_map/ppermute | solution.py:317
  55.1 6.6 %collective-permute-start.14 = (f32[2,2,512]{2,1,0:T(2,128)S(1)}, f32[2,2,512]{2,1,0:T(2,128)S(1)}, u32[]{:S(2)}, u32[]{:S(2)}) collective-permute-start(f32[2,2,512]{2,1,0:T(2,128)S(1)} %get-tuple-element.71), channel_id=1, source_target_pairs={{8,0},{10,2},{12,4},{14,6},{16,8},{18,10},{20,12},{22,14},{24,16},... | collective-permute-start | bytes 24584 | tf_op jit(solution)/shard_map/ppermute | solution.py:323
  57.2 4.5 %collective-permute-start.11 = (f32[8,128]{1,0:T(8,128)S(1)}, f32[8,128]{1,0:T(8,128)S(1)}, u32[]{:S(2)}, u32[]{:S(2)}) collective-permute-start(f32[8,128]{1,0:T(8,128)S(1)} %add.3.a), channel_id=1, source_target_pairs={{0,16},{2,18},{4,20},{6,22},{8,24},{10,26},{12,28},{14,30},{16,0},... | collective-permute-start | bytes 12296 | tf_op jit(solution)/shard_map/ppermute | solution.py:317
  61.7 1.4 %collective-permute-start.12 = (f32[8,128]{1,0:T(8,128)S(1)}, f32[8,128]{1,0:T(8,128)S(1)}, u32[]{:S(2)}, u32[]{:S(2)}) collective-permute-start(f32[8,128]{1,0:T(8,128)S(1)} %add.4.a), channel_id=1, source_target_pairs={{0,1},{1,0},{2,3},{3,2},{4,5},{5,4},{6,7},{7,6},{8,9},{9,8},{10,11... | collective-permute-start | bytes 12296 | tf_op jit(solution)/shard_map/ppermute | solution.py:317
  63.2 6.5 %collective-permute-start.15 = (bf16[272,256]{1,0:T(8,128)(2,1)S(1)}, bf16[272,256]{1,0:T(8,128)(2,1)S(1)}, u32[]{:S(2)}, u32[]{:S(2)}) collective-permute-start(bf16[272,256]{1,0:T(8,128)(2,1)S(1)} %get-tuple-element.79), channel_id=1, source_target_pairs={{0,2},{2,0},{4,6},{6,4},{8,10},{10,8},{12,14},{14,12},{16,18},{18,... | collective-permute-start | bytes 417800 | tf_op jit(solution)/shard_map/ppermute | solution.py:317
  64.7 8.8 %collective-permute-start.16 = (bf16[272,256]{1,0:T(8,128)(2,1)S(1)}, bf16[272,256]{1,0:T(8,128)(2,1)S(1)}, u32[]{:S(2)}, u32[]{:S(2)}) collective-permute-start(bf16[272,256]{1,0:T(8,128)(2,1)S(1)} %get-tuple-element.80), channel_id=1, source_target_pairs={{0,4},{2,6},{4,0},{6,2},{8,12},{10,14},{12,8},{14,10},{16,20},{18,... | collective-permute-start | bytes 417800 | tf_op jit(solution)/shard_map/ppermute | solution.py:317
  65.2 8.2 %collective-permute-start.17 = (bf16[272,256]{1,0:T(8,128)(2,1)S(1)}, bf16[272,256]{1,0:T(8,128)(2,1)S(1)}, u32[]{:S(2)}, u32[]{:S(2)}) collective-permute-start(bf16[272,256]{1,0:T(8,128)(2,1)S(1)} %get-tuple-element.81), channel_id=1, source_target_pairs={{0,6},{2,4},{4,2},{6,0},{8,14},{10,12},{12,10},{14,8},{16,22},{18,... | collective-permute-start | bytes 417800 | tf_op jit(solution)/shard_map/ppermute | solution.py:317

commit v8 on v7

--- a/solution.py
+++ b/solution.py
@@ -95,12 +95,13 @@
     return jnp.where(jnp.broadcast_to(row, (tok, tok)).T == lane, 1.0, 0.0).astype(BF16)
 
 
-def bias_rows(bias_ref, head, tok):
+def bias_columns(bias_ref, head, onehots):
     table = bias_ref[...].astype(F32)
     at = lax.broadcasted_iota(jnp.int32, table.shape, 0)
-    row = jnp.sum(jnp.where(at == head, table, 0.0), axis=0, keepdims=True) * (1.0 / FACTOR)
-    high = row.astype(BF16).astype(F32)
-    return jnp.broadcast_to(jnp.concatenate([high, row - high], axis=1), (2 * tok, tok)).astype(BF16)
+    row = jnp.sum(jnp.where(at == head, table, 0.0), axis=0, keepdims=True) * LOG2E
+    row = jnp.concatenate([row, jnp.zeros_like(row)], axis=1)
+    column = jnp.sum(onehots.astype(F32) * row, axis=1, keepdims=True)
+    return jnp.broadcast_to(column, onehots.shape)
 
 
 def three_parts(x):
@@ -130,7 +131,7 @@
 
 
 def rows_kernel(reach, tok, chunk, lengths, qd, kvo, kvp, bias_ref, sums_in, *rest):
-    *onehots, dq_out, dk_out, dv_out, stats_out, sums_out, k_scr, v_scr, kt_scr, acc_scr = rest
+    *onehots, dq_out, dk_out, dv_out, stats_out, sums_out, k_scr, v_scr, kt_scr, acc_scr, bias_scr = rest
     onehots = onehots[0]
     p, plane = place(reach)
     length = lengths[...]
@@ -140,7 +141,6 @@
         rows = slice(blk * tok, (blk + 1) * tok)
         if chunk == 0:
             onehots[rows] = onehot_of(kvp if blk < reach else kvo, p ^ (blk % reach), tok)
-        k_scr[rows, HEAD_DIM:] = onehots[rows]
     per = kvo.shape[2] // HEAD_DIM
     sums_out[...] = sums_in[...]
     shut = jnp.where(plane == 0, HIDDEN, 0.0).astype(F32)
@@ -150,19 +150,19 @@
     def _(h):
         head = pl.ds(pl.multiple_of(h * HEAD_DIM, HEAD_DIM), HEAD_DIM)
         at = chunk * per + h
-        bias = bias_rows(bias_ref, p * (HEADS // reach) + at, tok)
+        bias_scr[...] = bias_columns(bias_ref, p * (HEADS // reach) + at, onehots[...])
         for blk in range(2 * reach):
             rows = slice(blk * tok, (blk + 1) * tok)
             src, slot = (kvp if blk < reach else kvo), p ^ (blk % reach)
             key = src[slot, 0:tok, head]
-            k_scr[rows, :HEAD_DIM] = key
+            k_scr[rows] = key
             kt_scr[:, rows] = key.T
             v_scr[rows] = src[slot, tok : 2 * tok, head]
         acc_scr[...] = jnp.zeros_like(acc_scr)
         for pair in range(0, reach, 2):
             query, grad = query_pair(qd, p, pair, tok, head)
             wide = slice(pair * tok, (pair + reach + 2) * tok)
-            logits = dot_nt(k_scr[wide], jnp.concatenate([query, bias], axis=1))
+            logits = dot_nt(k_scr[wide], query)
             probs_both = dot_nt(v_scr[wide], grad)
             lows, ds_lows = [], []
             for half in range(2):
@@ -171,7 +171,7 @@
                 mine = slice(half * tok, (half + reach + 1) * tok)
                 there = slice(a * tok, (a + 1) * tok)
                 cols = slice(half * tok, (half + 1) * tok)
-                s = logits[mine, cols] * (FACTOR * LOG2E)
+                s = logits[mine, cols] * (FACTOR * LOG2E) + bias_scr[rows]
                 seen = [jnp.where(later, s[:tok], HIDDEN) + shut, s[tok : (reach - a) * tok] + shut]
                 seen += [s[(reach - a) * tok : -tok], jnp.where(later, HIDDEN, s[-tok:])]
                 s = jnp.concatenate([part for part in seen if part.shape[0]], axis=0)
@@ -210,27 +210,26 @@
 
 
 def columns_kernel(reach, tok, chunk, lengths, qd, kvo, onehots, stats, bias_ref, dk_in, dv_in, *rest):
-    k_scr, v_scr, dk_scr, dv_scr = rest[-4:]
-    outs, extras = rest[-4 - reach : -4], rest[: -4 - reach]
+    k_scr, v_scr, dk_scr, dv_scr, bias_scr = rest[-5:]
+    outs, extras = rest[-5 - reach : -5], rest[: -5 - reach]
     p, plane = place(reach)
     length = lengths[...]
     span = reach * tok
-    k_scr[:, HEAD_DIM:] = onehots[span:]
     later, lane = masks(tok)
 
     @pl.loop(0, kvo.shape[2] // HEAD_DIM, unroll=True)
     def _(h):
         head = pl.ds(pl.multiple_of(h * HEAD_DIM, HEAD_DIM), HEAD_DIM)
         at = chunk * (kvo.shape[2] // HEAD_DIM) + h
-        bias = bias_rows(bias_ref, p * (HEADS // reach) + at, tok)
+        bias_scr[...] = bias_columns(bias_ref, p * (HEADS // reach) + at, onehots[span:])
         for blk in range(reach):
             rows = slice(blk * tok, (blk + 1) * tok)
-            k_scr[rows, :HEAD_DIM] = kvo[p ^ blk, 0:tok, head]
+            k_scr[rows] = kvo[p ^ blk, 0:tok, head]
             v_scr[rows] = kvo[p ^ blk, tok : 2 * tok, head]
         for pair in range(0, reach, 2):
             query, grad = query_pair(qd, p, pair, tok, head)
             wide = slice(pair * tok, span)
-            logits = dot_nt(k_scr[wide], jnp.concatenate([query, bias], axis=1))
+            logits = dot_nt(k_scr[wide], query)
             probs_both = dot_nt(v_scr[wide], grad)
             lows, ds_lows = [], []
             for half in range(2):
@@ -240,7 +239,7 @@
                 live = (plane + 1) * span + a * tok + lane < length
                 norm = jnp.where(live, stats[h, 0:1, there], -HIDDEN)
                 delta = stats[h, 1:2, there]
-                s = logits[half * tok :, cols] * (FACTOR * LOG2E)
+                s = logits[half * tok :, cols] * (FACTOR * LOG2E) + bias_scr[a * tok :]
                 weight = jnp.exp2(s - norm)
                 first = jnp.where(later, weight[:tok], 0.0)
                 weight = jnp.concatenate([first, weight[tok:]], axis=0) if a < reach - 1 else first
@@ -383,9 +382,10 @@
         if chunk == 0:
             out = [vmem((2 * span, tok))] + out
         scratch = [
-            pltpu.VMEM((2 * span, 2 * HEAD_DIM), BF16),
+            pltpu.VMEM((2 * span, HEAD_DIM), BF16),
             pltpu.VMEM((2 * span, HEAD_DIM), BF16),
             pltpu.VMEM((HEAD_DIM, 2 * span), BF16),
+            pltpu.VMEM((2 * span, tok), F32),
             pltpu.VMEM((2 * span, tok), F32),
         ]
         kernel = functools.partial(rows_kernel, reach, tok, chunk)
@@ -395,10 +395,11 @@
     def columns_of(chunk, qd, kvo, onehots, stats, dk, dv, *extras):
         out = [vmem(((2 + len(extras)) * tok, width))] * reach
         scratch = [
-            pltpu.VMEM((span, 2 * HEAD_DIM), BF16),
+            pltpu.VMEM((span, HEAD_DIM), BF16),
             pltpu.VMEM((span, HEAD_DIM), BF16),
             pltpu.VMEM((span, HEAD_DIM), F32),
             pltpu.VMEM((span, HEAD_DIM), F32),
+            pltpu.VMEM((span, tok), F32),
         ]
         kernel = functools.partial(columns_kernel, reach, tok, chunk)
         args = (length, qd, kvo, onehots, stats, field_bias, dk, dv, *extras)

time: 74.7 us -> 74.5 us (level)
  transfers between devices with their start and end apart: 21 -> 21, of which waited for: 10 -> 10; matrix products, arithmetic and copies ran while one was open for 0% -> 0% of each run, Pallas kernels for 17% -> 16%
where the time goes in v8:
time: 74.5 us; the launch traced here: 74.1 us
  starting transfers between devices  34.5 us (46%)
  waiting for transfers between devices  24.2 us (32%)
  Pallas kernels  13.9 us (19%)
  between operations  1.45 us (2%)
    ppermute x15, starting transfers between devices, swapped(): lax.ppermute(value, axis, [(source, source ^ mask) for source in range(co...  22.3 us
    ppermute x15, waiting for transfers between devices, swapped(): lax.ppermute(value, axis, [(source, source ^ mask) for source in range(co...  18.8 us
    ppermute x6, starting transfers between devices, passed_along(): lax.ppermute(value, axis, [(source, source + steps) for source in range(f...  12.2 us
    pallas_call x10, Pallas kernels, local(): pl.pallas_call(kernel, in_specs=[VMEM] * len(args), out_specs=[VMEM] * le...  9.16 us
    ppermute x6, waiting for transfers between devices, passed_along(): lax.ppermute(value, axis, [(source, source + steps) for source in range(f...  5.45 us
    pallas_call x2, Pallas kernels, pack(): pl.pallas_call(functools.partial(pack_kernel, reach, tok, width, wanted),...  2.82 us
    pallas_call x2, Pallas kernels, shards(): pl.pallas_call(functools.partial(kernel, reach, tok, group * HEAD_DIM, mo...  1.96 us
  transfers between devices with their start and end apart: 21, of which 10 were waited for; matrix products, arithmetic and copies ran while one was open for 0% of the time, Pallas kernels for 16%

profile of v8, /device:TPU:0, one launch (start us, length us, event | category | flops | bytes accessed | tf_op | source)
XLA Modules:
  0.0 74.1 jit_solution(1990039201988675426)
XLA Ops:
  0.6 1.3 %pack.3 = (bf16[528,256]{1,0:T(8,128)(2,1)S(1)}, bf16[528,256]{1,0:T(8,128)(2,1)S(1)}, bf16[528,256]{1,0:T(8,128)(2,1)S(1)}) custom-call(bf16[1,128,2048]{2,1,0:T(8,128)(2,1)} %q.3, bf16[1,128,2048]{2,1,0:T(8,128)(2,1)} %g.3, bf16[1,128,2048]{2,1,0:T(8,128)(2,1)} %k.3, bf16[1,128,2048]{2,1,0:T(8,128)(2,1)} %v.3, s32[1,128]{1,0:T(1,128)} %fields.3), custom_call_target="tpu_custom_call" | custom-call | bytes 2097152 | tf_op jit(solution)/shard_map/pack/pallas_call | solution.py:344
  1.9 3.0 %collective-permute-start.4 = (bf16[528,256]{1,0:T(8,128)(2,1)S(1)}, bf16[528,256]{1,0:T(8,128)(2,1)S(1)}, u32[]{:S(2)}, u32[]{:S(2)}) collective-permute-start(bf16[528,256]{1,0:T(8,128)(2,1)S(1)} %get-tuple-element.53), channel_id=1, source_target_pairs={{0,2},{2,0},{4,6},{6,4},{8,10},{10,8},{12,14},{14,12},{16,18},{18,... | collective-permute-start | bytes 811016 | tf_op jit(solution)/shard_map/ppermute | solution.py:316
  4.9 1.5 %collective-permute-start.5 = (bf16[528,256]{1,0:T(8,128)(2,1)S(1)}, bf16[528,256]{1,0:T(8,128)(2,1)S(1)}, u32[]{:S(2)}, u32[]{:S(2)}) collective-permute-start(bf16[528,256]{1,0:T(8,128)(2,1)S(1)} %get-tuple-element.54), channel_id=1, source_target_pairs={{0,4},{2,6},{4,0},{6,2},{8,12},{10,14},{12,8},{14,10},{16,20},{18,... | collective-permute-start | bytes 811016 | tf_op jit(solution)/shard_map/ppermute | solution.py:316
  6.5 0.0 collective-permute-start.6
  6.5 1.5 %pack.2 = (bf16[512,256]{1,0:T(8,128)(2,1)S(1)}, bf16[512,256]{1,0:T(8,128)(2,1)S(1)}, bf16[512,256]{1,0:T(8,128)(2,1)S(1)}, bf16[512,256]{1,0:T(8,128)(2,1)S(1)}, bf16[528,256]{1,0:T(8,128)(2,1)S(1)}) custom-call(bf16[1,128,2048]{2,1,0:T(8,128)(2,1)} %q.3, bf16[1,128,2048]{2,1,0:T(8,128)(2,1)} %g.3, bf16[1,128,2048]{2,1,0:T(8,128)(2,1)} %k.3, ...), custom_call_target="tpu_custom_call" | custom-call | bytes 2097152 | tf_op jit(solution)/shard_map/pack/pallas_call | solution.py:344
  8.0 2.0 %collective-permute-start = (bf16[512,256]{1,0:T(8,128)(2,1)S(1)}, bf16[512,256]{1,0:T(8,128)(2,1)S(1)}, u32[]{:S(2)}, u32[]{:S(2)}) collective-permute-start(bf16[512,256]{1,0:T(8,128)(2,1)S(1)} %get-tuple-element.47), channel_id=1, source_target_pairs={{0,2},{2,0},{4,6},{6,4},{8,10},{10,8},{12,14},{14,12},{16,18},{18,... | collective-permute-start | bytes 786440 | tf_op jit(solution)/shard_map/ppermute | solution.py:316
  10.0 1.5 %collective-permute-start.1 = (bf16[512,256]{1,0:T(8,128)(2,1)S(1)}, bf16[512,256]{1,0:T(8,128)(2,1)S(1)}, u32[]{:S(2)}, u32[]{:S(2)}) collective-permute-start(bf16[512,256]{1,0:T(8,128)(2,1)S(1)} %get-tuple-element.48), channel_id=1, source_target_pairs={{0,4},{2,6},{4,0},{6,2},{8,12},{10,14},{12,8},{14,10},{16,20},{18,... | collective-permute-start | bytes 786440 | tf_op jit(solution)/shard_map/ppermute | solution.py:316
  11.5 0.7 collective-permute-done.4.refs_1_
  12.2 3.0 %collective-permute-start.2 = (bf16[512,256]{1,0:T(8,128)(2,1)S(1)}, bf16[512,256]{1,0:T(8,128)(2,1)S(1)}, u32[]{:S(2)}, u32[]{:S(2)}) collective-permute-start(bf16[512,256]{1,0:T(8,128)(2,1)S(1)} %get-tuple-element.49), channel_id=1, source_target_pairs={{0,6},{2,4},{4,2},{6,0},{8,14},{10,12},{12,10},{14,8},{16,22},{18,... | collective-permute-start | bytes 786440 | tf_op jit(solution)/shard_map/ppermute | solution.py:316
  15.3 4.9 %collective-permute-done.5.refs_2_ = bf16[528,256]{1,0:T(8,128)(2,1)S(1)} collective-permute-done((bf16[528,256]{1,0:T(8,128)(2,1)S(1)}, bf16[528,256]{1,0:T(8,128)(2,1)S(1)}, u32[]{:S(2)}, u32[]{:S(2)}) %collective-permute-start.5) | collective-permute-done | bytes 270368 | tf_op jit(solution)/shard_map/ppermute | solution.py:316
  20.1 0.0 collective-permute-done.6.refs_3_
  20.1 0.1 gather.3
  20.2 3.5 %collective-permute-start.7 = (bf16[4,272,256]{2,1,0:T(8,128)(2,1)S(1)}, bf16[4,272,256]{2,1,0:T(8,128)(2,1)S(1)}, u32[]{:S(2)}, u32[]{:S(2)}) collective-permute-start(bf16[4,272,256]{2,1,0:T(8,128)(2,1)S(1)} %get-tuple-element.57.kvo), channel_id=1, source_target_pairs={{0,8},{2,10},{4,12},{6,14},{8,16},{10,18},{12,20},{14,22},{16,24},... | collective-permute-start | bytes 1671176 | tf_op jit(solution)/shard_map/ppermute | solution.py:322
  23.7 1.3 %collective-permute-start.8 = (bf16[4,256,256]{2,1,0:T(8,128)(2,1)S(1)}, bf16[4,256,256]{2,1,0:T(8,128)(2,1)S(1)}, u32[]{:S(2)}, u32[]{:S(2)}) collective-permute-start(bf16[4,256,256]{2,1,0:T(8,128)(2,1)S(1)} %get-tuple-element.56.qd), channel_id=1, source_target_pairs={{8,0},{10,2},{12,4},{14,6},{16,8},{18,10},{20,12},{22,14},{24,16},... | collective-permute-start | bytes 1572872 | tf_op jit(solution)/shard_map/ppermute | solution.py:322
  25.0 0.0 collective-permute-done.refs_1_
  25.1 4.9 %collective-permute-done.1.refs_2_ = bf16[512,256]{1,0:T(8,128)(2,1)S(1)} collective-permute-done((bf16[512,256]{1,0:T(8,128)(2,1)S(1)}, bf16[512,256]{1,0:T(8,128)(2,1)S(1)}, u32[]{:S(2)}, u32[]{:S(2)}) %collective-permute-start.1) | collective-permute-done | bytes 262176 | tf_op jit(solution)/shard_map/ppermute | solution.py:316
  29.9 0.0 collective-permute-done.2.refs_3_
  29.9 0.1 gather.2
  30.0 3.5 %collective-permute-start.3 = (bf16[4,256,256]{2,1,0:T(8,128)(2,1)S(1)}, bf16[4,256,256]{2,1,0:T(8,128)(2,1)S(1)}, u32[]{:S(2)}, u32[]{:S(2)}) collective-permute-start(bf16[4,256,256]{2,1,0:T(8,128)(2,1)S(1)} %get-tuple-element.51.kvo), channel_id=1, source_target_pairs={{0,8},{2,10},{4,12},{6,14},{8,16},{10,18},{12,20},{14,22},{16,24},... | collective-permute-start | bytes 1572872 | tf_op jit(solution)/shard_map/ppermute | solution.py:322
  34.2 0.0 copy-start
  34.2 1.3 %collective-permute-start.13 = (bf16[4,256,256]{2,1,0:T(8,128)(2,1)S(1)}, bf16[4,256,256]{2,1,0:T(8,128)(2,1)S(1)}, u32[]{:S(2)}, u32[]{:S(2)}) collective-permute-start(bf16[4,256,256]{2,1,0:T(8,128)(2,1)S(1)} %get-tuple-element.50.qd), channel_id=1, source_target_pairs={{8,0},{10,2},{12,4},{14,6},{16,8},{18,10},{20,12},{22,14},{24,16},... | collective-permute-start | bytes 1572872 | tf_op jit(solution)/shard_map/ppermute | solution.py:322
  35.5 1.0 %collective-permute-done.8.qd = bf16[4,256,256]{2,1,0:T(8,128)(2,1)S(1)} collective-permute-done((bf16[4,256,256]{2,1,0:T(8,128)(2,1)S(1)}, bf16[4,256,256]{2,1,0:T(8,128)(2,1)S(1)}, u32[]{:S(2)}, u32[]{:S(2)}) %collective-permute-start.8) | collective-permute-done | bytes 524320 | tf_op jit(solution)/shard_map/ppermute | solution.py:322
  36.5 0.0 collective-permute-done.7.kvp
  36.5 0.0 copy-done
  36.5 3.2 %rows.2 = (bf16[1024,128]{1,0:T(8,128)(2,1)S(1)}, bf16[4,128,256]{2,1,0:T(8,128)(2,1)S(1)}, f32[512,256]{1,0:T(8,128)S(1)}, f32[512,256]{1,0:T(8,128)S(1)}, f32[...) custom-call(s32[1,128]{1,0:T(1,128)S(1)} %broadcast_in_dim.12.lengths, bf16[4,256,256]{2,1,0:T(8,128)(2,1)S(1)} %get-tuple-element.56.qd, ...), custom_call_target="tpu_custom_call" | custom-call | flops 2000000000 | bytes 2097152 | tf_op jit(solution)/shard_map/rows/pallas_call | solution.py:359
  39.7 1.3 %collective-permute-start.9 = (f32[2,2,512]{2,1,0:T(2,128)S(1)}, f32[2,2,512]{2,1,0:T(2,128)S(1)}, u32[]{:S(2)}, u32[]{:S(2)}) collective-permute-start(f32[2,2,512]{2,1,0:T(2,128)S(1)} %get-tuple-element.63), channel_id=1, source_target_pairs={{8,0},{10,2},{12,4},{14,6},{16,8},{18,10},{20,12},{22,14},{24,16},... | collective-permute-start | bytes 24584 | tf_op jit(solution)/shard_map/ppermute | solution.py:322
  41.0 3.3 %collective-permute-done.3.kvp = bf16[4,256,256]{2,1,0:T(8,128)(2,1)S(1)} collective-permute-done((bf16[4,256,256]{2,1,0:T(8,128)(2,1)S(1)}, bf16[4,256,256]{2,1,0:T(8,128)(2,1)S(1)}, u32[]{:S(2)}, u32[]{:S(2)}) %collective-permute-start.3) | collective-permute-done | bytes 524320 | tf_op jit(solution)/shard_map/ppermute | solution.py:322
  44.3 3.2 %rows.3 = (bf16[4,128,256]{2,1,0:T(8,128)(2,1)S(1)}, f32[512,256]{1,0:T(8,128)S(1)}, f32[512,256]{1,0:T(8,128)S(1)}, f32[2,2,512]{2,1,0:T(2,128)S(1)}, f32[8,128]{1,0:T(8,128)S(1)}) custom-call(s32[1,128]{1,0:T(1,128)S(1)} %broadcast_in_dim.12.lengths, bf16[4,256,256]{2,1,0:T(8,128)(2,1)S(1)} %get-tuple-element.50.qd, ...), custom_call_target="tpu_custom_call" | custom-call | flops 2000000000 | bytes 2097152 | tf_op jit(solution)/shard_map/rows/pallas_call | solution.py:359
  47.4 1.1 %collective-permute-done.9.stats = f32[2,2,512]{2,1,0:T(2,128)S(1)} collective-permute-done((f32[2,2,512]{2,1,0:T(2,128)S(1)}, f32[2,2,512]{2,1,0:T(2,128)S(1)}, u32[]{:S(2)}, u32[]{:S(2)}) %collective-permute-start.9) | collective-permute-done | bytes 8224 | tf_op jit(solution)/shard_map/ppermute | solution.py:322
  48.6 1.3 %columns.2 = (bf16[512,256]{1,0:T(8,128)(2,1)S(1)}, bf16[512,256]{1,0:T(8,128)(2,1)S(1)}, bf16[512,256]{1,0:T(8,128)(2,1)S(1)}, bf16[512,256]{1,0:T(8,128)(2,1)S(1)}) custom-call(s32[1,128]{1,0:T(1,128)S(1)} %broadcast_in_dim.12.lengths, bf16[4,256,256]{2,1,0:T(8,128)(2,1)S(1)} %collective-permute-done.8.qd, bf16[4,272,256]{2,1,0:T(8,128)(2,1)S(1)} %get-tuple-element.57.kvo, ...), custom_call_target="tpu_custom_call" | custom-call | flops 4000000000 | bytes 2097152 | tf_op jit(solution)/shard_map/columns/pallas_call | solution.py:359
  49.9 1.5 %collective-permute-start.18 = (bf16[512,256]{1,0:T(8,128)(2,1)S(1)}, bf16[512,256]{1,0:T(8,128)(2,1)S(1)}, u32[]{:S(2)}, u32[]{:S(2)}) collective-permute-start(bf16[512,256]{1,0:T(8,128)(2,1)S(1)} %get-tuple-element.82), channel_id=1, source_target_pairs={{0,2},{2,0},{4,6},{6,4},{8,10},{10,8},{12,14},{14,12},{16,18},{18,... | collective-permute-start | bytes 786440 | tf_op jit(solution)/shard_map/ppermute | solution.py:316
  51.4 0.6 collective-permute-start.19
  52.0 1.5 %collective-permute-start.20 = (bf16[512,256]{1,0:T(8,128)(2,1)S(1)}, bf16[512,256]{1,0:T(8,128)(2,1)S(1)}, u32[]{:S(2)}, u32[]{:S(2)}) collective-permute-start(bf16[512,256]{1,0:T(8,128)(2,1)S(1)} %get-tuple-element.84), channel_id=1, source_target_pairs={{0,6},{2,4},{4,2},{6,0},{8,14},{10,12},{12,10},{14,8},{16,22},{18,... | collective-permute-start | bytes 786440 | tf_op jit(solution)/shard_map/ppermute | solution.py:316
  53.5 1.5 %collective-permute-start.10 = (f32[8,128]{1,0:T(8,128)S(1)}, f32[8,128]{1,0:T(8,128)S(1)}, u32[]{:S(2)}, u32[]{:S(2)}) collective-permute-start(f32[8,128]{1,0:T(8,128)S(1)} %get-tuple-element.69.a), channel_id=1, source_target_pairs={{0,8},{2,10},{4,12},{6,14},{8,0},{10,2},{12,4},{14,6},{16,24},{18,... | collective-permute-start | bytes 12296 | tf_op jit(solution)/shard_map/ppermute | solution.py:316
  55.0 0.0 collective-permute-done.13.qd
  55.0 1.3 %collective-permute-start.14 = (f32[2,2,512]{2,1,0:T(2,128)S(1)}, f32[2,2,512]{2,1,0:T(2,128)S(1)}, u32[]{:S(2)}, u32[]{:S(2)}) collective-permute-start(f32[2,2,512]{2,1,0:T(2,128)S(1)} %get-tuple-element.71), channel_id=1, source_target_pairs={{8,0},{10,2},{12,4},{14,6},{16,8},{18,10},{20,12},{22,14},{24,16},... | collective-permute-start | bytes 24584 | tf_op jit(solution)/shard_map/ppermute | solution.py:322
  56.3 0.8 %collective-permute-done.10.b = f32[8,128]{1,0:T(8,128)S(1)} collective-permute-done((f32[8,128]{1,0:T(8,128)S(1)}, f32[8,128]{1,0:T(8,128)S(1)}, u32[]{:S(2)}, u32[]{:S(2)}) %collective-permute-start.10) | collective-permute-done | bytes 4128 | tf_op jit(solution)/shard_map/ppermute | solution.py:316
  57.1 2.6 %collective-permute-start.11 = (f32[8,128]{1,0:T(8,128)S(1)}, f32[8,128]{1,0:T(8,128)S(1)}, u32[]{:S(2)}, u32[]{:S(2)}) collective-permute-start(f32[8,128]{1,0:T(8,128)S(1)} %add.3.a), channel_id=1, source_target_pairs={{0,16},{2,18},{4,20},{6,22},{8,24},{10,26},{12,28},{14,30},{16,0},... | collective-permute-start | bytes 12296 | tf_op jit(solution)/shard_map/ppermute | solution.py:316
  59.6 1.9 %collective-permute-done.11.b = f32[8,128]{1,0:T(8,128)S(1)} collective-permute-done((f32[8,128]{1,0:T(8,128)S(1)}, f32[8,128]{1,0:T(8,128)S(1)}, u32[]{:S(2)}, u32[]{:S(2)}) %collective-permute-start.11) | collective-permute-done | bytes 4128 | tf_op jit(solution)/shard_map/ppermute | solution.py:316
  61.6 0.0 collective-permute-start.12
  61.6 0.0 collective-permute-done.14.stats
  61.6 1.3 %columns.3 = (bf16[256,256]{1,0:T(8,128)(2,1)S(1)}, bf16[256,256]{1,0:T(8,128)(2,1)S(1)}, bf16[256,256]{1,0:T(8,128)(2,1)S(1)}, bf16[256,256]{1,0:T(8,128)(2,1)S(1)}) custom-call(s32[1,128]{1,0:T(1,128)S(1)} %broadcast_in_dim.12.lengths, bf16[4,256,256]{2,1,0:T(8,128)(2,1)S(1)} %collective-permute-done.13.qd, ...), custom_call_target="tpu_custom_call" | custom-call | bytes 2097152 | tf_op jit(solution)/shard_map/columns/pallas_call | solution.py:359
  62.9 0.0 collective-permute-done.12.b
  63.0 1.5 %collective-permute-start.15 = (bf16[272,256]{1,0:T(8,128)(2,1)S(1)}, bf16[272,256]{1,0:T(8,128)(2,1)S(1)}, u32[]{:S(2)}, u32[]{:S(2)}) collective-permute-start(bf16[272,256]{1,0:T(8,128)(2,1)S(1)} %get-tuple-element.79), channel_id=1, source_target_pairs={{0,2},{2,0},{4,6},{6,4},{8,10},{10,8},{12,14},{14,12},{16,18},{18,... | collective-permute-start | bytes 417800 | tf_op jit(solution)/shard_map/ppermute | solution.py:316
  64.5 0.6 collective-permute-start.16
  65.1 0.0 collective-permute-done.18.rest_1_
  65.1 1.5 %collective-permute-start.17 = (bf16[272,256]{1,0:T(8,128)(2,1)S(1)}, bf16[272,256]{1,0:T(8,128)(2,1)S(1)}, u32[]{:S(2)}, u32[]{:S(2)}) collective-permute-start(bf16[272,256]{1,0:T(8,128)(2,1)S(1)} %get-tuple-element.81), channel_id=1, source_target_pairs={{0,6},{2,4},{4,2},{6,0},{8,14},{10,12},{12,10},{14,8},{16,22},{18,... | collective-permute-start | bytes 417800 | tf_op jit(solution)/shard_map/ppermute | solution.py:316
  66.5 0.0 collective-permute-done.19.rest_2_
  66.5 0.0 collective-permute-done.20.rest_3_
  66.6 1.1 %unpack.2 = (bf16[1,128,2048]{2,1,0:T(8,128)(2,1)}, bf16[1,128,2048]{2,1,0:T(8,128)(2,1)}, bf16[1,128,2048]{2,1,0:T(8,128)(2,1)}) custom-call(bf16[512,256]{1,0:T(8,128)(2,1)S(1)} %get-tuple-element.68.rest_0_, bf16[512,256]{1,0:T(8,128)(2,1)S(1)} %collective-permute-done.18.rest_1_, bf16[512,256]{1,0:T(8,128)(2,1)S(1)} %collective-permute-done.19.rest_2_, ...), custom_call_target="tpu_custom_call" | custom-call | bytes 2097152 | tf_op jit(solution)/shard_map/unpack/pallas_call | solution.py:455
  67.7 1.8 %collective-permute-done.15.rest_1_ = bf16[272,256]{1,0:T(8,128)(2,1)S(1)} collective-permute-done((bf16[272,256]{1,0:T(8,128)(2,1)S(1)}, bf16[272,256]{1,0:T(8,128)(2,1)S(1)}, u32[]{:S(2)}, u32[]{:S(2)}) %collective-permute-start.15) | collective-permute-done | bytes 139296 | tf_op jit(solution)/shard_map/ppermute | solution.py:316
  69.5 3.8 %collective-permute-done.16.rest_2_ = bf16[272,256]{1,0:T(8,128)(2,1)S(1)} collective-permute-done((bf16[272,256]{1,0:T(8,128)(2,1)S(1)}, bf16[272,256]{1,0:T(8,128)(2,1)S(1)}, u32[]{:S(2)}, u32[]{:S(2)}) %collective-permute-start.16) | collective-permute-done | bytes 139296 | tf_op jit(solution)/shard_map/ppermute | solution.py:316
  73.3 0.0 collective-permute-done.17.rest_3_
  73.3 0.8 %unpack.3 = (bf16[1,128,2048]{2,1,0:T(8,128)(2,1)}, bf16[1,128,2048]{2,1,0:T(8,128)(2,1)}, bf16[1,128,2048]{2,1,0:T(8,128)(2,1)}, f32[16,64]{1,0:T(8,128)}) custom-call(bf16[272,256]{1,0:T(8,128)(2,1)S(1)} %get-tuple-element.78.rest_4_.rest_0_, ...), custom_call_target="tpu_custom_call", output_to_operand_aliasing={{0}: (4, {}), {1}: (5, {}), {2}: (6, {})} | custom-call | bytes 2097152 | tf_op jit(solution)/shard_map/unpack/pallas_call | solution.py:455
  (6 shorter events, 0.1 us)
Async XLA Ops:
  1.9 10.3 %collective-permute-start.4 = (bf16[528,256]{1,0:T(8,128)(2,1)S(1)}, bf16[528,256]{1,0:T(8,128)(2,1)S(1)}, u32[]{:S(2)}, u32[]{:S(2)}) collective-permute-start(bf16[528,256]{1,0:T(8,128)(2,1)S(1)} %get-tuple-element.53), channel_id=1, source_target_pairs={{0,2},{2,0},{4,6},{6,4},{8,10},{10,8},{12,14},{14,12},{16,18},{18,... | collective-permute-start | bytes 811016 | tf_op jit(solution)/shard_map/ppermute | solution.py:316
  4.9 15.2 %collective-permute-start.5 = (bf16[528,256]{1,0:T(8,128)(2,1)S(1)}, bf16[528,256]{1,0:T(8,128)(2,1)S(1)}, u32[]{:S(2)}, u32[]{:S(2)}) collective-permute-start(bf16[528,256]{1,0:T(8,128)(2,1)S(1)} %get-tuple-element.54), channel_id=1, source_target_pairs={{0,4},{2,6},{4,0},{6,2},{8,12},{10,14},{12,8},{14,10},{16,20},{18,... | collective-permute-start | bytes 811016 | tf_op jit(solution)/shard_map/ppermute | solution.py:316
  6.5 13.7 %collective-permute-start.6 = (bf16[528,256]{1,0:T(8,128)(2,1)S(1)}, bf16[528,256]{1,0:T(8,128)(2,1)S(1)}, u32[]{:S(2)}, u32[]{:S(2)}) collective-permute-start(bf16[528,256]{1,0:T(8,128)(2,1)S(1)} %get-tuple-element.55), channel_id=1, source_target_pairs={{0,6},{2,4},{4,2},{6,0},{8,14},{10,12},{12,10},{14,8},{16,22},{18,... | collective-permute-start | bytes 811016 | tf_op jit(solution)/shard_map/ppermute | solution.py:316
  8.0 17.0 %collective-permute-start = (bf16[512,256]{1,0:T(8,128)(2,1)S(1)}, bf16[512,256]{1,0:T(8,128)(2,1)S(1)}, u32[]{:S(2)}, u32[]{:S(2)}) collective-permute-start(bf16[512,256]{1,0:T(8,128)(2,1)S(1)} %get-tuple-element.47), channel_id=1, source_target_pairs={{0,2},{2,0},{4,6},{6,4},{8,10},{10,8},{12,14},{14,12},{16,18},{18,... | collective-permute-start | bytes 786440 | tf_op jit(solution)/shard_map/ppermute | solution.py:316
  10.0 19.9 %collective-permute-start.1 = (bf16[512,256]{1,0:T(8,128)(2,1)S(1)}, bf16[512,256]{1,0:T(8,128)(2,1)S(1)}, u32[]{:S(2)}, u32[]{:S(2)}) collective-permute-start(bf16[512,256]{1,0:T(8,128)(2,1)S(1)} %get-tuple-element.48), channel_id=1, source_target_pairs={{0,4},{2,6},{4,0},{6,2},{8,12},{10,14},{12,8},{14,10},{16,20},{18,... | collective-permute-start | bytes 786440 | tf_op jit(solution)/shard_map/ppermute | solution.py:316
  12.2 17.7 %collective-permute-start.2 = (bf16[512,256]{1,0:T(8,128)(2,1)S(1)}, bf16[512,256]{1,0:T(8,128)(2,1)S(1)}, u32[]{:S(2)}, u32[]{:S(2)}) collective-permute-start(bf16[512,256]{1,0:T(8,128)(2,1)S(1)} %get-tuple-element.49), channel_id=1, source_target_pairs={{0,6},{2,4},{4,2},{6,0},{8,14},{10,12},{12,10},{14,8},{16,22},{18,... | collective-permute-start | bytes 786440 | tf_op jit(solution)/shard_map/ppermute | solution.py:316
  20.2 16.3 %collective-permute-start.7 = (bf16[4,272,256]{2,1,0:T(8,128)(2,1)S(1)}, bf16[4,272,256]{2,1,0:T(8,128)(2,1)S(1)}, u32[]{:S(2)}, u32[]{:S(2)}) collective-permute-start(bf16[4,272,256]{2,1,0:T(8,128)(2,1)S(1)} %get-tuple-element.57.kvo), channel_id=1, source_target_pairs={{0,8},{2,10},{4,12},{6,14},{8,16},{10,18},{12,20},{14,22},{16,24},... | collective-permute-start | bytes 1671176 | tf_op jit(solution)/shard_map/ppermute | solution.py:322
  23.7 12.7 %collective-permute-start.8 = (bf16[4,256,256]{2,1,0:T(8,128)(2,1)S(1)}, bf16[4,256,256]{2,1,0:T(8,128)(2,1)S(1)}, u32[]{:S(2)}, u32[]{:S(2)}) collective-permute-start(bf16[4,256,256]{2,1,0:T(8,128)(2,1)S(1)} %get-tuple-element.56.qd), channel_id=1, source_target_pairs={{8,0},{10,2},{12,4},{14,6},{16,8},{18,10},{20,12},{22,14},{24,16},... | collective-permute-start | bytes 1572872 | tf_op jit(solution)/shard_map/ppermute | solution.py:322
  30.0 14.3 %collective-permute-start.3 = (bf16[4,256,256]{2,1,0:T(8,128)(2,1)S(1)}, bf16[4,256,256]{2,1,0:T(8,128)(2,1)S(1)}, u32[]{:S(2)}, u32[]{:S(2)}) collective-permute-start(bf16[4,256,256]{2,1,0:T(8,128)(2,1)S(1)} %get-tuple-element.51.kvo), channel_id=1, source_target_pairs={{0,8},{2,10},{4,12},{6,14},{8,16},{10,18},{12,20},{14,22},{16,24},... | collective-permute-start | bytes 1572872 | tf_op jit(solution)/shard_map/ppermute | solution.py:322
  34.2 2.3 %copy-start = (bf16[16,64]{1,0:T(8,128)(2,1)S(1)}, bf16[16,64]{1,0:T(8,128)(2,1)}, u32[]{:S(2)}) copy-start(bf16[16,64]{1,0:T(8,128)(2,1)} %bias_ref.7) | copy-start | bytes 6148
  34.2 20.8 %collective-permute-start.13 = (bf16[4,256,256]{2,1,0:T(8,128)(2,1)S(1)}, bf16[4,256,256]{2,1,0:T(8,128)(2,1)S(1)}, u32[]{:S(2)}, u32[]{:S(2)}) collective-permute-start(bf16[4,256,256]{2,1,0:T(8,128)(2,1)S(1)} %get-tuple-element.50.qd), channel_id=1, source_target_pairs={{8,0},{10,2},{12,4},{14,6},{16,8},{18,10},{20,12},{22,14},{24,16},... | collective-permute-start | bytes 1572872 | tf_op jit(solution)/shard_map/ppermute | solution.py:322
  39.7 8.9 %collective-permute-start.9 = (f32[2,2,512]{2,1,0:T(2,128)S(1)}, f32[2,2,512]{2,1,0:T(2,128)S(1)}, u32[]{:S(2)}, u32[]{:S(2)}) collective-permute-start(f32[2,2,512]{2,1,0:T(2,128)S(1)} %get-tuple-element.63), channel_id=1, source_target_pairs={{8,0},{10,2},{12,4},{14,6},{16,8},{18,10},{20,12},{22,14},{24,16},... | collective-permute-start | bytes 24584 | tf_op jit(solution)/shard_map/ppermute | solution.py:322
  49.9 15.2 %collective-permute-start.18 = (bf16[512,256]{1,0:T(8,128)(2,1)S(1)}, bf16[512,256]{1,0:T(8,128)(2,1)S(1)}, u32[]{:S(2)}, u32[]{:S(2)}) collective-permute-start(bf16[512,256]{1,0:T(8,128)(2,1)S(1)} %get-tuple-element.82), channel_id=1, source_target_pairs={{0,2},{2,0},{4,6},{6,4},{8,10},{10,8},{12,14},{14,12},{16,18},{18,... | collective-permute-start | bytes 786440 | tf_op jit(solution)/shard_map/ppermute | solution.py:316
  51.4 15.1 %collective-permute-start.19 = (bf16[512,256]{1,0:T(8,128)(2,1)S(1)}, bf16[512,256]{1,0:T(8,128)(2,1)S(1)}, u32[]{:S(2)}, u32[]{:S(2)}) collective-permute-start(bf16[512,256]{1,0:T(8,128)(2,1)S(1)} %get-tuple-element.83), channel_id=1, source_target_pairs={{0,4},{2,6},{4,0},{6,2},{8,12},{10,14},{12,8},{14,10},{16,20},{18,... | collective-permute-start | bytes 786440 | tf_op jit(solution)/shard_map/ppermute | solution.py:316
  52.0 14.6 %collective-permute-start.20 = (bf16[512,256]{1,0:T(8,128)(2,1)S(1)}, bf16[512,256]{1,0:T(8,128)(2,1)S(1)}, u32[]{:S(2)}, u32[]{:S(2)}) collective-permute-start(bf16[512,256]{1,0:T(8,128)(2,1)S(1)} %get-tuple-element.84), channel_id=1, source_target_pairs={{0,6},{2,4},{4,2},{6,0},{8,14},{10,12},{12,10},{14,8},{16,22},{18,... | collective-permute-start | bytes 786440 | tf_op jit(solution)/shard_map/ppermute | solution.py:316
  53.5 3.6 %collective-permute-start.10 = (f32[8,128]{1,0:T(8,128)S(1)}, f32[8,128]{1,0:T(8,128)S(1)}, u32[]{:S(2)}, u32[]{:S(2)}) collective-permute-start(f32[8,128]{1,0:T(8,128)S(1)} %get-tuple-element.69.a), channel_id=1, source_target_pairs={{0,8},{2,10},{4,12},{6,14},{8,0},{10,2},{12,4},{14,6},{16,24},{18,... | collective-permute-start | bytes 12296 | tf_op jit(solution)/shard_map/ppermute | solution.py:316
  55.0 6.6 %collective-permute-start.14 = (f32[2,2,512]{2,1,0:T(2,128)S(1)}, f32[2,2,512]{2,1,0:T(2,128)S(1)}, u32[]{:S(2)}, u32[]{:S(2)}) collective-permute-start(f32[2,2,512]{2,1,0:T(2,128)S(1)} %get-tuple-element.71), channel_id=1, source_target_pairs={{8,0},{10,2},{12,4},{14,6},{16,8},{18,10},{20,12},{22,14},{24,16},... | collective-permute-start | bytes 24584 | tf_op jit(solution)/shard_map/ppermute | solution.py:322
  57.1 4.5 %collective-permute-start.11 = (f32[8,128]{1,0:T(8,128)S(1)}, f32[8,128]{1,0:T(8,128)S(1)}, u32[]{:S(2)}, u32[]{:S(2)}) collective-permute-start(f32[8,128]{1,0:T(8,128)S(1)} %add.3.a), channel_id=1, source_target_pairs={{0,16},{2,18},{4,20},{6,22},{8,24},{10,26},{12,28},{14,30},{16,0},... | collective-permute-start | bytes 12296 | tf_op jit(solution)/shard_map/ppermute | solution.py:316
  61.6 1.3 %collective-permute-start.12 = (f32[8,128]{1,0:T(8,128)S(1)}, f32[8,128]{1,0:T(8,128)S(1)}, u32[]{:S(2)}, u32[]{:S(2)}) collective-permute-start(f32[8,128]{1,0:T(8,128)S(1)} %add.4.a), channel_id=1, source_target_pairs={{0,1},{1,0},{2,3},{3,2},{4,5},{5,4},{6,7},{7,6},{8,9},{9,8},{10,11... | collective-permute-start | bytes 12296 | tf_op jit(solution)/shard_map/ppermute | solution.py:316
  63.0 6.5 %collective-permute-start.15 = (bf16[272,256]{1,0:T(8,128)(2,1)S(1)}, bf16[272,256]{1,0:T(8,128)(2,1)S(1)}, u32[]{:S(2)}, u32[]{:S(2)}) collective-permute-start(bf16[272,256]{1,0:T(8,128)(2,1)S(1)} %get-tuple-element.79), channel_id=1, source_target_pairs={{0,2},{2,0},{4,6},{6,4},{8,10},{10,8},{12,14},{14,12},{16,18},{18,... | collective-permute-start | bytes 417800 | tf_op jit(solution)/shard_map/ppermute | solution.py:316
  64.5 8.8 %collective-permute-start.16 = (bf16[272,256]{1,0:T(8,128)(2,1)S(1)}, bf16[272,256]{1,0:T(8,128)(2,1)S(1)}, u32[]{:S(2)}, u32[]{:S(2)}) collective-permute-start(bf16[272,256]{1,0:T(8,128)(2,1)S(1)} %get-tuple-element.80), channel_id=1, source_target_pairs={{0,4},{2,6},{4,0},{6,2},{8,12},{10,14},{12,8},{14,10},{16,20},{18,... | collective-permute-start | bytes 417800 | tf_op jit(solution)/shard_map/ppermute | solution.py:316
  65.1 8.2 %collective-permute-start.17 = (bf16[272,256]{1,0:T(8,128)(2,1)S(1)}, bf16[272,256]{1,0:T(8,128)(2,1)S(1)}, u32[]{:S(2)}, u32[]{:S(2)}) collective-permute-start(bf16[272,256]{1,0:T(8,128)(2,1)S(1)} %get-tuple-element.81), channel_id=1, source_target_pairs={{0,6},{2,4},{4,2},{6,0},{8,14},{10,12},{12,10},{14,8},{16,22},{18,... | collective-permute-start | bytes 417800 | tf_op jit(solution)/shard_map/ppermute | solution.py:316
